TPU v7x, 32 devices: a whole 2x2x4 slice. The times are simulated.
32 devices in a mesh: dp: 8 (over y, x, core), tensor: 4 (over z).
Axes of the slice: x: 2, y: 2, z: 4, core: 2. Of those that a mesh axis runs over, the one named last changes fastest.
Arguments:
- tokens: bfloat16 [16384, 1024], P('dp'), may hold values from -6 to 6
- qkv_weight: bfloat16 [3, 1024, 1024], P(None, None, 'tensor'), may hold values from -0.1875 to 0.1875
- out_weight: bfloat16 [1024, 1024], P('tensor'), may hold values from -3 to 3
- gate_up_weight: bfloat16 [2, 1024, 4096], P(None, None, 'tensor'), may hold values from -0.1875 to 0.1875
- down_weight: bfloat16 [4096, 1024], P('tensor'), may hold values from -0.09375 to 0.09375
- norm_gains: float32 [2, 1024], replicated, may hold values from 0.1 to 1.9
- species_weight: float32 [850], replicated, may hold values from 0.3 to 3
- species_ids: int32 [8], P('dp'), may hold values from 0 to 849
- lengths: int32 [8], P('dp'), may hold values from 256 to 2048, as said below
- cotangent: bfloat16 [16384, 1024], P('dp'), may hold values from -6 to 6
Outputs:
- out: float32 [16384, 1024], P(('dp', 'tensor'))
- grad_tokens: float32 [16384, 1024], P(('dp', 'tensor'))
- grad_qkv: float32 [3, 1024, 1024], P(None, 'dp', 'tensor')
- grad_out_proj: float32 [1024, 1024], P('tensor', 'dp')
- grad_gate_up: float32 [2, 1024, 4096], P(None, 'dp', 'tensor')
- grad_down: float32 [4096, 1024], P('tensor', 'dp')
- grad_gains: float32 [2, 1024], replicated
Inputs may be any that keep to these rules, and one draw needn't show every extreme that they name: `lengths`: each window's count of valid leading slots; in every draw some window has 2048 and another 2048 // 8.
All inputs are finite; a program needn't handle non-finite values.
Results may differ from a plain program's by a relative error of at most 0.019.
Values may be sent and summed in bfloat16 or wider, within the bound.
No kernel may reach another device: no remote copies, remote signals or barrier semaphores. Data moves between devices by JAX's collectives and lax.ppermute only.
A program may use at most 192 MiB of HBM per device.

v0:
```python
import jax
import jax.numpy as jnp
from jax import lax
from jax.sharding import PartitionSpec as P

HD = 64
WIN = 2048


EPSILON = 1e-05
NEG_FILL = -1e30


def rms_factor(values):
    return lax.rsqrt(jnp.mean(values * values, axis=-1, keepdims=True) + EPSILON)


def rotary_tables(length, width):
    position = jnp.arange(length).astype(jnp.float32)
    frequency = jnp.power(
        jnp.float32(10000.0), -(jnp.arange(width // 2).astype(jnp.float32) * 2.0) / width
    )
    angles = position[:, None] * frequency[None, :]
    angles = jnp.concatenate([angles, angles], axis=1)
    return (jnp.cos(angles), jnp.sin(angles))


def rotate(values, cosine, sine_part):
    half = values.shape[-1] // 2
    turned = jnp.concatenate([-values[..., half:], values[..., :half]], axis=-1)
    return values * cosine[:, None, :] + turned * sine_part[:, None, :]


def rotate_back(grads, cosine, sine_part):
    half = grads.shape[-1] // 2
    scaled = grads * sine_part[:, None, :]
    return grads * cosine[:, None, :] + jnp.concatenate(
        [scaled[..., half:], -scaled[..., :half]], axis=-1
    )


def masked_scores(query_block, keys, visible, factor):
    scores = (
        jnp.einsum("qhd,khd->hqk", query_block, keys, preferred_element_type=jnp.float32) * factor
    )
    return jnp.where(visible[None, None, :], scores, NEG_FILL)


def attend_forward(queries, keys, values, length, block, factor):
    slots, heads, width = queries.shape
    visible = jnp.arange(slots) < length

    def one_block(query_block):
        scores = masked_scores(query_block, keys, visible, factor)
        peak = jnp.max(scores, axis=-1, keepdims=True)
        expo = jnp.exp(scores - peak)
        total = jnp.sum(expo, axis=-1, keepdims=True)
        probs = expo / total
        attended = jnp.einsum(
            "hqk,khd->qhd", probs.astype(jnp.bfloat16), values, preferred_element_type=jnp.float32
        )
        return (attended, (peak + jnp.log(total))[..., 0])

    attended, log_totals = lax.map(one_block, queries.reshape(slots // block, block, heads, width))
    return (attended.reshape(slots, heads, width), log_totals)


def attend_backward(queries, keys, values, grad_att, log_totals, length, block, factor):
    slots, heads, width = queries.shape
    visible = jnp.arange(slots) < length

    def one_block(carry, inputs):
        key_grad, value_grad = carry
        query_block, grad_block, log_block = inputs
        scores = masked_scores(query_block, keys, visible, factor)
        probs = jnp.exp(scores - log_block[..., None])
        prob_grad = jnp.einsum(
            "qhd,khd->hqk", grad_block, values, preferred_element_type=jnp.float32
        )
        delta = jnp.sum(probs * prob_grad, axis=-1, keepdims=True)
        score_grad = (probs * (prob_grad - delta)).astype(jnp.bfloat16)
        query_grad = (
            jnp.einsum("hqk,khd->qhd", score_grad, keys, preferred_element_type=jnp.float32)
            * factor
        )
        key_grad = (
            key_grad
            + jnp.einsum(
                "hqk,qhd->khd", score_grad, query_block, preferred_element_type=jnp.float32
            )
            * factor
        )
        value_grad = value_grad + jnp.einsum(
            "hqk,qhd->khd",
            probs.astype(jnp.bfloat16),
            grad_block,
            preferred_element_type=jnp.float32,
        )
        return ((key_grad, value_grad), query_grad)

    zeros_kv = jnp.zeros((slots, heads, width), jnp.float32)
    (key_grad, value_grad), query_grads = lax.scan(
        one_block,
        (zeros_kv, zeros_kv),
        (
            queries.reshape(slots // block, block, heads, width),
            grad_att.reshape(slots // block, block, heads, width),
            log_totals,
        ),
    )
    return (query_grads.reshape(slots, heads, width), key_grad, value_grad)


def norm_back(grad_normed, gain, unit, factor):
    scaled = grad_normed * gain
    return factor * (scaled - unit * jnp.mean(scaled * unit, axis=-1, keepdims=True))


def body(
    tokens,
    qkv_weight,
    out_weight,
    gate_up_weight,
    down_weight,
    norm_gains,
    species_weight,
    species_ids,
    lengths,
    cotangent,
):
    rows_all = tokens.shape[0]
    local_width = out_weight.shape[0]
    heads = local_width // HD
    windows = lengths.shape[0]
    parts = lax.axis_size("tensor")
    share = rows_all // parts
    offset = lax.axis_index("tensor") * share
    block = min(512, WIN)
    factor = HD ** (-0.5)
    tok_float = tokens.astype(jnp.float32)
    scale_one = rms_factor(tok_float)
    unit_one = tok_float * scale_one
    normed_one = (unit_one * norm_gains[0]).astype(jnp.bfloat16)
    qkv = jnp.einsum("td,cde->cte", normed_one, qkv_weight, preferred_element_type=jnp.float32)
    cosine, sine_part = rotary_tables(WIN, HD)
    cosine_all = jnp.tile(cosine, (windows, 1))
    sine_all = jnp.tile(sine_part, (windows, 1))
    queries = rotate(qkv[0].reshape(rows_all, heads, HD), cosine_all, sine_all).astype(jnp.bfloat16)
    keys = rotate(qkv[1].reshape(rows_all, heads, HD), cosine_all, sine_all).astype(jnp.bfloat16)
    values = qkv[2].reshape(rows_all, heads, HD).astype(jnp.bfloat16)
    window = 0
    attended_w, log_w = attend_forward(queries, keys, values, lengths[window], block, factor)
    log_list = [log_w]
    att_low = attended_w.reshape(rows_all, local_width).astype(jnp.bfloat16)
    attn_term = lax.psum(jnp.dot(att_low, out_weight, preferred_element_type=jnp.float32), "tensor")
    resid = tok_float + attn_term
    scale_two = rms_factor(resid)
    unit_two = resid * scale_two
    normed_mid = (unit_two * norm_gains[1]).astype(jnp.bfloat16)
    gate_up = jnp.einsum(
        "td,cdf->ctf", normed_mid, gate_up_weight, preferred_element_type=jnp.float32
    )
    gate = gate_up[0]
    upper = gate_up[1]
    sigma = jax.nn.sigmoid(gate)
    activation = gate * sigma
    hidden = (activation * upper).astype(jnp.bfloat16)
    ffn_term = lax.psum(
        jnp.dot(hidden, down_weight, preferred_element_type=jnp.float32).astype(jnp.bfloat16),
        "tensor",
    ).astype(jnp.float32)
    out_rows = lax.dynamic_slice_in_dim(resid + ffn_term, offset, share, 0)
    matches = species_ids[:, None] == jnp.arange(species_weight.shape[0])[None, :]
    picked_weight = jnp.sum(jnp.where(matches, species_weight[None, :], jnp.float32(0.0)), axis=1)
    live = jnp.arange(WIN)[None, :] < lengths[:, None]
    row_weight = jnp.where(live, picked_weight[:, None], jnp.float32(0.0)).reshape(rows_all)
    grad_out = cotangent.astype(jnp.float32) * row_weight[:, None]
    grad_out_low = grad_out.astype(jnp.bfloat16)
    grad_down = jnp.einsum("tf,td->fd", hidden, grad_out_low, preferred_element_type=jnp.float32)
    grad_hidden = jnp.einsum(
        "td,fd->tf", grad_out_low, down_weight, preferred_element_type=jnp.float32
    )
    grad_upper = grad_hidden * activation
    grad_gate = grad_hidden * upper * sigma * (1.0 + gate * (1.0 - sigma))
    grad_stack = jnp.stack([grad_gate, grad_upper]).astype(jnp.bfloat16)
    grad_gu = jnp.einsum("td,ctf->cdf", normed_mid, grad_stack, preferred_element_type=jnp.float32)
    grad_normed_two = lax.psum(
        jnp.einsum(
            "ctf,cdf->td", grad_stack, gate_up_weight, preferred_element_type=jnp.float32
        ).astype(jnp.bfloat16),
        "tensor",
    ).astype(jnp.float32)
    grad_resid = grad_out + norm_back(grad_normed_two, norm_gains[1], unit_two, scale_two)
    gain_two = jnp.sum(
        lax.dynamic_slice_in_dim(grad_normed_two * unit_two, offset, share, 0), axis=0
    )
    grad_resid_share = lax.dynamic_slice_in_dim(grad_resid, offset, share, 0)
    grad_resid_low = grad_resid.astype(jnp.bfloat16)
    grad_out_proj = jnp.einsum(
        "te,td->ed", att_low, grad_resid_low, preferred_element_type=jnp.float32
    )
    grad_att = jnp.einsum(
        "td,ed->te", grad_resid_low, out_weight, preferred_element_type=jnp.float32
    )
    grad_att = grad_att.astype(jnp.bfloat16).reshape(rows_all, heads, HD)
    window = 0
    query_grad, key_grad, value_grad = attend_backward(
        queries, keys, values, grad_att, log_list[window], lengths[window], block, factor
    )
    query_list = rotate_back(query_grad, cosine, sine_part)
    key_list = rotate_back(key_grad, cosine, sine_part)
    grad_qkv_act = (
        jnp.stack([query_list, key_list, value_grad])
        .reshape(3, rows_all, local_width)
        .astype(jnp.bfloat16)
    )
    grad_qkv = jnp.einsum(
        "td,cte->cde", normed_one, grad_qkv_act, preferred_element_type=jnp.float32
    )
    unit_one_share = lax.dynamic_slice_in_dim(unit_one, offset, share, 0)
    scale_one_share = lax.dynamic_slice_in_dim(scale_one, offset, share, 0)
    grad_normed_one = lax.psum(
        jnp.einsum(
            "cte,cde->td", grad_qkv_act, qkv_weight, preferred_element_type=jnp.float32
        ).astype(jnp.bfloat16),
        "tensor",
    ).astype(jnp.float32)
    grad_normed_one_share = lax.dynamic_slice_in_dim(grad_normed_one, offset, share, 0)
    grad_tok_rows = grad_resid_share + norm_back(
        grad_normed_one_share, norm_gains[0], unit_one_share, scale_one_share
    )
    gain_one = jnp.sum(grad_normed_one_share * unit_one_share, axis=0)
    grad_gains = lax.psum(jnp.stack([gain_one, gain_two]), ("dp", "tensor"))
    summed = (
        lax.psum_scatter(
            grad_qkv.astype(jnp.bfloat16), "dp", scatter_dimension=1, tiled=True
        ).astype(jnp.float32),
        lax.psum_scatter(
            grad_out_proj.astype(jnp.bfloat16), "dp", scatter_dimension=1, tiled=True
        ).astype(jnp.float32),
        lax.psum_scatter(
            grad_gu.astype(jnp.bfloat16), "dp", scatter_dimension=1, tiled=True
        ).astype(jnp.float32),
        lax.psum_scatter(
            grad_down.astype(jnp.bfloat16), "dp", scatter_dimension=1, tiled=True
        ).astype(jnp.float32),
    )
    return (out_rows, grad_tok_rows, summed[0], summed[1], summed[2], summed[3], grad_gains)


def solution(mesh):
    in_specs = (
        P("dp", None),
        P(None, None, "tensor"),
        P("tensor", None),
        P(None, None, "tensor"),
        P("tensor", None),
        P(),
        P(),
        P("dp"),
        P("dp"),
        P("dp", None),
    )
    out_specs = (
        P(("dp", "tensor"), None),
        P(("dp", "tensor"), None),
        P(None, "dp", "tensor"),
        P("tensor", "dp"),
        P(None, "dp", "tensor"),
        P("tensor", "dp"),
        P(),
    )
    return jax.shard_map(body, mesh=mesh, in_specs=in_specs, out_specs=out_specs, check_vma=False)
```

profile of v0, /device:TPU:0, one launch (start us, length us, event | category | flops | bytes accessed | tf_op | source)
XLA Modules:
  0.0 1291.1 jit_solution(36644992743285088)
XLA Ops:
  12.7 5.3 convolution_bitcast_fusion.1
  45.7 55.4 %while.30 = (s32[]{:T(128)}, bf16[4,512,4,64]{1,3,2,0:T(8,128)(2,1)}, f32[4,4,512]{2,1,0:T(4,128)S(1)}, bf16[4,512,4,64]{1,3,2,0:T(8,128)(2,1)}, bf16[2048,4,64]...) while((s32[]{:T(128)}, bf16[4,512,4,64]{1,3,2,0:T(8,128)(2,1)}, ...), condition=%wide.region_4.5_spmd.clone.clone, body=%wide.region_1.4_spmd.clone.sunk.clone | while | flops 1124073472 | bytes 65872056 | solution.py:64
  53.7 4.9 fusion.155
  67.5 4.9 fusion.155
  81.3 4.9 fusion.155
  95.1 4.9 fusion.155
  111.7 291.1 %all-reduce.5.cloned.1.call-done = f32[2048,1024]{1,0:T(8,128)} async-done(((f32[2048,1024]{1,0:T(8,128)}), f32[2048,1024]{1,0:T(8,128)}) %all-reduce.5.cloned.1.call-update) | async-done | bytes 8388624 | tf_op jit(solution)/shard_map/psum | solution.py:155
  402.7 7.6 multiply_reduce_fusion.2
  416.8 14.1 %convolution_bitcast_fusion = f32[2,2048,1024]{2,1,0:T(8,128)} fusion(bf16[2,1024,1024]{2,1,0:T(8,128)(2,1)} %param.17, f32[2048,1024]{1,0:T(8,128)S(1)} %broadcast_multiply_fusion, f32[1024]{0:T(1024)S(1)} %bitcast.231), kind=kOutput, calls=%fused_computation.71 | convolution fusion | flops 8594128896 | bytes 29364224 | tf_op jit(solution)/shard_map/td,cdf->ctf/dot_general | solution.py:160
  430.9 16.0 %fusion.53 = (bf16[1,2048,1024]{2,1,0:T(8,128)(2,1)}, bf16[1,2048,1024]{2,1,0:T(8,128)(2,1)}, bf16[2048,1024]{1,0:T(8,128)(2,1)}) fusion(f32[2,2048,1024]{2,1,0:T(8,128)} %convolution_bitcast_fusion, bf16[1024,1024]{1,0:T(8,128)(2,1)S(1)} %copy-done, bf16[2048,1024]{1,0:T(8,128)(2,1)} %param.23, f32[2048]{0:T(1024)S(1)} %fusion.85), kind=kOutput, calls=%fused_computation.79 | convolution fusion | flops 4332716032 | bytes 35659776 | tf_op jit(solution)/shard_map/td,fd->tf/dot_general | solution.py:180
  446.9 13.3 %bitcast_convert_fusion.1 = bf16[2048,1024]{1,0:T(8,128)(2,1)} fusion(bf16[2,1024,1024]{2,1,0:T(8,128)(2,1)S(1)} %copy-done.34, bf16[1,2048,1024]{2,1,0:T(8,128)(2,1)} %get-tuple-element.267, bf16[1,2048,1024]{2,1,0:T(8,128)(2,1)} %get-tuple-element.266), kind=kOutput, calls=%fused_computation.58 | convolution fusion | flops 8596226048 | bytes 16777216 | tf_op jit(solution)/shard_map/ctf,cdf->td/dot_general | solution.py:188
  460.2 9.6 convolution_convert_fusion.2
  479.5 134.8 %all-reduce.7.cloned.1.call-done = bf16[2048,1024]{1,0:T(8,128)(2,1)} async-done(((bf16[2048,1024]{1,0:T(8,128)(2,1)}), bf16[2048,1024]{1,0:T(8,128)(2,1)}) %all-reduce.7.cloned.1.call-update) | async-done | bytes 4194320 | tf_op jit(solution)/shard_map/psum | solution.py:187
  614.3 5.6 multiply_reduce_fusion.1
  621.4 6.3 multiply_add_fusion
  635.2 15.6 %convert_bitcast_fusion = bf16[2,1024,1024]{1,2,0:T(8,128)(2,1)} fusion(bf16[1,2048,1024]{2,1,0:T(8,128)(2,1)} %get-tuple-element.267, bf16[1,2048,1024]{2,1,0:T(8,128)(2,1)} %get-tuple-element.266, f32[2048,1024]{1,0:T(8,128)} %copy-done.11, f32[1024]{0:T(1024)S(1)} %bitcast.234), kind=kOutput, calls=%fused_computation.77 | convolution fusion | flops 8600420352 | bytes 20975616 | tf_op jit(solution)/shard_map/td,ctf->cdf/dot_general | solution.py:186
  650.7 11.4 copy.73
  662.1 5.6 copy.81
  667.7 5.8 convolution_convert_fusion.1
  682.2 176.1 %while.31 = (s32[]{:T(128)}, f32[2048,4,64]{0,2,1:T(8,128)}, f32[2048,4,64]{0,2,1:T(8,128)}, f32[4,512,4,64]{1,3,2,0:T(8,128)}, bf16[4,512,4,64]{1,3,2,0:T(8,128...) while((s32[]{:T(128)}, f32[2048,4,64]{0,2,1:T(8,128)}, ...), condition=%wide.region_13.14_spmd.clone.clone, body=%wide.region_11.13_spmd.clone.sunk.clone | while | flops 2750021632 | bytes 180945120 | solution.py:102
  686.9 5.8 fusion.167
  692.7 9.9 multiply_reduce_fusion.5
  702.6 9.2 multiply_convert_fusion.8
  719.1 7.5 fusion.168
  731.3 6.2 fusion.167
  737.5 9.9 multiply_reduce_fusion.5
  747.4 8.2 multiply_convert_fusion.8
  758.9 4.8 fusion.166
  763.7 6.8 fusion.168
  775.2 6.2 fusion.167
  781.4 9.9 multiply_reduce_fusion.5
  791.3 8.1 multiply_convert_fusion.8
  802.6 4.7 fusion.166
  807.4 6.8 fusion.168
  818.9 6.2 fusion.167
  825.1 9.9 multiply_reduce_fusion.5
  835.0 8.1 multiply_convert_fusion.8
  846.4 4.7 fusion.166
  851.1 6.9 fusion.168
  861.4 4.8 copy.68
  883.2 5.3 reshape.245
  893.1 5.1 fusion.72
  905.5 8.7 convolution_convert_fusion
  914.2 5.0 bitcast_convert_fusion
  931.3 11.0 reduce-scatter.13.cloned.1.call-done
  944.4 292.0 %all-reduce.9.cloned.1.call-done = (bf16[2048,1024]{1,0:T(8,128)(2,1)}, bf16[2048,1024]{1,0:T(8,128)(2,1)}) async-done(((bf16[2048,1024]{1,0:T(8,128)(2,1)}, bf16[2048,1024]{1,0:T(8,128)(2,1)}), (bf16[2048,1024]{1,0:T(8,128)(2,1)}, bf16[2048,1024]{1,0:T(8,128)(2,1)})) %all-reduce.9.cloned.1.call-update) | async-done | bytes 8388624 | tf_op jit(solution)/shard_map/psum | solution.py:168
  1238.8 39.3 %psum.39 = f32[2,1024]{1,0:T(2,128)} all-reduce(f32[2,1024]{1,0:T(2,128)S(1)} %pad_maximum_fusion.13), channel_id=1, replica_groups=mesh['dp'=8,'tensor'=4] {'dp','tensor'}, use_global_device_ids=true, to_apply=%region_22.23 | all-reduce | flops 2048 | bytes 16384 | tf_op jit(solution)/shard_map/psum | solution.py:233
  1278.2 6.0 fusion.58
  (223 shorter events, 195.6 us)
Async XLA Ops:
  7.2 423.8 %copy-start = (bf16[1024,1024]{1,0:T(8,128)(2,1)S(1)}, bf16[1024,1024]{1,0:T(8,128)(2,1)}, u32[]{:S(2)}) copy-start(bf16[1024,1024]{1,0:T(8,128)(2,1)} %param.18) | copy-start | bytes 6291460
  7.2 4.9 copy-start.32
  7.2 395.5 %all-reduce.5.cloned.1.call-start = ((), (), s32[]{:S(2)}) async-start(), calls=%async_computation.4 | async-start | bytes 16777216 | tf_op jit(solution)/shard_map/psum | solution.py:155
  7.3 5.4 copy-start.9
  12.1 6.0 copy-start.26
  12.7 5.4 copy-start.29
  40.5 4.4 copy-start.8
  49.9 3.8 copy-start.6
  49.9 3.8 copy-start.18
  63.7 3.8 copy-start.6
  63.7 3.8 copy-start.18
  77.5 3.8 copy-start.6
  77.5 3.8 copy-start.18
  91.3 3.8 copy-start.6
  91.3 3.8 copy-start.18
  101.2 3.4 copy-start.21
  109.0 293.7 %copy-start.27 = (f32[2048]{0:T(1024)S(1)}, f32[2048]{0:T(1024)}, u32[]{:S(2)}) copy-start(f32[2048]{0:T(1024)} %copy-done.26) | copy-start | bytes 24580
  109.1 505.3 %all-reduce.7.cloned.1.call-start = ((), (), s32[]{:S(2)}) async-start(), calls=%async_computation.5 | async-start | bytes 8388608 | tf_op jit(solution)/shard_map/psum | solution.py:187
  410.3 3.2 copy-start.4
  410.3 6.5 copy-start.31
  413.6 3.2 copy-start.11
  430.9 16.0 %copy-start.34 = (bf16[2,1024,1024]{2,1,0:T(8,128)(2,1)S(1)}, bf16[2,1024,1024]{2,1,0:T(8,128)(2,1)}, u32[]{:S(2)}) copy-start(bf16[2,1024,1024]{2,1,0:T(8,128)(2,1)} %param.17) | copy-start | bytes 12582916
  460.2 459.2 %reduce-scatter.19.cloned.1.call-start = ((), (), s32[]{:S(2)}) async-start(), calls=%async_computation.9 | async-start | bytes 2359296
  473.8 452.7 %reduce-scatter.15.cloned.1.call-start = ((), (), s32[]{:S(2)}) async-start(), calls=%async_computation.7 | async-start | bytes 589824
  614.3 5.8 copy-start.7
  614.3 7.1 copy-start.20
  621.4 9.5 copy-start.13
  635.1 293.0 %reduce-scatter.17.cloned.1.call-start = ((), (), s32[]{:S(2)}) async-start(), calls=%async_computation.8 | async-start | bytes 4718592
  667.7 274.6 %reduce-scatter.13.cloned.1.call-start = ((), (), s32[]{:S(2)}) async-start(), calls=%async_computation.6 | async-start | bytes 1769472
  711.8 3.3 copy-start.1
  715.0 4.0 copy-start.3
  755.6 3.3 copy-start.1
  758.9 4.8 copy-start.3
  799.4 3.3 copy-start.1
  802.6 4.8 copy-start.3
  843.1 3.3 copy-start.1
  846.4 4.8 copy-start.3
  861.4 6.7 copy-start.17
  873.2 4.7 copy-start.15
  888.4 4.1 copy-start.10
  888.4 4.3 copy-start.22
  888.4 4.7 copy-start.24
  888.4 4.7 copy-start.28
  888.4 4.7 copy-start.30
  905.5 330.9 %all-reduce.9.cloned.1.call-start = ((), (), s32[]{:S(2)}) async-start(), calls=%async_computation.10 | async-start | bytes 16777216 | tf_op jit(solution)/shard_map/psum | solution.py:168
  905.5 8.7 copy-start.23
  905.5 8.7 copy-start.25
  905.5 8.7 copy-start.35
  (13 other events, 16.5 us)
Sparse Core Ops, SparseCore 0:
  109.2 293.5 all-reduce.4
  460.3 153.9 all-reduce.6
  618.0 40.2 reduce-scatter.18
  661.2 34.1 reduce-scatter.14
  698.9 51.3 reduce-scatter.16
  905.6 36.6 reduce-scatter.12
  944.8 291.4 all-reduce.8
where the time goes:
time: 1300 us; the launch traced here: 1290 us
  waiting for transfers between devices  729 us (56%)
  matrix products  264 us (20%)
  other arithmetic  124 us (10%)
  local copies, waits for them, and re-layouts  118 us (9%)
  blocking collectives  39.3 us (3%)
  between operations  16.1 us (1%)
    psum x1, waiting for transfers between devices, body(): lax.psum(jnp.dot(hidden, down_weight, preferred_element_type=jnp.float32)...  292 us
    psum x1, waiting for transfers between devices, body(): lax.psum(jnp.dot(att_low, out_weight, preferred_element_type=jnp.float32)...  291 us
    psum x1, waiting for transfers between devices, body(): lax.psum(jnp.einsum('ctf,cdf->td', grad_stack, gate_up_weight, preferred_...  135 us
    unnamed x77, local copies, waits for them, and re-layouts  55.9 us
    dot_general x4, matrix products, one_block(): jnp.einsum('qhd,khd->hqk', grad_block, values, preferred_element_type=jnp...  39.6 us
    psum x1, blocking collectives, body(): grad_gains = lax.psum(jnp.stack([gain_one, gain_two]), ('dp', 'tensor'))  39.3 us
    convert_element_type x4, other arithmetic, one_block(): score_grad = (probs * (prob_grad - delta)).astype(jnp.bfloat16)  33.6 us
    dot_general x8, matrix products, masked_scores(): jnp.einsum('qhd,khd->hqk', query_block, keys, preferred_element_type=jnp....  28.7 us
  transfers between devices with their start and end apart: 7, of which 4 were waited for; matrix products, arithmetic and copies ran while one was open for 25% of the time, Pallas kernels for 0%

commit v1 on v0

v1 whole, which is shorter than its diff:
```python
import functools
import math

import jax
import jax.numpy as jnp
import numpy as np
from jax import lax
from jax.experimental import pallas as pl
from jax.experimental.pallas import tpu as pltpu
from jax.sharding import PartitionSpec as P

HD = 64
WIN = 2048
EPSILON = 1e-05
NEG_FILL = -1e30
LOG2E = math.log2(math.e)
LN2 = math.log(2.0)
FACTOR = HD ** (-0.5)
VMEM = 60 * 2**20
F32 = jnp.float32
BF16 = jnp.bfloat16

NN = (((1,), (0,)), ((), ()))
NT = (((1,), (1,)), ((), ()))
TN = (((0,), (0,)), ((), ()))


def dot(a, b, dims=NN):
    return lax.dot_general(a, b, dims, preferred_element_type=F32)


def call(kernel, grid, in_specs, out_specs, out_shape, scratch=(), flops=0, nbytes=0, trans=0):
    return pl.pallas_call(
        kernel,
        grid=grid,
        in_specs=in_specs,
        out_specs=out_specs,
        out_shape=out_shape,
        scratch_shapes=scratch,
        compiler_params=pltpu.CompilerParams(vmem_limit_bytes=VMEM),
        cost_estimate=pl.CostEstimate(flops=flops, bytes_accessed=nbytes, transcendentals=trans),
    )


def whole(shape):
    return pl.BlockSpec(shape, lambda *_: (0,) * len(shape), pipeline_mode=pl.Buffered(1))


def smem():
    return pl.BlockSpec(memory_space=pltpu.SMEM)


def sds(shape, dtype):
    return jax.ShapeDtypeStruct(shape, dtype)


def rotary_tables():
    position = np.arange(WIN, dtype=np.float64)
    frequency = 10000.0 ** (-2.0 * np.arange(HD // 2, dtype=np.float64) / HD)
    angles = position[:, None] * frequency[None, :]
    cosine = np.cos(angles)
    sine = np.sin(angles)
    cos_full = np.tile(np.concatenate([cosine, cosine], axis=1), (1, 2))
    sin_full = np.tile(np.concatenate([-sine, sine], axis=1), (1, 2))
    return cos_full.astype(np.float32), sin_full.astype(np.float32)


def swap_halves(v):
    lane = lax.broadcasted_iota(jnp.int32, v.shape, 1)
    return jnp.where(lane % HD < HD // 2, pltpu.roll(v, 96, 1), pltpu.roll(v, 32, 1))


def rms(x):
    return lax.rsqrt(jnp.mean(x * x, axis=-1, keepdims=True) + EPSILON)


def split3(v):
    hi = v.astype(BF16)
    rest = v - hi.astype(F32)
    mid = rest.astype(BF16)
    low = (rest - mid.astype(F32)).astype(BF16)
    return hi, mid, low


def qkv_kernel(len_ref, x_ref, w_ref, gain_ref, cos_ref, sin_ref, q_ref, k_ref, v_ref):
    rows = x_ref.shape[0]
    x = x_ref[...].astype(F32)
    normed = (x * rms(x) * gain_ref[0:1, :]).astype(BF16)
    cosine = cos_ref[...]
    sine = sin_ref[...]
    lane = lax.broadcasted_iota(jnp.int32, (rows, 128), 1)
    slot = lax.broadcasted_iota(jnp.int32, (rows, 128), 0) + pl.program_id(0) * rows
    masked = jnp.where(slot < len_ref[0], 0.0, NEG_FILL).astype(BF16)
    one = jnp.ones((rows, 128), BF16)
    zero = jnp.zeros((rows, 128), BF16)
    pairs = w_ref.shape[2] // 128
    for c in range(3):
        y = dot(normed, w_ref[c])
        for j in range(pairs):
            v = y[:, 128 * j : 128 * (j + 1)]
            if c < 2:
                v = v * cosine + swap_halves(v) * sine
            if c == 0:
                v = v * (FACTOR * LOG2E)
            v = v.astype(BF16)
            for s in range(2):
                first = HD * (1 - s)
                own = (lane >= HD * s) & (lane < HD * (s + 1))
                if c == 0:
                    q_ref[2 * j + s] = jnp.where(own, v, jnp.where(lane == first, one, zero))
                elif c == 1:
                    tail = jnp.where(
                        lane == first, masked, jnp.where(lane < first + 4, one, zero)
                    )
                    tail = jnp.where(lane < first, zero, tail)
                    k_ref[2 * j + s] = jnp.where(own, v, tail)
                else:
                    v_ref[2 * j + s] = jnp.where(own, v, one)


def project(lengths, tokens, qkv_weight, gains, cosine, sine, block=512):
    rows, width = tokens.shape
    local = qkv_weight.shape[2]
    heads = local // HD
    spec = pl.BlockSpec((heads, block, 128), lambda i: (0, i, 0))
    return call(
        qkv_kernel,
        (rows // block,),
        [
            smem(),
            pl.BlockSpec((block, width), lambda i: (i, 0)),
            whole(qkv_weight.shape),
            whole(gains.shape),
            pl.BlockSpec((block, 128), lambda i: (i, 0)),
            pl.BlockSpec((block, 128), lambda i: (i, 0)),
        ],
        [spec] * 3,
        [sds((heads, rows, 128), BF16)] * 3,
        flops=2 * rows * width * 3 * local,
        nbytes=rows * width * 2 + 3 * heads * rows * 256,
    )(lengths, tokens, qkv_weight, gains, cosine, sine)


def attend_kernel(sub, q_ref, k_ref, v_ref, o_ref, qb_ref):
    rows = q_ref.shape[1]
    lane = lax.broadcasted_iota(jnp.int32, (sub, 128), 1)
    for r in range(rows // sub):
        part = slice(r * sub, (r + 1) * sub)
        outs = []
        for s in range(2):
            q = q_ref[s, part, :]
            scores = dot(q, k_ref[s], NT)
            peak = jnp.max(scores, axis=1, keepdims=True)
            expo = jnp.exp2(scores - peak).astype(BF16)
            acc = dot(expo, v_ref[s])
            outs.append(acc / pltpu.roll(acc, HD, 1))
            first = HD * (1 - s)
            total = jnp.where((lane >= first) & (lane < first + HD), acc, 1.0)
            hi, mid, low = split3(-(peak + jnp.log2(total)))
            tail = jnp.where(lane == first + 3, low, q)
            tail = jnp.where(lane == first + 2, mid, tail)
            qb_ref[s, part, :] = jnp.where(lane == first + 1, hi, tail)
        o_ref[part, :] = jnp.where(lane < HD, outs[0], outs[1]).astype(BF16)


def attend(q, k, v, block=512, sub=256):
    heads, rows, _ = q.shape
    keys = k.shape[1]
    return call(
        functools.partial(attend_kernel, sub),
        (heads // 2, rows // block),
        [
            pl.BlockSpec((2, block, 128), lambda j, i: (j, i, 0)),
            pl.BlockSpec((2, keys, 128), lambda j, i: (j, 0, 0)),
            pl.BlockSpec((2, keys, 128), lambda j, i: (j, 0, 0)),
        ],
        [
            pl.BlockSpec((block, 128), lambda j, i: (i, j)),
            pl.BlockSpec((2, block, 128), lambda j, i: (j, i, 0)),
        ],
        [sds((rows, heads * HD), BF16), sds((heads, rows, 128), BF16)],
        flops=heads * rows * keys * 128 * 4,
        nbytes=heads * (2 * rows + 2 * keys) * 256,
        trans=heads * rows * keys,
    )(q, k, v)


def ffn_kernel(
    len_ref, weight_ref, att_ref, x_ref, cot_ref, ow_ref, gu_ref, dw_ref, gain_ref,
    resid_ref, n2_ref, ffn_ref, gn2_ref, hid_ref, gg_ref, gup_ref, go_ref,
):
    rows = x_ref.shape[0]
    parts, _, local = att_ref.shape
    resid = x_ref[...].astype(F32)
    for z in range(parts):
        resid = resid + dot(att_ref[z], ow_ref[local * z : local * (z + 1), :])
    resid_ref[...] = resid
    normed = (resid * rms(resid) * gain_ref[1:2, :]).astype(BF16)
    n2_ref[...] = normed
    slot = lax.broadcasted_iota(jnp.int32, (rows, 1), 0) + pl.program_id(0) * rows
    row_weight = jnp.where(slot < len_ref[0], weight_ref[0], 0.0)
    go = (cot_ref[...].astype(F32) * row_weight).astype(BF16)
    go_ref[...] = go
    gate = dot(normed, gu_ref[0])
    upper = dot(normed, gu_ref[1])
    sigma = jax.nn.sigmoid(gate)
    act = gate * sigma
    hidden = (act * upper).astype(BF16)
    hid_ref[...] = hidden
    ffn_ref[...] = dot(hidden, dw_ref[...]).astype(BF16)
    grad_hidden = dot(go, dw_ref[...], NT)
    grad_up = (grad_hidden * act).astype(BF16)
    grad_gate = (grad_hidden * upper * (sigma + act * (1.0 - sigma))).astype(BF16)
    gup_ref[...] = grad_up
    gg_ref[...] = grad_gate
    gn2_ref[...] = (dot(grad_gate, gu_ref[0], NT) + dot(grad_up, gu_ref[1], NT)).astype(BF16)


def feed_forward(lengths, picked, att_all, tokens, cotangent, out_full, gate_up, down, gains, block=512):
    rows, width = tokens.shape
    parts, _, local = att_all.shape
    hidden = gate_up.shape[2]
    row = lambda n: pl.BlockSpec((block, n), lambda i: (i, 0))
    return call(
        ffn_kernel,
        (rows // block,),
        [
            smem(), smem(),
            pl.BlockSpec((parts, block, local), lambda i: (0, i, 0)),
            row(width), row(width),
            whole(out_full.shape), whole(gate_up.shape), whole(down.shape), whole(gains.shape),
        ],
        [row(width), row(width), row(width), row(width), row(hidden), row(hidden), row(hidden), row(width)],
        [
            sds((rows, width), F32), sds((rows, width), BF16), sds((rows, width), BF16),
            sds((rows, width), BF16), sds((rows, hidden), BF16), sds((rows, hidden), BF16),
            sds((rows, hidden), BF16), sds((rows, width), BF16),
        ],
        flops=2 * rows * width * (width + 6 * hidden),
        nbytes=rows * width * 20 + 8 * width * hidden,
        trans=rows * hidden,
    )(lengths, picked, att_all, tokens, cotangent, out_full, gate_up, down, gains)


def ffn_grad_kernel(n2_ref, hid_ref, gg_ref, gup_ref, go_ref, gu_ref, gain_ref, out_ref, sum_ref, acc):
    step = pl.program_id(0)

    @pl.when(step == 0)
    def _():
        acc[...] = jnp.zeros_like(acc)

    n2 = n2_ref[...]
    acc[0] += dot(n2, gg_ref[...], TN)
    acc[1] += dot(n2, gup_ref[...], TN)
    acc[2] += dot(go_ref[...], hid_ref[...], TN)

    @pl.when(step == pl.num_programs(0) - 1)
    def _():
        width = acc.shape[1]
        shares = out_ref.shape[0]
        part = width // shares
        for c in range(3):
            for d in range(shares):
                out_ref[d, c * part : (c + 1) * part, :] = acc[c, d * part : (d + 1) * part, :].astype(BF16)
        total = jnp.sum(
            acc[0] * gu_ref[0].astype(F32) + acc[1] * gu_ref[1].astype(F32), axis=1, keepdims=True
        )
        sum_ref[...] = jnp.broadcast_to(total, sum_ref.shape)


def ffn_grads(n2, hid, gg, gup, go, gate_up, gains, shares, block=512):
    rows, width = n2.shape
    hidden = hid.shape[1]
    row = lambda n: pl.BlockSpec((block, n), lambda i: (i, 0))
    return call(
        ffn_grad_kernel,
        (rows // block,),
        [row(width), row(hidden), row(hidden), row(hidden), row(width), whole(gate_up.shape), whole(gains.shape)],
        [whole((shares, 3 * width // shares, hidden)), whole((width, 128))],
        [sds((shares, 3 * width // shares, hidden), BF16), sds((width, 128), F32)],
        scratch=[pltpu.VMEM((3, width, hidden), F32)],
        flops=6 * rows * width * hidden,
        nbytes=rows * (2 * width + 3 * hidden) * 2,
    )(n2, hid, gg, gup, go, gate_up, gains)


def attend_back_kernel(gr_ref, ow_ref, q_ref, k_ref, v_ref, att_ref, dq_ref, dk_ref, dv_ref):
    rows = q_ref.shape[1]
    lane = lax.broadcasted_iota(jnp.int32, (rows, 128), 1)

    @pl.when(pl.program_id(1) == 0)
    def _():
        dk_ref[...] = jnp.zeros_like(dk_ref)
        dv_ref[...] = jnp.zeros_like(dv_ref)

    grad = dot(gr_ref[...], ow_ref[...], NT).astype(BF16)
    prod = grad.astype(F32) * att_ref[...].astype(F32)
    zero = jnp.zeros((rows, 128), BF16)
    dqs = []
    for s in range(2):
        first = HD * (1 - s)
        own = (lane >= HD * s) & (lane < HD * (s + 1))
        delta = jnp.sum(jnp.where(own, prod, 0.0), axis=1, keepdims=True)
        hi, mid, low = split3(-delta)
        grad_own = jnp.where(own, grad, zero)
        grad_aug = jnp.where(lane == first + 2, low, grad_own)
        grad_aug = jnp.where(lane == first + 1, mid, grad_aug)
        grad_aug = jnp.where(lane == first, hi, grad_aug)
        q = q_ref[s]
        probs = jnp.exp2(dot(k_ref[s], q, NT))
        scores_grad = (probs * dot(v_ref[s], grad_aug, NT)).astype(BF16)
        dv_ref[...] += dot(probs.astype(BF16), grad_own)
        dk_ref[...] += dot(scores_grad, jnp.where(own, q, zero))
        dqs.append(dot(k_ref[s], scores_grad, TN).T)
    dq_ref[...] = jnp.where(lane < HD, dqs[0], dqs[1])


def attend_back(grad_low, out_weight, q, k, v, att, block=512):
    heads, rows, _ = q.shape
    width = grad_low.shape[1]
    local = heads * HD
    return call(
        attend_back_kernel,
        (heads // 2, rows // block),
        [
            pl.BlockSpec((block, width), lambda j, i: (i, 0)),
            pl.BlockSpec((128, width), lambda j, i: (j, 0)),
            pl.BlockSpec((2, block, 128), lambda j, i: (j, i, 0)),
            pl.BlockSpec((2, rows, 128), lambda j, i: (j, 0, 0)),
            pl.BlockSpec((2, rows, 128), lambda j, i: (j, 0, 0)),
            pl.BlockSpec((block, 128), lambda j, i: (i, j)),
        ],
        [
            pl.BlockSpec((block, 128), lambda j, i: (i, j)),
            pl.BlockSpec((rows, 128), lambda j, i: (0, j)),
            pl.BlockSpec((rows, 128), lambda j, i: (0, j)),
        ],
        [sds((rows, local), F32)] * 3,
        flops=heads * rows * rows * 128 * 10 + 2 * rows * width * local,
        nbytes=heads * rows * 256 * 6,
        trans=heads * rows * rows,
    )(grad_low, out_weight, q, k, v, att)


def project_back_kernel(
    x_ref, dq_ref, dk_ref, dv_ref, gr_ref, att_ref, w_ref, gain_ref, cos_ref, sin_ref,
    gn1_ref, wg_ref, sum_ref, acc,
):
    step = pl.program_id(0)

    @pl.when(step == 0)
    def _():
        acc[...] = jnp.zeros_like(acc)

    x = x_ref[...].astype(F32)
    normed = (x * rms(x) * gain_ref[0:1, :]).astype(BF16)
    local = dq_ref.shape[1]
    cosine = cos_ref[...]
    sine = sin_ref[...]

    def back(g, scale):
        cols = []
        for j in range(local // 128):
            v = g[:, 128 * j : 128 * (j + 1)]
            cols.append((v * cosine - swap_halves(v) * sine) * scale)
        return jnp.concatenate(cols, axis=1).astype(BF16)

    acts = [back(dq_ref[...], FACTOR), back(dk_ref[...], LN2), dv_ref[...].astype(BF16)]
    total = dot(acts[0], w_ref[0], NT) + dot(acts[1], w_ref[1], NT) + dot(acts[2], w_ref[2], NT)
    gn1_ref[...] = total.astype(BF16)
    acc[:, : 3 * local] += dot(normed, jnp.concatenate(acts, axis=1), TN)
    acc[:, 3 * local :] += dot(gr_ref[...], att_ref[...], TN)

    @pl.when(step == pl.num_programs(0) - 1)
    def _():
        shares = wg_ref.shape[0]
        part = acc.shape[0] // shares
        for d in range(shares):
            wg_ref[d] = acc[d * part : (d + 1) * part, :].astype(BF16)
        gain_sum = acc[:, :local] * w_ref[0].astype(F32)
        for c in (1, 2):
            gain_sum += acc[:, c * local : (c + 1) * local] * w_ref[c].astype(F32)
        sum_ref[...] = jnp.broadcast_to(jnp.sum(gain_sum, axis=1, keepdims=True), sum_ref.shape)


def project_back(tokens, dq, dk, dv, grad_low, att, qkv_weight, gains, cosine, sine, shares, block=512):
    rows, width = tokens.shape
    local = dq.shape[1]
    row = lambda n: pl.BlockSpec((block, n), lambda i: (i, 0))
    return call(
        project_back_kernel,
        (rows // block,),
        [
            row(width), row(local), row(local), row(local), row(width), row(local),
            whole(qkv_weight.shape), whole(gains.shape), row(128), row(128),
        ],
        [row(width), whole((shares, width // shares, 4 * local)), whole((width, 128))],
        [
            sds((rows, width), BF16),
            sds((shares, width // shares, 4 * local), BF16),
            sds((width, 128), F32),
        ],
        scratch=[pltpu.VMEM((width, 4 * local), F32)],
        flops=2 * rows * width * 7 * local,
        nbytes=rows * width * 8,
    )(tokens, dq, dk, dv, grad_low, att, qkv_weight, gains, cosine, sine)


def norm_back(grad_normed, gain, unit, factor):
    scaled = grad_normed * gain
    return factor * (scaled - unit * jnp.mean(scaled * unit, axis=-1, keepdims=True))


def body(
    tokens, qkv_weight, out_weight, gate_up_weight, down_weight, norm_gains,
    species_weight, species_ids, lengths, cotangent,
):
    rows, width = tokens.shape
    local = out_weight.shape[0]
    hidden = down_weight.shape[0]
    parts = lax.axis_size("tensor")
    shares = lax.axis_size("dp")
    share = rows // parts
    offset = lax.axis_index("tensor") * share
    own = lambda a: lax.dynamic_slice_in_dim(a, offset, share, 0)
    cosine, sine = (jnp.asarray(t) for t in rotary_tables())

    matches = species_ids[:, None] == jnp.arange(species_weight.shape[0])[None, :]
    picked = jnp.sum(jnp.where(matches, species_weight[None, :], F32(0.0)), axis=1)

    out_full = lax.all_gather(out_weight, "tensor", axis=0, tiled=True)
    q, k, v = project(lengths, tokens, qkv_weight, norm_gains, cosine, sine)
    att, q_back = attend(q, k, v)
    att_all = lax.all_gather(att, "tensor", axis=0)
    resid, n2, ffn, gn2, hid, gg, gup, go = feed_forward(
        lengths, picked, att_all, tokens, cotangent, out_full, gate_up_weight, down_weight, norm_gains
    )
    gn2_own = lax.psum_scatter(gn2, "tensor", scatter_dimension=0, tiled=True).astype(F32)
    ffn_wg, gain_two = ffn_grads(n2, hid, gg, gup, go, gate_up_weight, norm_gains, shares)

    resid_own = own(resid)
    scale_two = rms(resid_own)
    unit_two = resid_own * scale_two
    slot = offset + jnp.arange(share)
    row_weight = jnp.where(slot < lengths[0], picked[0], F32(0.0))
    go_own = own(cotangent).astype(F32) * row_weight[:, None]
    grad_resid = go_own + norm_back(gn2_own, norm_gains[1], unit_two, scale_two)
    grad_low = lax.all_gather(grad_resid.astype(BF16), "tensor", axis=0, tiled=True)

    dq, dk, dv = attend_back(grad_low, out_weight, q_back, k, v, att)
    gn1, attn_wg, gain_one = project_back(
        tokens, dq, dk, dv, grad_low, att, qkv_weight, norm_gains, cosine, sine, shares
    )
    gn1_own = lax.psum_scatter(gn1, "tensor", scatter_dimension=0, tiled=True).astype(F32)
    ffn_own = lax.psum_scatter(ffn, "tensor", scatter_dimension=0, tiled=True).astype(F32)
    out = resid_own + ffn_own

    tok_own = own(tokens).astype(F32)
    scale_one = rms(tok_own)
    grad_tok = grad_resid + norm_back(gn1_own, norm_gains[0], tok_own * scale_one, scale_one)

    gains_grad = jnp.stack([gain_one[:, 0], gain_two[:, 0]]) / norm_gains
    gains_grad = lax.psum(gains_grad, ("dp", "tensor"))

    part = width // shares
    ffn_sum = lax.psum_scatter(ffn_wg, "dp", scatter_dimension=0, tiled=True)[0].astype(F32)
    attn_sum = lax.psum_scatter(attn_wg, "dp", scatter_dimension=0, tiled=True)[0].astype(F32)
    grad_gu = ffn_sum[: 2 * part].reshape(2, part, hidden)
    grad_down = ffn_sum[2 * part :].T
    grad_qkv = jnp.stack([attn_sum[:, c * local : (c + 1) * local] for c in range(3)])
    grad_op = attn_sum[:, 3 * local :].T
    return (out, grad_tok, grad_qkv, grad_op, grad_gu, grad_down, gains_grad)


def solution(mesh):
    in_specs = (
        P("dp", None),
        P(None, None, "tensor"),
        P("tensor", None),
        P(None, None, "tensor"),
        P("tensor", None),
        P(),
        P(),
        P("dp"),
        P("dp"),
        P("dp", None),
    )
    out_specs = (
        P(("dp", "tensor"), None),
        P(("dp", "tensor"), None),
        P(None, "dp", "tensor"),
        P("tensor", "dp"),
        P(None, "dp", "tensor"),
        P("tensor", "dp"),
        P(),
    )
    return jax.shard_map(body, mesh=mesh, in_specs=in_specs, out_specs=out_specs, check_vma=False)
```

time: 1300 us -> 623 us (0.48)
  waiting for transfers between devices: 729 us -> 379 us
  matrix products: 264 us -> 0 us
  Pallas kernels: 0 us -> 165 us
  local copies, waits for them, and re-layouts: 118 us -> 3.36 us
  other arithmetic: 124 us -> 20.3 us
    psum x3 -> x0, waiting for transfers between devices: 718 us -> none  [the longest x1 292 us: body(): lax.psum(jnp.dot(hidden, down_weight, preferred_element_type=jnp.float32)...]
    dot_general x40 -> x0, matrix products: 264 us -> none  [the longest x4 39.6 us: one_block(): jnp.einsum('qhd,khd->hqk', grad_block, values, preferred_element_type=jnp...]
    reduce_scatter x0 -> x5, waiting for transfers between devices: none -> 226 us  [the longest x1 77.4 us: body(): lax.psum_scatter(ffn, 'tensor', scatter_dimension=0, tiled=True).astype(F32)]
    pallas_call x0 -> x6, Pallas kernels: none -> 165 us  [the longest x1 48.4 us: attend_back(): call(attend_back_kernel, (heads // 2, rows // block), [pl.BlockSpec((bloc...]
    all_gather x0 -> x3, waiting for transfers between devices: none -> 151 us  [the longest x1 81.7 us: body(): att_all = lax.all_gather(att, 'tensor', axis=0)]
    unnamed x77 -> x18, local copies, waits for them, and re-layouts: 55.9 us -> 1.79 us
    convert_element_type x11 -> x3, other arithmetic: 41.9 us -> 5.89 us  [the longest x1 3.53 us: body(): grad_resid.astype(BF16)]
    reduce_sum x9 -> x3, other arithmetic: 31.2 us -> 3.92 us  [the longest x2 3.32 us: rms(): return lax.rsqrt(jnp.mean(x * x, axis=-1, keepdims=True) + EPSILON)]
  transfers between devices with their start and end apart: 7 -> 8, of which waited for: 4 -> 6; matrix products, arithmetic and copies ran while one was open for 25% -> 2% of each run, Pallas kernels for 0% -> 20%
where the time goes in v1:
time: 623 us
  waiting for transfers between devices  379 us (61%)
  Pallas kernels  165 us (26%)
  blocking collectives  38.9 us (6%)
  other arithmetic  20.3 us (3%)
  between operations  15.6 us (3%)
    all_gather x1, waiting for transfers between devices, body(): att_all = lax.all_gather(att, 'tensor', axis=0)  81.7 us
    reduce_scatter x1, waiting for transfers between devices, body(): lax.psum_scatter(ffn, 'tensor', scatter_dimension=0, tiled=True).astype(F32)  77.4 us
    reduce_scatter x1, waiting for transfers between devices, body(): lax.psum_scatter(gn1, 'tensor', scatter_dimension=0, tiled=True).astype(F32)  76.3 us
    reduce_scatter x1, waiting for transfers between devices, body(): lax.psum_scatter(gn2, 'tensor', scatter_dimension=0, tiled=True).astype(F32)  72.7 us
    all_gather x1, waiting for transfers between devices, body(): lax.all_gather(grad_resid.astype(BF16), 'tensor', axis=0, tiled=True)  57.9 us
    pallas_call x1, Pallas kernels, attend_back(): call(attend_back_kernel, (heads // 2, rows // block), [pl.BlockSpec((bloc...  48.4 us
    pallas_call x1, Pallas kernels, feed_forward(): call(ffn_kernel, (rows // block,), [smem(), smem(), pl.BlockSpec((parts,...  40.2 us
    psum x1, blocking collectives, body(): gains_grad = lax.psum(gains_grad, ('dp', 'tensor'))  38.9 us
  transfers between devices with their start and end apart: 8, of which 6 were waited for; matrix products, arithmetic and copies ran while one was open for 2% of the time, Pallas kernels for 20%

profile of v1, /device:TPU:0, one launch (start us, length us, event | category | flops | bytes accessed | tf_op | source)
XLA Modules:
  0.0 622.6 jit_solution(12436275421371623503)
XLA Ops:
  7.2 0.0 all-gather.5.cloned.1.call-start
  7.2 0.7 all-gather.5.cloned.1.call-update
  7.9 0.0 all-gather.9.cloned.1.call-start
  8.6 9.3 %shard_map.171 = (bf16[4,2048,128]{2,1,0:T(8,128)(2,1)}, bf16[4,2048,128]{2,1,0:T(8,128)(2,1)}, bf16[4,2048,128]{2,1,0:T(8,128)(2,1)}) custom-call(s32[1]{0:T(128)} %copy.24.len_ref, bf16[2048,1024]{1,0:T(8,128)(2,1)} %x_ref.5, bf16[3,1024,256]{2,1,0:T(8,128)(2,1)} %w_ref.3, f32[2,1024]{1,0:T(2,128)} %gain_ref.7, f32[2048,128]{1,0:T(8,128)} %constant.24.clone.cos_ref, ...), custom_call_target="tpu_custom_call" | custom-call | flops 3221225472 | bytes 10485760 | tf_op jit(solution)/shard_map/pallas_call | solution.py:126
  17.9 27.9 %shard_map.172 = (bf16[2048,256]{1,0:T(8,128)(2,1)}, bf16[4,2048,128]{2,1,0:T(8,128)(2,1)}) custom-call(bf16[4,2048,128]{2,1,0:T(8,128)(2,1)} %get-tuple-element.28.q_ref, bf16[4,2048,128]{2,1,0:T(8,128)(2,1)} %get-tuple-element.29.k_ref, bf16[4,2048,128]{2,1,0:T(8,128)(2,1)} %get-tuple-element.30.v_ref), custom_call_target="tpu_custom_call" | custom-call | flops 8589934592 | bytes 8388608 | tf_op jit(solution)/shard_map/pallas_call | solution.py:169
  45.8 0.0 all-gather.9.cloned.1.call-update
  45.9 0.0 reduce-scatter.8.cloned.1.call-start
  46.6 0.6 select_reduce_fusion
  47.2 11.1 %all-gather.5.cloned.1.call-done.ow_ref = bf16[1024,1024]{1,0:T(8,128)(2,1)} async-done(((bf16[256,1024]{1,0:T(8,128)(2,1)}), bf16[1024,1024]{1,0:T(8,128)(2,1)}) %all-gather.5.cloned.1.call-update) | async-done | bytes 2097168 | tf_op jit(solution)/shard_map/all_gather | solution.py:431
  58.2 81.7 %all-gather.9.cloned.1.call-done = bf16[8192,256]{1,0:T(8,128)(2,1)} async-done(((bf16[2048,256]{1,0:T(8,128)(2,1)}), bf16[8192,256]{1,0:T(8,128)(2,1)}) %all-gather.9.cloned.1.call-update) | async-done | bytes 4194320 | tf_op jit(solution)/shard_map/all_gather | solution.py:434
  139.9 40.2 %shard_map.173 = (f32[2048,1024]{1,0:T(8,128)}, bf16[2048,1024]{1,0:T(8,128)(2,1)}, bf16[2048,1024]{1,0:T(8,128)(2,1)}, bf16[2048,1024]{1,0:T(8,128)(2,1)}, bf16...) custom-call(s32[1]{0:T(128)} %copy.24.len_ref, ...), custom_call_target="tpu_custom_call" | custom-call | flops 30064771072 | bytes 50331648 | tf_op jit(solution)/shard_map/pallas_call | solution.py:224
  180.1 0.0 copy-start.5
  180.1 0.0 reduce-scatter.8.cloned.1.call-update
  180.1 0.2 all-gather.7.cloned.1.call-start
  180.4 0.7 fusion.7
  181.1 1.8 multiply_reduce_fusion.1
  182.9 72.7 %reduce-scatter.8.cloned.1.call-done = bf16[512,1024]{1,0:T(8,128)(2,1)} async-done(((bf16[2048,1024]{1,0:T(8,128)(2,1)}), bf16[512,1024]{1,0:T(8,128)(2,1)}) %reduce-scatter.8.cloned.1.call-update) | async-done | bytes 1048592 | tf_op jit(solution)/shard_map/reduce_scatter | solution.py:438
  255.6 2.4 multiply_reduce_fusion
  258.1 3.5 fusion.8
  261.6 0.0 all-gather.7.cloned.1.call-update
  261.6 0.0 reduce-scatter.14.cloned.1.call-start
  261.7 23.5 %shard_map.176 = (bf16[8,384,1024]{2,1,0:T(8,128)(2,1)}, f32[1024,128]{1,0:T(8,128)}) custom-call(bf16[2048,1024]{1,0:T(8,128)(2,1)} %get-tuple-element.41.n2_ref, bf16[2048,1024]{1,0:T(8,128)(2,1)} %get-tuple-element.42.hid_ref, bf16[2048,1024]{1,0:T(8,128)(2,1)} %get-tuple-element.43.gg_ref, bf16[2048,1024]{1,0:T(8,128)(2,1)} %get-tuple-element.44.gup_ref, ...), custom_call_target="tpu_custom_call" | custom-call | flops 12884901888 | bytes 20971520 | tf_op jit(solution)/shard_map/pallas_call | solution.py:275
  285.1 0.0 reduce-scatter.14.cloned.1.call-update
  285.2 0.0 reduce-scatter.12.cloned.1.call-start
  285.2 57.9 %all-gather.7.cloned.1.call-done.gr_ref = bf16[2048,1024]{1,0:T(8,128)(2,1)} async-done(((bf16[512,1024]{1,0:T(8,128)(2,1)}), bf16[2048,1024]{1,0:T(8,128)(2,1)}) %all-gather.7.cloned.1.call-update) | async-done | bytes 4194320 | tf_op jit(solution)/shard_map/all_gather | solution.py:448
  343.1 48.4 %shard_map.174 = (f32[2048,256]{1,0:T(8,128)}, f32[2048,256]{1,0:T(8,128)}, f32[2048,256]{1,0:T(8,128)}) custom-call(bf16[2048,1024]{1,0:T(8,128)(2,1)} %all-gather.7.cloned.1.call-done.gr_ref, bf16[256,1024]{1,0:T(8,128)(2,1)} %ow_ref.1, bf16[4,2048,128]{2,1,0:T(8,128)(2,1)} %get-tuple-element.35.q_ref, bf16[4,2048,128]{2,1,0:T(8,128)(2,1)} %get-tuple-element.29.k_ref, ...), custom_call_target="tpu_custom_call" | custom-call | flops 22548578304 | bytes 12582912 | tf_op jit(solution)/shard_map/pallas_call | solution.py:322
  391.5 15.5 %shard_map.175 = (bf16[2048,1024]{1,0:T(8,128)(2,1)}, bf16[8,128,1024]{2,1,0:T(8,128)(2,1)}, f32[1024,128]{1,0:T(8,128)}) custom-call(bf16[2048,1024]{1,0:T(8,128)(2,1)} %x_ref.5, f32[2048,256]{1,0:T(8,128)} %get-tuple-element.36.dq_ref, f32[2048,256]{1,0:T(8,128)} %get-tuple-element.37.dk_ref, f32[2048,256]{1,0:T(8,128)} %get-tuple-element.38.dv_ref, ...), custom_call_target="tpu_custom_call" | custom-call | flops 7516192768 | bytes 16777216 | tf_op jit(solution)/shard_map/pallas_call | solution.py:390
  407.0 0.0 reduce-scatter.12.cloned.1.call-update
  407.0 0.0 reduce-scatter.10.cloned.1.call-start
  407.0 0.7 reduce-scatter.10.cloned.1.call-update
  407.8 0.0 reduce-scatter.6.cloned.1.call-start
  407.8 0.0 copy-start.3
  407.8 0.7 reduce-scatter.6.cloned.1.call-update
  408.5 1.5 fusion.6
  410.0 0.2 slice_reduce_fusion
  410.2 0.0 reduce-scatter.14.cloned.1.call-done
  410.3 1.4 convert_element_type.36
  411.7 1.0 copy.22
  412.7 1.1 slice.49
  413.8 0.2 slice_reduce_fusion.1
  414.0 38.9 %psum.7 = f32[2,1024]{1,0:T(2,128)} all-reduce(f32[2,1024]{1,0:T(2,128)S(1)} %maximum_divide_fusion), channel_id=1, replica_groups=mesh['dp'=8,'tensor'=4] {'dp','tensor'}, use_global_device_ids=true, to_apply=%region_10.11 | all-reduce | flops 2048 | bytes 16384 | tf_op jit(solution)/shard_map/psum | solution.py:463
  452.9 1.0 bitcast_convert_fusion
  453.9 0.8 copy.21
  454.7 0.8 pad_maximum_fusion
  455.5 76.3 %reduce-scatter.10.cloned.1.call-done = bf16[512,1024]{1,0:T(8,128)(2,1)} async-done(((bf16[2048,1024]{1,0:T(8,128)(2,1)}), bf16[512,1024]{1,0:T(8,128)(2,1)}) %reduce-scatter.10.cloned.1.call-update) | async-done | bytes 1048592 | tf_op jit(solution)/shard_map/reduce_scatter | solution.py:454
  531.7 2.2 fusion.2
  533.9 77.4 %reduce-scatter.6.cloned.1.call-done = bf16[512,1024]{1,0:T(8,128)(2,1)} async-done(((bf16[2048,1024]{1,0:T(8,128)(2,1)}), bf16[512,1024]{1,0:T(8,128)(2,1)}) %reduce-scatter.6.cloned.1.call-update) | async-done | bytes 1048592 | tf_op jit(solution)/shard_map/reduce_scatter | solution.py:455
  611.3 4.4 fusion.5
  (23 shorter events, 0.2 us)
Async XLA Ops:
  7.2 51.1 %all-gather.5.cloned.1.call-start = ((), (), s32[]{:S(2)}) async-start(), calls=%async_computation.5 | async-start | bytes 2621440 | tf_op jit(solution)/shard_map/all_gather | solution.py:431
  7.9 132.0 %all-gather.9.cloned.1.call-start = ((), (), s32[]{:S(2)}) async-start(), calls=%async_computation.12 | async-start | bytes 5242880 | tf_op jit(solution)/shard_map/all_gather | solution.py:434
  17.9 28.6 %copy-start.7 = (f32[850]{0:T(1024)S(1)}, f32[850]{0:T(1024)}, u32[]{:S(2)}) copy-start(f32[850]{0:T(1024)} %param.18) | copy-start | bytes 10204
  45.9 209.8 %reduce-scatter.8.cloned.1.call-start = ((), (), s32[]{:S(2)}) async-start(), calls=%async_computation.7 | async-start | bytes 5242880 | tf_op jit(solution)/shard_map/reduce_scatter | solution.py:438
  180.1 0.9 copy-start.5
  180.1 162.9 %all-gather.7.cloned.1.call-start = ((), (), s32[]{:S(2)}) async-start(), calls=%async_computation.8 | async-start | bytes 5242880 | tf_op jit(solution)/shard_map/all_gather | solution.py:448
  255.6 2.5 copy-start
  261.6 148.6 %reduce-scatter.14.cloned.1.call-start = ((), (), s32[]{:S(2)}) async-start(), calls=%async_computation.11 | async-start | bytes 7077888 | tf_op jit(solution)/shard_map/reduce_scatter | solution.py:466
  285.2 167.7 %reduce-scatter.12.cloned.1.call-start = ((), (), s32[]{:S(2)}) async-start(), calls=%async_computation.10 | async-start | bytes 2359296 | tf_op jit(solution)/shard_map/reduce_scatter | solution.py:467
  407.0 124.7 %reduce-scatter.10.cloned.1.call-start = ((), (), s32[]{:S(2)}) async-start(), calls=%async_computation.9 | async-start | bytes 5242880 | tf_op jit(solution)/shard_map/reduce_scatter | solution.py:454
  407.8 203.6 %reduce-scatter.6.cloned.1.call-start = ((), (), s32[]{:S(2)}) async-start(), calls=%async_computation.6 | async-start | bytes 5242880 | tf_op jit(solution)/shard_map/reduce_scatter | solution.py:455
  407.8 2.2 copy-start.3
  410.3 2.5 copy-start.1
  411.7 2.2 copy-start.4
  411.7 2.3 copy-start.6
  531.7 79.6 %copy-start.2 = (bf16[512,1024]{1,0:T(8,128)(2,1)S(1)}, bf16[512,1024]{1,0:T(8,128)(2,1)}, u32[]{:S(2)}) copy-start(bf16[512,1024]{1,0:T(8,128)(2,1)} %reduce-scatter.10.cloned.1.call-done) | copy-start | bytes 3145732
Sparse Core Ops, SparseCore 0:
  9.6 48.6 all-gather.4
  60.4 79.4 all-gather.8
  180.3 75.2 reduce-scatter.7
  261.8 81.2 all-gather.6
  346.7 60.2 reduce-scatter.13
  410.7 41.4 reduce-scatter.11
  454.6 77.0 reduce-scatter.9
  534.0 77.2 reduce-scatter.5

commit v2 on v1

v2 whole, which is shorter than its diff:
```python
import functools
import math

import jax
import jax.numpy as jnp
import numpy as np
from jax import lax
from jax.experimental import pallas as pl
from jax.experimental.pallas import tpu as pltpu
from jax.sharding import PartitionSpec as P

HD = 64
WIN = 2048
EPSILON = 1e-05
NEG_FILL = -1e30
LOG2E = math.log2(math.e)
LN2 = math.log(2.0)
FACTOR = HD ** (-0.5)
VMEM = 60 * 2**20
F32 = jnp.float32
BF16 = jnp.bfloat16

NN = (((1,), (0,)), ((), ()))
NT = (((1,), (1,)), ((), ()))
TN = (((0,), (0,)), ((), ()))


def dot(a, b, dims=NN):
    return lax.dot_general(a, b, dims, preferred_element_type=F32)


def call(kernel, grid, in_specs, out_specs, out_shape, scratch=(), flops=0, nbytes=0, trans=0, prefetch=0):
    return pl.pallas_call(
        kernel,
        grid_spec=pltpu.PrefetchScalarGridSpec(
            num_scalar_prefetch=prefetch,
            grid=grid,
            in_specs=in_specs,
            out_specs=out_specs,
            scratch_shapes=list(scratch),
        ),
        out_shape=out_shape,
        compiler_params=pltpu.CompilerParams(vmem_limit_bytes=VMEM),
        cost_estimate=pl.CostEstimate(flops=flops, bytes_accessed=nbytes, transcendentals=trans),
    )


def whole(shape):
    return pl.BlockSpec(shape, lambda *_: (0,) * len(shape), pipeline_mode=pl.Buffered(1))


def smem():
    return pl.BlockSpec(memory_space=pltpu.SMEM)


def sds(shape, dtype):
    return jax.ShapeDtypeStruct(shape, dtype)


def rotary_tables():
    position = np.arange(WIN, dtype=np.float64)
    frequency = 10000.0 ** (-2.0 * np.arange(HD // 2, dtype=np.float64) / HD)
    angles = position[:, None] * frequency[None, :]
    cosine = np.cos(angles)
    sine = np.sin(angles)
    cos_full = np.tile(np.concatenate([cosine, cosine], axis=1), (1, 2))
    sin_full = np.tile(np.concatenate([-sine, sine], axis=1), (1, 2))
    return cos_full.astype(np.float32), sin_full.astype(np.float32)


def swap_halves(v):
    lane = lax.broadcasted_iota(jnp.int32, v.shape, 1)
    return jnp.where(lane % HD < HD // 2, pltpu.roll(v, 96, 1), pltpu.roll(v, 32, 1))


def rms(x):
    return lax.rsqrt(jnp.mean(x * x, axis=-1, keepdims=True) + EPSILON)


def split3(v):
    hi = v.astype(BF16)
    rest = v - hi.astype(F32)
    mid = rest.astype(BF16)
    low = (rest - mid.astype(F32)).astype(BF16)
    return hi, mid, low


def norm_back(grad_normed, gain, unit, factor):
    scaled = grad_normed * gain
    return factor * (scaled - unit * jnp.mean(scaled * unit, axis=-1, keepdims=True))


def qkv_kernel(len_ref, x_ref, w_ref, gain_ref, cos_ref, sin_ref, q_ref, k_ref, v_ref):
    rows = x_ref.shape[0]
    x = x_ref[...].astype(F32)
    normed = (x * rms(x) * gain_ref[0:1, :]).astype(BF16)
    cosine = cos_ref[...]
    sine = sin_ref[...]
    lane = lax.broadcasted_iota(jnp.int32, (rows, 128), 1)
    slot = lax.broadcasted_iota(jnp.int32, (rows, 128), 0) + pl.program_id(0) * rows
    masked = jnp.where(slot < len_ref[0], 0.0, NEG_FILL).astype(BF16)
    one = jnp.ones((rows, 128), BF16)
    zero = jnp.zeros((rows, 128), BF16)
    pairs = w_ref.shape[2] // 128
    for c in range(3):
        y = dot(normed, w_ref[c])
        for j in range(pairs):
            v = y[:, 128 * j : 128 * (j + 1)]
            if c < 2:
                v = v * cosine + swap_halves(v) * sine
            if c == 0:
                v = v * (FACTOR * LOG2E)
            v = v.astype(BF16)
            for s in range(2):
                first = HD * (1 - s)
                own = (lane >= HD * s) & (lane < HD * (s + 1))
                if c == 0:
                    q_ref[2 * j + s] = jnp.where(own, v, jnp.where(lane == first, one, zero))
                elif c == 1:
                    tail = jnp.where(
                        lane == first, masked, jnp.where(lane < first + 4, one, zero)
                    )
                    tail = jnp.where(lane < first, zero, tail)
                    k_ref[2 * j + s] = jnp.where(own, v, tail)
                else:
                    v_ref[2 * j + s] = jnp.where(own, v, one)


def project(lengths, tokens, qkv_weight, gains, cosine, sine, block=512):
    rows, width = tokens.shape
    local = qkv_weight.shape[2]
    heads = local // HD
    spec = pl.BlockSpec((heads, block, 128), lambda i: (0, i, 0))
    return call(
        qkv_kernel,
        (rows // block,),
        [
            smem(),
            pl.BlockSpec((block, width), lambda i: (i, 0)),
            whole(qkv_weight.shape),
            whole(gains.shape),
            pl.BlockSpec((block, 128), lambda i: (i, 0)),
            pl.BlockSpec((block, 128), lambda i: (i, 0)),
        ],
        [spec] * 3,
        [sds((heads, rows, 128), BF16)] * 3,
        flops=2 * rows * width * 3 * local,
        nbytes=rows * width * 2 + 3 * heads * rows * 256,
    )(lengths, tokens, qkv_weight, gains, cosine, sine)


def attend_kernel(sub, q_ref, k_ref, v_ref, o_ref, qb_ref):
    rows = q_ref.shape[1]
    lane = lax.broadcasted_iota(jnp.int32, (sub, 128), 1)
    for r in range(rows // sub):
        part = slice(r * sub, (r + 1) * sub)
        outs = []
        for s in range(2):
            q = q_ref[s, part, :]
            scores = dot(q, k_ref[s], NT)
            peak = jnp.max(scores, axis=1, keepdims=True)
            expo = jnp.exp2(scores - peak).astype(BF16)
            acc = dot(expo, v_ref[s])
            outs.append(acc / pltpu.roll(acc, HD, 1))
            first = HD * (1 - s)
            total = jnp.where((lane >= first) & (lane < first + HD), acc, 1.0)
            hi, mid, low = split3(-(peak + jnp.log2(total)))
            tail = jnp.where(lane == first + 3, low, q)
            tail = jnp.where(lane == first + 2, mid, tail)
            qb_ref[s, part, :] = jnp.where(lane == first + 1, hi, tail)
        o_ref[part, :] = jnp.where(lane < HD, outs[0], outs[1]).astype(BF16)


def attend(q, k, v, block=512, sub=256):
    heads, rows, _ = q.shape
    keys = k.shape[1]
    return call(
        functools.partial(attend_kernel, sub),
        (heads // 2, rows // block),
        [
            pl.BlockSpec((2, block, 128), lambda j, i: (j, i, 0)),
            pl.BlockSpec((2, keys, 128), lambda j, i: (j, 0, 0)),
            pl.BlockSpec((2, keys, 128), lambda j, i: (j, 0, 0)),
        ],
        [
            pl.BlockSpec((block, 128), lambda j, i: (i, j)),
            pl.BlockSpec((2, block, 128), lambda j, i: (j, i, 0)),
        ],
        [sds((rows, heads * HD), BF16), sds((heads, rows, 128), BF16)],
        flops=heads * rows * keys * 128 * 4,
        nbytes=heads * (2 * rows + 2 * keys) * 256,
        trans=heads * rows * keys,
    )(q, k, v)


def shard_weights(gu_ref, dt_ref, pb_ref, shard):
    width = gu_ref.shape[1]
    if shard == 0:
        return gu_ref[0], gu_ref[1], dt_ref[...]
    hidden = pb_ref.shape[2]
    part = pb_ref.shape[1] // 3
    return tuple(pb_ref[:, c * part : (c + 1) * part, :].reshape(width, hidden) for c in range(3))


def ffn_kernel(parts, idx_ref, len_ref, weight_ref, x_ref, cot_ref, ow_ref, gu_ref, dt_ref, pb_ref, gain_ref, *refs):
    att_refs = refs[:parts]
    resid_ref, n2_ref, ffn_ref, gn2_ref, hid_ref, gg_ref, gup_ref, go_ref = refs[parts:]
    rows, width = x_ref.shape
    local = att_refs[0].shape[1]
    hidden_units = gu_ref.shape[2]
    me = idx_ref[0]
    resid = x_ref[...].astype(F32)
    for d in range(parts):
        block = ow_ref[:, me ^ d].reshape(local, width)
        resid = resid + dot(att_refs[d][...], block)
    resid_ref[...] = resid
    normed = (resid * rms(resid) * gain_ref[1:2, :]).astype(BF16)
    n2_ref[...] = normed
    first = (idx_ref[1] * pl.num_programs(0) + pl.program_id(0)) * rows
    slot = lax.broadcasted_iota(jnp.int32, (rows, 1), 0) + first
    row_weight = jnp.where(slot < len_ref[0], weight_ref[0], 0.0)
    go = (cot_ref[...].astype(F32) * row_weight).astype(BF16)
    go_ref[...] = go
    ffn = jnp.zeros((rows, width), F32)
    gn2 = jnp.zeros((rows, width), F32)
    for shard in range(2):
        gate_w, up_w, down_t = shard_weights(gu_ref, dt_ref, pb_ref, shard)
        cols = slice(shard * hidden_units, (shard + 1) * hidden_units)
        gate = dot(normed, gate_w)
        upper = dot(normed, up_w)
        sigma = jax.nn.sigmoid(gate)
        act = gate * sigma
        hidden = (act * upper).astype(BF16)
        hid_ref[:, cols] = hidden
        ffn = ffn + dot(hidden, down_t, NT)
        grad_hidden = dot(go, down_t)
        grad_up = (grad_hidden * act).astype(BF16)
        grad_gate = (grad_hidden * upper * (sigma + act * (1.0 - sigma))).astype(BF16)
        gup_ref[:, cols] = grad_up
        gg_ref[:, cols] = grad_gate
        gn2 = gn2 + dot(grad_gate, gate_w, NT) + dot(grad_up, up_w, NT)
    ffn_ref[...] = ffn.astype(BF16)
    gn2_ref[...] = gn2.astype(BF16)


def feed_forward(index, lengths, picked, atts, tokens, cotangent, out_full, gate_up, down_t, partner, gains, block=256):
    width = tokens.shape[1]
    parts = len(atts)
    rows = tokens.shape[0] // 2
    local = atts[0].shape[1]
    hidden = 2 * gate_up.shape[2]
    steps = rows // block
    row = lambda n: pl.BlockSpec((block, n), lambda i, idx: (i, 0))
    half = lambda n: pl.BlockSpec((block, n), lambda i, idx: (idx[1] * steps + i, 0))
    att_specs = [half(local)] + [row(local)] * (parts - 1)
    return call(
        functools.partial(ffn_kernel, parts),
        (steps,),
        [
            smem(), smem(), half(width), half(width),
            whole(out_full.shape), whole(gate_up.shape), whole(down_t.shape), whole(partner.shape), whole(gains.shape),
        ]
        + att_specs,
        [row(width), row(width), row(width), row(width), row(hidden), row(hidden), row(hidden), row(width)],
        [
            sds((rows, width), F32), sds((rows, width), BF16), sds((rows, width), BF16),
            sds((rows, width), BF16), sds((rows, hidden), BF16), sds((rows, hidden), BF16),
            sds((rows, hidden), BF16), sds((rows, width), BF16),
        ],
        flops=2 * rows * width * (width + 6 * hidden),
        nbytes=rows * width * 30 + 8 * width * hidden,
        trans=rows * hidden,
        prefetch=1,
    )(index, lengths, picked, tokens, cotangent, out_full, gate_up, down_t, partner, gains, *atts)


def ffn_grad_kernel(n2_ref, hid_ref, gg_ref, gup_ref, go_ref, gu_ref, dt_ref, pb_ref, out_ref, sum_ref, acc):
    shard = pl.program_id(0)
    step = pl.program_id(1)

    @pl.when(step == 0)
    def _():
        acc[...] = jnp.zeros_like(acc)

    n2 = n2_ref[...]
    acc[0] += dot(n2, gg_ref[...], TN)
    acc[1] += dot(n2, gup_ref[...], TN)
    acc[2] += dot(go_ref[...], hid_ref[...], TN)

    def gain_sum(which):
        gate_w, up_w, _ = shard_weights(gu_ref, dt_ref, pb_ref, which)
        total = jnp.sum(acc[0] * gate_w.astype(F32) + acc[1] * up_w.astype(F32), axis=1, keepdims=True)
        return jnp.broadcast_to(total, sum_ref.shape)

    @pl.when(step == pl.num_programs(1) - 1)
    def _():
        width = acc.shape[1]
        shares = out_ref.shape[0]
        part = width // shares
        for c in range(3):
            for d in range(shares):
                out_ref[d, 0, c * part : (c + 1) * part, :] = acc[c, d * part : (d + 1) * part, :].astype(BF16)

        @pl.when(shard == 0)
        def _():
            sum_ref[...] = gain_sum(0)

        @pl.when(shard == 1)
        def _():
            sum_ref[...] += gain_sum(1)


def ffn_grads(n2, hid, gg, gup, go, gate_up, down_t, partner, shares, block=512):
    rows, width = n2.shape
    hidden = hid.shape[1] // 2
    row = lambda n: pl.BlockSpec((block, n), lambda s, i: (i, 0))
    col = lambda n: pl.BlockSpec((block, n), lambda s, i: (i, s))
    part = width // shares
    return call(
        ffn_grad_kernel,
        (2, rows // block),
        [row(width), col(hidden), col(hidden), col(hidden), row(width),
         whole(gate_up.shape), whole(down_t.shape), whole(partner.shape)],
        [pl.BlockSpec((shares, 1, 3 * part, hidden), lambda s, i: (0, s, 0, 0)), whole((width, 128))],
        [sds((shares, 2, 3 * part, hidden), BF16), sds((width, 128), F32)],
        scratch=[pltpu.VMEM((3, width, hidden), F32)],
        flops=12 * rows * width * hidden,
        nbytes=rows * (2 * width + 3 * hidden) * 4 + 12 * width * hidden,
    )(n2, hid, gg, gup, go, gate_up, down_t, partner)


def resid_kernel(parts, members, idx_ref, len_ref, weight_ref, cot_ref, resid_ref, gn2_ref, ow_ref, gain_ref, *refs):
    gn2_refs = refs[: members - 1]
    att_refs = refs[members - 1 : members - 1 + parts]
    gr_ref, wg_ref, acc = refs[members - 1 + parts], refs[members + parts], refs[-1]
    g_refs = refs[members + parts + 1 : -1]
    rows, width = cot_ref.shape
    local = att_refs[0].shape[1]
    me = idx_ref[0]
    step = pl.program_id(0)
    first = me * rows * pl.num_programs(0) + step * rows
    slot = lax.broadcasted_iota(jnp.int32, (rows, 1), 0) + first
    row_weight = jnp.where(slot < len_ref[0], weight_ref[0], 0.0)
    gn2 = gn2_ref[...].astype(F32)
    for ref in gn2_refs:
        gn2 = gn2 + ref[...].astype(F32)
    resid = resid_ref[...]
    factor = rms(resid)
    grad = cot_ref[...].astype(F32) * row_weight + norm_back(gn2, gain_ref[1:2, :], resid * factor, factor)
    gr_ref[...] = grad
    low = grad.astype(BF16)

    @pl.when(step == 0)
    def _():
        acc[...] = jnp.zeros_like(acc)

    for d in range(parts):
        block = ow_ref[:, me ^ d].reshape(local, width)
        g_refs[d][...] = dot(low, block, NT).astype(BF16)
        acc[:, d * local : (d + 1) * local] += dot(low, att_refs[d][...], TN)

    @pl.when(step == pl.num_programs(0) - 1)
    def _():
        shares, part, _ = wg_ref.shape
        for d in range(shares):
            wg_ref[d] = acc[d * part : (d + 1) * part, :].astype(BF16)


def resid_back(index, lengths, picked, cotangent, resid, gn2, gn2_others, out_full, gains, atts, share, shares, block=256):
    width = cotangent.shape[1]
    parts = len(atts)
    local = atts[0].shape[1]
    members = len(gn2_others) + 1
    steps = share // block
    row = lambda n: pl.BlockSpec((block, n), lambda i, idx: (i, 0))
    full = lambda n: pl.BlockSpec((block, n), lambda i, idx: (idx[0] * steps + i, 0))
    half = lambda n: pl.BlockSpec((block, n), lambda i, idx: (idx[2] * steps + i, 0))
    return call(
        functools.partial(resid_kernel, parts, members),
        (steps,),
        [smem(), smem(), full(width), half(width), half(width), whole(out_full.shape), whole(gains.shape)]
        + [row(width)] * (members - 1)
        + [full(local)] + [half(local)] * (parts - 1),
        [row(width), whole((shares, width // shares, parts * local))] + [row(local)] * parts,
        [sds((share, width), F32), sds((shares, width // shares, parts * local), BF16)]
        + [sds((share, local), BF16)] * parts,
        scratch=[pltpu.VMEM((width, parts * local), F32)],
        flops=4 * share * width * width,
        nbytes=share * width * 20,
        prefetch=1,
    )(index, lengths, picked, cotangent, resid, gn2, out_full, gains, *gn2_others, *atts)


def attend_back_kernel(parts, idx_ref, g_ref, q_ref, k_ref, v_ref, att_ref, cos_ref, sin_ref, *refs):
    outs = refs[:parts]
    dk_acc, dv_acc = refs[parts:]
    rows = q_ref.shape[1]
    step = pl.program_id(0)
    me = idx_ref[0]
    lane = lax.broadcasted_iota(jnp.int32, (rows, 128), 1)

    def table(ref, d):
        return ref[pl.ds(pl.multiple_of((me ^ d) * rows, rows), rows), :]

    def back(v, d, scale):
        return ((v * table(cos_ref, d) - swap_halves(v) * table(sin_ref, d)) * scale).astype(BF16)

    @pl.when(step == 0)
    def _():
        dk_acc[...] = jnp.zeros_like(dk_acc)
        dv_acc[...] = jnp.zeros_like(dv_acc)

    grad = g_ref[0]
    prod = grad.astype(F32) * att_ref[...].astype(F32)
    zero = jnp.zeros((rows, 128), BF16)
    dqs = []
    for s in range(2):
        first = HD * (1 - s)
        own = (lane >= HD * s) & (lane < HD * (s + 1))
        delta = jnp.sum(jnp.where(own, prod, 0.0), axis=1, keepdims=True)
        hi, mid, low = split3(-delta)
        grad_own = jnp.where(own, grad, zero)
        grad_aug = jnp.where(lane == first + 2, low, grad_own)
        grad_aug = jnp.where(lane == first + 1, mid, grad_aug)
        grad_aug = jnp.where(lane == first, hi, grad_aug)
        q = q_ref[s]
        probs = jnp.exp2(dot(k_ref[s], q, NT))
        scores_grad = (probs * dot(v_ref[s], grad_aug, NT)).astype(BF16)
        dv_acc[...] += dot(probs.astype(BF16), grad_own)
        dk_acc[...] += dot(scores_grad, jnp.where(own, q, zero))
        dqs.append(dot(k_ref[s], scores_grad, TN).T)
    dq = jnp.where(lane < HD, dqs[0], dqs[1])
    for d in range(parts):

        @pl.when(step == d)
        def _():
            outs[d][0] = back(dq, d, FACTOR)

    @pl.when(step == parts - 1)
    def _():
        for d in range(parts):
            outs[d][1] = back(table(dk_acc, d), d, LN2)
            outs[d][2] = table(dv_acc, d).astype(BF16)


def attend_back(index, grads, q, k, v, att, cosine, sine, pair):
    parts, share, _ = grads.shape
    rows = q.shape[1]
    keys = pl.BlockSpec((2, rows, 128), lambda i, idx: (pair, 0, 0), pipeline_mode=pl.Buffered(1))
    return call(
        functools.partial(attend_back_kernel, parts),
        (parts,),
        [
            pl.BlockSpec((1, share, 128), lambda i, idx: (i, 0, pair)),
            pl.BlockSpec((2, share, 128), lambda i, idx: (pair, idx[0] ^ i, 0)),
            keys,
            keys,
            pl.BlockSpec((share, 128), lambda i, idx: (idx[0] ^ i, pair)),
            whole(cosine.shape),
            whole(sine.shape),
        ],
        [whole((3, share, 128))] * parts,
        [sds((3, share, 128), BF16)] * parts,
        scratch=[pltpu.VMEM((rows, 128), F32)] * 2,
        flops=2 * rows * rows * 128 * 10,
        nbytes=rows * 256 * 16,
        trans=2 * rows * rows,
        prefetch=1,
    )(index, grads, q, k, v, att, cosine, sine)


def project_grad_kernel(parts, pairs, idx_ref, x_ref, w_ref, gain_ref, *refs):
    act_refs = refs[: parts * pairs]
    wg_ref, sum_ref, acc = refs[parts * pairs :]
    step = pl.program_id(0)

    @pl.when(step == 0)
    def _():
        acc[...] = jnp.zeros_like(acc)

    x = x_ref[...].astype(F32)
    normed = (x * rms(x) * gain_ref[0:1, :]).astype(BF16)
    for d in range(parts):

        @pl.when(step == d)
        def _():
            acts = [act_refs[j * parts + d][c] for c in range(3) for j in range(pairs)]
            acc[...] += dot(normed, jnp.concatenate(acts, axis=1), TN)

    @pl.when(step == pl.num_programs(0) - 1)
    def _():
        shares, part, _ = wg_ref.shape
        local = w_ref.shape[2]
        for d in range(shares):
            wg_ref[d] = acc[d * part : (d + 1) * part, :].astype(BF16)
        gain_sum = acc[:, :local] * w_ref[0].astype(F32)
        for c in (1, 2):
            gain_sum += acc[:, c * local : (c + 1) * local] * w_ref[c].astype(F32)
        sum_ref[...] = jnp.broadcast_to(jnp.sum(gain_sum, axis=1, keepdims=True), sum_ref.shape)


def project_grads(index, tokens, acts, qkv_weight, gains, shares):
    width = tokens.shape[1]
    local = qkv_weight.shape[2]
    pairs, parts = len(acts), len(acts[0])
    share = acts[0][0].shape[1]
    flat = [a for group in acts for a in group]
    return call(
        functools.partial(project_grad_kernel, parts, pairs),
        (parts,),
        [
            pl.BlockSpec((share, width), lambda i, idx: (idx[0] ^ i, 0)),
            whole(qkv_weight.shape),
            whole(gains.shape),
        ]
        + [whole(a.shape) for a in flat],
        [whole((shares, width // shares, 3 * local)), whole((width, 128))],
        [sds((shares, width // shares, 3 * local), BF16), sds((width, 128), F32)],
        scratch=[pltpu.VMEM((width, 3 * local), F32)],
        flops=2 * tokens.shape[0] * width * 3 * local,
        nbytes=tokens.size * 2 + 8 * width * local * 3,
        prefetch=1,
    )(index, tokens, qkv_weight, gains, *flat)


def token_grad_kernel(parts, pairs, idx_ref, x_ref, gr_ref, w_ref, gain_ref, *refs):
    act_refs = refs[: parts * pairs]
    out_ref = refs[-1]
    me = idx_ref[0]
    width = x_ref.shape[1]
    local = 128 * pairs
    grad = jnp.zeros(x_ref.shape, F32)
    for d in range(parts):
        for c in range(3):
            act = jnp.concatenate([act_refs[j * parts + d][c] for j in range(pairs)], axis=1)
            grad = grad + dot(act, w_ref[:, me ^ d, c].reshape(width, local), NT)
    x = x_ref[...].astype(F32)
    factor = rms(x)
    out_ref[...] = gr_ref[...] + norm_back(grad, gain_ref[0:1, :], x * factor, factor)


def token_grad(index, tokens, grad_resid, qkv_full, gains, acts, block=256):
    share, width = grad_resid.shape
    pairs, parts = len(acts), len(acts[0])
    flat = [a for group in acts for a in group]
    steps = share // block
    return call(
        functools.partial(token_grad_kernel, parts, pairs),
        (steps,),
        [
            pl.BlockSpec((block, width), lambda i, idx: (idx[0] * steps + i, 0)),
            pl.BlockSpec((block, width), lambda i, idx: (i, 0)),
            whole(qkv_full.shape),
            whole(gains.shape),
        ]
        + [pl.BlockSpec((3, block, 128), lambda i, idx: (0, i, 0))] * len(flat),
        pl.BlockSpec((block, width), lambda i, idx: (i, 0)),
        sds((share, width), F32),
        flops=2 * share * width * width * 3,
        nbytes=share * width * 10 + 6 * width * width,
        prefetch=1,
    )(index, tokens, grad_resid, qkv_full, gains, *flat)


def body(
    tokens, qkv_weight, out_weight, gate_up_weight, down_weight, norm_gains,
    species_weight, species_ids, lengths, cotangent,
):
    rows, width = tokens.shape
    local = out_weight.shape[0]
    hidden = down_weight.shape[0]
    parts = lax.axis_size("tensor")
    members = parts // 2
    shares = lax.axis_size("dp")
    part = width // shares
    share = rows // parts
    me = lax.axis_index("tensor")
    dp = lax.axis_index("dp")
    half = me // members
    seat = me % members
    index = jnp.stack([me, half, seat]).astype(jnp.int32)
    cosine, sine = (jnp.asarray(t) for t in rotary_tables())
    pairs = local // 128

    def swap(a, d):
        return lax.ppermute(a, "tensor", [(i, i ^ d) for i in range(parts)])

    def cut(a, start, size, axis=0):
        return lax.dynamic_slice_in_dim(a, start, size, axis)

    def spread(a):
        stacked = [a] + [swap(a, d) for d in range(1, parts)]
        order = [lax.dynamic_index_in_dim(jnp.stack(stacked), me ^ d, 0, keepdims=False) for d in range(parts)]
        return lax.all_gather(jnp.stack(order), "dp", axis=0)

    matches = species_ids[:, None] == jnp.arange(species_weight.shape[0])[None, :]
    picked = jnp.sum(jnp.where(matches, species_weight[None, :], F32(0.0)), axis=1)

    down_t = down_weight.T
    out_full = spread(cut(out_weight, dp * (local // shares), local // shares))
    mine = jnp.concatenate(
        [cut(gate_up_weight[0], dp * part, part), cut(gate_up_weight[1], dp * part, part), cut(down_t, dp * part, part)]
    )
    partner = lax.all_gather(swap(mine, members), "dp", axis=0)
    qkv_full = spread(cut(qkv_weight, dp * part, part, 1))

    q, k, v = project(lengths, tokens, qkv_weight, norm_gains, cosine, sine)
    att, q_back = attend(q, k, v)
    near = cut(att, half * (rows // 2), rows // 2)
    far = cut(att, (1 - half) * (rows // 2), rows // 2)
    atts = [att] + [swap(near if d < members else far, d) for d in range(1, parts)]

    resid, n2, ffn, gn2, hid, gg, gup, go = feed_forward(
        index, lengths, picked, atts, tokens, cotangent, out_full, gate_up_weight, down_t, partner, norm_gains
    )
    gn2_others = [swap(cut(gn2, (seat ^ d) * share, share), d) for d in range(1, members)]
    ffn_wg, gain_two = ffn_grads(n2, hid, gg, gup, go, gate_up_weight, down_t, partner, shares)
    grad_resid, op_wg, *grads = resid_back(
        index, lengths, picked, cotangent, resid, gn2, gn2_others, out_full, norm_gains, atts, share, shares
    )
    grads = jnp.stack([grads[0]] + [swap(grads[d], d) for d in range(1, parts)])

    acts, got = [], []
    for j in range(pairs):
        group = attend_back(index, grads, q_back, k, v, att, cosine, sine, j)
        acts.append(group)
        got.append([group[0]] + [swap(group[d], d) for d in range(1, parts)])
    qkv_wg, gain_one = project_grads(index, tokens, acts, qkv_weight, norm_gains, shares)
    grad_tok = token_grad(index, tokens, grad_resid, qkv_full, norm_gains, got)

    ffn_own = cut(ffn, seat * share, share).astype(F32)
    for d in range(1, members):
        ffn_own = ffn_own + swap(cut(ffn, (seat ^ d) * share, share), d).astype(F32)
    out = cut(resid, seat * share, share) + ffn_own

    gains_grad = jnp.stack([gain_one[:, 0], gain_two[:, 0]]) / norm_gains
    for name, size in (("dp", shares), ("tensor", parts)):
        d = 1
        while d < size:
            gains_grad = gains_grad + lax.ppermute(gains_grad, name, [(i, i ^ d) for i in range(size)])
            d *= 2

    ffn_sum = lax.psum_scatter(ffn_wg, "dp", scatter_dimension=0, tiled=True)[0]
    ffn_sum = ffn_sum[0].astype(F32) + swap(ffn_sum[1], members).astype(F32)
    op_sum = lax.psum_scatter(op_wg, "dp", scatter_dimension=0, tiled=True)[0]
    grad_op = op_sum[:, :local].astype(F32)
    for d in range(1, parts):
        grad_op = grad_op + swap(op_sum[:, d * local : (d + 1) * local], d).astype(F32)
    qkv_sum = lax.psum_scatter(qkv_wg, "dp", scatter_dimension=0, tiled=True)[0].astype(F32)

    grad_gu = ffn_sum[: 2 * part].reshape(2, part, hidden)
    grad_down = ffn_sum[2 * part :].T
    grad_qkv = jnp.stack([qkv_sum[:, c * local : (c + 1) * local] for c in range(3)])
    return (out, grad_tok, grad_qkv, grad_op.T, grad_gu, grad_down, gains_grad)


def solution(mesh):
    in_specs = (
        P("dp", None),
        P(None, None, "tensor"),
        P("tensor", None),
        P(None, None, "tensor"),
        P("tensor", None),
        P(),
        P(),
        P("dp"),
        P("dp"),
        P("dp", None),
    )
    out_specs = (
        P(("dp", "tensor"), None),
        P(("dp", "tensor"), None),
        P(None, "dp", "tensor"),
        P("tensor", "dp"),
        P(None, "dp", "tensor"),
        P("tensor", "dp"),
        P(),
    )
    return jax.shard_map(body, mesh=mesh, in_specs=in_specs, out_specs=out_specs, check_vma=False)
```

time: 623 us -> 550 us (0.88); the launches traced: 623 us -> 543 us
  waiting for transfers between devices: 379 us -> 228 us
  starting transfers between devices: 0.5 us -> 56.4 us
  blocking collectives: 38.9 us -> 0 us
  local copies, waits for them, and re-layouts: 3.36 us -> 34.8 us
  Pallas kernels: 165 us -> 193 us
    ppermute x0 -> x30, waiting for transfers between devices: none -> 197 us  [the longest x25 156 us: swap(): return lax.ppermute(a, 'tensor', [(i, i ^ d) for i in range(parts)])]
    reduce_scatter x5 -> x3, waiting for transfers between devices: 226 us -> 30.3 us  [the longest x1 30.3 us: body(): op_sum = lax.psum_scatter(op_wg, 'dp', scatter_dimension=0, tiled=True)[0]]
    all_gather x3, waiting for transfers between devices: 151 us -> 0.01 us  [the longest x2 0.01 us: spread(): return lax.all_gather(jnp.stack(order), 'dp', axis=0)]
    ppermute x0 -> x30, starting transfers between devices: none -> 56.2 us  [the longest x25 53.7 us: swap(): return lax.ppermute(a, 'tensor', [(i, i ^ d) for i in range(parts)])]
    psum x1 -> x0, blocking collectives: 38.9 us -> none  [body(): gains_grad = lax.psum(gains_grad, ('dp', 'tensor'))]
    pallas_call x4 -> x7, Pallas kernels: 128 us -> 156 us  [the longest x2 54.1 us: attend_back(): call(functools.partial(attend_back_kernel, parts), (parts,), [pl.BlockSpe...]
    all_gather x0 -> x1, local copies, waits for them, and re-layouts: none -> 8.79 us  [body(): partner = lax.all_gather(swap(mine, members), 'dp', axis=0)]
    dynamic_slice x0 -> x11, local copies, waits for them, and re-layouts: none -> 8.49 us  [the longest x9 8.39 us: cut(): return lax.dynamic_slice_in_dim(a, start, size, axis)]
  transfers between devices with their start and end apart: 8 -> 36, of which waited for: 6 -> 21; matrix products, arithmetic and copies ran while one was open for 2% -> 6% of each run, Pallas kernels for 20% -> 36%
where the time goes in v2:
time: 550 us; the launch traced here: 543 us
  waiting for transfers between devices  228 us (41%)
  Pallas kernels  193 us (35%)
  starting transfers between devices  56.4 us (10%)
  local copies, waits for them, and re-layouts  34.8 us (6%)
  between operations  15.9 us (3%)
  other arithmetic  14.8 us (3%)
    ppermute x25, waiting for transfers between devices, swap(): return lax.ppermute(a, 'tensor', [(i, i ^ d) for i in range(parts)])  156 us
    pallas_call x2, Pallas kernels, attend_back(): call(functools.partial(attend_back_kernel, parts), (parts,), [pl.BlockSpe...  54.1 us
    ppermute x25, starting transfers between devices, swap(): return lax.ppermute(a, 'tensor', [(i, i ^ d) for i in range(parts)])  53.7 us
    pallas_call x1, Pallas kernels, feed_forward(): call(functools.partial(ffn_kernel, parts), (steps,), [smem(), smem(), hal...  41.1 us
    ppermute x5, waiting for transfers between devices, body(): lax.ppermute(gains_grad, name, [(i, i ^ d) for i in range(size)])  40.8 us
    reduce_scatter x1, waiting for transfers between devices, body(): op_sum = lax.psum_scatter(op_wg, 'dp', scatter_dimension=0, tiled=True)[0]  30.3 us
    pallas_call x1, Pallas kernels, ffn_grads(): call(ffn_grad_kernel, (2, rows // block), [row(width), col(hidden), col(h...  29.3 us
    pallas_call x1, Pallas kernels, attend(): call(functools.partial(attend_kernel, sub), (heads // 2, rows // block),...  27.8 us
  transfers between devices with their start and end apart: 36, of which 21 were waited for; matrix products, arithmetic and copies ran while one was open for 6% of the time, Pallas kernels for 36%

profile of v2, /device:TPU:0, one launch (start us, length us, event | category | flops | bytes accessed | tf_op | source)
XLA Modules:
  0.0 542.8 jit_solution(15999566791163650130)
XLA Ops:
  7.2 4.8 fusion
  12.1 1.8 constant_dynamic-slice_fusion.9
  16.9 4.1 collective-permute-start.3
  21.0 34.4 %collective-permute-done.3 = bf16[384,1024]{0,1:T(8,128)(2,1)S(1)} collective-permute-done((bf16[384,1024]{0,1:T(8,128)(2,1)S(1)}, bf16[384,1024]{0,1:T(8,128)(2,1)S(1)}, u32[]{:S(2)}, u32[]{:S(2)}) %collective-permute-start.3) | collective-permute-done | bytes 786464 | tf_op jit(solution)/shard_map/ppermute | solution.py:586
  56.4 3.6 collective-permute-start.2
  60.9 2.2 collective-permute-done.2
  63.1 2.1 collective-permute-done.1
  67.5 2.4 collective-permute-start.11
  70.3 1.7 collective-permute-start.9
  72.9 4.3 collective-permute-done.11
  77.2 9.3 %collective-permute-done.10 = bf16[3,128,256]{2,1,0:T(8,128)(2,1)S(1)} collective-permute-done((bf16[3,128,256]{2,1,0:T(8,128)(2,1)S(1)}, bf16[3,128,256]{2,1,0:T(8,128)(2,1)S(1)}, u32[]{:S(2)}, u32[]{:S(2)}) %collective-permute-start.10) | collective-permute-done | bytes 196640 | tf_op jit(solution)/shard_map/ppermute | solution.py:586
  88.5 9.4 %shard_map.171 = (bf16[4,2048,128]{2,1,0:T(8,128)(2,1)}, bf16[4,2048,128]{2,1,0:T(8,128)(2,1)}, bf16[4,2048,128]{2,1,0:T(8,128)(2,1)}) custom-call(s32[1]{0:T(128)S(6)} %copy.38.len_ref, bf16[2048,1024]{1,0:T(8,128)(2,1)} %x_ref.7, bf16[3,1024,256]{2,1,0:T(8,128)(2,1)} %w_ref.3, f32[2,1024]{1,0:T(2,128)} %gain_ref.9, f32[2048,128]{1,0:T(8,128)} %constant.78.clone.cos_ref, ...), custom_call_target="tpu_custom_call" | custom-call | flops 3221225472 | bytes 10485760 | tf_op jit(solution)/shard_map/pallas_call | solution.py:134
  97.9 27.8 %shard_map.172 = (bf16[2048,256]{1,0:T(8,128)(2,1)}, bf16[4,2048,128]{2,1,0:T(8,128)(2,1)}) custom-call(bf16[4,2048,128]{2,1,0:T(8,128)(2,1)} %get-tuple-element.38.q_ref, bf16[4,2048,128]{2,1,0:T(8,128)(2,1)} %get-tuple-element.39.k_ref, bf16[4,2048,128]{2,1,0:T(8,128)(2,1)} %get-tuple-element.40.v_ref), custom_call_target="tpu_custom_call" | custom-call | flops 8589934592 | bytes 8388608 | tf_op jit(solution)/shard_map/pallas_call | solution.py:177
  125.7 2.2 constant_dynamic-slice_fusion.7
  127.9 2.1 collective-permute-start.5
  130.0 2.3 collective-permute-start.6
  132.3 2.5 copy.31
  136.7 8.8 %copy.34 = bf16[3072,1024]{1,0:T(8,128)(2,1)} copy(bf16[3072,1024]{0,1:T(8,128)(2,1)} %all-gather.9.cloned.1.call-done) | data formatting | bytes 12582912 | tf_op jit(solution)/shard_map/all_gather | solution.py:604
  145.5 6.4 %collective-permute-done.4.refs_1_.refs_2_ = bf16[1024,256]{1,0:T(8,128)(2,1)S(1)} collective-permute-done((bf16[1024,256]{1,0:T(8,128)(2,1)}, bf16[1024,256]{1,0:T(8,128)(2,1)S(1)}, u32[]{:S(2)}, u32[]{:S(2)}) %collective-permute-start.4) | collective-permute-done | bytes 524320 | tf_op jit(solution)/shard_map/ppermute | solution.py:586
  151.9 14.5 %collective-permute-done.5.refs_2_.refs_3_ = bf16[1024,256]{1,0:T(8,128)(2,1)S(1)} collective-permute-done((bf16[1024,256]{1,0:T(8,128)(2,1)}, bf16[1024,256]{1,0:T(8,128)(2,1)S(1)}, u32[]{:S(2)}, u32[]{:S(2)}) %collective-permute-start.5) | collective-permute-done | bytes 524320 | tf_op jit(solution)/shard_map/ppermute | solution.py:586
  167.2 41.1 %shard_map.173 = (f32[1024,1024]{1,0:T(8,128)}, bf16[1024,1024]{1,0:T(8,128)(2,1)}, bf16[1024,1024]{1,0:T(8,128)(2,1)}, bf16[1024,1024]{1,0:T(8,128)(2,1)}, bf16...) custom-call(s32[3]{0:T(128)} %pad_add_fusion.idx_ref, ...), custom_call_target="tpu_custom_call" | custom-call | flops 27917287424 | bytes 48234496 | tf_op jit(solution)/shard_map/pallas_call | solution.py:256
  209.5 9.4 %collective-permute-start.8 = (bf16[512,1024]{1,0:T(8,128)(2,1)S(1)}, bf16[512,1024]{1,0:T(8,128)(2,1)S(1)}, u32[]{:S(2)}, u32[]{:S(2)}) collective-permute-start(bf16[512,1024]{1,0:T(8,128)(2,1)S(1)} %constant_dynamic-slice_fusion.5), channel_id=1, source_target_pairs={{0,1},{1,0},{2,3},{3,2},{4,5},{5,4},{6,7},{7,6},{8,9},{9,8},{10,11... | collective-permute-start | bytes 3145736 | tf_op jit(solution)/shard_map/ppermute | solution.py:586
  219.0 21.5 %collective-permute-done.8.refs_0_ = bf16[512,1024]{1,0:T(8,128)(2,1)S(1)} collective-permute-done((bf16[512,1024]{1,0:T(8,128)(2,1)S(1)}, bf16[512,1024]{1,0:T(8,128)(2,1)S(1)}, u32[]{:S(2)}, u32[]{:S(2)}) %collective-permute-start.8) | collective-permute-done | bytes 1048608 | tf_op jit(solution)/shard_map/ppermute | solution.py:586
  241.4 10.6 %shard_map.174 = (f32[512,1024]{1,0:T(8,128)}, bf16[8,128,1024]{2,1,0:T(8,128)(2,1)}, bf16[512,256]{1,0:T(8,128)(2,1)}, bf16[512,256]{1,0:T(8,128)(2,1)}, bf16[5...) custom-call(s32[3]{0:T(128)} %pad_add_fusion.idx_ref, s32[1]{0:T(128)S(6)} %copy.38.len_ref, f32[1]{0:T(128)} %bitcast.4.weight_ref, ...), custom_call_target="tpu_custom_call" | custom-call | flops 2147483648 | bytes 10485760 | tf_op jit(solution)/shard_map/pallas_call | solution.py:378
  253.6 1.7 collective-permute-start.13
  256.5 6.9 %collective-permute-done.14 = bf16[512,256]{1,0:T(8,128)(2,1)S(1)} collective-permute-done((bf16[512,256]{1,0:T(8,128)(2,1)}, bf16[512,256]{1,0:T(8,128)(2,1)S(1)}, u32[]{:S(2)}, u32[]{:S(2)}) %collective-permute-start.14) | collective-permute-done | bytes 262176 | tf_op jit(solution)/shard_map/ppermute | solution.py:586
  263.4 12.4 %collective-permute-done.13 = bf16[512,256]{1,0:T(8,128)(2,1)S(1)} collective-permute-done((bf16[512,256]{1,0:T(8,128)(2,1)}, bf16[512,256]{1,0:T(8,128)(2,1)S(1)}, u32[]{:S(2)}, u32[]{:S(2)}) %collective-permute-start.13) | collective-permute-done | bytes 262176 | tf_op jit(solution)/shard_map/ppermute | solution.py:586
  275.8 2.1 pad_maximum_fusion.g_ref
  277.9 27.0 %shard_map.175 = (bf16[3,512,128]{2,1,0:T(8,128)(2,1)}, bf16[3,512,128]{2,1,0:T(8,128)(2,1)}, bf16[3,512,128]{2,1,0:T(8,128)(2,1)}, bf16[3,512,128]{2,1,0:T(8,128)(2,1)}) custom-call(s32[3]{0:T(128)} %pad_add_fusion.idx_ref, bf16[4,512,256]{2,1,0:T(8,128)(2,1)} %pad_maximum_fusion.g_ref, bf16[4,2048,128]{2,1,0:T(8,128)(2,1)} %get-tuple-element.50.q_ref, ...), custom_call_target="tpu_custom_call" | custom-call | flops 10737418240 | bytes 8388608 | tf_op jit(solution)/shard_map/pallas_call | solution.py:450
  304.8 27.2 %shard_map.176 = (bf16[3,512,128]{2,1,0:T(8,128)(2,1)}, bf16[3,512,128]{2,1,0:T(8,128)(2,1)}, bf16[3,512,128]{2,1,0:T(8,128)(2,1)}, bf16[3,512,128]{2,1,0:T(8,128)(2,1)}) custom-call(s32[3]{0:T(128)} %pad_add_fusion.idx_ref, bf16[4,512,256]{2,1,0:T(8,128)(2,1)} %pad_maximum_fusion.g_ref, bf16[4,2048,128]{2,1,0:T(8,128)(2,1)} %get-tuple-element.50.q_ref, ...), custom_call_target="tpu_custom_call" | custom-call | flops 10737418240 | bytes 8388608 | tf_op jit(solution)/shard_map/pallas_call | solution.py:450
  332.0 10.9 %shard_map.178 = (bf16[8,128,768]{2,1,0:T(8,128)(2,1)}, f32[1024,128]{1,0:T(8,128)}) custom-call(s32[3]{0:T(128)} %pad_add_fusion.idx_ref, bf16[2048,1024]{1,0:T(8,128)(2,1)} %x_ref.7, bf16[3,1024,256]{2,1,0:T(8,128)(2,1)} %w_ref.3, f32[2,1024]{1,0:T(2,128)} %gain_ref.9, bf16[3,512,128]{2,1,0:T(8,128)(2,1)} %get-tuple-element.51.refs_0_, ...), custom_call_target="tpu_custom_call" | custom-call | flops 3221225472 | bytes 10485760 | tf_op jit(solution)/shard_map/pallas_call | solution.py:508
  343.0 29.3 %shard_map.179 = (bf16[8,2,384,1024]{3,2,1,0:T(8,128)(2,1)}, f32[1024,128]{1,0:T(8,128)}) custom-call(bf16[1024,1024]{1,0:T(8,128)(2,1)} %get-tuple-element.61.n2_ref, bf16[1024,2048]{1,0:T(8,128)(2,1)} %get-tuple-element.62.hid_ref, bf16[1024,2048]{1,0:T(8,128)(2,1)} %get-tuple-element.63.gg_ref, bf16[1024,2048]{1,0:T(8,128)(2,1)} %get-tuple-element.64.gup_ref, ...), custom_call_target="tpu_custom_call" | custom-call | flops 12884901888 | bytes 33554432 | tf_op jit(solution)/shard_map/pallas_call | solution.py:319
  374.3 2.1 collective-permute-start.15
  379.1 2.5 collective-permute-done.26
  382.7 2.5 collective-permute-done.27
  385.3 21.5 %collective-permute-done.28 = f32[2,1024]{1,0:T(2,128)S(1)} collective-permute-done((f32[2,1024]{1,0:T(2,128)S(1)}, f32[2,1024]{1,0:T(2,128)S(1)}, u32[]{:S(2)}, u32[]{:S(2)}) %collective-permute-start.28) | collective-permute-done | bytes 8224 | tf_op jit(solution)/shard_map/ppermute | solution.py:640
  406.9 2.8 collective-permute-start.16
  411.0 13.1 %collective-permute-done.29 = f32[2,1024]{1,0:T(2,128)S(1)} collective-permute-done((f32[2,1024]{1,0:T(2,128)S(1)}, f32[2,1024]{1,0:T(2,128)S(1)}, u32[]{:S(2)}, u32[]{:S(2)}) %collective-permute-start.29) | collective-permute-done | bytes 8224 | tf_op jit(solution)/shard_map/ppermute | solution.py:640
  424.1 2.7 collective-permute-start.20
  426.8 3.8 add_add_fusion
  431.2 20.9 %collective-permute-done.16.refs_2_ = bf16[3,512,128]{2,1,0:T(8,128)(2,1)S(1)} collective-permute-done((bf16[3,512,128]{2,1,0:T(8,128)(2,1)}, bf16[3,512,128]{2,1,0:T(8,128)(2,1)S(1)}, u32[]{:S(2)}, u32[]{:S(2)}) %collective-permute-start.16) | collective-permute-done | bytes 393248 | tf_op jit(solution)/shard_map/ppermute | solution.py:586
  452.1 16.9 %collective-permute-done.19.refs_6_ = bf16[3,512,128]{2,1,0:T(8,128)(2,1)} collective-permute-done((bf16[3,512,128]{2,1,0:T(8,128)(2,1)}, bf16[3,512,128]{2,1,0:T(8,128)(2,1)}, u32[]{:S(2)}, u32[]{:S(2)}) %collective-permute-start.19) | collective-permute-done | bytes 393248 | tf_op jit(solution)/shard_map/ppermute | solution.py:586
  469.1 9.7 %shard_map.177 = f32[512,1024]{1,0:T(8,128)} custom-call(s32[3]{0:T(128)} %pad_add_fusion.idx_ref, bf16[2048,1024]{1,0:T(8,128)(2,1)} %x_ref.7, f32[512,1024]{1,0:T(8,128)} %get-tuple-element.45.gr_ref, bf16[8,4,3,128,256]{4,3,2,1,0:T(8,128)(2,1)} %bitcast.52, f32[2,1024]{1,0:T(2,128)} %gain_ref.9, bf16[3,512,128]{2,1,0:T(8,128)(2,1)} %get-tuple-element.51.refs_0_, ...), custom_call_target="tpu_custom_call" | custom-call | flops 3221225472 | bytes 11534336 | tf_op jit(solution)/shard_map/pallas_call | solution.py:547
  481.2 9.0 %collective-permute-start.24 = (bf16[384,1024]{1,0:T(8,128)(2,1)S(1)}, bf16[384,1024]{1,0:T(8,128)(2,1)}, u32[]{:S(2)}, u32[]{:S(2)}) collective-permute-start(bf16[384,1024]{1,0:T(8,128)(2,1)S(1)} %slice_bitcast_fusion), channel_id=1, source_target_pairs={{0,2},{1,3},{2,0},{3,1},{4,6},{5,7},{6,4},{7,5},{8,10},{9,11},{10,... | collective-permute-start | bytes 2359304 | tf_op jit(solution)/shard_map/ppermute | solution.py:586
  490.2 30.3 %reduce-scatter.6.cloned.1.call-done = bf16[1,128,1024]{2,1,0:T(8,128)(2,1)} async-done(((bf16[8,128,1024]{2,1,0:T(8,128)(2,1)}), bf16[1,128,1024]{2,1,0:T(8,128)(2,1)}) %reduce-scatter.6.cloned.1.call-update) | async-done | bytes 262160 | tf_op jit(solution)/shard_map/reduce_scatter | solution.py:645
  521.4 3.4 collective-permute-start.23
  526.6 1.6 collective-permute-done.23
  528.1 2.4 collective-permute-done.22
  (117 shorter events, 34.9 us)
Async XLA Ops:
  7.2 49.2 %copy-start = (bf16[256,1024]{1,0:T(8,128)(2,1)S(1)}, bf16[256,1024]{1,0:T(8,128)(2,1)}, u32[]{:S(2)}) copy-start(bf16[256,1024]{1,0:T(8,128)(2,1)} %param.14) | copy-start | bytes 1572868
  7.2 129.5 %all-gather.9.cloned.1.call-start = ((), (), s32[]{:S(2)}) async-start(), calls=%async_computation.7 | async-start | bytes 7077888 | tf_op jit(solution)/shard_map/all_gather | solution.py:604
  7.2 4.8 copy-start.2
  16.9 38.5 %collective-permute-start.3 = (bf16[384,1024]{0,1:T(8,128)(2,1)S(1)}, bf16[384,1024]{0,1:T(8,128)(2,1)S(1)}, u32[]{:S(2)}, u32[]{:S(2)}) collective-permute-start(bf16[384,1024]{0,1:T(8,128)(2,1)S(1)} %pad_maximum_fusion.1), channel_id=1, source_target_pairs={{0,2},{1,3},{2,0},{3,1},{4,6},{5,7},{6,4},{7,5},{8,10},{9,11},{10,... | collective-permute-start | bytes 2359304 | tf_op jit(solution)/shard_map/ppermute | solution.py:586
  56.4 110.0 %all-gather.7.cloned.1.call-start = ((), (), s32[]{:S(2)}) async-start(), calls=%async_computation.6 | async-start | bytes 2359296 | tf_op jit(solution)/shard_map/all_gather | solution.py:594
  56.4 6.7 %collective-permute-start.2 = (bf16[32,1024]{1,0:T(8,128)(2,1)S(1)}, bf16[32,1024]{1,0:T(8,128)(2,1)S(1)}, u32[]{:S(2)}, u32[]{:S(2)}) collective-permute-start(bf16[32,1024]{1,0:T(8,128)(2,1)S(1)} %constant_dynamic-slice_fusion.15), channel_id=1, source_target_pairs={{0,3},{1,2},{2,1},{3,0},{4,7},{5,6},{6,5},{7,4},{8,11},{9,10},{10,... | collective-permute-start | bytes 196616 | tf_op jit(solution)/shard_map/ppermute | solution.py:586
  60.0 5.2 collective-permute-start.1
  60.0 5.6 %collective-permute-start = (bf16[32,1024]{1,0:T(8,128)(2,1)S(1)}, bf16[32,1024]{1,0:T(8,128)(2,1)S(1)}, u32[]{:S(2)}, u32[]{:S(2)}) collective-permute-start(bf16[32,1024]{1,0:T(8,128)(2,1)S(1)} %constant_dynamic-slice_fusion.15), channel_id=1, source_target_pairs={{0,1},{1,0},{2,3},{3,2},{4,5},{5,4},{6,7},{7,6},{8,9},{9,8},{10,11... | collective-permute-start | bytes 196616 | tf_op jit(solution)/shard_map/ppermute | solution.py:586
  66.5 364.7 %all-gather.11.cloned.1.call-start = ((), (), s32[]{:S(2)}) async-start(), calls=%async_computation.8 | async-start | bytes 7077888 | tf_op jit(solution)/shard_map/all_gather | solution.py:594
  67.5 9.7 %collective-permute-start.11 = (bf16[3,128,256]{2,1,0:T(8,128)(2,1)S(1)}, bf16[3,128,256]{2,1,0:T(8,128)(2,1)S(1)}, u32[]{:S(2)}, u32[]{:S(2)}) collective-permute-start(bf16[3,128,256]{2,1,0:T(8,128)(2,1)S(1)} %constant_dynamic-slice_fusion.4), channel_id=1, source_target_pairs={{0,3},{1,2},{2,1},{3,0},{4,7},{5,6},{6,5},{7,4},{8,11},{9,10},{10,... | collective-permute-start | bytes 589832 | tf_op jit(solution)/shard_map/ppermute | solution.py:586
  69.9 16.7 %collective-permute-start.10 = (bf16[3,128,256]{2,1,0:T(8,128)(2,1)S(1)}, bf16[3,128,256]{2,1,0:T(8,128)(2,1)S(1)}, u32[]{:S(2)}, u32[]{:S(2)}) collective-permute-start(bf16[3,128,256]{2,1,0:T(8,128)(2,1)S(1)} %constant_dynamic-slice_fusion.4), channel_id=1, source_target_pairs={{0,2},{1,3},{2,0},{3,1},{4,6},{5,7},{6,4},{7,5},{8,10},{9,11},{10,... | collective-permute-start | bytes 589832 | tf_op jit(solution)/shard_map/ppermute | solution.py:586
  70.3 16.3 %collective-permute-start.9 = (bf16[3,128,256]{2,1,0:T(8,128)(2,1)S(1)}, bf16[3,128,256]{2,1,0:T(8,128)(2,1)S(1)}, u32[]{:S(2)}, u32[]{:S(2)}) collective-permute-start(bf16[3,128,256]{2,1,0:T(8,128)(2,1)S(1)} %constant_dynamic-slice_fusion.4), channel_id=1, source_target_pairs={{0,1},{1,0},{2,3},{3,2},{4,5},{5,4},{6,7},{7,6},{8,9},{9,8},{10,11... | collective-permute-start | bytes 589832 | tf_op jit(solution)/shard_map/ppermute | solution.py:586
  87.8 391.1 %reduce-scatter.4.cloned.1.call-start = ((), (), s32[]{:S(2)}) async-start(), calls=%async_computation.3 | async-start | bytes 1769472 | tf_op jit(solution)/shard_map/reduce_scatter | solution.py:649
  127.9 24.0 %collective-permute-start.4 = (bf16[1024,256]{1,0:T(8,128)(2,1)}, bf16[1024,256]{1,0:T(8,128)(2,1)S(1)}, u32[]{:S(2)}, u32[]{:S(2)}) collective-permute-start(bf16[1024,256]{1,0:T(8,128)(2,1)} %get-tuple-element.93), channel_id=1, source_target_pairs={{0,1},{1,0},{2,3},{3,2},{4,5},{5,4},{6,7},{7,6},{8,9},{9,8},{10,11... | collective-permute-start | bytes 1572872 | tf_op jit(solution)/shard_map/ppermute | solution.py:586
  127.9 38.4 %collective-permute-start.5 = (bf16[1024,256]{1,0:T(8,128)(2,1)}, bf16[1024,256]{1,0:T(8,128)(2,1)S(1)}, u32[]{:S(2)}, u32[]{:S(2)}) collective-permute-start(bf16[1024,256]{1,0:T(8,128)(2,1)} %get-tuple-element.92), channel_id=1, source_target_pairs={{0,2},{1,3},{2,0},{3,1},{4,6},{5,7},{6,4},{7,5},{8,10},{9,11},{10,... | collective-permute-start | bytes 1572872 | tf_op jit(solution)/shard_map/ppermute | solution.py:586
  130.0 36.4 %collective-permute-start.6 = (bf16[1024,256]{1,0:T(8,128)(2,1)}, bf16[1024,256]{1,0:T(8,128)(2,1)}, u32[]{:S(2)}, u32[]{:S(2)}) collective-permute-start(bf16[1024,256]{1,0:T(8,128)(2,1)} %get-tuple-element.92), channel_id=1, source_target_pairs={{0,3},{1,2},{2,1},{3,0},{4,7},{5,6},{6,5},{7,4},{8,11},{9,10},{10,... | collective-permute-start | bytes 1572872 | tf_op jit(solution)/shard_map/ppermute | solution.py:586
  132.3 3.8 copy-start.15
  151.9 14.5 %copy-start.7 = (bf16[1024,256]{1,0:T(8,128)(2,1)}, bf16[1024,256]{1,0:T(8,128)(2,1)S(1)}, u32[]{:S(2)}) copy-start(bf16[1024,256]{1,0:T(8,128)(2,1)S(1)} %collective-permute-done.4.refs_1_.refs_2_) | copy-start | bytes 1572868
  209.5 30.9 %collective-permute-start.8 = (bf16[512,1024]{1,0:T(8,128)(2,1)S(1)}, bf16[512,1024]{1,0:T(8,128)(2,1)S(1)}, u32[]{:S(2)}, u32[]{:S(2)}) collective-permute-start(bf16[512,1024]{1,0:T(8,128)(2,1)S(1)} %constant_dynamic-slice_fusion.5), channel_id=1, source_target_pairs={{0,1},{1,0},{2,3},{3,2},{4,5},{5,4},{6,7},{7,6},{8,9},{9,8},{10,11... | collective-permute-start | bytes 3145736 | tf_op jit(solution)/shard_map/ppermute | solution.py:586
  252.0 11.3 %collective-permute-start.14 = (bf16[512,256]{1,0:T(8,128)(2,1)}, bf16[512,256]{1,0:T(8,128)(2,1)S(1)}, u32[]{:S(2)}, u32[]{:S(2)}) collective-permute-start(bf16[512,256]{1,0:T(8,128)(2,1)} %get-tuple-element.49), channel_id=1, source_target_pairs={{0,3},{1,2},{2,1},{3,0},{4,7},{5,6},{6,5},{7,4},{8,11},{9,10},{10,... | collective-permute-start | bytes 786440 | tf_op jit(solution)/shard_map/ppermute | solution.py:586
  253.6 22.2 %collective-permute-start.13 = (bf16[512,256]{1,0:T(8,128)(2,1)}, bf16[512,256]{1,0:T(8,128)(2,1)S(1)}, u32[]{:S(2)}, u32[]{:S(2)}) collective-permute-start(bf16[512,256]{1,0:T(8,128)(2,1)} %get-tuple-element.48), channel_id=1, source_target_pairs={{0,2},{1,3},{2,0},{3,1},{4,6},{5,7},{6,4},{7,5},{8,10},{9,11},{10,... | collective-permute-start | bytes 786440 | tf_op jit(solution)/shard_map/ppermute | solution.py:586
  255.3 20.5 %collective-permute-start.12 = (bf16[512,256]{1,0:T(8,128)(2,1)}, bf16[512,256]{1,0:T(8,128)(2,1)S(1)}, u32[]{:S(2)}, u32[]{:S(2)}) collective-permute-start(bf16[512,256]{1,0:T(8,128)(2,1)} %get-tuple-element.47), channel_id=1, source_target_pairs={{0,1},{1,0},{2,3},{3,2},{4,5},{5,4},{6,7},{7,6},{8,9},{9,8},{10,11... | collective-permute-start | bytes 786440 | tf_op jit(solution)/shard_map/ppermute | solution.py:586
  343.0 136.8 %reduce-scatter.8.cloned.1.call-start = ((), (), s32[]{:S(2)}) async-start(), calls=%async_computation.5 | async-start | bytes 14155776 | tf_op jit(solution)/shard_map/reduce_scatter | solution.py:643
  372.3 148.1 %reduce-scatter.6.cloned.1.call-start = ((), (), s32[]{:S(2)}) async-start(), calls=%async_computation.4 | async-start | bytes 2359296 | tf_op jit(solution)/shard_map/reduce_scatter | solution.py:645
  372.4 1.7 copy-start.10
  372.4 4.0 copy-start.9
  372.9 3.7 copy-start.14
  374.0 37.0 %collective-permute-start.7 = (bf16[512,1024]{1,0:T(8,128)(2,1)S(1)}, bf16[512,1024]{1,0:T(8,128)(2,1)}, u32[]{:S(2)}, u32[]{:S(2)}) collective-permute-start(bf16[512,1024]{1,0:T(8,128)(2,1)S(1)} %constant_dynamic-slice_fusion.6), channel_id=1, source_target_pairs={{0,1},{1,0},{2,3},{3,2},{4,5},{5,4},{6,7},{7,6},{8,9},{9,8},{10,11... | collective-permute-start | bytes 3145736 | tf_op jit(solution)/shard_map/ppermute | solution.py:586
  374.3 49.8 %collective-permute-start.15 = (bf16[3,512,128]{2,1,0:T(8,128)(2,1)S(1)}, bf16[3,512,128]{2,1,0:T(8,128)(2,1)S(1)}, u32[]{:S(2)}, u32[]{:S(2)}) collective-permute-start(bf16[3,512,128]{2,1,0:T(8,128)(2,1)S(1)} %copy-done.16), channel_id=1, source_target_pairs={{0,1},{1,0},{2,3},{3,2},{4,5},{5,4},{6,7},{7,6},{8,9},{9,8},{10,11... | collective-permute-start | bytes 1179656 | tf_op jit(solution)/shard_map/ppermute | solution.py:586
  376.6 1.2 collective-permute-start.25
  377.9 3.7 collective-permute-start.26
  381.6 3.7 collective-permute-start.27
  385.2 21.5 %collective-permute-start.28 = (f32[2,1024]{1,0:T(2,128)S(1)}, f32[2,1024]{1,0:T(2,128)S(1)}, u32[]{:S(2)}, u32[]{:S(2)}) collective-permute-start(f32[2,1024]{1,0:T(2,128)S(1)} %add.104), channel_id=1, source_target_pairs={{0,1},{1,0},{2,3},{3,2},{4,5},{5,4},{6,7},{7,6},{8,9},{9,8},{10,11... | collective-permute-start | bytes 24584 | tf_op jit(solution)/shard_map/ppermute | solution.py:640
  406.8 17.3 %collective-permute-start.29 = (f32[2,1024]{1,0:T(2,128)S(1)}, f32[2,1024]{1,0:T(2,128)S(1)}, u32[]{:S(2)}, u32[]{:S(2)}) collective-permute-start(f32[2,1024]{1,0:T(2,128)S(1)} %add.105), channel_id=1, source_target_pairs={{0,2},{1,3},{2,0},{3,1},{4,6},{5,7},{6,4},{7,5},{8,10},{9,11},{10,... | collective-permute-start | bytes 24584 | tf_op jit(solution)/shard_map/ppermute | solution.py:640
  406.9 45.3 %collective-permute-start.16 = (bf16[3,512,128]{2,1,0:T(8,128)(2,1)}, bf16[3,512,128]{2,1,0:T(8,128)(2,1)S(1)}, u32[]{:S(2)}, u32[]{:S(2)}) collective-permute-start(bf16[3,512,128]{2,1,0:T(8,128)(2,1)} %get-tuple-element.53.refs_2_), channel_id=1, source_target_pairs={{0,2},{1,3},{2,0},{3,1},{4,6},{5,7},{6,4},{7,5},{8,10},{9,11},{10,... | collective-permute-start | bytes 1179656 | tf_op jit(solution)/shard_map/ppermute | solution.py:586
  409.7 42.4 %collective-permute-start.17 = (bf16[3,512,128]{2,1,0:T(8,128)(2,1)}, bf16[3,512,128]{2,1,0:T(8,128)(2,1)S(1)}, u32[]{:S(2)}, u32[]{:S(2)}) collective-permute-start(bf16[3,512,128]{2,1,0:T(8,128)(2,1)} %get-tuple-element.54.refs_3_), channel_id=1, source_target_pairs={{0,3},{1,2},{2,1},{3,0},{4,7},{5,6},{6,5},{7,4},{8,11},{9,10},{10,... | collective-permute-start | bytes 1179656 | tf_op jit(solution)/shard_map/ppermute | solution.py:586
  411.0 41.2 %collective-permute-start.18 = (bf16[3,512,128]{2,1,0:T(8,128)(2,1)}, bf16[3,512,128]{2,1,0:T(8,128)(2,1)}, u32[]{:S(2)}, u32[]{:S(2)}) collective-permute-start(bf16[3,512,128]{2,1,0:T(8,128)(2,1)} %get-tuple-element.56.refs_5_), channel_id=1, source_target_pairs={{0,1},{1,0},{2,3},{3,2},{4,5},{5,4},{6,7},{7,6},{8,9},{9,8},{10,11... | collective-permute-start | bytes 1179656 | tf_op jit(solution)/shard_map/ppermute | solution.py:586
  424.0 45.0 %collective-permute-start.19 = (bf16[3,512,128]{2,1,0:T(8,128)(2,1)}, bf16[3,512,128]{2,1,0:T(8,128)(2,1)}, u32[]{:S(2)}, u32[]{:S(2)}) collective-permute-start(bf16[3,512,128]{2,1,0:T(8,128)(2,1)} %get-tuple-element.57.refs_6_), channel_id=1, source_target_pairs={{0,2},{1,3},{2,0},{3,1},{4,6},{5,7},{6,4},{7,5},{8,10},{9,11},{10,... | collective-permute-start | bytes 1179656 | tf_op jit(solution)/shard_map/ppermute | solution.py:586
  424.1 6.5 %copy-start.11 = (bf16[3,512,128]{2,1,0:T(8,128)(2,1)}, bf16[3,512,128]{2,1,0:T(8,128)(2,1)S(1)}, u32[]{:S(2)}) copy-start(bf16[3,512,128]{2,1,0:T(8,128)(2,1)S(1)} %collective-permute-done.15.refs_1_) | copy-start | bytes 1179652
  424.1 45.0 %collective-permute-start.20 = (bf16[3,512,128]{2,1,0:T(8,128)(2,1)}, bf16[3,512,128]{2,1,0:T(8,128)(2,1)}, u32[]{:S(2)}, u32[]{:S(2)}) collective-permute-start(bf16[3,512,128]{2,1,0:T(8,128)(2,1)} %get-tuple-element.58.refs_7_), channel_id=1, source_target_pairs={{0,3},{1,2},{2,1},{3,0},{4,7},{5,6},{6,5},{7,4},{8,11},{9,10},{10,... | collective-permute-start | bytes 1179656 | tf_op jit(solution)/shard_map/ppermute | solution.py:586
  452.1 17.0 %copy-start.12 = (bf16[3,512,128]{2,1,0:T(8,128)(2,1)}, bf16[3,512,128]{2,1,0:T(8,128)(2,1)S(1)}, u32[]{:S(2)}) copy-start(bf16[3,512,128]{2,1,0:T(8,128)(2,1)S(1)} %collective-permute-done.16.refs_2_) | copy-start | bytes 1179652
  452.1 17.0 %copy-start.13 = (bf16[3,512,128]{2,1,0:T(8,128)(2,1)}, bf16[3,512,128]{2,1,0:T(8,128)(2,1)S(1)}, u32[]{:S(2)}) copy-start(bf16[3,512,128]{2,1,0:T(8,128)(2,1)S(1)} %collective-permute-done.17.refs_3_) | copy-start | bytes 1179652
  479.8 52.4 %copy-start.4 = (bf16[1,2,384,1024]{3,2,1,0:T(8,128)(2,1)S(1)}, bf16[1,2,384,1024]{3,2,1,0:T(8,128)(2,1)}, u32[]{:S(2)}) copy-start(bf16[1,2,384,1024]{3,2,1,0:T(8,128)(2,1)} %reduce-scatter.8.cloned.1.call-done) | copy-start | bytes 4718596
  481.2 51.1 %collective-permute-start.24 = (bf16[384,1024]{1,0:T(8,128)(2,1)S(1)}, bf16[384,1024]{1,0:T(8,128)(2,1)}, u32[]{:S(2)}, u32[]{:S(2)}) collective-permute-start(bf16[384,1024]{1,0:T(8,128)(2,1)S(1)} %slice_bitcast_fusion), channel_id=1, source_target_pairs={{0,2},{1,3},{2,0},{3,1},{4,6},{5,7},{6,4},{7,5},{8,10},{9,11},{10,... | collective-permute-start | bytes 2359304 | tf_op jit(solution)/shard_map/ppermute | solution.py:586
  521.4 6.8 %collective-permute-start.23 = (bf16[128,256]{1,0:T(8,128)(2,1)S(1)}, bf16[128,256]{1,0:T(8,128)(2,1)S(1)}, u32[]{:S(2)}, u32[]{:S(2)}) collective-permute-start(bf16[128,256]{1,0:T(8,128)(2,1)S(1)} %get-tuple-element.102), channel_id=1, source_target_pairs={{0,3},{1,2},{2,1},{3,0},{4,7},{5,6},{6,5},{7,4},{8,11},{9,10},{10,... | collective-permute-start | bytes 196616 | tf_op jit(solution)/shard_map/ppermute | solution.py:586
  524.8 5.8 %collective-permute-start.22 = (bf16[128,256]{1,0:T(8,128)(2,1)S(1)}, bf16[128,256]{1,0:T(8,128)(2,1)S(1)}, u32[]{:S(2)}, u32[]{:S(2)}) collective-permute-start(bf16[128,256]{1,0:T(8,128)(2,1)S(1)} %get-tuple-element.103), channel_id=1, source_target_pairs={{0,2},{1,3},{2,0},{3,1},{4,6},{5,7},{6,4},{7,5},{8,10},{9,11},{10,... | collective-permute-start | bytes 196616 | tf_op jit(solution)/shard_map/ppermute | solution.py:586
  524.8 5.8 %collective-permute-start.21 = (bf16[128,256]{1,0:T(8,128)(2,1)S(1)}, bf16[128,256]{1,0:T(8,128)(2,1)S(1)}, u32[]{:S(2)}, u32[]{:S(2)}) collective-permute-start(bf16[128,256]{1,0:T(8,128)(2,1)S(1)} %get-tuple-element.101), channel_id=1, source_target_pairs={{0,1},{1,0},{2,3},{3,2},{4,5},{5,4},{6,7},{7,6},{8,9},{9,8},{10,11... | collective-permute-start | bytes 196616 | tf_op jit(solution)/shard_map/ppermute | solution.py:586
  532.2 3.6 copy-start.1
  (5 other events, 5.6 us)
Sparse Core Ops, SparseCore 0:
  56.5 47.8 all-gather.8
  106.8 27.8 all-gather.6
  136.6 45.5 all-gather.10
  343.1 36.9 reduce-scatter.3
  383.5 92.5 reduce-scatter.7
  479.2 41.1 reduce-scatter.5

commit v3 on v2

v3 whole, which is shorter than its diff:
```python
import functools
import math

import jax
import jax.numpy as jnp
import numpy as np
from jax import lax
from jax.experimental import pallas as pl
from jax.experimental.pallas import tpu as pltpu
from jax.sharding import PartitionSpec as P

HD = 64
WIN = 2048
EPSILON = 1e-05
NEG_FILL = -1e30
LOG2E = math.log2(math.e)
LN2 = math.log(2.0)
FACTOR = HD ** (-0.5)
VMEM = 60 * 2**20
F32 = jnp.float32
BF16 = jnp.bfloat16

NN = (((1,), (0,)), ((), ()))
NT = (((1,), (1,)), ((), ()))
TN = (((0,), (0,)), ((), ()))


def dot(a, b, dims=NN):
    return lax.dot_general(a, b, dims, preferred_element_type=F32)


def call(kernel, grid, in_specs, out_specs, out_shape, scratch=(), flops=0, nbytes=0, trans=0, prefetch=0):
    return pl.pallas_call(
        kernel,
        grid_spec=pltpu.PrefetchScalarGridSpec(
            num_scalar_prefetch=prefetch,
            grid=grid,
            in_specs=in_specs,
            out_specs=out_specs,
            scratch_shapes=list(scratch),
        ),
        out_shape=out_shape,
        compiler_params=pltpu.CompilerParams(vmem_limit_bytes=VMEM),
        cost_estimate=pl.CostEstimate(flops=flops, bytes_accessed=nbytes, transcendentals=trans),
    )


def whole(shape):
    return pl.BlockSpec(shape, lambda *_: (0,) * len(shape), pipeline_mode=pl.Buffered(1))


def smem():
    return pl.BlockSpec(memory_space=pltpu.SMEM)


def sds(shape, dtype):
    return jax.ShapeDtypeStruct(shape, dtype)


def rotary_tables():
    position = np.arange(WIN, dtype=np.float64)
    frequency = 10000.0 ** (-2.0 * np.arange(HD // 2, dtype=np.float64) / HD)
    angles = position[:, None] * frequency[None, :]
    cosine = np.cos(angles)
    sine = np.sin(angles)
    cos_full = np.tile(np.concatenate([cosine, cosine], axis=1), (1, 2))
    sin_full = np.tile(np.concatenate([-sine, sine], axis=1), (1, 2))
    return cos_full.astype(np.float32), sin_full.astype(np.float32)


def swap_halves(v):
    lane = lax.broadcasted_iota(jnp.int32, v.shape, 1)
    return jnp.where(lane % HD < HD // 2, pltpu.roll(v, 96, 1), pltpu.roll(v, 32, 1))


def rms(x):
    return lax.rsqrt(jnp.mean(x * x, axis=-1, keepdims=True) + EPSILON)


def split3(v):
    hi = v.astype(BF16)
    rest = v - hi.astype(F32)
    mid = rest.astype(BF16)
    low = (rest - mid.astype(F32)).astype(BF16)
    return hi, mid, low


def norm_back(grad_normed, gain, unit, factor):
    scaled = grad_normed * gain
    return factor * (scaled - unit * jnp.mean(scaled * unit, axis=-1, keepdims=True))


def qkv_kernel(len_ref, x_ref, w_ref, gain_ref, cos_ref, sin_ref, q_ref, k_ref, v_ref):
    rows = x_ref.shape[0]
    x = x_ref[...].astype(F32)
    normed = (x * rms(x) * gain_ref[0:1, :]).astype(BF16)
    cosine = cos_ref[...]
    sine = sin_ref[...]
    lane = lax.broadcasted_iota(jnp.int32, (rows, 128), 1)
    slot = lax.broadcasted_iota(jnp.int32, (rows, 128), 0) + pl.program_id(0) * rows
    masked = jnp.where(slot < len_ref[0], 0.0, NEG_FILL).astype(BF16)
    one = jnp.ones((rows, 128), BF16)
    zero = jnp.zeros((rows, 128), BF16)
    pairs = w_ref.shape[2] // 128
    for c in range(3):
        y = dot(normed, w_ref[c])
        for j in range(pairs):
            v = y[:, 128 * j : 128 * (j + 1)]
            if c < 2:
                v = v * cosine + swap_halves(v) * sine
            if c == 0:
                v = v * (FACTOR * LOG2E)
            v = v.astype(BF16)
            for s in range(2):
                first = HD * (1 - s)
                own = (lane >= HD * s) & (lane < HD * (s + 1))
                if c == 0:
                    q_ref[2 * j + s] = jnp.where(own, v, jnp.where(lane == first, one, zero))
                elif c == 1:
                    tail = jnp.where(
                        lane == first, masked, jnp.where(lane < first + 4, one, zero)
                    )
                    tail = jnp.where(lane < first, zero, tail)
                    k_ref[2 * j + s] = jnp.where(own, v, tail)
                else:
                    v_ref[2 * j + s] = jnp.where(own, v, one)


def project(lengths, tokens, qkv_weight, gains, cosine, sine, block=512):
    rows, width = tokens.shape
    local = qkv_weight.shape[2]
    heads = local // HD
    spec = pl.BlockSpec((heads, block, 128), lambda i: (0, i, 0))
    return call(
        qkv_kernel,
        (rows // block,),
        [
            smem(),
            pl.BlockSpec((block, width), lambda i: (i, 0)),
            whole(qkv_weight.shape),
            whole(gains.shape),
            pl.BlockSpec((block, 128), lambda i: (i, 0)),
            pl.BlockSpec((block, 128), lambda i: (i, 0)),
        ],
        [spec] * 3,
        [sds((heads, rows, 128), BF16)] * 3,
        flops=2 * rows * width * 3 * local,
        nbytes=rows * width * 2 + 3 * heads * rows * 256,
    )(lengths, tokens, qkv_weight, gains, cosine, sine)


def attend_kernel(sub, parts, idx_ref, q_ref, k_ref, v_ref, *refs):
    o_refs = refs[:parts]
    nat_ref, qb_ref = refs[parts:]
    rows = q_ref.shape[1]
    lane = lax.broadcasted_iota(jnp.int32, (sub, 128), 1)
    for r in range(rows // sub):
        part = slice(r * sub, (r + 1) * sub)
        outs = []
        for s in range(2):
            q = q_ref[s, part, :]
            scores = dot(q, k_ref[s], NT)
            peak = jnp.max(scores, axis=1, keepdims=True)
            expo = jnp.exp2(scores - peak).astype(BF16)
            acc = dot(expo, v_ref[s])
            outs.append(acc / pltpu.roll(acc, HD, 1))
            first = HD * (1 - s)
            total = jnp.where((lane >= first) & (lane < first + HD), acc, 1.0)
            hi, mid, low = split3(-(peak + jnp.log2(total)))
            tail = jnp.where(lane == first + 3, low, q)
            tail = jnp.where(lane == first + 2, mid, tail)
            qb_ref[s, part, :] = jnp.where(lane == first + 1, hi, tail)
        nat_ref[part, :] = jnp.where(lane < HD, outs[0], outs[1]).astype(BF16)
    for d in range(parts):

        @pl.when(pl.program_id(1) == d)
        def _():
            o_refs[d][...] = nat_ref[...]


def attend(index, q, k, v, parts, sub=256):
    heads, rows, _ = q.shape
    keys = k.shape[1]
    share = rows // parts
    local = heads * HD
    return call(
        functools.partial(attend_kernel, min(sub, share), parts),
        (heads // 2, parts),
        [
            pl.BlockSpec((2, share, 128), lambda j, i, idx: (j, idx[0] ^ i, 0)),
            pl.BlockSpec((2, keys, 128), lambda j, i, idx: (j, 0, 0)),
            pl.BlockSpec((2, keys, 128), lambda j, i, idx: (j, 0, 0)),
        ],
        [pl.BlockSpec((share, 128), lambda j, i, idx: (0, j))] * parts
        + [
            pl.BlockSpec((share, 128), lambda j, i, idx: (idx[0] ^ i, j)),
            pl.BlockSpec((2, share, 128), lambda j, i, idx: (j, idx[0] ^ i, 0)),
        ],
        [sds((share, local), BF16)] * parts + [sds((rows, local), BF16), sds((heads, rows, 128), BF16)],
        flops=heads * rows * keys * 128 * 4,
        nbytes=heads * (2 * rows + 2 * keys) * 256,
        trans=heads * rows * keys,
        prefetch=1,
    )(index, q, k, v)


def cut_kernel(idx_ref, gu_ref, dw_ref, first_ref, second_ref):
    part = gu_ref.shape[1]
    half = part // 2
    first_ref[:part, :] = gu_ref[0]
    first_ref[part:, :] = gu_ref[1, :half, :]
    second_ref[:half, :] = gu_ref[1, half:, :]
    second_ref[half:, :] = dw_ref[...].T


def cut_weights(dp, gate_up, down, shares):
    _, width, hidden = gate_up.shape
    part = width // shares
    if part % 128:
        down = lax.dynamic_slice_in_dim(down, dp[0] * part, part, 1)
        spec = whole(down.shape)
    else:
        spec = pl.BlockSpec((hidden, part), lambda i, idx: (0, idx[0]))
    chunk = (3 * part // 2, hidden)
    return call(
        cut_kernel,
        (1,),
        [pl.BlockSpec((2, part, hidden), lambda i, idx: (0, idx[0], 0)), spec],
        [whole(chunk)] * 2,
        [sds(chunk, BF16)] * 2,
        nbytes=12 * part * hidden,
        prefetch=1,
    )(dp, gate_up, down)


def ffn_kernel(parts, shares, slot, idx_ref, len_ref, weight_ref, gain_ref, x_h, cot_h, ow_h, gu_h, dw_h, *refs):
    own = slot == 0
    att_h = refs[:parts]
    pieces_h = refs[parts : parts + 2 * shares]
    refs = refs[parts + 2 * shares :]
    count = 5 if own else 4
    outs, scratch = refs[:count], refs[count:]
    x_v, cot_v, att_v, ow_v, gu_v, dw_v, pb_v, left_v, act_v, ffn_v, gn2_v, low_v, sem_in, sem_out = scratch
    rows, width = x_v.shape
    local = att_v.shape[2]
    hidden_units = gu_v.shape[2]
    part = pb_v.shape[1] // 3
    row0 = pl.multiple_of((idx_ref[0] ^ slot) * rows, rows)
    mine = pl.ds(row0, rows)

    def fetch(src, dst, i):
        copy = pltpu.make_async_copy(src, dst, sem_in.at[i])
        copy.start()
        return copy

    pending = []

    def store(src, dst, i):
        copy = pltpu.make_async_copy(src, dst, sem_out.at[i])
        copy.start()
        pending.append(copy)

    get_x = fetch(x_h.at[mine], x_v, 0)
    get_ow = fetch(ow_h, ow_v, 1)
    get_att = [fetch(att_h[d], att_v.at[d], 2 + d) for d in range(parts)]
    get_cot = fetch(cot_h.at[mine], cot_v, 2 + parts)
    get_gu = fetch(gu_h, gu_v, 3 + parts)
    get_dw = fetch(dw_h, dw_v, 4 + parts)
    chunk = pb_v.shape[1] // 2
    get_pb = []
    for c in range(2):
        for x in range(shares):
            rows_at = pl.ds(c * chunk, chunk)
            get_pb.append(fetch(pieces_h[c * shares + x], pb_v.at[idx_ref[3] ^ x, rows_at], 5 + parts + len(get_pb)))

    get_x.wait()
    get_ow.wait()
    resid = x_v[...].astype(F32)
    for d in range(parts):
        get_att[d].wait()
        resid = resid + dot(att_v[d], ow_v[:, d].reshape(local, width))
    if own:
        ffn_v[...] = resid
        store(ffn_v, outs[4], 4)
    normed = (resid * rms(resid) * gain_ref[1:2, :]).astype(BF16)
    left_v[0] = normed
    position = lax.broadcasted_iota(jnp.int32, (rows, 1), 0) + row0
    row_weight = jnp.where(position < len_ref[0], weight_ref[0], 0.0)
    get_cot.wait()
    left_v[1] = (cot_v[...].astype(F32) * row_weight).astype(BF16)
    store(left_v, outs[0], 0)
    for shard in range(2):
        cols = slice(shard * hidden_units, (shard + 1) * hidden_units)
        if shard == 0:
            get_gu.wait()
            get_dw.wait()
            gate_w, up_w, down_w = gu_v[0], gu_v[1], dw_v[...]
        else:
            for copy in get_pb:
                copy.wait()
            gate_w, up_w, down_w = (
                pb_v[:, c * part : (c + 1) * part, :].reshape(width, hidden_units) for c in range(3)
            )
        gate = dot(left_v[0], gate_w)
        upper = dot(left_v[0], up_w)
        grad_hidden = dot(left_v[1], down_w, NT if shard == 0 else NN)
        sigma = jax.nn.sigmoid(gate)
        act = gate * sigma
        hidden = (act * upper).astype(BF16)
        grad_up = (grad_hidden * act).astype(BF16)
        grad_gate = (grad_hidden * upper * (sigma + act * (1.0 - sigma))).astype(BF16)
        act_v[0, :, cols] = grad_gate
        act_v[1, :, cols] = grad_up
        act_v[2, :, cols] = hidden
        grad = dot(grad_gate, gate_w, NT) + dot(grad_up, up_w, NT)
        term = dot(hidden, down_w, NN if shard == 0 else NT)
        if shard == 0:
            gn2_v[...] = grad
            if own:
                pending.pop(0).wait()
            ffn_v[...] = term
        else:
            low_v[0] = (gn2_v[...] + grad).astype(BF16)
            store(low_v.at[0], outs[2], 2)
            low_v[1] = (ffn_v[...] + term).astype(BF16)
            store(low_v.at[1], outs[3], 3)
    store(act_v, outs[1], 1)
    for copy in pending:
        copy.wait()


def feed_forward(slot, index, lengths, picked, atts, tokens, cotangent, out_full, gate_up, down, partner, gains):
    parts = len(atts)
    shares = len(partner) // 2
    rows, local = atts[0].shape
    width = tokens.shape[1]
    hidden = gate_up.shape[2]
    anywhere = pl.BlockSpec(memory_space=pl.ANY)
    out_shape = [
        sds((2, rows, width), BF16), sds((3, rows, 2 * hidden), BF16),
        sds((rows, width), BF16), sds((rows, width), BF16),
    ]
    if slot == 0:
        out_shape.append(sds((rows, width), F32))
    return call(
        functools.partial(ffn_kernel, parts, shares, slot),
        (1,),
        [smem(), smem(), whole(gains.shape)] + [anywhere] * (5 + parts + 2 * shares),
        [anywhere] * len(out_shape),
        out_shape,
        scratch=[
            pltpu.VMEM((rows, width), BF16),
            pltpu.VMEM((rows, width), BF16),
            pltpu.VMEM((parts, rows, local), BF16),
            pltpu.VMEM(out_full.shape, BF16),
            pltpu.VMEM(gate_up.shape, BF16),
            pltpu.VMEM(down.shape, BF16),
            pltpu.VMEM((shares, 2 * partner[0].shape[0], hidden), BF16),
            pltpu.VMEM((2, rows, width), BF16),
            pltpu.VMEM((3, rows, 2 * hidden), BF16),
            pltpu.VMEM((rows, width), F32),
            pltpu.VMEM((rows, width), F32),
            pltpu.VMEM((2, rows, width), BF16),
            pltpu.SemaphoreType.DMA((5 + parts + 2 * shares,)),
            pltpu.SemaphoreType.DMA((5,)),
        ],
        flops=2 * rows * width * (width + 12 * hidden),
        nbytes=rows * width * 30 + 12 * width * hidden,
        trans=rows * hidden * 2,
        prefetch=1,
    )(index, lengths, picked, gains, tokens, cotangent, out_full, gate_up, down, *atts, *partner)


def ffn_grad_kernel(sets, split, extra, idx_ref, *refs):
    left = refs[:sets]
    act = refs[sets : 2 * sets]
    refs = refs[2 * sets :]
    step = pl.program_id(0)

    def write(total, outs):
        part = outs[0].shape[-2]
        for out in outs:
            count = out.shape[0]
            for j in range(count):
                if len(outs) == 1:
                    out[j] = total[j * part : (j + 1) * part, :].astype(BF16)
        if len(outs) == 2:
            for keep in range(2):
                for bit in range(2):

                    @pl.when((idx_ref[3] & 1) == bit)
                    def _():
                        for j in range(outs[0].shape[0]):
                            d = 2 * j + (bit if keep else 1 - bit)
                            outs[keep][j] = total[d * part : (d + 1) * part, :].astype(BF16)

    outs = refs[2:] if extra else refs

    @pl.when(step < 3)
    def _():
        total = dot(left[0][0], act[0][0], TN)
        for e in range(1, sets):
            total = total + dot(left[e][0], act[e][0], TN)
        write(total, outs)

    if extra:

        @pl.when(step >= 3)
        def _():
            write(dot(refs[0][...], refs[1][...], TN), outs)


def ffn_grads(index, lefts, acts, shard, shares, split, grad_low=None, att_own=None):
    sets = len(lefts)
    _, rows, width = lefts[0].shape
    hidden = acts[0].shape[2] // 2
    part = width // shares
    extra = 0 if grad_low is None else att_own.shape[1] // hidden
    steps = 3 + extra
    specs = [pl.BlockSpec((1, rows, width), lambda c, idx: (jnp.minimum(c // 2, 1), 0, 0))] * sets
    specs += [pl.BlockSpec((1, rows, hidden), lambda c, idx: (jnp.minimum(c, 2), 0, shard))] * sets
    args = list(lefts) + list(acts)
    if extra:
        specs += [
            pl.BlockSpec(grad_low.shape, lambda c, idx: (0, 0)),
            pl.BlockSpec((att_own.shape[0], hidden), lambda c, idx: (0, jnp.maximum(c - 3, 0))),
        ]
        args += [grad_low, att_own]
    count = shares // 2 if split else shares
    out_spec = pl.BlockSpec((count, part, hidden), lambda c, idx: (0, c, 0))
    out_shape = sds((count, steps * part, hidden), BF16)
    outs = 2 if split else 1
    return call(
        functools.partial(ffn_grad_kernel, sets, split, extra),
        (steps,),
        specs,
        [out_spec] * outs,
        [out_shape] * outs,
        flops=2 * sets * rows * width * hidden * steps,
        nbytes=sets * rows * (2 * width + 3 * hidden) * 2 + steps * width * hidden * 2,
        prefetch=1,
    )(index, *args)


def resid_kernel(parts, members, idx_ref, len_ref, weight_ref, cot_ref, resid_ref, ow_ref, gain_ref, *refs):
    gn2_refs = refs[:members]
    att_refs = refs[members : members + parts]
    gr_ref, low_ref, cat_ref, sum_ref = refs[members + parts : members + parts + 4]
    g_refs = refs[members + parts + 4 :]
    rows, width = cot_ref.shape
    local = att_refs[0].shape[1]
    step = pl.program_id(0)
    first = (idx_ref[0] * pl.num_programs(0) + step) * rows
    slot = lax.broadcasted_iota(jnp.int32, (rows, 1), 0) + first
    row_weight = jnp.where(slot < len_ref[0], weight_ref[0], 0.0)
    gn2 = gn2_refs[0][...].astype(F32)
    for ref in gn2_refs[1:]:
        gn2 = gn2 + ref[...].astype(F32)
    resid = resid_ref[...]
    factor = rms(resid)
    unit = resid * factor
    grad = cot_ref[...].astype(F32) * row_weight + norm_back(gn2, gain_ref[1:2, :], unit, factor)
    gr_ref[...] = grad
    low = grad.astype(BF16)
    low_ref[...] = low

    @pl.when(step == 0)
    def _():
        sum_ref[...] = jnp.zeros_like(sum_ref)

    sum_ref[...] += jnp.sum((gn2 * unit).reshape(rows // 8, 8, width), axis=0)
    for d in range(parts):
        g_refs[d][...] = dot(low, ow_ref[:, d].reshape(local, width), NT).astype(BF16)
        cat_ref[:, d * local : (d + 1) * local] = att_refs[d][...]


def resid_back(index, lengths, picked, cotangent, resid, gn2s, out_full, gains, atts, block=256):
    share, width = resid.shape
    parts, members = len(atts), len(gn2s)
    local = atts[0].shape[1]
    steps = share // block
    row = lambda n: pl.BlockSpec((block, n), lambda i, idx: (i, 0))
    return call(
        functools.partial(resid_kernel, parts, members),
        (steps,),
        [
            smem(), smem(),
            pl.BlockSpec((block, width), lambda i, idx: (idx[0] * steps + i, 0)),
            row(width), whole(out_full.shape), whole(gains.shape),
        ]
        + [row(width)] * members
        + [row(local)] * parts,
        [row(width), row(width), row(parts * local), whole((8, width))] + [row(local)] * parts,
        [sds((share, width), F32), sds((share, width), BF16), sds((share, parts * local), BF16), sds((8, width), F32)]
        + [sds((share, local), BF16)] * parts,
        flops=2 * share * width * width,
        nbytes=share * width * 20,
        prefetch=1,
    )(index, lengths, picked, cotangent, resid, out_full, gains, *gn2s, *atts)


def attend_back_kernel(parts, idx_ref, q_ref, k_ref, v_ref, att_ref, cos_ref, sin_ref, *refs):
    grad_refs = refs[:parts]
    outs = refs[parts : 2 * parts]
    dk_acc, dv_acc = refs[2 * parts :]
    rows = q_ref.shape[1]
    step = pl.program_id(0)
    me = idx_ref[0]
    lane = lax.broadcasted_iota(jnp.int32, (rows, 128), 1)

    def table(ref, d):
        return ref[pl.ds(pl.multiple_of((me ^ d) * rows, rows), rows), :]

    def back(v, d, scale):
        return ((v * table(cos_ref, d) - swap_halves(v) * table(sin_ref, d)) * scale).astype(BF16)

    @pl.when(step == 0)
    def _():
        dk_acc[...] = jnp.zeros_like(dk_acc)
        dv_acc[...] = jnp.zeros_like(dv_acc)

    grad = grad_refs[0][...]
    for d in range(1, parts):
        grad = jnp.where(step == d, grad_refs[d][...], grad)
    prod = grad.astype(F32) * att_ref[...].astype(F32)
    zero = jnp.zeros((rows, 128), BF16)
    dqs = []
    for s in range(2):
        first = HD * (1 - s)
        own = (lane >= HD * s) & (lane < HD * (s + 1))
        delta = jnp.sum(jnp.where(own, prod, 0.0), axis=1, keepdims=True)
        hi, mid, low = split3(-delta)
        grad_own = jnp.where(own, grad, zero)
        grad_aug = jnp.where(lane == first + 2, low, grad_own)
        grad_aug = jnp.where(lane == first + 1, mid, grad_aug)
        grad_aug = jnp.where(lane == first, hi, grad_aug)
        q = q_ref[s]
        probs = jnp.exp2(dot(k_ref[s], q, NT))
        scores_grad = (probs * dot(v_ref[s], grad_aug, NT)).astype(BF16)
        dv_acc[...] += dot(probs.astype(BF16), grad_own)
        dk_acc[...] += dot(scores_grad, jnp.where(own, q, zero))
        dqs.append(dot(k_ref[s], scores_grad, TN).T)
    dq = jnp.where(lane < HD, dqs[0], dqs[1])
    for d in range(parts):

        @pl.when(step == d)
        def _():
            outs[d][0] = back(dq, d, FACTOR)

    @pl.when(step == parts - 1)
    def _():
        for d in range(parts):
            outs[d][1] = back(table(dk_acc, d), d, LN2)
            outs[d][2] = table(dv_acc, d).astype(BF16)


def attend_back(index, grads, q, k, v, att, cosine, sine, pair):
    parts = len(grads)
    share = grads[0].shape[0]
    rows = q.shape[1]
    keys = pl.BlockSpec((2, rows, 128), lambda i, idx: (pair, 0, 0), pipeline_mode=pl.Buffered(1))
    return call(
        functools.partial(attend_back_kernel, parts),
        (parts,),
        [
            pl.BlockSpec((2, share, 128), lambda i, idx: (pair, idx[0] ^ i, 0)),
            keys,
            keys,
            pl.BlockSpec((share, 128), lambda i, idx: (idx[0] ^ i, pair)),
            whole(cosine.shape),
            whole(sine.shape),
        ]
        + [pl.BlockSpec((share, 128), lambda i, idx: (0, pair))] * parts,
        [whole((3, share, 128))] * parts,
        [sds((3, share, 128), BF16)] * parts,
        scratch=[pltpu.VMEM((rows, 128), F32)] * 2,
        flops=2 * rows * rows * 128 * 10,
        nbytes=rows * 256 * 16,
        trans=2 * rows * rows,
        prefetch=1,
    )(index, q, k, v, att, cosine, sine, *grads)


def project_grad_kernel(parts, pairs, idx_ref, x_ref, w_ref, gain_ref, *refs):
    act_refs = refs[: parts * pairs]
    away_ref, keep_ref, sum_ref, acc = refs[parts * pairs :]
    step = pl.program_id(0)

    @pl.when(step == 0)
    def _():
        acc[...] = jnp.zeros_like(acc)

    x = x_ref[...].astype(F32)
    normed = (x * rms(x) * gain_ref[0:1, :]).astype(BF16)
    for d in range(parts):

        @pl.when(step == d)
        def _():
            acts = [act_refs[j * parts + d][c] for c in range(3) for j in range(pairs)]
            acc[...] += dot(normed, jnp.concatenate(acts, axis=1), TN)

    @pl.when(step == pl.num_programs(0) - 1)
    def _():
        count, part, _ = keep_ref.shape
        local = w_ref.shape[2]
        core = idx_ref[3] & 1
        for j in range(count):
            keep_ref[j] = acc[pl.ds(pl.multiple_of((2 * j + core) * part, part), part), :].astype(BF16)
            away_ref[j] = acc[pl.ds(pl.multiple_of((2 * j + 1 - core) * part, part), part), :].astype(BF16)
        gain_sum = acc[:, :local] * w_ref[0].astype(F32)
        for c in (1, 2):
            gain_sum += acc[:, c * local : (c + 1) * local] * w_ref[c].astype(F32)
        sum_ref[...] = jnp.broadcast_to(jnp.sum(gain_sum, axis=1, keepdims=True), sum_ref.shape)


def project_grads(index, tokens, acts, qkv_weight, gains, shares):
    width = tokens.shape[1]
    local = qkv_weight.shape[2]
    pairs, parts = len(acts), len(acts[0])
    share = acts[0][0].shape[1]
    flat = [a for group in acts for a in group]
    half = (shares // 2, width // shares, 3 * local)
    return call(
        functools.partial(project_grad_kernel, parts, pairs),
        (parts,),
        [
            pl.BlockSpec((share, width), lambda i, idx: (idx[0] ^ i, 0)),
            whole(qkv_weight.shape),
            whole(gains.shape),
        ]
        + [whole(a.shape) for a in flat],
        [whole(half), whole(half), whole((width, 128))],
        [sds(half, BF16), sds(half, BF16), sds((width, 128), F32)],
        scratch=[pltpu.VMEM((width, 3 * local), F32)],
        flops=2 * tokens.shape[0] * width * 3 * local,
        nbytes=tokens.size * 2 + 8 * width * local * 3,
        prefetch=1,
    )(index, tokens, qkv_weight, gains, *flat)


def token_grad_kernel(parts, pairs, idx_ref, x_ref, gr_ref, w_ref, gain_ref, *refs):
    act_refs = refs[: parts * pairs]
    out_ref = refs[-1]
    width = x_ref.shape[1]
    local = 128 * pairs
    grad = jnp.zeros(x_ref.shape, F32)
    for d in range(parts):
        for c in range(3):
            act = jnp.concatenate([act_refs[j * parts + d][c] for j in range(pairs)], axis=1)
            grad = grad + dot(act, w_ref[:, d, c].reshape(width, local), NT)
    x = x_ref[...].astype(F32)
    factor = rms(x)
    out_ref[...] = gr_ref[...] + norm_back(grad, gain_ref[0:1, :], x * factor, factor)


def token_grad(index, tokens, grad_resid, qkv_full, gains, acts, block=256):
    share, width = grad_resid.shape
    pairs, parts = len(acts), len(acts[0])
    flat = [a for group in acts for a in group]
    steps = share // block
    return call(
        functools.partial(token_grad_kernel, parts, pairs),
        (steps,),
        [
            pl.BlockSpec((block, width), lambda i, idx: (idx[0] * steps + i, 0)),
            pl.BlockSpec((block, width), lambda i, idx: (i, 0)),
            whole(qkv_full.shape),
            whole(gains.shape),
        ]
        + [pl.BlockSpec((3, block, 128), lambda i, idx: (0, i, 0))] * len(flat),
        pl.BlockSpec((block, width), lambda i, idx: (i, 0)),
        sds((share, width), F32),
        flops=2 * share * width * width * 3,
        nbytes=share * width * 10 + 6 * width * width,
        prefetch=1,
    )(index, tokens, grad_resid, qkv_full, gains, *flat)


def after(value, *others):
    return lax.optimization_barrier((value, *others))[0]


def body(
    tokens, qkv_weight, out_weight, gate_up_weight, down_weight, norm_gains,
    species_weight, species_ids, lengths, cotangent,
):
    rows, width = tokens.shape
    local = out_weight.shape[0]
    hidden = down_weight.shape[0]
    parts = lax.axis_size("tensor")
    members = parts // 2
    shares = lax.axis_size("dp")
    part = width // shares
    me = lax.axis_index("tensor")
    dp = lax.axis_index("dp")
    index = jnp.stack([me, me // members, me % members, dp]).astype(jnp.int32)
    cosine, sine = (jnp.asarray(t) for t in rotary_tables())
    pairs = local // 128
    valid = lengths[0] >= 0

    def region(f):
        shapes = jax.eval_shape(f)
        zeros = lambda: jax.tree.map(lambda a: jnp.zeros(a.shape, a.dtype), shapes)
        return lax.optimization_barrier(lax.cond(valid, f, zeros))

    def swap(a, d, name="tensor"):
        return lax.ppermute(a, name, [(i, i ^ d) for i in range(lax.axis_size(name))])

    def cut(a, start, size, axis=0):
        return lax.dynamic_slice_in_dim(a, start, size, axis)

    def exchange(pieces):
        return [swap(pieces[d], d) for d in range(1, parts)]

    def add(a, b):
        return (a.astype(F32) + b.astype(F32)).astype(BF16)

    bits = shares.bit_length() - 1

    def lanes_of(total):
        half = total.shape[1] // 2
        lead = list(range(bits - 1, 0, -1))
        shape = (2,) * (bits - 1) + (half, total.shape[2])
        return [
            (total[:, h * half : (h + 1) * half].reshape(shape), lead, order)
            for h, order in enumerate((lead, lead[::-1]))
        ]

    def halve(lanes, step):
        out = []
        for a, lead, order in lanes:
            bit = order[step]
            at = lead.index(bit)
            mine = (dp >> bit) & 1
            pick = lambda b: lax.dynamic_index_in_dim(a, b, at, keepdims=False)
            out.append((pick(mine), pick(1 - mine), [b for b in lead if b != bit], order, bit))
        return out

    def send(halves):
        return [swap(away, 1 << bit, "dp") for _, away, _, _, bit in halves]

    def merge(halves, got):
        return [(add(keep, g), lead, order) for (keep, _, lead, order, _), g in zip(halves, got)]

    def joined(lanes):
        return jnp.concatenate([a for a, _, _ in lanes], axis=0)

    matches = species_ids[:, None] == jnp.arange(species_weight.shape[0])[None, :]
    picked = jnp.sum(jnp.where(matches, species_weight[None, :], F32(0.0)), axis=1)

    chunks = cut_weights(index[3:], gate_up_weight, down_weight, shares)
    ow_cut = cut(out_weight, dp * (local // shares), local // shares)
    qkv_cut = cut(qkv_weight, dp * part, part, 1)

    def fan_out(a):
        return [swap(a, x, "dp") for x in range(2, shares, 2)]

    def cores(pieces):
        return [swap(a, 1, "dp") for a in pieces]

    def first():
        projected = project(lengths, tokens, qkv_weight, norm_gains, cosine, sine)
        ow = exchange([after(ow_cut, projected[0])] * parts)
        return jnp.stack([ow_cut] + ow), swap(chunks[0], members), projected

    ow, chunk_0, (q, k, v) = region(first)
    out_full = lax.all_gather(ow, "dp", axis=0)

    def second():
        return fan_out(chunk_0), swap(chunks[1], members), attend(index, q, k, v, parts)

    fan_0, chunk_1, (*att, att_nat, q_back) = region(second)
    slots = list(range(members - 1, -1, -1))
    rows_for = lambda e: exchange([att[d ^ e] for d in range(parts)])

    def third():
        fan_1 = fan_out(chunk_1)
        rows = rows_for(slots[0])
        return fan_1, cores([chunk_0] + fan_0), cores([chunk_1] + fan_1), rows

    fan_1, cores_0, cores_1, rows_now = region(third)
    even = [chunk_0, *fan_0, chunk_1, *fan_1]
    partner = [p for pair in zip(even, cores_0 + cores_1) for p in pair]

    lefts, acts, gn2s, terms, gn2_got = {}, {}, {}, {}, {}
    tied = tokens
    for e in slots:

        def feed():
            later = rows_for(e - 1) if e else []
            got = swap(gn2s[e + 1], e + 1) if e + 1 in gn2s else None
            qkv_all = exchange([qkv_cut] * parts) if e == 0 else None
            return later, got, qkv_all, feed_forward(
                e, index, lengths, picked, [att[e]] + rows_now, tied, cotangent, out_full,
                gate_up_weight, down_weight, partner, norm_gains
            )

        later, got, qkv_all, outs = region(feed)
        if got is not None:
            gn2_got[e + 1] = got
        if e:
            rows_now = later
        lefts[e], acts[e], gn2s[e], terms[e] = outs[:4]
        tied = after(tokens, gn2s[e])
    resid = outs[4]
    qkv_full = lax.all_gather(jnp.stack([qkv_cut] + qkv_all), "dp", axis=0)
    gn2_all = [gn2s[0]] + [gn2_got[e] for e in range(1, members)]
    grad_resid, grad_low, att_own, gain_two, *grads = resid_back(
        index, lengths, picked, cotangent, resid, gn2_all, out_full, norm_gains, [att[0]] + rows_now
    )
    lefts, acts = [lefts[e] for e in slots], [acts[e] for e in slots]

    def grads_partner():
        near = [swap(grads[d], d) for d in range(1, parts - 1)]
        return near, ffn_grads(index, lefts, acts, 1, shares, True)

    near, (away_b, keep_b) = region(grads_partner)

    def grads_own():
        far = swap(grads[parts - 1], parts - 1)
        got_b = swap(away_b, 1, "dp")
        (wg_a,) = ffn_grads(index, lefts, acts, 0, shares, False, grad_low, att_own)
        return far, got_b, wg_a

    far, got_b, wg_a = region(grads_own)
    sum_a = lax.psum_scatter(after(wg_a, qkv_full), "dp", scatter_dimension=0, tiled=True)[0]
    grads_all = [grads[0], *near, far]
    halves = halve(lanes_of(add(keep_b, got_b)), 0)

    def back(j):
        return attend_back(index, grads_all, q_back, k, v, att_nat, cosine, sine, j)

    def back_first():
        others = [swap(terms[e], e) for e in range(1, members)]
        return others, send(halves), back(0)

    others, got, group = region(back_first)
    out = resid + terms[0].astype(F32)
    for term in others:
        out = out + term.astype(F32)
    lanes = merge(halves, got)
    step = 1
    qkv_acts, acts_got = [group], []
    for j in range(1, pairs):
        halves = halve(lanes, step)

        def back_next():
            return exchange(group), send(halves), back(j)

        group_got, got, group = region(back_next)
        acts_got.append([qkv_acts[-1][0]] + group_got)
        qkv_acts.append(group)
        lanes = merge(halves, got)
        step += 1

    b_lanes = lanes
    for s in range(step, bits - 1):
        h = halve(b_lanes, s)
        b_lanes = merge(h, send(h))
    sum_b = joined(b_lanes)

    def finish():
        last = exchange(group)
        got_b = swap(sum_b, members)

        def inner():
            away_q, keep_q, gain_one = project_grads(index, tokens, qkv_acts, qkv_weight, norm_gains, shares)
            qkv_lanes = lanes_of(add(keep_q, swap(away_q, 1, "dp")))
            for s in range(bits - 1):
                h = halve(qkv_lanes, s)
                qkv_lanes = merge(h, send(h))
            gains_grad = jnp.stack([gain_one[:, 0] / norm_gains[0], jnp.sum(gain_two, axis=0)])
            for name, size in (("dp", shares), ("tensor", parts)):
                d = 1
                while d < size:
                    gains_grad = gains_grad + swap(gains_grad, d, name)
                    d *= 2
            return joined(qkv_lanes), gains_grad

        return last, got_b, region(inner)

    last, got_b, (qkv_sum, gains_grad) = region(finish)
    acts_got.append([group[0]] + last)
    op_sum = jnp.concatenate(
        [sum_a[(3 + c) * part : (4 + c) * part] for c in range(parts * local // hidden)], axis=1
    )

    def end():
        op_got = exchange([op_sum[:, d * local : (d + 1) * local] for d in range(parts)])
        return op_got, token_grad(index, tokens, grad_resid, qkv_full, norm_gains, acts_got)

    op_got, grad_tok = region(end)
    ffn_sum = sum_a[: 3 * part].astype(F32) + got_b.astype(F32)
    grad_op = op_sum[:, :local].astype(F32)
    for piece in op_got:
        grad_op = grad_op + piece.astype(F32)
    grad_gu = ffn_sum[: 2 * part].reshape(2, part, hidden)
    grad_down = ffn_sum[2 * part :].T
    qkv_sum = qkv_sum.astype(F32)
    grad_qkv = jnp.stack([qkv_sum[:, c * local : (c + 1) * local] for c in range(3)])
    return (out, grad_tok, grad_qkv, grad_op.T, grad_gu, grad_down, gains_grad)


def solution(mesh):
    in_specs = (
        P("dp", None),
        P(None, None, "tensor"),
        P("tensor", None),
        P(None, None, "tensor"),
        P("tensor", None),
        P(),
        P(),
        P("dp"),
        P("dp"),
        P("dp", None),
    )
    out_specs = (
        P(("dp", "tensor"), None),
        P(("dp", "tensor"), None),
        P(None, "dp", "tensor"),
        P("tensor", "dp"),
        P(None, "dp", "tensor"),
        P("tensor", "dp"),
        P(),
    )
    return jax.shard_map(body, mesh=mesh, in_specs=in_specs, out_specs=out_specs, check_vma=False)
```

time: 550 us -> 424 us (0.77)
  waiting for transfers between devices: 228 us -> 90 us
  local copies, waits for them, and re-layouts: 34.8 us -> 13.5 us
  starting transfers between devices: 56.4 us -> 74.9 us
  other arithmetic: 14.8 us -> 23.9 us
    ppermute x30 -> x58, waiting for transfers between devices: 197 us -> 85.4 us  [swap(): lax.ppermute(a, name, [(i, i ^ d) for i in range(lax.axis_size(name))])]
    reduce_scatter x3 -> x1, waiting for transfers between devices: 30.3 us -> 0.01 us  [body(): lax.psum_scatter(after(wg_a, qkv_full), 'dp', scatter_dimension=0, tiled=...]
    ppermute x30 -> x58, starting transfers between devices: 56.2 us -> 74.6 us  [swap(): lax.ppermute(a, name, [(i, i ^ d) for i in range(lax.axis_size(name))])]
    convert_element_type x1 -> x10, other arithmetic: 0.95 us -> 12 us  [the longest x9 11 us: add(): return (a.astype(F32) + b.astype(F32)).astype(BF16)]
    all_gather x1 -> x0, local copies, waits for them, and re-layouts: 8.79 us -> none  [body(): partner = lax.all_gather(swap(mine, members), 'dp', axis=0)]
    dynamic_slice x9 -> x2, local copies, waits for them, and re-layouts: 8.39 us -> 1.62 us  [cut(): return lax.dynamic_slice_in_dim(a, start, size, axis)]
    pallas_call x3 -> x6, Pallas kernels: 98.1 us -> 105 us  [the longest x2 47.2 us: feed_forward(): call(functools.partial(ffn_kernel, parts, shares, slot), (1,), [smem(), s...]
  transfers between devices with their start and end apart: 36 -> 61, of which waited for: 21 -> 21; matrix products, arithmetic and copies ran while one was open for 6% -> 6% of each run, Pallas kernels for 36% -> 47%
where the time goes in v3:
time: 424 us; the launch traced here: 417 us
  Pallas kernels  197 us (46%)
  waiting for transfers between devices  90 us (21%)
  starting transfers between devices  74.9 us (18%)
  other arithmetic  23.9 us (6%)
  between operations  15.9 us (4%)
  local copies, waits for them, and re-layouts  13.5 us (3%)
    ppermute x58, waiting for transfers between devices, swap(): lax.ppermute(a, name, [(i, i ^ d) for i in range(lax.axis_size(name))])  85.4 us
    ppermute x58, starting transfers between devices, swap(): lax.ppermute(a, name, [(i, i ^ d) for i in range(lax.axis_size(name))])  74.6 us
    pallas_call x2, Pallas kernels, attend_back(): call(functools.partial(attend_back_kernel, parts), (parts,), [pl.BlockSpe...  54.2 us
    pallas_call x2, Pallas kernels, feed_forward(): call(functools.partial(ffn_kernel, parts, shares, slot), (1,), [smem(), s...  47.2 us
    pallas_call x1, Pallas kernels, attend(): call(functools.partial(attend_kernel, min(sub, share), parts), (heads //...  28.9 us
    pallas_call x2, Pallas kernels, ffn_grads(): call(functools.partial(ffn_grad_kernel, sets, split, extra), (steps,), sp...  26.6 us
    pallas_call x1, Pallas kernels, project_grads(): call(functools.partial(project_grad_kernel, parts, pairs), (parts,), [pl....  11.4 us
    convert_element_type x9, other arithmetic, add(): return (a.astype(F32) + b.astype(F32)).astype(BF16)  11 us
  transfers between devices with their start and end apart: 61, of which 21 were waited for; matrix products, arithmetic and copies ran while one was open for 6% of the time, Pallas kernels for 47%

profile of v3, /device:TPU:0, one launch (start us, length us, event | category | flops | bytes accessed | tf_op | source)
XLA Modules:
  0.0 416.6 jit_solution(6493652268057684722)
XLA Ops:
  10.3 27.2 %conditional.12 = (bf16[4,32,1024]{2,1,0:T(8,128)(2,1)S(1)}, bf16[192,1024]{1,0:T(8,128)(2,1)}, bf16[4,2048,128]{2,1,0:T(8,128)(2,1)S(1)}, bf16[4,2048,128]{2,1,0:T(8,128)(2,1)}, bf16[4,2048,128]{2,1,0:T(8,128)(2,1)}) conditional(s32[]{:T(128)} %convert_element_type.160, () %tuple.110, (bf16[32,1024]{1,0:T(8,128)(2,1)S(1)}, s32[1]{0:T(128)}, ...), branch_computations={%region_0.1_spmd, %region_1.2_spmd} | conditional | flops 3221618688 | bytes 13369544 | solution.py:704
  10.3 4.0 collective-permute-start.40
  14.3 9.6 %branch_1_fun.10 = (bf16[4,2048,128]{2,1,0:T(8,128)(2,1)S(1)}, bf16[4,2048,128]{2,1,0:T(8,128)(2,1)}, bf16[4,2048,128]{2,1,0:T(8,128)(2,1)}) custom-call(s32[1]{0:T(128)} %get-tuple-element.349.len_ref, bf16[2048,1024]{1,0:T(8,128)(2,1)} %get-tuple-element.350.x_ref, bf16[3,1024,256]{2,1,0:T(8,128)(2,1)} %get-tuple-element.351.w_ref, ...), custom_call_target="tpu_custom_call" | custom-call | flops 3221225472 | bytes 10485760 | tf_op jit(solution)/shard_map/cond/branch_1_fun/pallas_call | solution.py:134
  28.3 2.4 collective-permute-done.39
  30.8 6.7 %collective-permute-done.38 = bf16[32,1024]{1,0:T(8,128)(2,1)S(1)} collective-permute-done((bf16[32,1024]{1,0:T(8,128)(2,1)S(1)}, bf16[32,1024]{1,0:T(8,128)(2,1)S(1)}, u32[]{:S(2)}, u32[]{:S(2)}) %collective-permute-start.38) | collective-permute-done | bytes 65568 | tf_op jit(solution)/shard_map/cond/branch_1_fun/ppermute | solution.py:707
  38.4 33.8 %conditional.13 = (bf16[192,1024]{1,0:T(8,128)(2,1)}, bf16[192,1024]{1,0:T(8,128)(2,1)}, bf16[192,1024]{1,0:T(8,128)(2,1)}, bf16[192,1024]{1,0:T(8,128)(2,1)}, b...) conditional(s32[]{:T(128)} %convert_element_type.160, ...), branch_computations={%region_2.3_spmd, %region_3.4_spmd} | conditional | flops 8589934592 | bytes 14680304 | solution.py:704
  43.2 28.9 %branch_1_fun.11 = (bf16[512,256]{1,0:T(8,128)(2,1)S(1)}, bf16[512,256]{1,0:T(8,128)(2,1)S(1)}, bf16[512,256]{1,0:T(8,128)(2,1)S(1)}, bf16[512,256]{1,0:T(8,128)...) custom-call(s32[4]{0:T(128)S(1)} %get-tuple-element.362.idx_ref, ...), custom_call_target="tpu_custom_call" | custom-call | flops 8589934592 | bytes 8388608 | tf_op jit(solution)/shard_map/cond/branch_1_fun/pallas_call | solution.py:186
  72.9 30.6 %conditional.14 = (bf16[192,1024]{1,0:T(8,128)(2,1)}, bf16[192,1024]{1,0:T(8,128)(2,1)}, bf16[192,1024]{1,0:T(8,128)(2,1)}, bf16[192,1024]{1,0:T(8,128)(2,1)}, b...) conditional(s32[]{:T(128)} %convert_element_type.160, ...), branch_computations={%region_5.6_spmd, %region_6.7_spmd} | conditional | bytes 20447904 | solution.py:704
  74.4 2.8 collective-permute-start.15
  77.2 2.4 collective-permute-start.17
  81.1 4.7 %collective-permute-done.15 = bf16[512,256]{1,0:T(8,128)(2,1)} collective-permute-done((bf16[512,256]{1,0:T(8,128)(2,1)S(1)}, bf16[512,256]{1,0:T(8,128)(2,1)}, u32[]{:S(2)}, u32[]{:S(2)}) %collective-permute-start.15) | collective-permute-done | bytes 262176 | tf_op jit(solution)/shard_map/cond/branch_1_fun/ppermute | solution.py:707
  87.3 10.2 %collective-permute-done.16 = bf16[512,256]{1,0:T(8,128)(2,1)} collective-permute-done((bf16[512,256]{1,0:T(8,128)(2,1)S(1)}, bf16[512,256]{1,0:T(8,128)(2,1)}, u32[]{:S(2)}, u32[]{:S(2)}) %collective-permute-start.16) | collective-permute-done | bytes 262176 | tf_op jit(solution)/shard_map/cond/branch_1_fun/ppermute | solution.py:707
  106.7 30.2 %conditional.15 = (bf16[512,256]{1,0:T(8,128)(2,1)}, bf16[512,256]{1,0:T(8,128)(2,1)}, bf16[512,256]{1,0:T(8,128)(2,1)}, bf16[2,512,1024]{2,1,0:T(8,128)(2,1)}, ...) conditional(s32[]{:T(128)} %convert_element_type.160, () %tuple.108, ...), branch_computations={%region_7.8_spmd, %region_8.9_spmd} | conditional | flops 13958643712 | bytes 31457456 | solution.py:704
  106.9 4.2 collective-permute-start.18
  111.1 2.4 collective-permute-start.20
  113.5 23.3 %branch_1_fun.12 = (bf16[2,512,1024]{2,1,0:T(8,128)(2,1)}, bf16[3,512,2048]{2,1,0:T(8,128)(2,1)}, bf16[512,1024]{1,0:T(8,128)(2,1)}, bf16[512,1024]{1,0:T(8,128)(2,1)}) custom-call(s32[4]{0:T(128)S(1)} %get-tuple-element.383.idx_ref, s32[1]{0:T(128)} %get-tuple-element.384.len_ref, f32[1]{0:T(128)} %get-tuple-element.385.weight_ref, ...), custom_call_target="tpu_custom_call" | custom-call | flops 13958643712 | bytes 28311552 | tf_op jit(solution)/shard_map/cond/branch_1_fun/pallas_call | solution.py:345
  136.9 38.1 %conditional.16 = (bf16[512,1024]{1,0:T(8,128)(2,1)}, bf16[3,128,256]{2,1,0:T(8,128)(2,1)}, bf16[3,128,256]{2,1,0:T(8,128)(2,1)}, bf16[3,128,256]{2,1,0:T(8,128)...) conditional(s32[]{:T(128)} %convert_element_type.160, ...), branch_computations={%region_9.10_spmd, %region_10.11_spmd} | conditional | flops 13958643712 | bytes 43254020 | solution.py:704
  139.3 2.4 collective-permute-start.24
  141.9 23.9 %branch_1_fun.13 = (bf16[2,512,1024]{2,1,0:T(8,128)(2,1)}, bf16[3,512,2048]{2,1,0:T(8,128)(2,1)}, bf16[512,1024]{1,0:T(8,128)(2,1)}, bf16[512,1024]{1,0:T(8,128)(2,1)}, f32[512,1024]{1,0:T(8,128)S(1)}) custom-call(s32[4]{0:T(128)S(1)} %get-tuple-element.417.idx_ref, s32[1]{0:T(128)} %get-tuple-element.418.len_ref, f32[1]{0:T(128)} %get-tuple-element.419.weight_ref, ...), custom_call_target="tpu_custom_call" | custom-call | flops 13958643712 | bytes 28311552 | tf_op jit(solution)/shard_map/cond/branch_1_fun/pallas_call | solution.py:345
  165.8 9.2 %collective-permute-done.21 = bf16[512,1024]{1,0:T(8,128)(2,1)} collective-permute-done((bf16[512,1024]{1,0:T(8,128)(2,1)}, bf16[512,1024]{1,0:T(8,128)(2,1)}, u32[]{:S(2)}, u32[]{:S(2)}) %collective-permute-start.21) | collective-permute-done | bytes 1048608 | tf_op jit(solution)/shard_map/cond/branch_1_fun/ppermute | solution.py:707
  177.3 7.7 %shard_map.172 = (f32[512,1024]{1,0:T(8,128)}, bf16[512,1024]{1,0:T(8,128)(2,1)}, bf16[512,1024]{1,0:T(8,128)(2,1)}, f32[8,1024]{1,0:T(8,128)S(1)}, bf16[512,256...) custom-call(s32[4]{0:T(128)S(1)} %pad_add_fusion.idx_ref, ...), custom_call_target="tpu_custom_call" | custom-call | flops 1073741824 | bytes 10485760 | tf_op jit(solution)/shard_map/pallas_call | solution.py:483
  185.1 14.2 %conditional.17 = (bf16[512,256]{1,0:T(8,128)(2,1)}, bf16[512,256]{1,0:T(8,128)(2,1)}, bf16[4,384,1024]{2,1,0:T(8,128)(2,1)}, bf16[4,384,1024]{2,1,0:T(8,128)(2,1)}) conditional(s32[]{:T(128)} %convert_element_type.160, () %tuple.119, (bf16[512,256]{1,0:T(8,128)(2,1)S(1)}, bf16[512,256]{1,0:T(8,128)(2,1)S(1)}, s32[4]{0:T(128)S(1)}, ...), branch_computations={%region_11.12_spmd, %region_12.13_spmd} | conditional | flops 6442450944 | bytes 18874480 | solution.py:704
  187.1 12.2 %branch_1_fun.14 = (bf16[4,384,1024]{2,1,0:T(8,128)(2,1)}, bf16[4,384,1024]{2,1,0:T(8,128)(2,1)}) custom-call(s32[4]{0:T(128)S(1)} %get-tuple-element.453.idx_ref, bf16[2,512,1024]{2,1,0:T(8,128)(2,1)} %get-tuple-element.454.refs_0_, bf16[2,512,1024]{2,1,0:T(8,128)(2,1)} %get-tuple-element.455.refs_1_, bf16[3,512,2048]{2,1,0:T(8,128)(2,1)} %get-tuple-element.456.refs_2_, ...), custom_call_target="tpu_custom_call" | custom-call | flops 6442450944 | bytes 16777216 | tf_op jit(solution)/shard_map/cond/branch_1_fun/pallas_call | solution.py:433
  199.3 17.0 %conditional.18 = (bf16[512,256]{1,0:T(8,128)(2,1)}, bf16[4,384,1024]{2,1,0:T(8,128)(2,1)}, bf16[8,512,1024]{2,1,0:T(8,128)(2,1)}) conditional(s32[]{:T(128)} %convert_element_type.160, () %tuple.121, (bf16[512,256]{1,0:T(8,128)(2,1)S(1)}, bf16[4,384,1024]{2,1,0:T(8,128)(2,1)}, s32[4]{0:T(128)S(1)}, bf16[2,512,1024]{2,1,0:T(8,128)(2,1)}, ...), branch_computations={%region_13.14_spmd, %region_14.15_spmd} | conditional | flops 8589934592 | bytes 32505960 | solution.py:704
  199.4 2.5 collective-permute-start.27
  201.9 14.4 %branch_1_fun.15 = bf16[8,512,1024]{2,1,0:T(8,128)(2,1)} custom-call(s32[4]{0:T(128)S(1)} %get-tuple-element.462.idx_ref, bf16[2,512,1024]{2,1,0:T(8,128)(2,1)} %get-tuple-element.463.refs_0_, bf16[2,512,1024]{2,1,0:T(8,128)(2,1)} %get-tuple-element.464.refs_1_, bf16[3,512,2048]{2,1,0:T(8,128)(2,1)} %get-tuple-element.465.refs_2_, ...), custom_call_target="tpu_custom_call" | custom-call | flops 8589934592 | bytes 18874368 | tf_op jit(solution)/shard_map/cond/branch_1_fun/pallas_call | solution.py:433
  216.4 4.5 %all-gather.7.cloned.1.call-done = bf16[32,3,128,256]{3,2,1,0:T(8,128)(2,1)} async-done(((bf16[4,3,128,256]{3,2,1,0:T(8,128)(2,1)}), bf16[32,3,128,256]{3,2,1,0:T(8,128)(2,1)}) %all-gather.7.cloned.1.call-update) | async-done | bytes 6291472 | tf_op jit(solution)/shard_map/all_gather | solution.py:806
  220.9 4.4 %add_convert_fusion.1 = bf16[4,384,1024]{2,1,0:T(8,128)(2,1)S(1)} fusion(bf16[4,384,1024]{2,1,0:T(8,128)(2,1)} %get-tuple-element.703, bf16[4,384,1024]{2,1,0:T(8,128)(2,1)} %get-tuple-element.698), kind=kLoop, calls=%fused_computation.19 | loop fusion | flops 6291456 | bytes 9437184 | tf_op jit(solution)/shard_map/convert_element_type | solution.py:716
  227.6 31.3 %conditional.19 = (bf16[512,1024]{1,0:T(8,128)(2,1)}, bf16[2,192,1024]{2,1,0:T(8,128)(2,1)}, bf16[2,192,1024]{2,1,0:T(8,128)(2,1)}, bf16[3,512,128]{2,1,0:T(8,12...) conditional(s32[]{:T(128)} %convert_element_type.160, ...), branch_computations={%region_15.16_spmd, %region_16.17_spmd} | conditional | flops 10737418240 | bytes 18874544 | solution.py:704
  231.3 27.5 %branch_1_fun.16 = (bf16[3,512,128]{2,1,0:T(8,128)(2,1)}, bf16[3,512,128]{2,1,0:T(8,128)(2,1)S(1)}, bf16[3,512,128]{2,1,0:T(8,128)(2,1)S(1)}, bf16[3,512,128]{2,1,0:T(8,128)(2,1)}) custom-call(s32[4]{0:T(128)S(1)} %get-tuple-element.472.idx_ref, bf16[4,2048,128]{2,1,0:T(8,128)(2,1)} %get-tuple-element.473.q_ref, ...), custom_call_target="tpu_custom_call" | custom-call | flops 10737418240 | bytes 8388608 | tf_op jit(solution)/shard_map/cond/branch_1_fun/pallas_call | solution.py:562
  258.9 2.8 fusion.5
  263.3 33.3 %conditional.20 = (bf16[3,512,128]{2,1,0:T(8,128)(2,1)}, bf16[3,512,128]{2,1,0:T(8,128)(2,1)}, bf16[3,512,128]{2,1,0:T(8,128)(2,1)}, bf16[192,1024]{1,0:T(8,128)...) conditional(s32[]{:T(128)} %convert_element_type.160, ...), branch_computations={%region_18.19_spmd, %region_19.20_spmd} | conditional | flops 10737418240 | bytes 16253200 | solution.py:704
  264.2 2.4 collective-permute-start.33
  269.9 26.7 %branch_1_fun.17 = (bf16[3,512,128]{2,1,0:T(8,128)(2,1)}, bf16[3,512,128]{2,1,0:T(8,128)(2,1)}, bf16[3,512,128]{2,1,0:T(8,128)(2,1)}, bf16[3,512,128]{2,1,0:T(8,128)(2,1)}) custom-call(s32[4]{0:T(128)S(1)} %get-tuple-element.492.idx_ref, bf16[4,2048,128]{2,1,0:T(8,128)(2,1)} %get-tuple-element.493.q_ref, bf16[4,2048,128]{2,1,0:T(8,128)(2,1)} %get-tuple-element.494.k_ref, ...), custom_call_target="tpu_custom_call" | custom-call | flops 10737418240 | bytes 8388608 | tf_op jit(solution)/shard_map/cond/branch_1_fun/pallas_call | solution.py:562
  300.0 80.7 %conditional.21 = (bf16[3,512,128]{2,1,0:T(8,128)(2,1)}, bf16[3,512,128]{2,1,0:T(8,128)(2,1)}, bf16[3,512,128]{2,1,0:T(8,128)(2,1)}, bf16[384,1024]{1,0:T(8,128)...) conditional(s32[]{:T(128)} %convert_element_type.160, () %tuple.128, (bf16[3,512,128]{2,1,0:T(8,128)(2,1)}, ...), branch_computations={%region_20.21_spmd, %region_21.25_spmd} | conditional | flops 3224397824 | bytes 31499216 | solution.py:704
  300.0 6.3 %collective-permute-start.57 = (bf16[384,1024]{1,0:T(8,128)(2,1)}, bf16[384,1024]{1,0:T(8,128)(2,1)}, u32[]{:S(2)}, u32[]{:S(2)}) collective-permute-start(bf16[384,1024]{1,0:T(8,128)(2,1)} %get-tuple-element.527), channel_id=1, source_target_pairs={{0,2},{1,3},{2,0},{3,1},{4,6},{5,7},{6,4},{7,5},{8,10},{9,11},{10,... | collective-permute-start | bytes 2359304 | tf_op jit(solution)/shard_map/cond/branch_1_fun/ppermute | solution.py:707
  307.4 63.0 %conditional = (bf16[128,768]{1,0:T(8,128)(2,1)}, f32[2,1024]{1,0:T(2,128)}) conditional(s32[]{:T(128)} %convert_element_type.129, () %tuple.76, (s32[4]{0:T(128)S(1)}, bf16[2048,1024]{1,0:T(8,128)(2,1)}, bf16[3,1024,256]{2,1,0:T(8,128)(2,1)}, f32[2,1024]{1,0:T(2,128)S(1)}, bf16[3,512,128]{2,1,0:T(8,128)(2,1)}, ...), branch_computations={%region_22.22_spmd, %region_23.24_spmd} | conditional | flops 3224397824 | bytes 23634572 | solution.py:704
  307.4 11.4 %branch_1_fun.18 = (bf16[4,128,768]{2,1,0:T(8,128)(2,1)}, bf16[4,128,768]{2,1,0:T(8,128)(2,1)}, f32[1024,128]{1,0:T(8,128)}) custom-call(s32[4]{0:T(128)S(1)} %get-tuple-element.507.idx_ref, bf16[2048,1024]{1,0:T(8,128)(2,1)} %get-tuple-element.508.x_ref, bf16[3,1024,256]{2,1,0:T(8,128)(2,1)} %get-tuple-element.509.w_ref, ...), custom_call_target="tpu_custom_call" | custom-call | flops 3221225472 | bytes 10485760 | tf_op jit(solution)/shard_map/cond/branch_1_fun/cond/branch_1_fun/pallas_call | solution.py:623
  326.6 2.3 collective-permute-done.51
  329.9 8.9 %collective-permute-done.52 = f32[2,1024]{1,0:T(2,128)S(1)} collective-permute-done((f32[2,1024]{1,0:T(2,128)S(1)}, f32[2,1024]{1,0:T(2,128)S(1)}, u32[]{:S(2)}, u32[]{:S(2)}) %collective-permute-start.52) | collective-permute-done | bytes 8224 | tf_op jit(solution)/shard_map/cond/branch_1_fun/cond/branch_1_fun/ppermute | solution.py:707
  340.2 16.2 %collective-permute-done.53 = f32[2,1024]{1,0:T(2,128)S(1)} collective-permute-done((f32[2,1024]{1,0:T(2,128)S(1)}, f32[2,1024]{1,0:T(2,128)S(1)}, u32[]{:S(2)}, u32[]{:S(2)}) %collective-permute-start.53) | collective-permute-done | bytes 8224 | tf_op jit(solution)/shard_map/cond/branch_1_fun/cond/branch_1_fun/ppermute | solution.py:707
  359.3 5.6 %collective-permute-done.45 = bf16[2,64,768]{2,1,0:T(8,128)(2,1)S(1)} collective-permute-done((bf16[2,64,768]{2,1,0:T(8,128)(2,1)S(1)}, bf16[2,64,768]{2,1,0:T(8,128)(2,1)S(1)}, u32[]{:S(2)}, u32[]{:S(2)}) %collective-permute-start.45) | collective-permute-done | bytes 196640 | tf_op jit(solution)/shard_map/cond/branch_1_fun/cond/branch_1_fun/ppermute | solution.py:707
  366.0 3.7 collective-permute-done.46
  370.4 10.1 %collective-permute-done.56 = bf16[3,512,128]{2,1,0:T(8,128)(2,1)} collective-permute-done((bf16[3,512,128]{2,1,0:T(8,128)(2,1)}, bf16[3,512,128]{2,1,0:T(8,128)(2,1)}, u32[]{:S(2)}, u32[]{:S(2)}) %collective-permute-start.56) | collective-permute-done | bytes 393248 | tf_op jit(solution)/shard_map/cond/branch_1_fun/ppermute | solution.py:707
  382.5 3.3 convert_add_fusion.4
  390.4 16.4 %conditional.22 = (bf16[128,256]{1,0:T(8,128)(2,1)}, bf16[128,256]{1,0:T(8,128)(2,1)}, bf16[128,256]{1,0:T(8,128)(2,1)}, f32[512,1024]{1,0:T(8,128)}) conditional(s32[]{:T(128)} %convert_element_type.160, () %tuple.124, (bf16[128,1024]{1,0:T(8,128)(2,1)S(1)}, s32[4]{0:T(128)S(1)}, bf16[2048,1024]{1,0:T(8,128)(2,1)}, f32[512,1024]{1,0:T(8,128)S(1)}, ...), branch_computations={%region_25.26_spmd, %region_26.27_spmd} | conditional | flops 3221225472 | bytes 12714136 | solution.py:704
  390.4 4.7 %collective-permute-start.41 = (bf16[128,256]{1,0:T(8,128)(2,1)S(1)}, bf16[128,256]{1,0:T(8,128)(2,1)}, u32[]{:S(2)}, u32[]{:S(2)}) collective-permute-start(bf16[128,256]{1,0:T(8,128)(2,1)S(1)} %get-tuple-element.773), channel_id=1, source_target_pairs={{0,1},{1,0},{2,3},{3,2},{4,5},{5,4},{6,7},{7,6},{8,9},{9,8},{10,11... | collective-permute-start | bytes 196616 | tf_op jit(solution)/shard_map/cond/branch_1_fun/ppermute | solution.py:707
  397.8 9.0 %branch_1_fun.19 = f32[512,1024]{1,0:T(8,128)} custom-call(s32[4]{0:T(128)S(1)} %get-tuple-element.543.idx_ref, bf16[2048,1024]{1,0:T(8,128)(2,1)} %get-tuple-element.544.x_ref, f32[512,1024]{1,0:T(8,128)S(1)} %get-tuple-element.545.gr_ref, bf16[8,4,3,128,256]{4,3,2,1,0:T(8,128)(2,1)} %get-tuple-element.546.w_ref, ...), custom_call_target="tpu_custom_call" | custom-call | flops 3221225472 | bytes 11534336 | tf_op jit(solution)/shard_map/cond/branch_1_fun/pallas_call | solution.py:661
  (182 shorter events, 75.3 us)
Async XLA Ops:
  7.2 99.5 %all-gather.5.cloned.1.call-start = ((), (), s32[]{:S(2)}) async-start(), calls=%async_computation.2 | async-start | bytes 2359296 | tf_op jit(solution)/shard_map/all_gather | solution.py:767
  10.3 27.2 %collective-permute-start.40 = (bf16[192,1024]{1,0:T(8,128)(2,1)S(1)}, bf16[192,1024]{1,0:T(8,128)(2,1)}, u32[]{:S(2)}, u32[]{:S(2)}) collective-permute-start(bf16[192,1024]{1,0:T(8,128)(2,1)S(1)} %get-tuple-element.357), channel_id=1, source_target_pairs={{0,2},{1,3},{2,0},{3,1},{4,6},{5,7},{6,4},{7,5},{8,10},{9,11},{10,... | collective-permute-start | bytes 1179656 | tf_op jit(solution)/shard_map/cond/branch_1_fun/ppermute | solution.py:707
  23.9 6.8 %collective-permute-start.39 = (bf16[32,1024]{1,0:T(8,128)(2,1)S(1)}, bf16[32,1024]{1,0:T(8,128)(2,1)S(1)}, u32[]{:S(2)}, u32[]{:S(2)}) collective-permute-start(bf16[32,1024]{1,0:T(8,128)(2,1)S(1)} %get-tuple-element.356), channel_id=1, source_target_pairs={{0,3},{1,2},{2,1},{3,0},{4,7},{5,6},{6,5},{7,4},{8,11},{9,10},{10,... | collective-permute-start | bytes 196616 | tf_op jit(solution)/shard_map/cond/branch_1_fun/ppermute | solution.py:707
  25.3 12.2 %collective-permute-start.38 = (bf16[32,1024]{1,0:T(8,128)(2,1)S(1)}, bf16[32,1024]{1,0:T(8,128)(2,1)S(1)}, u32[]{:S(2)}, u32[]{:S(2)}) collective-permute-start(bf16[32,1024]{1,0:T(8,128)(2,1)S(1)} %get-tuple-element.356), channel_id=1, source_target_pairs={{0,2},{1,3},{2,0},{3,1},{4,6},{5,7},{6,4},{7,5},{8,10},{9,11},{10,... | collective-permute-start | bytes 196616 | tf_op jit(solution)/shard_map/cond/branch_1_fun/ppermute | solution.py:707
  27.0 10.5 %collective-permute-start.37 = (bf16[32,1024]{1,0:T(8,128)(2,1)S(1)}, bf16[32,1024]{1,0:T(8,128)(2,1)S(1)}, u32[]{:S(2)}, u32[]{:S(2)}) collective-permute-start(bf16[32,1024]{1,0:T(8,128)(2,1)S(1)} %get-tuple-element.356), channel_id=1, source_target_pairs={{0,1},{1,0},{2,3},{3,2},{4,5},{5,4},{6,7},{7,6},{8,9},{9,8},{10,11... | collective-permute-start | bytes 196616 | tf_op jit(solution)/shard_map/cond/branch_1_fun/ppermute | solution.py:707
  38.2 182.7 %all-gather.7.cloned.1.call-start = ((), (), s32[]{:S(2)}) async-start(), calls=%async_computation.3 | async-start | bytes 7077888 | tf_op jit(solution)/shard_map/all_gather | solution.py:806
  38.4 33.8 %collective-permute-start = (bf16[192,1024]{1,0:T(8,128)(2,1)}, bf16[192,1024]{1,0:T(8,128)(2,1)}, u32[]{:S(2)}, u32[]{:S(2)}) collective-permute-start(bf16[192,1024]{1,0:T(8,128)(2,1)} %get-tuple-element.360), channel_id=1, source_target_pairs={{0,8},{4,12},{8,0},{12,4},{16,24},{20,28},{24,16},{28,20},{1,9},{5... | collective-permute-start | bytes 1179656 | tf_op jit(solution)/shard_map/cond/branch_1_fun/ppermute | solution.py:707
  40.0 32.2 %collective-permute-start.1 = (bf16[192,1024]{1,0:T(8,128)(2,1)}, bf16[192,1024]{1,0:T(8,128)(2,1)}, u32[]{:S(2)}, u32[]{:S(2)}) collective-permute-start(bf16[192,1024]{1,0:T(8,128)(2,1)} %get-tuple-element.360), channel_id=1, source_target_pairs={{0,16},{4,20},{8,24},{12,28},{16,0},{20,4},{24,8},{28,12},{1,17},{... | collective-permute-start | bytes 1179656 | tf_op jit(solution)/shard_map/cond/branch_1_fun/ppermute | solution.py:707
  41.5 30.7 %collective-permute-start.2 = (bf16[192,1024]{1,0:T(8,128)(2,1)}, bf16[192,1024]{1,0:T(8,128)(2,1)}, u32[]{:S(2)}, u32[]{:S(2)}) collective-permute-start(bf16[192,1024]{1,0:T(8,128)(2,1)} %get-tuple-element.360), channel_id=1, source_target_pairs={{0,24},{4,28},{8,16},{12,20},{16,8},{20,12},{24,0},{28,4},{1,25},{... | collective-permute-start | bytes 1179656 | tf_op jit(solution)/shard_map/cond/branch_1_fun/ppermute | solution.py:707
  41.9 30.3 %collective-permute-start.3 = (bf16[192,1024]{1,0:T(8,128)(2,1)}, bf16[192,1024]{1,0:T(8,128)(2,1)}, u32[]{:S(2)}, u32[]{:S(2)}) collective-permute-start(bf16[192,1024]{1,0:T(8,128)(2,1)} %get-tuple-element.361), channel_id=1, source_target_pairs={{0,2},{1,3},{2,0},{3,1},{4,6},{5,7},{6,4},{7,5},{8,10},{9,11},{10,... | collective-permute-start | bytes 1179656 | tf_op jit(solution)/shard_map/cond/branch_1_fun/ppermute | solution.py:707
  72.9 25.1 %collective-permute-start.4 = (bf16[192,1024]{1,0:T(8,128)(2,1)}, bf16[192,1024]{1,0:T(8,128)(2,1)}, u32[]{:S(2)}, u32[]{:S(2)}) collective-permute-start(bf16[192,1024]{1,0:T(8,128)(2,1)} %get-tuple-element.372), channel_id=1, source_target_pairs={{0,8},{4,12},{8,0},{12,4},{16,24},{20,28},{24,16},{28,20},{1,9},{5... | collective-permute-start | bytes 1179656 | tf_op jit(solution)/shard_map/cond/branch_1_fun/ppermute | solution.py:707
  74.4 11.4 %collective-permute-start.15 = (bf16[512,256]{1,0:T(8,128)(2,1)S(1)}, bf16[512,256]{1,0:T(8,128)(2,1)}, u32[]{:S(2)}, u32[]{:S(2)}) collective-permute-start(bf16[512,256]{1,0:T(8,128)(2,1)S(1)} %get-tuple-element.377), channel_id=1, source_target_pairs={{0,1},{1,0},{2,3},{3,2},{4,5},{5,4},{6,7},{7,6},{8,9},{9,8},{10,11... | collective-permute-start | bytes 786440 | tf_op jit(solution)/shard_map/cond/branch_1_fun/ppermute | solution.py:707
  77.2 20.3 %collective-permute-start.16 = (bf16[512,256]{1,0:T(8,128)(2,1)S(1)}, bf16[512,256]{1,0:T(8,128)(2,1)}, u32[]{:S(2)}, u32[]{:S(2)}) collective-permute-start(bf16[512,256]{1,0:T(8,128)(2,1)S(1)} %get-tuple-element.378), channel_id=1, source_target_pairs={{0,2},{1,3},{2,0},{3,1},{4,6},{5,7},{6,4},{7,5},{8,10},{9,11},{10,... | collective-permute-start | bytes 786440 | tf_op jit(solution)/shard_map/cond/branch_1_fun/ppermute | solution.py:707
  77.2 20.3 %collective-permute-start.17 = (bf16[512,256]{1,0:T(8,128)(2,1)S(1)}, bf16[512,256]{1,0:T(8,128)(2,1)}, u32[]{:S(2)}, u32[]{:S(2)}) collective-permute-start(bf16[512,256]{1,0:T(8,128)(2,1)S(1)} %get-tuple-element.379), channel_id=1, source_target_pairs={{0,3},{1,2},{2,1},{3,0},{4,7},{5,6},{6,5},{7,4},{8,11},{9,10},{10,... | collective-permute-start | bytes 786440 | tf_op jit(solution)/shard_map/cond/branch_1_fun/ppermute | solution.py:707
  79.6 18.5 %collective-permute-start.5 = (bf16[192,1024]{1,0:T(8,128)(2,1)}, bf16[192,1024]{1,0:T(8,128)(2,1)}, u32[]{:S(2)}, u32[]{:S(2)}) collective-permute-start(bf16[192,1024]{1,0:T(8,128)(2,1)} %get-tuple-element.372), channel_id=1, source_target_pairs={{0,16},{4,20},{8,24},{12,28},{16,0},{20,4},{24,8},{28,12},{1,17},{... | collective-permute-start | bytes 1179656 | tf_op jit(solution)/shard_map/cond/branch_1_fun/ppermute | solution.py:707
  85.9 12.7 %collective-permute-start.6 = (bf16[192,1024]{1,0:T(8,128)(2,1)}, bf16[192,1024]{1,0:T(8,128)(2,1)}, u32[]{:S(2)}, u32[]{:S(2)}) collective-permute-start(bf16[192,1024]{1,0:T(8,128)(2,1)} %get-tuple-element.372), channel_id=1, source_target_pairs={{0,24},{4,28},{8,16},{12,20},{16,8},{20,12},{24,0},{28,4},{1,25},{... | collective-permute-start | bytes 1179656 | tf_op jit(solution)/shard_map/cond/branch_1_fun/ppermute | solution.py:707
  106.9 29.9 %collective-permute-start.18 = (bf16[512,256]{1,0:T(8,128)(2,1)S(1)}, bf16[512,256]{1,0:T(8,128)(2,1)}, u32[]{:S(2)}, u32[]{:S(2)}) collective-permute-start(bf16[512,256]{1,0:T(8,128)(2,1)S(1)} %get-tuple-element.380.refs_0_), channel_id=1, source_target_pairs={{0,1},{1,0},{2,3},{3,2},{4,5},{5,4},{6,7},{7,6},{8,9},{9,8},{10,11... | collective-permute-start | bytes 786440 | tf_op jit(solution)/shard_map/cond/branch_1_fun/ppermute | solution.py:707
  111.1 25.8 %collective-permute-start.19 = (bf16[512,256]{1,0:T(8,128)(2,1)S(1)}, bf16[512,256]{1,0:T(8,128)(2,1)}, u32[]{:S(2)}, u32[]{:S(2)}) collective-permute-start(bf16[512,256]{1,0:T(8,128)(2,1)S(1)} %get-tuple-element.381), channel_id=1, source_target_pairs={{0,2},{1,3},{2,0},{3,1},{4,6},{5,7},{6,4},{7,5},{8,10},{9,11},{10,... | collective-permute-start | bytes 786440 | tf_op jit(solution)/shard_map/cond/branch_1_fun/ppermute | solution.py:707
  111.1 25.8 %collective-permute-start.20 = (bf16[512,256]{1,0:T(8,128)(2,1)S(1)}, bf16[512,256]{1,0:T(8,128)(2,1)}, u32[]{:S(2)}, u32[]{:S(2)}) collective-permute-start(bf16[512,256]{1,0:T(8,128)(2,1)S(1)} %get-tuple-element.382), channel_id=1, source_target_pairs={{0,3},{1,2},{2,1},{3,0},{4,7},{5,6},{6,5},{7,4},{8,11},{9,10},{10,... | collective-permute-start | bytes 786440 | tf_op jit(solution)/shard_map/cond/branch_1_fun/ppermute | solution.py:707
  137.3 28.5 %collective-permute-start.22 = (bf16[3,128,256]{2,1,0:T(8,128)(2,1)}, bf16[3,128,256]{2,1,0:T(8,128)(2,1)}, u32[]{:S(2)}, u32[]{:S(2)}) collective-permute-start(bf16[3,128,256]{2,1,0:T(8,128)(2,1)} %get-tuple-element.416), channel_id=1, source_target_pairs={{0,1},{1,0},{2,3},{3,2},{4,5},{5,4},{6,7},{7,6},{8,9},{9,8},{10,11... | collective-permute-start | bytes 589832 | tf_op jit(solution)/shard_map/cond/branch_1_fun/ppermute | solution.py:707
  138.4 27.4 %collective-permute-start.23 = (bf16[3,128,256]{2,1,0:T(8,128)(2,1)}, bf16[3,128,256]{2,1,0:T(8,128)(2,1)}, u32[]{:S(2)}, u32[]{:S(2)}) collective-permute-start(bf16[3,128,256]{2,1,0:T(8,128)(2,1)} %get-tuple-element.416), channel_id=1, source_target_pairs={{0,2},{1,3},{2,0},{3,1},{4,6},{5,7},{6,4},{7,5},{8,10},{9,11},{10,... | collective-permute-start | bytes 589832 | tf_op jit(solution)/shard_map/cond/branch_1_fun/ppermute | solution.py:707
  139.3 26.5 %collective-permute-start.24 = (bf16[3,128,256]{2,1,0:T(8,128)(2,1)}, bf16[3,128,256]{2,1,0:T(8,128)(2,1)}, u32[]{:S(2)}, u32[]{:S(2)}) collective-permute-start(bf16[3,128,256]{2,1,0:T(8,128)(2,1)} %get-tuple-element.416), channel_id=1, source_target_pairs={{0,3},{1,2},{2,1},{3,0},{4,7},{5,6},{6,5},{7,4},{8,11},{9,10},{10,... | collective-permute-start | bytes 589832 | tf_op jit(solution)/shard_map/cond/branch_1_fun/ppermute | solution.py:707
  141.8 33.2 %collective-permute-start.21 = (bf16[512,1024]{1,0:T(8,128)(2,1)}, bf16[512,1024]{1,0:T(8,128)(2,1)}, u32[]{:S(2)}, u32[]{:S(2)}) collective-permute-start(bf16[512,1024]{1,0:T(8,128)(2,1)} %get-tuple-element.415), channel_id=1, source_target_pairs={{0,1},{1,0},{2,3},{3,2},{4,5},{5,4},{6,7},{7,6},{8,9},{9,8},{10,11... | collective-permute-start | bytes 3145736 | tf_op jit(solution)/shard_map/cond/branch_1_fun/ppermute | solution.py:707
  177.1 208.7 %reduce-scatter.2.cloned.1.call-start = ((), (), s32[]{:S(2)}) async-start(), calls=%async_computation.1 | async-start | bytes 9437184 | tf_op jit(solution)/shard_map/reduce_scatter | solution.py:826
  185.1 14.2 %collective-permute-start.25 = (bf16[512,256]{1,0:T(8,128)(2,1)S(1)}, bf16[512,256]{1,0:T(8,128)(2,1)}, u32[]{:S(2)}, u32[]{:S(2)}) collective-permute-start(bf16[512,256]{1,0:T(8,128)(2,1)S(1)} %get-tuple-element.451), channel_id=1, source_target_pairs={{0,1},{1,0},{2,3},{3,2},{4,5},{5,4},{6,7},{7,6},{8,9},{9,8},{10,11... | collective-permute-start | bytes 786440 | tf_op jit(solution)/shard_map/cond/branch_1_fun/ppermute | solution.py:707
  186.0 13.3 %collective-permute-start.26 = (bf16[512,256]{1,0:T(8,128)(2,1)S(1)}, bf16[512,256]{1,0:T(8,128)(2,1)}, u32[]{:S(2)}, u32[]{:S(2)}) collective-permute-start(bf16[512,256]{1,0:T(8,128)(2,1)S(1)} %get-tuple-element.452), channel_id=1, source_target_pairs={{0,2},{1,3},{2,0},{3,1},{4,6},{5,7},{6,4},{7,5},{8,10},{9,11},{10,... | collective-permute-start | bytes 786440 | tf_op jit(solution)/shard_map/cond/branch_1_fun/ppermute | solution.py:707
  199.3 17.0 %collective-permute-start.28 = (bf16[4,384,1024]{2,1,0:T(8,128)(2,1)}, bf16[4,384,1024]{2,1,0:T(8,128)(2,1)}, u32[]{:S(2)}, u32[]{:S(2)}) collective-permute-start(bf16[4,384,1024]{2,1,0:T(8,128)(2,1)} %get-tuple-element.461), channel_id=1, source_target_pairs={{0,4},{4,0},{8,12},{12,8},{16,20},{20,16},{24,28},{28,24},{1,5},{5... | collective-permute-start | bytes 9437192 | tf_op jit(solution)/shard_map/cond/branch_1_fun/ppermute | solution.py:707
  199.4 16.9 %collective-permute-start.27 = (bf16[512,256]{1,0:T(8,128)(2,1)S(1)}, bf16[512,256]{1,0:T(8,128)(2,1)}, u32[]{:S(2)}, u32[]{:S(2)}) collective-permute-start(bf16[512,256]{1,0:T(8,128)(2,1)S(1)} %get-tuple-element.460), channel_id=1, source_target_pairs={{0,3},{1,2},{2,1},{3,0},{4,7},{5,6},{6,5},{7,4},{8,11},{9,10},{10,... | collective-permute-start | bytes 786440 | tf_op jit(solution)/shard_map/cond/branch_1_fun/ppermute | solution.py:707
  227.8 31.1 %collective-permute-start.29 = (bf16[512,1024]{1,0:T(8,128)(2,1)}, bf16[512,1024]{1,0:T(8,128)(2,1)}, u32[]{:S(2)}, u32[]{:S(2)}) collective-permute-start(bf16[512,1024]{1,0:T(8,128)(2,1)} %get-tuple-element.469), channel_id=1, source_target_pairs={{0,1},{1,0},{2,3},{3,2},{4,5},{5,4},{6,7},{7,6},{8,9},{9,8},{10,11... | collective-permute-start | bytes 3145736 | tf_op jit(solution)/shard_map/cond/branch_1_fun/ppermute | solution.py:707
  229.3 29.5 %collective-permute-start.30 = (bf16[2,192,1024]{2,1,0:T(8,128)(2,1)S(1)}, bf16[2,192,1024]{2,1,0:T(8,128)(2,1)}, u32[]{:S(2)}, u32[]{:S(2)}) collective-permute-start(bf16[2,192,1024]{2,1,0:T(8,128)(2,1)S(1)} %get-tuple-element.470), channel_id=1, source_target_pairs={{0,16},{4,20},{8,24},{12,28},{16,0},{20,4},{24,8},{28,12},{1,17},{... | collective-permute-start | bytes 2359304 | tf_op jit(solution)/shard_map/cond/branch_1_fun/ppermute | solution.py:707
  230.6 28.3 %collective-permute-start.31 = (bf16[2,192,1024]{2,1,0:T(8,128)(2,1)}, bf16[2,192,1024]{2,1,0:T(8,128)(2,1)}, u32[]{:S(2)}, u32[]{:S(2)}) collective-permute-start(bf16[2,192,1024]{2,1,0:T(8,128)(2,1)} %get-tuple-element.471), channel_id=1, source_target_pairs={{0,8},{4,12},{8,0},{12,4},{16,24},{20,28},{24,16},{28,20},{1,9},{5... | collective-permute-start | bytes 2359304 | tf_op jit(solution)/shard_map/cond/branch_1_fun/ppermute | solution.py:707
  263.6 33.0 %collective-permute-start.32 = (bf16[3,512,128]{2,1,0:T(8,128)(2,1)S(1)}, bf16[3,512,128]{2,1,0:T(8,128)(2,1)}, u32[]{:S(2)}, u32[]{:S(2)}) collective-permute-start(bf16[3,512,128]{2,1,0:T(8,128)(2,1)S(1)} %get-tuple-element.487), channel_id=1, source_target_pairs={{0,1},{1,0},{2,3},{3,2},{4,5},{5,4},{6,7},{7,6},{8,9},{9,8},{10,11... | collective-permute-start | bytes 1179656 | tf_op jit(solution)/shard_map/cond/branch_1_fun/ppermute | solution.py:707
  264.2 32.4 %collective-permute-start.33 = (bf16[3,512,128]{2,1,0:T(8,128)(2,1)S(1)}, bf16[3,512,128]{2,1,0:T(8,128)(2,1)}, u32[]{:S(2)}, u32[]{:S(2)}) collective-permute-start(bf16[3,512,128]{2,1,0:T(8,128)(2,1)S(1)} %get-tuple-element.488), channel_id=1, source_target_pairs={{0,2},{1,3},{2,0},{3,1},{4,6},{5,7},{6,4},{7,5},{8,10},{9,11},{10,... | collective-permute-start | bytes 1179656 | tf_op jit(solution)/shard_map/cond/branch_1_fun/ppermute | solution.py:707
  266.6 30.0 %collective-permute-start.34 = (bf16[3,512,128]{2,1,0:T(8,128)(2,1)}, bf16[3,512,128]{2,1,0:T(8,128)(2,1)}, u32[]{:S(2)}, u32[]{:S(2)}) collective-permute-start(bf16[3,512,128]{2,1,0:T(8,128)(2,1)} %get-tuple-element.489), channel_id=1, source_target_pairs={{0,3},{1,2},{2,1},{3,0},{4,7},{5,6},{6,5},{7,4},{8,11},{9,10},{10,... | collective-permute-start | bytes 1179656 | tf_op jit(solution)/shard_map/cond/branch_1_fun/ppermute | solution.py:707
  268.0 28.6 %collective-permute-start.35 = (bf16[192,1024]{1,0:T(8,128)(2,1)}, bf16[192,1024]{1,0:T(8,128)(2,1)}, u32[]{:S(2)}, u32[]{:S(2)}) collective-permute-start(bf16[192,1024]{1,0:T(8,128)(2,1)} %get-tuple-element.490), channel_id=1, source_target_pairs={{0,8},{4,12},{8,0},{12,4},{16,24},{20,28},{24,16},{28,20},{1,9},{5... | collective-permute-start | bytes 1179656 | tf_op jit(solution)/shard_map/cond/branch_1_fun/ppermute | solution.py:707
  269.3 27.4 %collective-permute-start.36 = (bf16[192,1024]{1,0:T(8,128)(2,1)}, bf16[192,1024]{1,0:T(8,128)(2,1)}, u32[]{:S(2)}, u32[]{:S(2)}) collective-permute-start(bf16[192,1024]{1,0:T(8,128)(2,1)} %get-tuple-element.491), channel_id=1, source_target_pairs={{0,16},{4,20},{8,24},{12,28},{16,0},{20,4},{24,8},{28,12},{1,17},{... | collective-permute-start | bytes 1179656 | tf_op jit(solution)/shard_map/cond/branch_1_fun/ppermute | solution.py:707
  300.0 80.4 %collective-permute-start.57 = (bf16[384,1024]{1,0:T(8,128)(2,1)}, bf16[384,1024]{1,0:T(8,128)(2,1)}, u32[]{:S(2)}, u32[]{:S(2)}) collective-permute-start(bf16[384,1024]{1,0:T(8,128)(2,1)} %get-tuple-element.527), channel_id=1, source_target_pairs={{0,2},{1,3},{2,0},{3,1},{4,6},{5,7},{6,4},{7,5},{8,10},{9,11},{10,... | collective-permute-start | bytes 2359304 | tf_op jit(solution)/shard_map/cond/branch_1_fun/ppermute | solution.py:707
  306.3 64.0 %collective-permute-start.54 = (bf16[3,512,128]{2,1,0:T(8,128)(2,1)}, bf16[3,512,128]{2,1,0:T(8,128)(2,1)}, u32[]{:S(2)}, u32[]{:S(2)}) collective-permute-start(bf16[3,512,128]{2,1,0:T(8,128)(2,1)} %get-tuple-element.524), channel_id=1, source_target_pairs={{0,1},{1,0},{2,3},{3,2},{4,5},{5,4},{6,7},{7,6},{8,9},{9,8},{10,11... | collective-permute-start | bytes 1179656 | tf_op jit(solution)/shard_map/cond/branch_1_fun/ppermute | solution.py:707
  306.3 64.0 %collective-permute-start.55 = (bf16[3,512,128]{2,1,0:T(8,128)(2,1)}, bf16[3,512,128]{2,1,0:T(8,128)(2,1)}, u32[]{:S(2)}, u32[]{:S(2)}) collective-permute-start(bf16[3,512,128]{2,1,0:T(8,128)(2,1)} %get-tuple-element.525), channel_id=1, source_target_pairs={{0,2},{1,3},{2,0},{3,1},{4,6},{5,7},{6,4},{7,5},{8,10},{9,11},{10,... | collective-permute-start | bytes 1179656 | tf_op jit(solution)/shard_map/cond/branch_1_fun/ppermute | solution.py:707
  324.0 34.5 %collective-permute-start.47 = (bf16[2,64,768]{2,1,0:T(8,128)(2,1)S(1)}, bf16[2,64,768]{2,1,0:T(8,128)(2,1)S(1)}, u32[]{:S(2)}, u32[]{:S(2)}) collective-permute-start(bf16[2,64,768]{2,1,0:T(8,128)(2,1)S(1)} %dynamic-slice_bitcast_fusion), channel_id=1, source_target_pairs={{0,8},{4,12},{8,0},{12,4},{16,24},{20,28},{24,16},{28,20},{1,9},{5... | collective-permute-start | bytes 589832 | tf_op jit(solution)/shard_map/cond/branch_1_fun/cond/branch_1_fun/ppermute | solution.py:707
  328.9 9.9 %collective-permute-start.52 = (f32[2,1024]{1,0:T(2,128)S(1)}, f32[2,1024]{1,0:T(2,128)S(1)}, u32[]{:S(2)}, u32[]{:S(2)}) collective-permute-start(f32[2,1024]{1,0:T(2,128)S(1)} %add.97), channel_id=1, source_target_pairs={{0,1},{1,0},{2,3},{3,2},{4,5},{5,4},{6,7},{7,6},{8,9},{9,8},{10,11... | collective-permute-start | bytes 24584 | tf_op jit(solution)/shard_map/cond/branch_1_fun/cond/branch_1_fun/ppermute | solution.py:707
  338.8 17.6 %collective-permute-start.53 = (f32[2,1024]{1,0:T(2,128)S(1)}, f32[2,1024]{1,0:T(2,128)S(1)}, u32[]{:S(2)}, u32[]{:S(2)}) collective-permute-start(f32[2,1024]{1,0:T(2,128)S(1)} %add.98), channel_id=1, source_target_pairs={{0,2},{1,3},{2,0},{3,1},{4,6},{5,7},{6,4},{7,5},{8,10},{9,11},{10,... | collective-permute-start | bytes 24584 | tf_op jit(solution)/shard_map/cond/branch_1_fun/cond/branch_1_fun/ppermute | solution.py:707
  357.0 7.8 %collective-permute-start.45 = (bf16[2,64,768]{2,1,0:T(8,128)(2,1)S(1)}, bf16[2,64,768]{2,1,0:T(8,128)(2,1)S(1)}, u32[]{:S(2)}, u32[]{:S(2)}) collective-permute-start(bf16[2,64,768]{2,1,0:T(8,128)(2,1)S(1)} %dynamic-slice_bitcast_fusion.1), channel_id=1, source_target_pairs={{0,16},{4,20},{8,24},{12,28},{16,0},{20,4},{24,8},{28,12},{1,17},{... | collective-permute-start | bytes 589832 | tf_op jit(solution)/shard_map/cond/branch_1_fun/cond/branch_1_fun/ppermute | solution.py:707
  358.6 7.4 %collective-permute-start.48 = (bf16[64,768]{1,0:T(8,128)(2,1)S(1)}, bf16[64,768]{1,0:T(8,128)(2,1)S(1)}, u32[]{:S(2)}, u32[]{:S(2)}) collective-permute-start(bf16[64,768]{1,0:T(8,128)(2,1)S(1)} %dynamic-slice_bitcast_fusion.2), channel_id=1, source_target_pairs={{0,16},{4,20},{8,24},{12,28},{16,0},{20,4},{24,8},{28,12},{1,17},{... | collective-permute-start | bytes 294920 | tf_op jit(solution)/shard_map/cond/branch_1_fun/cond/branch_1_fun/ppermute | solution.py:707
  370.3 10.1 %collective-permute-start.56 = (bf16[3,512,128]{2,1,0:T(8,128)(2,1)}, bf16[3,512,128]{2,1,0:T(8,128)(2,1)}, u32[]{:S(2)}, u32[]{:S(2)}) collective-permute-start(bf16[3,512,128]{2,1,0:T(8,128)(2,1)} %get-tuple-element.526), channel_id=1, source_target_pairs={{0,3},{1,2},{2,1},{3,0},{4,7},{5,6},{6,5},{7,4},{8,11},{9,10},{10,... | collective-permute-start | bytes 1179656 | tf_op jit(solution)/shard_map/cond/branch_1_fun/ppermute | solution.py:707
  390.4 16.4 %collective-permute-start.41 = (bf16[128,256]{1,0:T(8,128)(2,1)S(1)}, bf16[128,256]{1,0:T(8,128)(2,1)}, u32[]{:S(2)}, u32[]{:S(2)}) collective-permute-start(bf16[128,256]{1,0:T(8,128)(2,1)S(1)} %get-tuple-element.773), channel_id=1, source_target_pairs={{0,1},{1,0},{2,3},{3,2},{4,5},{5,4},{6,7},{7,6},{8,9},{9,8},{10,11... | collective-permute-start | bytes 196616 | tf_op jit(solution)/shard_map/cond/branch_1_fun/ppermute | solution.py:707
  395.1 11.7 %collective-permute-start.42 = (bf16[128,256]{1,0:T(8,128)(2,1)S(1)}, bf16[128,256]{1,0:T(8,128)(2,1)}, u32[]{:S(2)}, u32[]{:S(2)}) collective-permute-start(bf16[128,256]{1,0:T(8,128)(2,1)S(1)} %get-tuple-element.772), channel_id=1, source_target_pairs={{0,2},{1,3},{2,0},{3,1},{4,6},{5,7},{6,4},{7,5},{8,10},{9,11},{10,... | collective-permute-start | bytes 196616 | tf_op jit(solution)/shard_map/cond/branch_1_fun/ppermute | solution.py:707
  396.4 10.4 %collective-permute-start.43 = (bf16[128,256]{1,0:T(8,128)(2,1)S(1)}, bf16[128,256]{1,0:T(8,128)(2,1)}, u32[]{:S(2)}, u32[]{:S(2)}) collective-permute-start(bf16[128,256]{1,0:T(8,128)(2,1)S(1)} %get-tuple-element.771), channel_id=1, source_target_pairs={{0,3},{1,2},{2,1},{3,0},{4,7},{5,6},{6,5},{7,4},{8,11},{9,10},{10,... | collective-permute-start | bytes 196616 | tf_op jit(solution)/shard_map/cond/branch_1_fun/ppermute | solution.py:707
  (29 other events, 137.2 us)
Sparse Core Ops, SparseCore 0:
  38.4 39.3 all-gather.4
  177.2 43.6 all-gather.6
  224.4 76.5 reduce-scatter.1

commit v4 on v3

--- a/solution.py
+++ b/solution.py
@@ -144,14 +144,13 @@
         ],
         [spec] * 3,
         [sds((heads, rows, 128), BF16)] * 3,
-        flops=2 * rows * width * 3 * local,
-        nbytes=rows * width * 2 + 3 * heads * rows * 256,
     )(lengths, tokens, qkv_weight, gains, cosine, sine)
 
 
-def attend_kernel(sub, parts, idx_ref, q_ref, k_ref, v_ref, *refs):
-    o_refs = refs[:parts]
-    nat_ref, qb_ref = refs[parts:]
+def attend_kernel(sub, parts, done, idx_ref, q_ref, k_ref, v_ref, *refs):
+    prev_refs = refs[:parts] if done else ()
+    o_refs = refs[len(prev_refs) : len(prev_refs) + parts]
+    nat_ref, qb_ref = refs[len(prev_refs) + parts :]
     rows = q_ref.shape[1]
     lane = lax.broadcasted_iota(jnp.int32, (sub, 128), 1)
     for r in range(rows // sub):
@@ -173,44 +172,42 @@
         nat_ref[part, :] = jnp.where(lane < HD, outs[0], outs[1]).astype(BF16)
     for d in range(parts):
 
-        @pl.when(pl.program_id(1) == d)
+        @pl.when(pl.program_id(0) == d)
         def _():
-            o_refs[d][...] = nat_ref[...]
-
-
-def attend(index, q, k, v, parts, sub=256):
-    heads, rows, _ = q.shape
+            if done:
+                o_refs[d][:, :done] = prev_refs[d][...]
+            o_refs[d][:, done:] = nat_ref[...]
+
+
+def attend(index, q, k, v, parts, pair, prev=(), sub=256):
+    _, rows, _ = q.shape
     keys = k.shape[1]
     share = rows // parts
-    local = heads * HD
+    cols = 128 * (pair + 1)
     return call(
-        functools.partial(attend_kernel, min(sub, share), parts),
-        (heads // 2, parts),
+        functools.partial(attend_kernel, min(sub, share), parts, 128 * pair),
+        (parts,),
         [
-            pl.BlockSpec((2, share, 128), lambda j, i, idx: (j, idx[0] ^ i, 0)),
-            pl.BlockSpec((2, keys, 128), lambda j, i, idx: (j, 0, 0)),
-            pl.BlockSpec((2, keys, 128), lambda j, i, idx: (j, 0, 0)),
+            pl.BlockSpec((2, share, 128), lambda i, idx: (pair, idx[0] ^ i, 0)),
+            pl.BlockSpec((2, keys, 128), lambda i, idx: (pair, 0, 0), pipeline_mode=pl.Buffered(1)),
+            pl.BlockSpec((2, keys, 128), lambda i, idx: (pair, 0, 0), pipeline_mode=pl.Buffered(1)),
+        ]
+        + [whole(p.shape) for p in prev],
+        [whole((share, cols))] * parts
+        + [
+            pl.BlockSpec((share, 128), lambda i, idx: (idx[0] ^ i, 0)),
+            pl.BlockSpec((2, share, 128), lambda i, idx: (0, idx[0] ^ i, 0)),
         ],
-        [pl.BlockSpec((share, 128), lambda j, i, idx: (0, j))] * parts
-        + [
-            pl.BlockSpec((share, 128), lambda j, i, idx: (idx[0] ^ i, j)),
-            pl.BlockSpec((2, share, 128), lambda j, i, idx: (j, idx[0] ^ i, 0)),
-        ],
-        [sds((share, local), BF16)] * parts + [sds((rows, local), BF16), sds((heads, rows, 128), BF16)],
-        flops=heads * rows * keys * 128 * 4,
-        nbytes=heads * (2 * rows + 2 * keys) * 256,
-        trans=heads * rows * keys,
+        [sds((share, cols), BF16)] * parts + [sds((rows, 128), BF16), sds((2, rows, 128), BF16)],
         prefetch=1,
-    )(index, q, k, v)
-
-
-def cut_kernel(idx_ref, gu_ref, dw_ref, first_ref, second_ref):
+    )(index, q, k, v, *prev)
+
+
+def cut_kernel(idx_ref, gu_ref, dw_ref, out_ref):
     part = gu_ref.shape[1]
-    half = part // 2
-    first_ref[:part, :] = gu_ref[0]
-    first_ref[part:, :] = gu_ref[1, :half, :]
-    second_ref[:half, :] = gu_ref[1, half:, :]
-    second_ref[half:, :] = dw_ref[...].T
+    out_ref[:part, :] = gu_ref[0]
+    out_ref[part : 2 * part, :] = gu_ref[1]
+    out_ref[2 * part :, :] = dw_ref[...].T
 
 
 def cut_weights(dp, gate_up, down, shares):
@@ -221,23 +218,22 @@
         spec = whole(down.shape)
     else:
         spec = pl.BlockSpec((hidden, part), lambda i, idx: (0, idx[0]))
-    chunk = (3 * part // 2, hidden)
     return call(
         cut_kernel,
         (1,),
         [pl.BlockSpec((2, part, hidden), lambda i, idx: (0, idx[0], 0)), spec],
-        [whole(chunk)] * 2,
-        [sds(chunk, BF16)] * 2,
+        whole((3 * part, hidden)),
+        sds((3 * part, hidden), BF16),
         nbytes=12 * part * hidden,
         prefetch=1,
     )(dp, gate_up, down)
 
 
-def ffn_kernel(parts, shares, slot, idx_ref, len_ref, weight_ref, gain_ref, x_h, cot_h, ow_h, gu_h, dw_h, *refs):
+def ffn_kernel(parts, shares, slot, idx_ref, len_ref, weight_ref, gain_ref, x_h, cot_h, gu_h, dw_h, pb_h, *refs):
     own = slot == 0
     att_h = refs[:parts]
-    pieces_h = refs[parts : parts + 2 * shares]
-    refs = refs[parts + 2 * shares :]
+    pieces_h = refs[parts : parts + shares]
+    refs = refs[parts + shares :]
     count = 5 if own else 4
     outs, scratch = refs[:count], refs[count:]
     x_v, cot_v, att_v, ow_v, gu_v, dw_v, pb_v, left_v, act_v, ffn_v, gn2_v, low_v, sem_in, sem_out = scratch
@@ -261,20 +257,16 @@
         pending.append(copy)
 
     get_x = fetch(x_h.at[mine], x_v, 0)
-    get_ow = fetch(ow_h, ow_v, 1)
+    get_ow = [fetch(pieces_h[x], ow_v.at[idx_ref[1] ^ x], 6 + parts + x) for x in range(shares)]
     get_att = [fetch(att_h[d], att_v.at[d], 2 + d) for d in range(parts)]
     get_cot = fetch(cot_h.at[mine], cot_v, 2 + parts)
     get_gu = fetch(gu_h, gu_v, 3 + parts)
     get_dw = fetch(dw_h, dw_v, 4 + parts)
-    chunk = pb_v.shape[1] // 2
-    get_pb = []
-    for c in range(2):
-        for x in range(shares):
-            rows_at = pl.ds(c * chunk, chunk)
-            get_pb.append(fetch(pieces_h[c * shares + x], pb_v.at[idx_ref[3] ^ x, rows_at], 5 + parts + len(get_pb)))
+    get_pb = fetch(pb_h, pb_v, 1)
 
     get_x.wait()
-    get_ow.wait()
+    for copy in get_ow:
+        copy.wait()
     resid = x_v[...].astype(F32)
     for d in range(parts):
         get_att[d].wait()
@@ -296,8 +288,7 @@
             get_dw.wait()
             gate_w, up_w, down_w = gu_v[0], gu_v[1], dw_v[...]
         else:
-            for copy in get_pb:
-                copy.wait()
+            get_pb.wait()
             gate_w, up_w, down_w = (
                 pb_v[:, c * part : (c + 1) * part, :].reshape(width, hidden_units) for c in range(3)
             )
@@ -331,7 +322,7 @@
 
 def feed_forward(slot, index, lengths, picked, atts, tokens, cotangent, out_full, gate_up, down, partner, gains):
     parts = len(atts)
-    shares = len(partner) // 2
+    shares = len(out_full)
     rows, local = atts[0].shape
     width = tokens.shape[1]
     hidden = gate_up.shape[2]
@@ -345,30 +336,30 @@
     return call(
         functools.partial(ffn_kernel, parts, shares, slot),
         (1,),
-        [smem(), smem(), whole(gains.shape)] + [anywhere] * (5 + parts + 2 * shares),
+        [smem(), smem(), whole(gains.shape)] + [anywhere] * (5 + parts + shares),
         [anywhere] * len(out_shape),
         out_shape,
         scratch=[
             pltpu.VMEM((rows, width), BF16),
             pltpu.VMEM((rows, width), BF16),
             pltpu.VMEM((parts, rows, local), BF16),
-            pltpu.VMEM(out_full.shape, BF16),
+            pltpu.VMEM((shares,) + out_full[0].shape, BF16),
             pltpu.VMEM(gate_up.shape, BF16),
             pltpu.VMEM(down.shape, BF16),
-            pltpu.VMEM((shares, 2 * partner[0].shape[0], hidden), BF16),
+            pltpu.VMEM(partner.shape, BF16),
             pltpu.VMEM((2, rows, width), BF16),
             pltpu.VMEM((3, rows, 2 * hidden), BF16),
             pltpu.VMEM((rows, width), F32),
             pltpu.VMEM((rows, width), F32),
             pltpu.VMEM((2, rows, width), BF16),
-            pltpu.SemaphoreType.DMA((5 + parts + 2 * shares,)),
+            pltpu.SemaphoreType.DMA((6 + parts + shares,)),
             pltpu.SemaphoreType.DMA((5,)),
         ],
         flops=2 * rows * width * (width + 12 * hidden),
         nbytes=rows * width * 30 + 12 * width * hidden,
         trans=rows * hidden * 2,
         prefetch=1,
-    )(index, lengths, picked, gains, tokens, cotangent, out_full, gate_up, down, *atts, *partner)
+    )(index, lengths, picked, gains, tokens, cotangent, gate_up, down, partner, *atts, *out_full)
 
 
 def ffn_grad_kernel(sets, split, extra, idx_ref, *refs):
@@ -388,7 +379,7 @@
             for keep in range(2):
                 for bit in range(2):
 
-                    @pl.when((idx_ref[3] & 1) == bit)
+                    @pl.when((idx_ref[1] & 1) == bit)
                     def _():
                         for j in range(outs[0].shape[0]):
                             d = 2 * j + (bit if keep else 1 - bit)
@@ -442,7 +433,8 @@
     )(index, *args)
 
 
-def resid_kernel(parts, members, idx_ref, len_ref, weight_ref, cot_ref, resid_ref, ow_ref, gain_ref, *refs):
+def resid_kernel(parts, members, shares, idx_ref, len_ref, weight_ref, cot_ref, resid_ref, gain_ref, *refs):
+    pieces, refs, ow_ref = refs[:shares], refs[shares:-1], refs[-1]
     gn2_refs = refs[:members]
     att_refs = refs[members : members + parts]
     gr_ref, low_ref, cat_ref, sum_ref = refs[members + parts : members + parts + 4]
@@ -467,6 +459,8 @@
     @pl.when(step == 0)
     def _():
         sum_ref[...] = jnp.zeros_like(sum_ref)
+        for x in range(shares):
+            ow_ref[idx_ref[1] ^ x] = pieces[x][...]
 
     sum_ref[...] += jnp.sum((gn2 * unit).reshape(rows // 8, 8, width), axis=0)
     for d in range(parts):
@@ -481,22 +475,24 @@
     steps = share // block
     row = lambda n: pl.BlockSpec((block, n), lambda i, idx: (i, 0))
     return call(
-        functools.partial(resid_kernel, parts, members),
+        functools.partial(resid_kernel, parts, members, len(out_full)),
         (steps,),
         [
             smem(), smem(),
             pl.BlockSpec((block, width), lambda i, idx: (idx[0] * steps + i, 0)),
-            row(width), whole(out_full.shape), whole(gains.shape),
+            row(width), whole(gains.shape),
         ]
+        + [whole(p.shape) for p in out_full]
         + [row(width)] * members
         + [row(local)] * parts,
         [row(width), row(width), row(parts * local), whole((8, width))] + [row(local)] * parts,
         [sds((share, width), F32), sds((share, width), BF16), sds((share, parts * local), BF16), sds((8, width), F32)]
         + [sds((share, local), BF16)] * parts,
+        scratch=[pltpu.VMEM((len(out_full),) + out_full[0].shape, BF16)],
         flops=2 * share * width * width,
         nbytes=share * width * 20,
         prefetch=1,
-    )(index, lengths, picked, cotangent, resid, out_full, gains, *gn2s, *atts)
+    )(index, lengths, picked, cotangent, resid, gains, *out_full, *gn2s, *atts)
 
 
 def attend_back_kernel(parts, idx_ref, q_ref, k_ref, v_ref, att_ref, cos_ref, sin_ref, *refs):
@@ -563,10 +559,10 @@
         functools.partial(attend_back_kernel, parts),
         (parts,),
         [
-            pl.BlockSpec((2, share, 128), lambda i, idx: (pair, idx[0] ^ i, 0)),
+            pl.BlockSpec((2, share, 128), lambda i, idx: (0, idx[0] ^ i, 0)),
             keys,
             keys,
-            pl.BlockSpec((share, 128), lambda i, idx: (idx[0] ^ i, pair)),
+            pl.BlockSpec((share, 128), lambda i, idx: (idx[0] ^ i, 0)),
             whole(cosine.shape),
             whole(sine.shape),
         ]
@@ -603,7 +599,7 @@
     def _():
         count, part, _ = keep_ref.shape
         local = w_ref.shape[2]
-        core = idx_ref[3] & 1
+        core = idx_ref[1] & 1
         for j in range(count):
             keep_ref[j] = acc[pl.ds(pl.multiple_of((2 * j + core) * part, part), part), :].astype(BF16)
             away_ref[j] = acc[pl.ds(pl.multiple_of((2 * j + 1 - core) * part, part), part), :].astype(BF16)
@@ -638,9 +634,9 @@
     )(index, tokens, qkv_weight, gains, *flat)
 
 
-def token_grad_kernel(parts, pairs, idx_ref, x_ref, gr_ref, w_ref, gain_ref, *refs):
+def token_grad_kernel(parts, pairs, idx_ref, x_ref, gr_ref, w_ref, gain_ref, own_ref, got_ref, *refs):
     act_refs = refs[: parts * pairs]
-    out_ref = refs[-1]
+    out_ref, gu_ref, down_ref = refs[parts * pairs :]
     width = x_ref.shape[1]
     local = 128 * pairs
     grad = jnp.zeros(x_ref.shape, F32)
@@ -652,12 +648,21 @@
     factor = rms(x)
     out_ref[...] = gr_ref[...] + norm_back(grad, gain_ref[0:1, :], x * factor, factor)
 
-
-def token_grad(index, tokens, grad_resid, qkv_full, gains, acts, block=256):
+    @pl.when(pl.program_id(0) == 0)
+    def _():
+        part = gu_ref.shape[1]
+        total = own_ref[: 3 * part, :].astype(F32) + got_ref[...].astype(F32)
+        gu_ref[0] = total[:part]
+        gu_ref[1] = total[part : 2 * part]
+        down_ref[...] = total[2 * part :].T
+
+
+def token_grad(index, tokens, grad_resid, qkv_full, gains, acts, ffn_own, ffn_got, block=256):
     share, width = grad_resid.shape
     pairs, parts = len(acts), len(acts[0])
     flat = [a for group in acts for a in group]
     steps = share // block
+    part, hidden = ffn_got.shape[0] // 3, ffn_got.shape[1]
     return call(
         functools.partial(token_grad_kernel, parts, pairs),
         (steps,),
@@ -666,14 +671,20 @@
             pl.BlockSpec((block, width), lambda i, idx: (i, 0)),
             whole(qkv_full.shape),
             whole(gains.shape),
+            whole(ffn_own.shape),
+            whole(ffn_got.shape),
         ]
         + [pl.BlockSpec((3, block, 128), lambda i, idx: (0, i, 0))] * len(flat),
-        pl.BlockSpec((block, width), lambda i, idx: (i, 0)),
-        sds((share, width), F32),
+        [
+            pl.BlockSpec((block, width), lambda i, idx: (i, 0)),
+            whole((2, part, hidden)),
+            whole((hidden, part)),
+        ],
+        [sds((share, width), F32), sds((2, part, hidden), F32), sds((hidden, part), F32)],
         flops=2 * share * width * width * 3,
         nbytes=share * width * 10 + 6 * width * width,
         prefetch=1,
-    )(index, tokens, grad_resid, qkv_full, gains, *flat)
+    )(index, tokens, grad_resid, qkv_full, gains, ffn_own, ffn_got, *flat)
 
 
 def after(value, *others):
@@ -689,11 +700,12 @@
     hidden = down_weight.shape[0]
     parts = lax.axis_size("tensor")
     members = parts // 2
+    slots = list(range(members - 1, -1, -1))
     shares = lax.axis_size("dp")
     part = width // shares
     me = lax.axis_index("tensor")
     dp = lax.axis_index("dp")
-    index = jnp.stack([me, me // members, me % members, dp]).astype(jnp.int32)
+    index = jnp.stack([me, dp]).astype(jnp.int32)
     cosine, sine = (jnp.asarray(t) for t in rotary_tables())
     pairs = local // 128
     valid = lengths[0] >= 0
@@ -703,14 +715,20 @@
         zeros = lambda: jax.tree.map(lambda a: jnp.zeros(a.shape, a.dtype), shapes)
         return lax.optimization_barrier(lax.cond(valid, f, zeros))
 
+    def beside(sends, f, apart=False):
+        return region(lambda: ([swap(*x) for x in sends], region(f) if apart else f()))
+
     def swap(a, d, name="tensor"):
         return lax.ppermute(a, name, [(i, i ^ d) for i in range(lax.axis_size(name))])
 
     def cut(a, start, size, axis=0):
         return lax.dynamic_slice_in_dim(a, start, size, axis)
 
+    def outgoing(pieces):
+        return [(pieces[d], d, "tensor") for d in range(1, parts)]
+
     def exchange(pieces):
-        return [swap(pieces[d], d) for d in range(1, parts)]
+        return [swap(*send) for send in outgoing(pieces)]
 
     def add(a, b):
         return (a.astype(F32) + b.astype(F32)).astype(BF16)
@@ -736,8 +754,8 @@
             out.append((pick(mine), pick(1 - mine), [b for b in lead if b != bit], order, bit))
         return out
 
-    def send(halves):
-        return [swap(away, 1 << bit, "dp") for _, away, _, _, bit in halves]
+    def leaving(halves):
+        return [(away, 1 << bit, "dp") for _, away, _, _, bit in halves]
 
     def merge(halves, got):
         return [(add(keep, g), lead, order) for (keep, _, lead, order, _), g in zip(halves, got)]
@@ -748,106 +766,99 @@
     matches = species_ids[:, None] == jnp.arange(species_weight.shape[0])[None, :]
     picked = jnp.sum(jnp.where(matches, species_weight[None, :], F32(0.0)), axis=1)
 
-    chunks = cut_weights(index[3:], gate_up_weight, down_weight, shares)
+    mine = cut_weights(index[1:], gate_up_weight, down_weight, shares)
     ow_cut = cut(out_weight, dp * (local // shares), local // shares)
     qkv_cut = cut(qkv_weight, dp * part, part, 1)
 
-    def fan_out(a):
-        return [swap(a, x, "dp") for x in range(2, shares, 2)]
-
-    def cores(pieces):
-        return [swap(a, 1, "dp") for a in pieces]
-
     def first():
         projected = project(lengths, tokens, qkv_weight, norm_gains, cosine, sine)
-        ow = exchange([after(ow_cut, projected[0])] * parts)
-        return jnp.stack([ow_cut] + ow), swap(chunks[0], members), projected
-
-    ow, chunk_0, (q, k, v) = region(first)
-    out_full = lax.all_gather(ow, "dp", axis=0)
+        return projected, attend(index, *projected, parts, 0)
+
+    (partner_cut,), ((q, k, v), heads) = beside([(mine, members, "tensor")], first)
+    partner = lax.all_gather(partner_cut, "dp", axis=0)
+    heads = [heads]
 
     def second():
-        return fan_out(chunk_0), swap(chunks[1], members), attend(index, q, k, v, parts)
-
-    fan_0, chunk_1, (*att, att_nat, q_back) = region(second)
-    slots = list(range(members - 1, -1, -1))
-    rows_for = lambda e: exchange([att[d ^ e] for d in range(parts)])
+        more = heads[:]
+        for j in range(1, pairs):
+            more.append(attend(index, q, k, v, parts, j, more[-1][:parts]))
+        return more[1:]
+
+    ow, more = beside(outgoing([after(ow_cut, partner_cut)] * parts), second)
+    heads += more
+    att = heads[-1][:parts]
+    att_nat = [h[parts] for h in heads]
+    q_back = [h[parts + 1] for h in heads]
+    rows_for = lambda e: outgoing([att[d ^ e] for d in range(parts)])
+    ow = jnp.stack([ow_cut] + ow)
 
     def third():
-        fan_1 = fan_out(chunk_1)
-        rows = rows_for(slots[0])
-        return fan_1, cores([chunk_0] + fan_0), cores([chunk_1] + fan_1), rows
-
-    fan_1, cores_0, cores_1, rows_now = region(third)
-    even = [chunk_0, *fan_0, chunk_1, *fan_1]
-    partner = [p for pair in zip(even, cores_0 + cores_1) for p in pair]
-
-    lefts, acts, gn2s, terms, gn2_got = {}, {}, {}, {}, {}
+        even = [ow] + [swap(ow, x, "dp") for x in range(2, shares, 2)]
+        return [p for a in even for p in (a, swap(a, 1, "dp"))][1:]
+
+    def third_all():
+        rows = [swap(*x) for x in rows_for(slots[0])]
+        return rows, third()
+
+    rows_now, ow_got = region(third_all)
+    out_full = [ow] + ow_got
+
+    lefts, acts, gn2s, terms, gn2_got, qkv_all = {}, {}, {}, {}, {}, {0: qkv_cut}
     tied = tokens
     for e in slots:
 
         def feed():
-            later = rows_for(e - 1) if e else []
-            got = swap(gn2s[e + 1], e + 1) if e + 1 in gn2s else None
-            qkv_all = exchange([qkv_cut] * parts) if e == 0 else None
-            return later, got, qkv_all, feed_forward(
+            return feed_forward(
                 e, index, lengths, picked, [att[e]] + rows_now, tied, cotangent, out_full,
                 gate_up_weight, down_weight, partner, norm_gains
             )
 
-        later, got, qkv_all, outs = region(feed)
-        if got is not None:
-            gn2_got[e + 1] = got
+        later = rows_for(e - 1) if e else []
+        sums = [(gn2s[e + 1], e + 1, "tensor")] if e + 1 in gn2s else []
+        sent = [d for d in range(1, parts) if (d == 1) == (e == slots[0])] if e in (slots[0], 0) else []
+        got, outs = beside(later + sums + [(qkv_cut, d, "tensor") for d in sent], feed)
+        later, got = got[: len(later)], got[len(later) :]
+        if sums:
+            gn2_got[e + 1] = got.pop(0)
+        qkv_all.update(zip(sent, got))
         if e:
             rows_now = later
         lefts[e], acts[e], gn2s[e], terms[e] = outs[:4]
         tied = after(tokens, gn2s[e])
     resid = outs[4]
-    qkv_full = lax.all_gather(jnp.stack([qkv_cut] + qkv_all), "dp", axis=0)
+    qkv_full = lax.all_gather(jnp.stack([qkv_all[d] for d in range(parts)]), "dp", axis=0)
     gn2_all = [gn2s[0]] + [gn2_got[e] for e in range(1, members)]
     grad_resid, grad_low, att_own, gain_two, *grads = resid_back(
         index, lengths, picked, cotangent, resid, gn2_all, out_full, norm_gains, [att[0]] + rows_now
     )
     lefts, acts = [lefts[e] for e in slots], [acts[e] for e in slots]
 
-    def grads_partner():
-        near = [swap(grads[d], d) for d in range(1, parts - 1)]
-        return near, ffn_grads(index, lefts, acts, 1, shares, True)
-
-    near, (away_b, keep_b) = region(grads_partner)
-
-    def grads_own():
-        far = swap(grads[parts - 1], parts - 1)
-        got_b = swap(away_b, 1, "dp")
-        (wg_a,) = ffn_grads(index, lefts, acts, 0, shares, False, grad_low, att_own)
-        return far, got_b, wg_a
-
-    far, got_b, wg_a = region(grads_own)
+    near, (away_b, keep_b) = beside(
+        [(grads[d], d, "tensor") for d in range(1, parts - 1)],
+        lambda: ffn_grads(index, lefts, acts, 1, shares, True),
+    )
+    (far, got_b), (wg_a,) = beside(
+        [(grads[parts - 1], parts - 1, "tensor"), (away_b, 1, "dp")],
+        lambda: ffn_grads(index, lefts, acts, 0, shares, False, grad_low, att_own),
+    )
     sum_a = lax.psum_scatter(after(wg_a, qkv_full), "dp", scatter_dimension=0, tiled=True)[0]
     grads_all = [grads[0], *near, far]
     halves = halve(lanes_of(add(keep_b, got_b)), 0)
 
     def back(j):
-        return attend_back(index, grads_all, q_back, k, v, att_nat, cosine, sine, j)
-
-    def back_first():
-        others = [swap(terms[e], e) for e in range(1, members)]
-        return others, send(halves), back(0)
-
-    others, got, group = region(back_first)
-    out = resid + terms[0].astype(F32)
-    for term in others:
-        out = out + term.astype(F32)
+        return attend_back(index, grads_all, q_back[j], k, v, att_nat[j], cosine, sine, j)
+
+    terms_out = [(terms[e], e, "tensor") for e in range(1, members)]
+    got, group = beside(terms_out + leaving(halves), lambda: back(0))
+    others, got = got[: len(terms_out)], got[len(terms_out) :]
     lanes = merge(halves, got)
     step = 1
     qkv_acts, acts_got = [group], []
     for j in range(1, pairs):
         halves = halve(lanes, step)
 
-        def back_next():
-            return exchange(group), send(halves), back(j)
-
-        group_got, got, group = region(back_next)
+        got, group = beside(outgoing(group) + leaving(halves), lambda: back(j))
+        group_got, got = got[: parts - 1], got[parts - 1 :]
         acts_got.append([qkv_acts[-1][0]] + group_got)
         qkv_acts.append(group)
         lanes = merge(halves, got)
@@ -856,49 +867,50 @@
     b_lanes = lanes
     for s in range(step, bits - 1):
         h = halve(b_lanes, s)
-        b_lanes = merge(h, send(h))
+        b_lanes = merge(h, [swap(*x) for x in leaving(h)])
     sum_b = joined(b_lanes)
 
     def finish():
-        last = exchange(group)
-        got_b = swap(sum_b, members)
-
-        def inner():
-            away_q, keep_q, gain_one = project_grads(index, tokens, qkv_acts, qkv_weight, norm_gains, shares)
-            qkv_lanes = lanes_of(add(keep_q, swap(away_q, 1, "dp")))
-            for s in range(bits - 1):
-                h = halve(qkv_lanes, s)
-                qkv_lanes = merge(h, send(h))
-            gains_grad = jnp.stack([gain_one[:, 0] / norm_gains[0], jnp.sum(gain_two, axis=0)])
-            for name, size in (("dp", shares), ("tensor", parts)):
-                d = 1
-                while d < size:
-                    gains_grad = gains_grad + swap(gains_grad, d, name)
-                    d *= 2
-            return joined(qkv_lanes), gains_grad
-
-        return last, got_b, region(inner)
-
-    last, got_b, (qkv_sum, gains_grad) = region(finish)
+        away_q, keep_q, gain_one = project_grads(index, tokens, qkv_acts, qkv_weight, norm_gains, shares)
+        total = add(keep_q, swap(away_q, 1, "dp"))
+        one, two = lanes_of(total)
+        for s in range(bits - 1):
+            (h1,), (h2,) = halve([one], s), halve([two], s)
+            g1 = swap(*leaving([h1])[0])
+            g2 = swap(after(leaving([h2])[0][0], g1), 1 << h2[4], "dp")
+            one, two = merge([h1, h2], [g1, g2])
+        qkv_sum = joined([one, two]).astype(F32)
+        grad_qkv = jnp.stack([qkv_sum[:, c * local : (c + 1) * local] for c in range(3)])
+        gains_grad = after(jnp.stack([gain_one[:, 0] / norm_gains[0], jnp.sum(gain_two, axis=0)]), g2)
+        for s in range(bits):
+            gains_grad = gains_grad + swap(gains_grad, 1 << s, "dp")
+        out = resid + terms[0].astype(F32)
+        for term in others:
+            out = out + term.astype(F32)
+        return grad_qkv, gains_grad, out
+
+    got, (grad_qkv, gains_grad, out) = beside(
+        outgoing(group) + [(sum_b, members, "tensor")], finish, apart=True
+    )
+    *last, got_b = got
     acts_got.append([group[0]] + last)
     op_sum = jnp.concatenate(
         [sum_a[(3 + c) * part : (4 + c) * part] for c in range(parts * local // hidden)], axis=1
     )
-
-    def end():
-        op_got = exchange([op_sum[:, d * local : (d + 1) * local] for d in range(parts)])
-        return op_got, token_grad(index, tokens, grad_resid, qkv_full, norm_gains, acts_got)
-
-    op_got, grad_tok = region(end)
-    ffn_sum = sum_a[: 3 * part].astype(F32) + got_b.astype(F32)
-    grad_op = op_sum[:, :local].astype(F32)
-    for piece in op_got:
-        grad_op = grad_op + piece.astype(F32)
-    grad_gu = ffn_sum[: 2 * part].reshape(2, part, hidden)
-    grad_down = ffn_sum[2 * part :].T
-    qkv_sum = qkv_sum.astype(F32)
-    grad_qkv = jnp.stack([qkv_sum[:, c * local : (c + 1) * local] for c in range(3)])
-    return (out, grad_tok, grad_qkv, grad_op.T, grad_gu, grad_down, gains_grad)
+    gains_low = jnp.concatenate([a.reshape(-1, local) for a in split3(gains_grad)])
+    pieces = [jnp.concatenate([op_sum[:, d * local : (d + 1) * local], gains_low]) for d in range(parts)]
+    got, (grad_tok, grad_gu, grad_down) = beside(
+        outgoing(pieces),
+        lambda: token_grad(index, tokens, grad_resid, qkv_full, norm_gains, acts_got, sum_a, got_b),
+    )
+    got = jnp.stack([pieces[0]] + got).astype(F32)
+    grad_op = jnp.sum(got[:, :part], axis=0).T
+    gains_all = got[:, part:].reshape(parts, 3, 2, width)
+    gains_all = gains_all[:, 0] + gains_all[:, 1] + gains_all[:, 2]
+    gains_grad = jnp.zeros_like(gains_all[0])
+    for z in range(parts):
+        gains_grad = gains_grad + lax.dynamic_index_in_dim(gains_all, me ^ z, 0, keepdims=False)
+    return (out, grad_tok, grad_qkv, grad_op, grad_gu, grad_down, gains_grad)
 
 
 def solution(mesh):

time: 424 us -> 408 us (0.962)
  waiting for transfers between devices: 90 us -> 75.9 us
  loops' own time: 1.74 us -> 10.6 us
  local copies, waits for them, and re-layouts: 13.5 us -> 7.25 us
    ppermute x58 -> x48, waiting for transfers between devices: 85.4 us -> 67.8 us  [swap(): lax.ppermute(a, name, [(i, i ^ d) for i in range(lax.axis_size(name))])]
    another operation x12, loops' own time: 1.74 us -> 10.6 us  [region(): return lax.optimization_barrier(lax.cond(valid, f, zeros))]
    ppermute x58 -> x48, starting transfers between devices: 74.6 us -> 70.5 us  [swap(): lax.ppermute(a, name, [(i, i ^ d) for i in range(lax.axis_size(name))])]
    pallas_call x2 -> x3, Pallas kernels: 36.7 us -> 39.4 us  [the longest x2 31.7 us: attend(): call(functools.partial(attend_kernel, min(sub, share), parts, 128 * pair)...]
  transfers between devices with their start and end apart: 61 -> 51, of which waited for: 21 -> 18; matrix products, arithmetic and copies ran while one was open for 6% -> 6% of each run, Pallas kernels for 47% -> 49%
where the time goes in v4:
time: 408 us; the launch traced here: 404 us
  Pallas kernels  201 us (49%)
  waiting for transfers between devices  75.9 us (19%)
  starting transfers between devices  70.8 us (17%)
  other arithmetic  22.8 us (6%)
  between operations  15.6 us (4%)
  loops' own time  10.6 us (3%)
  local copies, waits for them, and re-layouts  7.25 us (2%)
    ppermute x48, starting transfers between devices, swap(): lax.ppermute(a, name, [(i, i ^ d) for i in range(lax.axis_size(name))])  70.5 us
    ppermute x48, waiting for transfers between devices, swap(): lax.ppermute(a, name, [(i, i ^ d) for i in range(lax.axis_size(name))])  67.8 us
    pallas_call x2, Pallas kernels, attend_back(): call(functools.partial(attend_back_kernel, parts), (parts,), [pl.BlockSpe...  54.2 us
    pallas_call x2, Pallas kernels, feed_forward(): call(functools.partial(ffn_kernel, parts, shares, slot), (1,), [smem(), s...  47.3 us
    pallas_call x2, Pallas kernels, attend(): call(functools.partial(attend_kernel, min(sub, share), parts, 128 * pair)...  31.7 us
    pallas_call x2, Pallas kernels, ffn_grads(): call(functools.partial(ffn_grad_kernel, sets, split, extra), (steps,), sp...  26.6 us
    pallas_call x1, Pallas kernels, project_grads(): call(functools.partial(project_grad_kernel, parts, pairs), (parts,), [pl....  11.4 us
    convert_element_type x9, other arithmetic, add(): return (a.astype(F32) + b.astype(F32)).astype(BF16)  10.8 us
  transfers between devices with their start and end apart: 51, of which 18 were waited for; matrix products, arithmetic and copies ran while one was open for 6% of the time, Pallas kernels for 49%

profile of v4, /device:TPU:0, one launch (start us, length us, event | category | flops | bytes accessed | tf_op | source)
XLA Modules:
  0.0 404.0 jit_solution(15519524937288164916)
XLA Ops:
  10.3 38.8 %conditional.12 = (bf16[384,1024]{1,0:T(8,128)(2,1)}, bf16[4,2048,128]{2,1,0:T(8,128)(2,1)}, bf16[4,2048,128]{2,1,0:T(8,128)(2,1)}, bf16[4,2048,128]{2,1,0:T(8,1...) conditional(s32[]{:T(128)} %convert_element_type.157, ...), branch_computations={%region_0.1_spmd, %region_1.2_spmd} | conditional | bytes 9175140 | solution.py:716
  10.3 4.1 %collective-permute-start = (bf16[384,1024]{1,0:T(8,128)(2,1)}, bf16[384,1024]{1,0:T(8,128)(2,1)}, u32[]{:S(2)}, u32[]{:S(2)}) collective-permute-start(bf16[384,1024]{1,0:T(8,128)(2,1)} %get-tuple-element.336), channel_id=1, source_target_pairs={{0,2},{1,3},{2,0},{3,1},{4,6},{5,7},{6,4},{7,5},{8,10},{9,11},{10,... | collective-permute-start | bytes 2359304 | tf_op jit(solution)/shard_map/cond/branch_1_fun/ppermute | solution.py:722
  14.4 9.2 %branch_1_fun.11 = (bf16[4,2048,128]{2,1,0:T(8,128)(2,1)}, bf16[4,2048,128]{2,1,0:T(8,128)(2,1)}, bf16[4,2048,128]{2,1,0:T(8,128)(2,1)}) custom-call(s32[1]{0:T(128)} %get-tuple-element.337.len_ref, bf16[2048,1024]{1,0:T(8,128)(2,1)} %get-tuple-element.338.x_ref, bf16[3,1024,256]{2,1,0:T(8,128)(2,1)S(1)} %get-tuple-element.339.w_ref, ...), custom_call_target="tpu_custom_call" | custom-call | tf_op jit(solution)/shard_map/cond/branch_1_fun/pallas_call | solution.py:134
  23.6 15.8 %branch_1_fun.12 = (bf16[512,128]{1,0:T(8,128)(2,1)S(1)}, bf16[512,128]{1,0:T(8,128)(2,1)S(1)}, bf16[512,128]{1,0:T(8,128)(2,1)S(1)}, bf16[512,128]{1,0:T(8,128)...) custom-call(s32[2]{0:T(128)S(1)} %get-tuple-element.346.idx_ref, ...), custom_call_target="tpu_custom_call" | custom-call | tf_op jit(solution)/shard_map/cond/branch_1_fun/pallas_call | solution.py:187
  39.4 9.8 %collective-permute-done = bf16[384,1024]{1,0:T(8,128)(2,1)} collective-permute-done((bf16[384,1024]{1,0:T(8,128)(2,1)}, bf16[384,1024]{1,0:T(8,128)(2,1)}, u32[]{:S(2)}, u32[]{:S(2)}) %collective-permute-start) | collective-permute-done | bytes 786464 | tf_op jit(solution)/shard_map/cond/branch_1_fun/ppermute | solution.py:722
  49.2 20.4 %conditional.13 = (bf16[32,1024]{1,0:T(8,128)(2,1)}, bf16[32,1024]{1,0:T(8,128)(2,1)}, bf16[32,1024]{1,0:T(8,128)(2,1)}, bf16[512,256]{1,0:T(8,128)(2,1)S(1)}, b...) conditional(s32[]{:T(128)} %convert_element_type.157, ...), branch_computations={%region_2.3_spmd, %region_3.4_spmd} | conditional | bytes 2818138 | solution.py:716
  50.1 3.4 collective-permute-start.2
  53.7 15.9 %branch_1_fun.13 = (bf16[512,256]{1,0:T(8,128)(2,1)S(1)}, bf16[512,256]{1,0:T(8,128)(2,1)S(1)}, bf16[512,256]{1,0:T(8,128)(2,1)S(1)}, bf16[512,256]{1,0:T(8,128)...) custom-call(s32[2]{0:T(128)S(1)} %get-tuple-element.354.idx_ref, ...), custom_call_target="tpu_custom_call" | custom-call | tf_op jit(solution)/shard_map/cond/branch_1_fun/pallas_call | solution.py:187
  71.3 31.9 %conditional.14 = (bf16[512,256]{1,0:T(8,128)(2,1)}, bf16[512,256]{1,0:T(8,128)(2,1)}, bf16[512,256]{1,0:T(8,128)(2,1)}, bf16[4,32,1024]{2,1,0:T(8,128)(2,1)}, b...) conditional(s32[]{:T(128)} %convert_element_type.157, ...), branch_computations={%region_5.6_spmd, %region_6.7_spmd} | conditional | bytes 10486240 | solution.py:716
  71.6 3.8 collective-permute-start.5
  78.9 5.3 %collective-permute-done.4 = bf16[512,256]{1,0:T(8,128)(2,1)} collective-permute-done((bf16[512,256]{1,0:T(8,128)(2,1)S(1)}, bf16[512,256]{1,0:T(8,128)(2,1)}, u32[]{:S(2)}, u32[]{:S(2)}) %collective-permute-start.4) | collective-permute-done | bytes 262176 | tf_op jit(solution)/shard_map/cond/branch_1_fun/ppermute | solution.py:722
  86.6 2.7 collective-permute-start.6
  90.1 2.6 collective-permute-done.10
  92.8 8.4 %collective-permute-done.12 = bf16[4,32,1024]{2,1,0:T(8,128)(2,1)} collective-permute-done((bf16[4,32,1024]{2,1,0:T(8,128)(2,1)S(1)}, bf16[4,32,1024]{2,1,0:T(8,128)(2,1)}, u32[]{:S(2)}, u32[]{:S(2)}) %collective-permute-start.12) | collective-permute-done | bytes 262176 | tf_op jit(solution)/shard_map/cond/branch_1_fun/ppermute | solution.py:722
  103.8 3.5 all-gather.5.cloned.1.call-done
  107.3 28.3 %conditional.15 = (bf16[512,256]{1,0:T(8,128)(2,1)}, bf16[512,256]{1,0:T(8,128)(2,1)}, bf16[512,256]{1,0:T(8,128)(2,1)}, bf16[3,128,256]{2,1,0:T(8,128)(2,1)}, b...) conditional(s32[]{:T(128)} %convert_element_type.157, ...), branch_computations={%region_7.8_spmd, %region_8.9_spmd} | conditional | flops 13958643712 | bytes 32243936 | solution.py:716
  109.0 3.0 collective-permute-start.16
  112.0 23.6 %branch_1_fun.14 = (bf16[2,512,1024]{2,1,0:T(8,128)(2,1)}, bf16[3,512,2048]{2,1,0:T(8,128)(2,1)}, bf16[512,1024]{1,0:T(8,128)(2,1)}, bf16[512,1024]{1,0:T(8,128)(2,1)}) custom-call(s32[2]{0:T(128)S(1)} %get-tuple-element.376.idx_ref, s32[1]{0:T(128)} %get-tuple-element.377.len_ref, f32[1]{0:T(128)} %get-tuple-element.378.weight_ref, ...), custom_call_target="tpu_custom_call" | custom-call | flops 13958643712 | bytes 28311552 | tf_op jit(solution)/shard_map/cond/branch_1_fun/pallas_call | solution.py:336
  135.6 44.7 %conditional.16 = (bf16[512,1024]{1,0:T(8,128)(2,1)}, bf16[3,128,256]{2,1,0:T(8,128)(2,1)}, bf16[3,128,256]{2,1,0:T(8,128)(2,1)}, bf16[2,512,1024]{2,1,0:T(8,128...) conditional(s32[]{:T(128)} %convert_element_type.157, ...), branch_computations={%region_9.10_spmd, %region_10.11_spmd} | conditional | flops 13958643712 | bytes 34078904 | solution.py:716
  146.2 3.0 collective-permute-start.20
  149.2 23.7 %branch_1_fun.15 = (bf16[2,512,1024]{2,1,0:T(8,128)(2,1)}, bf16[3,512,2048]{2,1,0:T(8,128)(2,1)}, bf16[512,1024]{1,0:T(8,128)(2,1)}, bf16[512,1024]{1,0:T(8,128)(2,1)}, f32[512,1024]{1,0:T(8,128)S(1)}) custom-call(s32[2]{0:T(128)S(1)} %get-tuple-element.402.idx_ref, s32[1]{0:T(128)} %get-tuple-element.403.len_ref, f32[1]{0:T(128)} %get-tuple-element.404.weight_ref, ...), custom_call_target="tpu_custom_call" | custom-call | flops 13958643712 | bytes 28311552 | tf_op jit(solution)/shard_map/cond/branch_1_fun/pallas_call | solution.py:336
  173.0 7.3 %collective-permute-done.18 = bf16[512,1024]{1,0:T(8,128)(2,1)} collective-permute-done((bf16[512,1024]{1,0:T(8,128)(2,1)}, bf16[512,1024]{1,0:T(8,128)(2,1)}, u32[]{:S(2)}, u32[]{:S(2)}) %collective-permute-start.18) | collective-permute-done | bytes 1048608 | tf_op jit(solution)/shard_map/cond/branch_1_fun/ppermute | solution.py:722
  182.7 7.7 %shard_map.172 = (f32[512,1024]{1,0:T(8,128)}, bf16[512,1024]{1,0:T(8,128)(2,1)}, bf16[512,1024]{1,0:T(8,128)(2,1)}, f32[8,1024]{1,0:T(8,128)S(1)}, bf16[512,256...) custom-call(s32[2]{0:T(128)S(1)} %pad_add_fusion.idx_ref, ...), custom_call_target="tpu_custom_call" | custom-call | flops 1073741824 | bytes 10485760 | tf_op jit(solution)/shard_map/pallas_call | solution.py:477
  190.4 14.3 %conditional.17 = (bf16[512,256]{1,0:T(8,128)(2,1)}, bf16[512,256]{1,0:T(8,128)(2,1)}, bf16[4,384,1024]{2,1,0:T(8,128)(2,1)}, bf16[4,384,1024]{2,1,0:T(8,128)(2,1)}) conditional(s32[]{:T(128)} %convert_element_type.157, () %tuple.122, (bf16[512,256]{1,0:T(8,128)(2,1)S(1)}, bf16[512,256]{1,0:T(8,128)(2,1)S(1)}, s32[2]{0:T(128)S(1)}, ...), branch_computations={%region_11.12_spmd, %region_12.13_spmd} | conditional | flops 6442450944 | bytes 18874480 | solution.py:716
  192.5 12.2 %branch_1_fun.16 = (bf16[4,384,1024]{2,1,0:T(8,128)(2,1)}, bf16[4,384,1024]{2,1,0:T(8,128)(2,1)}) custom-call(s32[2]{0:T(128)S(1)} %get-tuple-element.430.idx_ref, bf16[2,512,1024]{2,1,0:T(8,128)(2,1)} %get-tuple-element.431.refs_0_, bf16[2,512,1024]{2,1,0:T(8,128)(2,1)} %get-tuple-element.432.refs_1_, bf16[3,512,2048]{2,1,0:T(8,128)(2,1)} %get-tuple-element.433.refs_2_, ...), custom_call_target="tpu_custom_call" | custom-call | flops 6442450944 | bytes 16777216 | tf_op jit(solution)/shard_map/cond/branch_1_fun/pallas_call | solution.py:424
  204.7 17.0 %conditional.18 = (bf16[512,256]{1,0:T(8,128)(2,1)}, bf16[4,384,1024]{2,1,0:T(8,128)(2,1)}, bf16[8,512,1024]{2,1,0:T(8,128)(2,1)}) conditional(s32[]{:T(128)} %convert_element_type.157, () %tuple.127, (bf16[512,256]{1,0:T(8,128)(2,1)S(1)}, bf16[4,384,1024]{2,1,0:T(8,128)(2,1)}, s32[2]{0:T(128)S(1)}, bf16[2,512,1024]{2,1,0:T(8,128)(2,1)}, ...), branch_computations={%region_13.14_spmd, %region_14.15_spmd} | conditional | flops 8589934592 | bytes 32505960 | solution.py:716
  207.2 14.4 %branch_1_fun.17 = bf16[8,512,1024]{2,1,0:T(8,128)(2,1)} custom-call(s32[2]{0:T(128)S(1)} %get-tuple-element.439.idx_ref, bf16[2,512,1024]{2,1,0:T(8,128)(2,1)} %get-tuple-element.440.refs_0_, bf16[2,512,1024]{2,1,0:T(8,128)(2,1)} %get-tuple-element.441.refs_1_, bf16[3,512,2048]{2,1,0:T(8,128)(2,1)} %get-tuple-element.442.refs_2_, ...), custom_call_target="tpu_custom_call" | custom-call | flops 8589934592 | bytes 18874368 | tf_op jit(solution)/shard_map/cond/branch_1_fun/pallas_call | solution.py:424
  221.7 4.6 %all-gather.7.cloned.1.call-done = bf16[32,3,128,256]{3,2,1,0:T(8,128)(2,1)} async-done(((bf16[4,3,128,256]{3,2,1,0:T(8,128)(2,1)}), bf16[32,3,128,256]{3,2,1,0:T(8,128)(2,1)}) %all-gather.7.cloned.1.call-update) | async-done | bytes 6291472 | tf_op jit(solution)/shard_map/all_gather | solution.py:829
  226.3 4.4 %add_convert_fusion.1 = bf16[4,384,1024]{2,1,0:T(8,128)(2,1)S(1)} fusion(bf16[4,384,1024]{2,1,0:T(8,128)(2,1)} %get-tuple-element.695, bf16[4,384,1024]{2,1,0:T(8,128)(2,1)} %get-tuple-element.690), kind=kLoop, calls=%fused_computation.22 | loop fusion | flops 6291456 | bytes 9437184 | tf_op jit(solution)/shard_map/convert_element_type | solution.py:734
  232.9 31.7 %conditional.19 = (bf16[512,1024]{1,0:T(8,128)(2,1)}, bf16[2,192,1024]{2,1,0:T(8,128)(2,1)}, bf16[2,192,1024]{2,1,0:T(8,128)(2,1)}, bf16[3,512,128]{2,1,0:T(8,12...) conditional(s32[]{:T(128)} %convert_element_type.157, ...), branch_computations={%region_15.16_spmd, %region_16.17_spmd} | conditional | flops 10737418240 | bytes 18874544 | solution.py:716
  236.9 27.7 %branch_1_fun.18 = (bf16[3,512,128]{2,1,0:T(8,128)(2,1)}, bf16[3,512,128]{2,1,0:T(8,128)(2,1)}, bf16[3,512,128]{2,1,0:T(8,128)(2,1)}, bf16[3,512,128]{2,1,0:T(8,128)(2,1)}) custom-call(s32[2]{0:T(128)S(1)} %get-tuple-element.449.idx_ref, bf16[2,2048,128]{2,1,0:T(8,128)(2,1)} %get-tuple-element.450.q_ref, bf16[4,2048,128]{2,1,0:T(8,128)(2,1)} %get-tuple-element.451.k_ref, ...), custom_call_target="tpu_custom_call" | custom-call | flops 10737418240 | bytes 8388608 | tf_op jit(solution)/shard_map/cond/branch_1_fun/pallas_call | solution.py:558
  264.6 2.6 fusion.4
  268.9 33.2 %conditional.20 = (bf16[3,512,128]{2,1,0:T(8,128)(2,1)}, bf16[3,512,128]{2,1,0:T(8,128)(2,1)}, bf16[3,512,128]{2,1,0:T(8,128)(2,1)}, bf16[192,1024]{1,0:T(8,128)...) conditional(s32[]{:T(128)} %convert_element_type.157, ...), branch_computations={%region_17.18_spmd, %region_18.19_spmd} | conditional | flops 10737418240 | bytes 16253200 | solution.py:716
  275.5 26.6 %branch_1_fun.19 = (bf16[3,512,128]{2,1,0:T(8,128)(2,1)}, bf16[3,512,128]{2,1,0:T(8,128)(2,1)}, bf16[3,512,128]{2,1,0:T(8,128)(2,1)}, bf16[3,512,128]{2,1,0:T(8,128)(2,1)}) custom-call(s32[2]{0:T(128)S(1)} %get-tuple-element.469.idx_ref, bf16[2,2048,128]{2,1,0:T(8,128)(2,1)} %get-tuple-element.470.q_ref, bf16[4,2048,128]{2,1,0:T(8,128)(2,1)} %get-tuple-element.471.k_ref, ...), custom_call_target="tpu_custom_call" | custom-call | flops 10737418240 | bytes 8388608 | tf_op jit(solution)/shard_map/cond/branch_1_fun/pallas_call | solution.py:558
  304.6 67.2 %conditional.21 = (bf16[3,512,128]{2,1,0:T(8,128)(2,1)}, bf16[3,512,128]{2,1,0:T(8,128)(2,1)}, bf16[3,512,128]{2,1,0:T(8,128)(2,1)}, bf16[384,1024]{1,0:T(8,128)...) conditional(s32[]{:T(128)} %convert_element_type.157, () %tuple.110, ...), branch_computations={%region_19.20_spmd, %region_20.24_spmd} | conditional | flops 3226681344 | bytes 42582980 | solution.py:716
  304.6 6.7 %collective-permute-start.47 = (bf16[384,1024]{1,0:T(8,128)(2,1)S(1)}, bf16[384,1024]{1,0:T(8,128)(2,1)}, u32[]{:S(2)}, u32[]{:S(2)}) collective-permute-start(bf16[384,1024]{1,0:T(8,128)(2,1)S(1)} %get-tuple-element.510), channel_id=1, source_target_pairs={{0,2},{1,3},{2,0},{3,1},{4,6},{5,7},{6,4},{7,5},{8,10},{9,11},{10,... | collective-permute-start | bytes 2359304 | tf_op jit(solution)/shard_map/cond/branch_1_fun/ppermute | solution.py:722
  312.4 47.3 %conditional = (f32[3,128,256]{2,1,0:T(8,128)}, f32[2,1024]{1,0:T(2,128)}, f32[512,1024]{1,0:T(8,128)}) conditional(s32[]{:T(128)} %convert_element_type.130, () %tuple.78, (s32[2]{0:T(128)S(1)}, bf16[2048,1024]{1,0:T(8,128)(2,1)}, bf16[3,1024,256]{2,1,0:T(8,128)(2,1)}, f32[2,1024]{1,0:T(2,128)S(1)}, bf16[3,512,128]{2,1,0:T(8,128)(2,1)}, ...), branch_computations={%region_21.21_spmd, %region_22.23_spmd} | conditional | flops 3226681344 | bytes 34718304 | solution.py:716
  312.4 11.4 %branch_1_fun.20 = (bf16[4,128,768]{2,1,0:T(8,128)(2,1)}, bf16[4,128,768]{2,1,0:T(8,128)(2,1)}, f32[1024,128]{1,0:T(8,128)}) custom-call(s32[2]{0:T(128)S(1)} %get-tuple-element.484.idx_ref, bf16[2048,1024]{1,0:T(8,128)(2,1)} %get-tuple-element.485.x_ref, bf16[3,1024,256]{2,1,0:T(8,128)(2,1)} %get-tuple-element.486.w_ref, ...), custom_call_target="tpu_custom_call" | custom-call | flops 3221225472 | bytes 10485760 | tf_op jit(solution)/shard_map/cond/branch_1_fun/cond/branch_1_fun/pallas_call | solution.py:619
  325.0 3.4 convert_add_fusion
  331.4 5.8 %collective-permute-done.37 = bf16[2,64,768]{2,1,0:T(8,128)(2,1)S(1)} collective-permute-done((bf16[2,64,768]{2,1,0:T(8,128)(2,1)S(1)}, bf16[2,64,768]{2,1,0:T(8,128)(2,1)S(1)}, u32[]{:S(2)}, u32[]{:S(2)}) %collective-permute-start.37) | collective-permute-done | bytes 196640 | tf_op jit(solution)/shard_map/cond/branch_1_fun/cond/branch_1_fun/ppermute | solution.py:722
  339.4 5.5 %collective-permute-done.39 = bf16[2,64,768]{2,1,0:T(8,128)(2,1)S(1)} collective-permute-done((bf16[2,64,768]{2,1,0:T(8,128)(2,1)S(1)}, bf16[2,64,768]{2,1,0:T(8,128)(2,1)S(1)}, u32[]{:S(2)}, u32[]{:S(2)}) %collective-permute-start.39) | collective-permute-done | bytes 196640 | tf_op jit(solution)/shard_map/cond/branch_1_fun/cond/branch_1_fun/ppermute | solution.py:722
  347.5 3.1 collective-permute-done.40
  352.9 2.6 collective-permute-done.42
  359.7 3.4 collective-permute-start.46
  363.1 8.5 %collective-permute-done.46 = bf16[3,512,128]{2,1,0:T(8,128)(2,1)} collective-permute-done((bf16[3,512,128]{2,1,0:T(8,128)(2,1)}, bf16[3,512,128]{2,1,0:T(8,128)(2,1)}, u32[]{:S(2)}, u32[]{:S(2)}) %collective-permute-start.46) | collective-permute-done | bytes 393248 | tf_op jit(solution)/shard_map/cond/branch_1_fun/ppermute | solution.py:722
  373.7 20.2 %conditional.22 = (bf16[152,256]{1,0:T(8,128)(2,1)}, bf16[152,256]{1,0:T(8,128)(2,1)}, bf16[152,256]{1,0:T(8,128)(2,1)}, f32[512,1024]{1,0:T(8,128)}, f32[2,128,1024]{2,1,0:T(8,128)}, /*index=5*/f32[1024,128]{1,0:T(8,128)}) conditional(s32[]{:T(128)} %convert_element_type.157, () %tuple.132, (bf16[152,256]{1,0:T(8,128)(2,1)S(1)}, ...), branch_computations={%region_25.26_spmd, %region_26.27_spmd} | conditional | flops 3221225472 | bytes 12468392 | solution.py:716
  373.7 7.0 %collective-permute-start.33 = (bf16[152,256]{1,0:T(8,128)(2,1)S(1)}, bf16[152,256]{1,0:T(8,128)(2,1)}, u32[]{:S(2)}, u32[]{:S(2)}) collective-permute-start(bf16[152,256]{1,0:T(8,128)(2,1)S(1)} %get-tuple-element.529), channel_id=1, source_target_pairs={{0,1},{1,0},{2,3},{3,2},{4,5},{5,4},{6,7},{7,6},{8,9},{9,8},{10,11... | collective-permute-start | bytes 233480 | tf_op jit(solution)/shard_map/cond/branch_1_fun/ppermute | solution.py:722
  383.1 10.8 %branch_1_fun.21 = (f32[512,1024]{1,0:T(8,128)}, f32[2,128,1024]{2,1,0:T(8,128)}, f32[1024,128]{1,0:T(8,128)}) custom-call(s32[2]{0:T(128)S(1)} %get-tuple-element.532.idx_ref, bf16[2048,1024]{1,0:T(8,128)(2,1)} %get-tuple-element.533.x_ref, f32[512,1024]{1,0:T(8,128)} %get-tuple-element.534.gr_ref, bf16[8,4,3,128,256]{4,3,2,1,0:T(8,128)(2,1)} %get-tuple-element.535.w_ref, ...), custom_call_target="tpu_custom_call" | custom-call | flops 3221225472 | bytes 11534336 | tf_op jit(solution)/shard_map/cond/branch_1_fun/pallas_call | solution.py:666
  (161 shorter events, 64.6 us)
Async XLA Ops:
  7.2 100.1 %all-gather.5.cloned.1.call-start = ((), (), s32[]{:S(2)}) async-start(), calls=%async_computation.2 | async-start | bytes 7077888 | tf_op jit(solution)/shard_map/all_gather | solution.py:778
  10.3 38.8 %collective-permute-start = (bf16[384,1024]{1,0:T(8,128)(2,1)}, bf16[384,1024]{1,0:T(8,128)(2,1)}, u32[]{:S(2)}, u32[]{:S(2)}) collective-permute-start(bf16[384,1024]{1,0:T(8,128)(2,1)} %get-tuple-element.336), channel_id=1, source_target_pairs={{0,2},{1,3},{2,0},{3,1},{4,6},{5,7},{6,4},{7,5},{8,10},{9,11},{10,... | collective-permute-start | bytes 2359304 | tf_op jit(solution)/shard_map/cond/branch_1_fun/ppermute | solution.py:722
  49.2 177.1 %all-gather.7.cloned.1.call-start = ((), (), s32[]{:S(2)}) async-start(), calls=%async_computation.3 | async-start | bytes 7077888 | tf_op jit(solution)/shard_map/all_gather | solution.py:829
  49.3 20.4 %collective-permute-start.1 = (bf16[32,1024]{1,0:T(8,128)(2,1)S(1)}, bf16[32,1024]{1,0:T(8,128)(2,1)}, u32[]{:S(2)}, u32[]{:S(2)}) collective-permute-start(bf16[32,1024]{1,0:T(8,128)(2,1)S(1)} %get-tuple-element.353), channel_id=1, source_target_pairs={{0,1},{1,0},{2,3},{3,2},{4,5},{5,4},{6,7},{7,6},{8,9},{9,8},{10,11... | collective-permute-start | bytes 196616 | tf_op jit(solution)/shard_map/cond/branch_1_fun/ppermute | solution.py:722
  50.1 19.6 %collective-permute-start.2 = (bf16[32,1024]{1,0:T(8,128)(2,1)S(1)}, bf16[32,1024]{1,0:T(8,128)(2,1)}, u32[]{:S(2)}, u32[]{:S(2)}) collective-permute-start(bf16[32,1024]{1,0:T(8,128)(2,1)S(1)} %get-tuple-element.353), channel_id=1, source_target_pairs={{0,2},{1,3},{2,0},{3,1},{4,6},{5,7},{6,4},{7,5},{8,10},{9,11},{10,... | collective-permute-start | bytes 196616 | tf_op jit(solution)/shard_map/cond/branch_1_fun/ppermute | solution.py:722
  53.4 16.2 %collective-permute-start.3 = (bf16[32,1024]{1,0:T(8,128)(2,1)S(1)}, bf16[32,1024]{1,0:T(8,128)(2,1)}, u32[]{:S(2)}, u32[]{:S(2)}) collective-permute-start(bf16[32,1024]{1,0:T(8,128)(2,1)S(1)} %get-tuple-element.353), channel_id=1, source_target_pairs={{0,3},{1,2},{2,1},{3,0},{4,7},{5,6},{6,5},{7,4},{8,11},{9,10},{10,... | collective-permute-start | bytes 196616 | tf_op jit(solution)/shard_map/cond/branch_1_fun/ppermute | solution.py:722
  71.3 12.9 %collective-permute-start.4 = (bf16[512,256]{1,0:T(8,128)(2,1)S(1)}, bf16[512,256]{1,0:T(8,128)(2,1)}, u32[]{:S(2)}, u32[]{:S(2)}) collective-permute-start(bf16[512,256]{1,0:T(8,128)(2,1)S(1)} %get-tuple-element.368), channel_id=1, source_target_pairs={{0,1},{1,0},{2,3},{3,2},{4,5},{5,4},{6,7},{7,6},{8,9},{9,8},{10,11... | collective-permute-start | bytes 786440 | tf_op jit(solution)/shard_map/cond/branch_1_fun/ppermute | solution.py:722
  71.6 14.9 %collective-permute-start.5 = (bf16[512,256]{1,0:T(8,128)(2,1)S(1)}, bf16[512,256]{1,0:T(8,128)(2,1)}, u32[]{:S(2)}, u32[]{:S(2)}) collective-permute-start(bf16[512,256]{1,0:T(8,128)(2,1)S(1)} %get-tuple-element.369), channel_id=1, source_target_pairs={{0,2},{1,3},{2,0},{3,1},{4,6},{5,7},{6,4},{7,5},{8,10},{9,11},{10,... | collective-permute-start | bytes 786440 | tf_op jit(solution)/shard_map/cond/branch_1_fun/ppermute | solution.py:722
  75.4 14.7 %collective-permute-start.8 = (bf16[4,32,1024]{2,1,0:T(8,128)(2,1)S(1)}, bf16[4,32,1024]{2,1,0:T(8,128)(2,1)}, u32[]{:S(2)}, u32[]{:S(2)}) collective-permute-start(bf16[4,32,1024]{2,1,0:T(8,128)(2,1)S(1)} %get-tuple-element.371), channel_id=1, source_target_pairs={{0,8},{4,12},{8,0},{12,4},{16,24},{20,28},{24,16},{28,20},{1,9},{5... | collective-permute-start | bytes 786440 | tf_op jit(solution)/shard_map/cond/branch_1_fun/ppermute | solution.py:722
  76.9 15.8 %collective-permute-start.10 = (bf16[4,32,1024]{2,1,0:T(8,128)(2,1)S(1)}, bf16[4,32,1024]{2,1,0:T(8,128)(2,1)}, u32[]{:S(2)}, u32[]{:S(2)}) collective-permute-start(bf16[4,32,1024]{2,1,0:T(8,128)(2,1)S(1)} %get-tuple-element.371), channel_id=1, source_target_pairs={{0,16},{4,20},{8,24},{12,28},{16,0},{20,4},{24,8},{28,12},{1,17},{... | collective-permute-start | bytes 786440 | tf_op jit(solution)/shard_map/cond/branch_1_fun/ppermute | solution.py:722
  78.4 22.8 %collective-permute-start.12 = (bf16[4,32,1024]{2,1,0:T(8,128)(2,1)S(1)}, bf16[4,32,1024]{2,1,0:T(8,128)(2,1)}, u32[]{:S(2)}, u32[]{:S(2)}) collective-permute-start(bf16[4,32,1024]{2,1,0:T(8,128)(2,1)S(1)} %get-tuple-element.371), channel_id=1, source_target_pairs={{0,24},{4,28},{8,16},{12,20},{16,8},{20,12},{24,0},{28,4},{1,25},{... | collective-permute-start | bytes 786440 | tf_op jit(solution)/shard_map/cond/branch_1_fun/ppermute | solution.py:722
  84.2 17.0 %collective-permute-start.7 = (bf16[4,32,1024]{2,1,0:T(8,128)(2,1)S(1)}, bf16[4,32,1024]{2,1,0:T(8,128)(2,1)}, u32[]{:S(2)}, u32[]{:S(2)}) collective-permute-start(bf16[4,32,1024]{2,1,0:T(8,128)(2,1)S(1)} %get-tuple-element.371), channel_id=1, source_target_pairs={{0,4},{4,0},{8,12},{12,8},{16,20},{20,16},{24,28},{28,24},{1,5},{5... | collective-permute-start | bytes 786440 | tf_op jit(solution)/shard_map/cond/branch_1_fun/ppermute | solution.py:722
  86.6 14.7 %collective-permute-start.6 = (bf16[512,256]{1,0:T(8,128)(2,1)S(1)}, bf16[512,256]{1,0:T(8,128)(2,1)}, u32[]{:S(2)}, u32[]{:S(2)}) collective-permute-start(bf16[512,256]{1,0:T(8,128)(2,1)S(1)} %get-tuple-element.370), channel_id=1, source_target_pairs={{0,3},{1,2},{2,1},{3,0},{4,7},{5,6},{6,5},{7,4},{8,11},{9,10},{10,... | collective-permute-start | bytes 786440 | tf_op jit(solution)/shard_map/cond/branch_1_fun/ppermute | solution.py:722
  90.1 11.1 %collective-permute-start.9 = (bf16[4,32,1024]{2,1,0:T(8,128)(2,1)}, bf16[4,32,1024]{2,1,0:T(8,128)(2,1)}, u32[]{:S(2)}, u32[]{:S(2)}) collective-permute-start(bf16[4,32,1024]{2,1,0:T(8,128)(2,1)} %collective-permute-done.8), channel_id=1, source_target_pairs={{0,4},{4,0},{8,12},{12,8},{16,20},{20,16},{24,28},{28,24},{1,5},{5... | collective-permute-start | bytes 786440 | tf_op jit(solution)/shard_map/cond/branch_1_fun/ppermute | solution.py:722
  92.8 8.5 %collective-permute-start.11 = (bf16[4,32,1024]{2,1,0:T(8,128)(2,1)}, bf16[4,32,1024]{2,1,0:T(8,128)(2,1)}, u32[]{:S(2)}, u32[]{:S(2)}) collective-permute-start(bf16[4,32,1024]{2,1,0:T(8,128)(2,1)} %collective-permute-done.10), channel_id=1, source_target_pairs={{0,4},{4,0},{8,12},{12,8},{16,20},{20,16},{24,28},{28,24},{1,5},{5... | collective-permute-start | bytes 786440 | tf_op jit(solution)/shard_map/cond/branch_1_fun/ppermute | solution.py:722
  107.5 28.0 %collective-permute-start.14 = (bf16[512,256]{1,0:T(8,128)(2,1)S(1)}, bf16[512,256]{1,0:T(8,128)(2,1)}, u32[]{:S(2)}, u32[]{:S(2)}) collective-permute-start(bf16[512,256]{1,0:T(8,128)(2,1)S(1)} %get-tuple-element.372.refs_0_), channel_id=1, source_target_pairs={{0,1},{1,0},{2,3},{3,2},{4,5},{5,4},{6,7},{7,6},{8,9},{9,8},{10,11... | collective-permute-start | bytes 786440 | tf_op jit(solution)/shard_map/cond/branch_1_fun/ppermute | solution.py:722
  108.5 27.1 %collective-permute-start.15 = (bf16[512,256]{1,0:T(8,128)(2,1)S(1)}, bf16[512,256]{1,0:T(8,128)(2,1)}, u32[]{:S(2)}, u32[]{:S(2)}) collective-permute-start(bf16[512,256]{1,0:T(8,128)(2,1)S(1)} %get-tuple-element.373), channel_id=1, source_target_pairs={{0,2},{1,3},{2,0},{3,1},{4,6},{5,7},{6,4},{7,5},{8,10},{9,11},{10,... | collective-permute-start | bytes 786440 | tf_op jit(solution)/shard_map/cond/branch_1_fun/ppermute | solution.py:722
  109.0 26.6 %collective-permute-start.16 = (bf16[512,256]{1,0:T(8,128)(2,1)S(1)}, bf16[512,256]{1,0:T(8,128)(2,1)}, u32[]{:S(2)}, u32[]{:S(2)}) collective-permute-start(bf16[512,256]{1,0:T(8,128)(2,1)S(1)} %get-tuple-element.374), channel_id=1, source_target_pairs={{0,3},{1,2},{2,1},{3,0},{4,7},{5,6},{6,5},{7,4},{8,11},{9,10},{10,... | collective-permute-start | bytes 786440 | tf_op jit(solution)/shard_map/cond/branch_1_fun/ppermute | solution.py:722
  112.0 23.6 %collective-permute-start.17 = (bf16[3,128,256]{2,1,0:T(8,128)(2,1)S(1)}, bf16[3,128,256]{2,1,0:T(8,128)(2,1)}, u32[]{:S(2)}, u32[]{:S(2)}) collective-permute-start(bf16[3,128,256]{2,1,0:T(8,128)(2,1)S(1)} %get-tuple-element.375), channel_id=1, source_target_pairs={{0,1},{1,0},{2,3},{3,2},{4,5},{5,4},{6,7},{7,6},{8,9},{9,8},{10,11... | collective-permute-start | bytes 589832 | tf_op jit(solution)/shard_map/cond/branch_1_fun/ppermute | solution.py:722
  144.7 28.2 %collective-permute-start.19 = (bf16[3,128,256]{2,1,0:T(8,128)(2,1)S(1)}, bf16[3,128,256]{2,1,0:T(8,128)(2,1)}, u32[]{:S(2)}, u32[]{:S(2)}) collective-permute-start(bf16[3,128,256]{2,1,0:T(8,128)(2,1)S(1)} %get-tuple-element.401), channel_id=1, source_target_pairs={{0,2},{1,3},{2,0},{3,1},{4,6},{5,7},{6,4},{7,5},{8,10},{9,11},{10,... | collective-permute-start | bytes 589832 | tf_op jit(solution)/shard_map/cond/branch_1_fun/ppermute | solution.py:722
  146.2 26.7 %collective-permute-start.20 = (bf16[3,128,256]{2,1,0:T(8,128)(2,1)S(1)}, bf16[3,128,256]{2,1,0:T(8,128)(2,1)}, u32[]{:S(2)}, u32[]{:S(2)}) collective-permute-start(bf16[3,128,256]{2,1,0:T(8,128)(2,1)S(1)} %get-tuple-element.401), channel_id=1, source_target_pairs={{0,3},{1,2},{2,1},{3,0},{4,7},{5,6},{6,5},{7,4},{8,11},{9,10},{10,... | collective-permute-start | bytes 589832 | tf_op jit(solution)/shard_map/cond/branch_1_fun/ppermute | solution.py:722
  149.2 31.1 %collective-permute-start.18 = (bf16[512,1024]{1,0:T(8,128)(2,1)}, bf16[512,1024]{1,0:T(8,128)(2,1)}, u32[]{:S(2)}, u32[]{:S(2)}) collective-permute-start(bf16[512,1024]{1,0:T(8,128)(2,1)} %get-tuple-element.400), channel_id=1, source_target_pairs={{0,1},{1,0},{2,3},{3,2},{4,5},{5,4},{6,7},{7,6},{8,9},{9,8},{10,11... | collective-permute-start | bytes 3145736 | tf_op jit(solution)/shard_map/cond/branch_1_fun/ppermute | solution.py:722
  182.4 190.2 %reduce-scatter.2.cloned.1.call-start = ((), (), s32[]{:S(2)}) async-start(), calls=%async_computation.1 | async-start | bytes 9437184 | tf_op jit(solution)/shard_map/reduce_scatter | solution.py:844
  190.4 14.3 %collective-permute-start.21 = (bf16[512,256]{1,0:T(8,128)(2,1)S(1)}, bf16[512,256]{1,0:T(8,128)(2,1)}, u32[]{:S(2)}, u32[]{:S(2)}) collective-permute-start(bf16[512,256]{1,0:T(8,128)(2,1)S(1)} %get-tuple-element.428), channel_id=1, source_target_pairs={{0,1},{1,0},{2,3},{3,2},{4,5},{5,4},{6,7},{7,6},{8,9},{9,8},{10,11... | collective-permute-start | bytes 786440 | tf_op jit(solution)/shard_map/cond/branch_1_fun/ppermute | solution.py:722
  190.5 14.2 %collective-permute-start.22 = (bf16[512,256]{1,0:T(8,128)(2,1)S(1)}, bf16[512,256]{1,0:T(8,128)(2,1)}, u32[]{:S(2)}, u32[]{:S(2)}) collective-permute-start(bf16[512,256]{1,0:T(8,128)(2,1)S(1)} %get-tuple-element.429), channel_id=1, source_target_pairs={{0,2},{1,3},{2,0},{3,1},{4,6},{5,7},{6,4},{7,5},{8,10},{9,11},{10,... | collective-permute-start | bytes 786440 | tf_op jit(solution)/shard_map/cond/branch_1_fun/ppermute | solution.py:722
  204.7 16.9 %collective-permute-start.24 = (bf16[4,384,1024]{2,1,0:T(8,128)(2,1)}, bf16[4,384,1024]{2,1,0:T(8,128)(2,1)}, u32[]{:S(2)}, u32[]{:S(2)}) collective-permute-start(bf16[4,384,1024]{2,1,0:T(8,128)(2,1)} %get-tuple-element.438), channel_id=1, source_target_pairs={{0,4},{4,0},{8,12},{12,8},{16,20},{20,16},{24,28},{28,24},{1,5},{5... | collective-permute-start | bytes 9437192 | tf_op jit(solution)/shard_map/cond/branch_1_fun/ppermute | solution.py:722
  204.8 16.8 %collective-permute-start.23 = (bf16[512,256]{1,0:T(8,128)(2,1)S(1)}, bf16[512,256]{1,0:T(8,128)(2,1)}, u32[]{:S(2)}, u32[]{:S(2)}) collective-permute-start(bf16[512,256]{1,0:T(8,128)(2,1)S(1)} %get-tuple-element.437), channel_id=1, source_target_pairs={{0,3},{1,2},{2,1},{3,0},{4,7},{5,6},{6,5},{7,4},{8,11},{9,10},{10,... | collective-permute-start | bytes 786440 | tf_op jit(solution)/shard_map/cond/branch_1_fun/ppermute | solution.py:722
  233.3 31.3 %collective-permute-start.25 = (bf16[512,1024]{1,0:T(8,128)(2,1)}, bf16[512,1024]{1,0:T(8,128)(2,1)}, u32[]{:S(2)}, u32[]{:S(2)}) collective-permute-start(bf16[512,1024]{1,0:T(8,128)(2,1)} %get-tuple-element.446), channel_id=1, source_target_pairs={{0,1},{1,0},{2,3},{3,2},{4,5},{5,4},{6,7},{7,6},{8,9},{9,8},{10,11... | collective-permute-start | bytes 3145736 | tf_op jit(solution)/shard_map/cond/branch_1_fun/ppermute | solution.py:722
  234.9 29.7 %collective-permute-start.26 = (bf16[2,192,1024]{2,1,0:T(8,128)(2,1)S(1)}, bf16[2,192,1024]{2,1,0:T(8,128)(2,1)}, u32[]{:S(2)}, u32[]{:S(2)}) collective-permute-start(bf16[2,192,1024]{2,1,0:T(8,128)(2,1)S(1)} %get-tuple-element.447), channel_id=1, source_target_pairs={{0,16},{4,20},{8,24},{12,28},{16,0},{20,4},{24,8},{28,12},{1,17},{... | collective-permute-start | bytes 2359304 | tf_op jit(solution)/shard_map/cond/branch_1_fun/ppermute | solution.py:722
  236.1 28.5 %collective-permute-start.27 = (bf16[2,192,1024]{2,1,0:T(8,128)(2,1)}, bf16[2,192,1024]{2,1,0:T(8,128)(2,1)}, u32[]{:S(2)}, u32[]{:S(2)}) collective-permute-start(bf16[2,192,1024]{2,1,0:T(8,128)(2,1)} %get-tuple-element.448), channel_id=1, source_target_pairs={{0,8},{4,12},{8,0},{12,4},{16,24},{20,28},{24,16},{28,20},{1,9},{5... | collective-permute-start | bytes 2359304 | tf_op jit(solution)/shard_map/cond/branch_1_fun/ppermute | solution.py:722
  269.0 33.0 %collective-permute-start.28 = (bf16[3,512,128]{2,1,0:T(8,128)(2,1)S(1)}, bf16[3,512,128]{2,1,0:T(8,128)(2,1)}, u32[]{:S(2)}, u32[]{:S(2)}) collective-permute-start(bf16[3,512,128]{2,1,0:T(8,128)(2,1)S(1)} %get-tuple-element.464), channel_id=1, source_target_pairs={{0,1},{1,0},{2,3},{3,2},{4,5},{5,4},{6,7},{7,6},{8,9},{9,8},{10,11... | collective-permute-start | bytes 1179656 | tf_op jit(solution)/shard_map/cond/branch_1_fun/ppermute | solution.py:722
  269.7 32.3 %collective-permute-start.29 = (bf16[3,512,128]{2,1,0:T(8,128)(2,1)}, bf16[3,512,128]{2,1,0:T(8,128)(2,1)}, u32[]{:S(2)}, u32[]{:S(2)}) collective-permute-start(bf16[3,512,128]{2,1,0:T(8,128)(2,1)} %get-tuple-element.465), channel_id=1, source_target_pairs={{0,2},{1,3},{2,0},{3,1},{4,6},{5,7},{6,4},{7,5},{8,10},{9,11},{10,... | collective-permute-start | bytes 1179656 | tf_op jit(solution)/shard_map/cond/branch_1_fun/ppermute | solution.py:722
  272.1 29.9 %collective-permute-start.30 = (bf16[3,512,128]{2,1,0:T(8,128)(2,1)}, bf16[3,512,128]{2,1,0:T(8,128)(2,1)}, u32[]{:S(2)}, u32[]{:S(2)}) collective-permute-start(bf16[3,512,128]{2,1,0:T(8,128)(2,1)} %get-tuple-element.466), channel_id=1, source_target_pairs={{0,3},{1,2},{2,1},{3,0},{4,7},{5,6},{6,5},{7,4},{8,11},{9,10},{10,... | collective-permute-start | bytes 1179656 | tf_op jit(solution)/shard_map/cond/branch_1_fun/ppermute | solution.py:722
  273.5 28.6 %collective-permute-start.31 = (bf16[192,1024]{1,0:T(8,128)(2,1)}, bf16[192,1024]{1,0:T(8,128)(2,1)}, u32[]{:S(2)}, u32[]{:S(2)}) collective-permute-start(bf16[192,1024]{1,0:T(8,128)(2,1)} %get-tuple-element.467), channel_id=1, source_target_pairs={{0,8},{4,12},{8,0},{12,4},{16,24},{20,28},{24,16},{28,20},{1,9},{5... | collective-permute-start | bytes 1179656 | tf_op jit(solution)/shard_map/cond/branch_1_fun/ppermute | solution.py:722
  274.7 27.4 %collective-permute-start.32 = (bf16[192,1024]{1,0:T(8,128)(2,1)}, bf16[192,1024]{1,0:T(8,128)(2,1)}, u32[]{:S(2)}, u32[]{:S(2)}) collective-permute-start(bf16[192,1024]{1,0:T(8,128)(2,1)} %get-tuple-element.468), channel_id=1, source_target_pairs={{0,16},{4,20},{8,24},{12,28},{16,0},{20,4},{24,8},{28,12},{1,17},{... | collective-permute-start | bytes 1179656 | tf_op jit(solution)/shard_map/cond/branch_1_fun/ppermute | solution.py:722
  304.6 67.0 %collective-permute-start.47 = (bf16[384,1024]{1,0:T(8,128)(2,1)S(1)}, bf16[384,1024]{1,0:T(8,128)(2,1)}, u32[]{:S(2)}, u32[]{:S(2)}) collective-permute-start(bf16[384,1024]{1,0:T(8,128)(2,1)S(1)} %get-tuple-element.510), channel_id=1, source_target_pairs={{0,2},{1,3},{2,0},{3,1},{4,6},{5,7},{6,4},{7,5},{8,10},{9,11},{10,... | collective-permute-start | bytes 2359304 | tf_op jit(solution)/shard_map/cond/branch_1_fun/ppermute | solution.py:722
  311.3 51.7 %collective-permute-start.44 = (bf16[3,512,128]{2,1,0:T(8,128)(2,1)}, bf16[3,512,128]{2,1,0:T(8,128)(2,1)}, u32[]{:S(2)}, u32[]{:S(2)}) collective-permute-start(bf16[3,512,128]{2,1,0:T(8,128)(2,1)} %get-tuple-element.507), channel_id=1, source_target_pairs={{0,1},{1,0},{2,3},{3,2},{4,5},{5,4},{6,7},{7,6},{8,9},{9,8},{10,11... | collective-permute-start | bytes 1179656 | tf_op jit(solution)/shard_map/cond/branch_1_fun/ppermute | solution.py:722
  311.3 51.7 %collective-permute-start.45 = (bf16[3,512,128]{2,1,0:T(8,128)(2,1)}, bf16[3,512,128]{2,1,0:T(8,128)(2,1)}, u32[]{:S(2)}, u32[]{:S(2)}) collective-permute-start(bf16[3,512,128]{2,1,0:T(8,128)(2,1)} %get-tuple-element.508), channel_id=1, source_target_pairs={{0,2},{1,3},{2,0},{3,1},{4,6},{5,7},{6,4},{7,5},{8,10},{9,11},{10,... | collective-permute-start | bytes 1179656 | tf_op jit(solution)/shard_map/cond/branch_1_fun/ppermute | solution.py:722
  323.7 4.7 %collective-permute-start.36 = (bf16[4,128,768]{2,1,0:T(8,128)(2,1)}, bf16[4,128,768]{2,1,0:T(8,128)(2,1)}, u32[]{:S(2)}, u32[]{:S(2)}) collective-permute-start(bf16[4,128,768]{2,1,0:T(8,128)(2,1)} %get-tuple-element.497), channel_id=1, source_target_pairs={{0,4},{4,0},{8,12},{12,8},{16,20},{20,16},{24,28},{28,24},{1,5},{5... | collective-permute-start | bytes 2359304 | tf_op jit(solution)/shard_map/cond/branch_1_fun/cond/branch_1_fun/ppermute | solution.py:722
  329.9 7.4 %collective-permute-start.37 = (bf16[2,64,768]{2,1,0:T(8,128)(2,1)S(1)}, bf16[2,64,768]{2,1,0:T(8,128)(2,1)S(1)}, u32[]{:S(2)}, u32[]{:S(2)}) collective-permute-start(bf16[2,64,768]{2,1,0:T(8,128)(2,1)S(1)} %dynamic-slice_bitcast_fusion.1), channel_id=1, source_target_pairs={{0,16},{4,20},{8,24},{12,28},{16,0},{20,4},{24,8},{28,12},{1,17},{... | collective-permute-start | bytes 589832 | tf_op jit(solution)/shard_map/cond/branch_1_fun/cond/branch_1_fun/ppermute | solution.py:722
  337.2 7.7 %collective-permute-start.39 = (bf16[2,64,768]{2,1,0:T(8,128)(2,1)S(1)}, bf16[2,64,768]{2,1,0:T(8,128)(2,1)S(1)}, u32[]{:S(2)}, u32[]{:S(2)}) collective-permute-start(bf16[2,64,768]{2,1,0:T(8,128)(2,1)S(1)} %dynamic-slice_bitcast_fusion), channel_id=1, source_target_pairs={{0,8},{4,12},{8,0},{12,4},{16,24},{20,28},{24,16},{28,20},{1,9},{5... | collective-permute-start | bytes 589832 | tf_op jit(solution)/shard_map/cond/branch_1_fun/cond/branch_1_fun/ppermute | solution.py:722
  338.4 7.6 %collective-permute-start.38 = (bf16[64,768]{1,0:T(8,128)(2,1)S(1)}, bf16[64,768]{1,0:T(8,128)(2,1)S(1)}, u32[]{:S(2)}, u32[]{:S(2)}) collective-permute-start(bf16[64,768]{1,0:T(8,128)(2,1)S(1)} %dynamic-slice_bitcast_fusion.3), channel_id=1, source_target_pairs={{0,8},{4,12},{8,0},{12,4},{16,24},{20,28},{24,16},{28,20},{1,9},{5... | collective-permute-start | bytes 294920 | tf_op jit(solution)/shard_map/cond/branch_1_fun/cond/branch_1_fun/ppermute | solution.py:722
  346.0 4.6 %collective-permute-start.40 = (bf16[64,768]{1,0:T(8,128)(2,1)S(1)}, bf16[64,768]{1,0:T(8,128)(2,1)S(1)}, u32[]{:S(2)}, u32[]{:S(2)}) collective-permute-start(bf16[64,768]{1,0:T(8,128)(2,1)S(1)} %dynamic-slice_bitcast_fusion.2), channel_id=1, source_target_pairs={{0,16},{4,20},{8,24},{12,28},{16,0},{20,4},{24,8},{28,12},{1,17},{... | collective-permute-start | bytes 294920 | tf_op jit(solution)/shard_map/cond/branch_1_fun/cond/branch_1_fun/ppermute | solution.py:722
  355.4 3.7 collective-permute-start.43
  359.7 11.9 %collective-permute-start.46 = (bf16[3,512,128]{2,1,0:T(8,128)(2,1)}, bf16[3,512,128]{2,1,0:T(8,128)(2,1)}, u32[]{:S(2)}, u32[]{:S(2)}) collective-permute-start(bf16[3,512,128]{2,1,0:T(8,128)(2,1)} %get-tuple-element.509), channel_id=1, source_target_pairs={{0,3},{1,2},{2,1},{3,0},{4,7},{5,6},{6,5},{7,4},{8,11},{9,10},{10,... | collective-permute-start | bytes 1179656 | tf_op jit(solution)/shard_map/cond/branch_1_fun/ppermute | solution.py:722
  373.7 20.2 %collective-permute-start.33 = (bf16[152,256]{1,0:T(8,128)(2,1)S(1)}, bf16[152,256]{1,0:T(8,128)(2,1)}, u32[]{:S(2)}, u32[]{:S(2)}) collective-permute-start(bf16[152,256]{1,0:T(8,128)(2,1)S(1)} %get-tuple-element.529), channel_id=1, source_target_pairs={{0,1},{1,0},{2,3},{3,2},{4,5},{5,4},{6,7},{7,6},{8,9},{9,8},{10,11... | collective-permute-start | bytes 233480 | tf_op jit(solution)/shard_map/cond/branch_1_fun/ppermute | solution.py:722
  380.7 13.2 %collective-permute-start.34 = (bf16[152,256]{1,0:T(8,128)(2,1)S(1)}, bf16[152,256]{1,0:T(8,128)(2,1)}, u32[]{:S(2)}, u32[]{:S(2)}) collective-permute-start(bf16[152,256]{1,0:T(8,128)(2,1)S(1)} %get-tuple-element.530), channel_id=1, source_target_pairs={{0,2},{1,3},{2,0},{3,1},{4,6},{5,7},{6,4},{7,5},{8,10},{9,11},{10,... | collective-permute-start | bytes 233480 | tf_op jit(solution)/shard_map/cond/branch_1_fun/ppermute | solution.py:722
  381.5 12.4 %collective-permute-start.35 = (bf16[152,256]{1,0:T(8,128)(2,1)S(1)}, bf16[152,256]{1,0:T(8,128)(2,1)}, u32[]{:S(2)}, u32[]{:S(2)}) collective-permute-start(bf16[152,256]{1,0:T(8,128)(2,1)S(1)} %get-tuple-element.531), channel_id=1, source_target_pairs={{0,3},{1,2},{2,1},{3,0},{4,7},{5,6},{6,5},{7,4},{8,11},{9,10},{10,... | collective-permute-start | bytes 233480 | tf_op jit(solution)/shard_map/cond/branch_1_fun/ppermute | solution.py:722
  (16 other events, 151.2 us)
Sparse Core Ops, SparseCore 0:
  49.3 57.9 all-gather.4
  182.5 43.6 all-gather.6
  229.7 76.3 reduce-scatter.1

commit v5 on v4

--- a/solution.py
+++ b/solution.py
@@ -147,10 +147,9 @@
     )(lengths, tokens, qkv_weight, gains, cosine, sine)
 
 
-def attend_kernel(sub, parts, done, idx_ref, q_ref, k_ref, v_ref, *refs):
-    prev_refs = refs[:parts] if done else ()
-    o_refs = refs[len(prev_refs) : len(prev_refs) + parts]
-    nat_ref, qb_ref = refs[len(prev_refs) + parts :]
+def attend_kernel(sub, parts, idx_ref, q_ref, k_ref, v_ref, *refs):
+    o_refs = refs[:parts]
+    nat_ref, qb_ref = refs[parts:]
     rows = q_ref.shape[1]
     lane = lax.broadcasted_iota(jnp.int32, (sub, 128), 1)
     for r in range(rows // sub):
@@ -172,35 +171,32 @@
         nat_ref[part, :] = jnp.where(lane < HD, outs[0], outs[1]).astype(BF16)
     for d in range(parts):
 
-        @pl.when(pl.program_id(0) == d)
+        @pl.when(pl.program_id(1) == d)
         def _():
-            if done:
-                o_refs[d][:, :done] = prev_refs[d][...]
-            o_refs[d][:, done:] = nat_ref[...]
-
-
-def attend(index, q, k, v, parts, pair, prev=(), sub=256):
-    _, rows, _ = q.shape
+            o_refs[d][...] = nat_ref[...]
+
+
+def attend(index, q, k, v, parts, sub=256):
+    heads, rows, _ = q.shape
     keys = k.shape[1]
     share = rows // parts
-    cols = 128 * (pair + 1)
+    local = heads * HD
     return call(
-        functools.partial(attend_kernel, min(sub, share), parts, 128 * pair),
-        (parts,),
+        functools.partial(attend_kernel, min(sub, share), parts),
+        (heads // 2, parts),
         [
-            pl.BlockSpec((2, share, 128), lambda i, idx: (pair, idx[0] ^ i, 0)),
-            pl.BlockSpec((2, keys, 128), lambda i, idx: (pair, 0, 0), pipeline_mode=pl.Buffered(1)),
-            pl.BlockSpec((2, keys, 128), lambda i, idx: (pair, 0, 0), pipeline_mode=pl.Buffered(1)),
-        ]
-        + [whole(p.shape) for p in prev],
-        [whole((share, cols))] * parts
+            pl.BlockSpec((2, share, 128), lambda j, i, idx: (j, idx[0] ^ i, 0)),
+            pl.BlockSpec((2, keys, 128), lambda j, i, idx: (j, 0, 0)),
+            pl.BlockSpec((2, keys, 128), lambda j, i, idx: (j, 0, 0)),
+        ],
+        [pl.BlockSpec((share, 128), lambda j, i, idx: (0, j))] * parts
         + [
-            pl.BlockSpec((share, 128), lambda i, idx: (idx[0] ^ i, 0)),
-            pl.BlockSpec((2, share, 128), lambda i, idx: (0, idx[0] ^ i, 0)),
+            pl.BlockSpec((share, 128), lambda j, i, idx: (idx[0] ^ i, j)),
+            pl.BlockSpec((2, share, 128), lambda j, i, idx: (j, idx[0] ^ i, 0)),
         ],
-        [sds((share, cols), BF16)] * parts + [sds((rows, 128), BF16), sds((2, rows, 128), BF16)],
+        [sds((share, local), BF16)] * parts + [sds((rows, local), BF16), sds((heads, rows, 128), BF16)],
         prefetch=1,
-    )(index, q, k, v, *prev)
+    )(index, q, k, v)
 
 
 def cut_kernel(idx_ref, gu_ref, dw_ref, out_ref):
@@ -229,12 +225,23 @@
     )(dp, gate_up, down)
 
 
-def ffn_kernel(parts, shares, slot, idx_ref, len_ref, weight_ref, gain_ref, x_h, cot_h, gu_h, dw_h, pb_h, *refs):
+def pack_kernel(*refs):
+    out_ref, row = refs[-1], 0
+    for ref in refs[:-1]:
+        out_ref[row : row + ref.shape[0], :] = ref[...]
+        row += ref.shape[0]
+
+
+def pack(arrays):
+    shape = (sum(a.shape[0] for a in arrays), arrays[0].shape[1])
+    return call(pack_kernel, (1,), [whole(a.shape) for a in arrays], whole(shape), sds(shape, BF16))(*arrays)
+
+
+def ffn_kernel(parts, ow_row, slot, idx_ref, len_ref, weight_ref, gain_ref, x_h, cot_h, gu_h, dw_h, pb_h, ow_h, *refs):
     own = slot == 0
     att_h = refs[:parts]
-    pieces_h = refs[parts : parts + shares]
-    refs = refs[parts + shares :]
-    count = 5 if own else 4
+    refs = refs[parts:]
+    count = 6 if own else 5
     outs, scratch = refs[:count], refs[count:]
     x_v, cot_v, att_v, ow_v, gu_v, dw_v, pb_v, left_v, act_v, ffn_v, gn2_v, low_v, sem_in, sem_out = scratch
     rows, width = x_v.shape
@@ -257,23 +264,23 @@
         pending.append(copy)
 
     get_x = fetch(x_h.at[mine], x_v, 0)
-    get_ow = [fetch(pieces_h[x], ow_v.at[idx_ref[1] ^ x], 6 + parts + x) for x in range(shares)]
+    get_ow = fetch(ow_h.at[:, pl.ds(ow_row, ow_v.shape[1])], ow_v, 6 + parts)
     get_att = [fetch(att_h[d], att_v.at[d], 2 + d) for d in range(parts)]
     get_cot = fetch(cot_h.at[mine], cot_v, 2 + parts)
     get_gu = fetch(gu_h, gu_v, 3 + parts)
     get_dw = fetch(dw_h, dw_v, 4 + parts)
-    get_pb = fetch(pb_h, pb_v, 1)
+    get_pb = fetch(pb_h.at[:, pl.ds(0, pb_v.shape[1])], pb_v, 1)
 
     get_x.wait()
-    for copy in get_ow:
-        copy.wait()
+    get_ow.wait()
+    piece = ow_v.shape[1] // parts
     resid = x_v[...].astype(F32)
     for d in range(parts):
         get_att[d].wait()
-        resid = resid + dot(att_v[d], ow_v[:, d].reshape(local, width))
+        resid = resid + dot(att_v[d], ow_v[:, d * piece : (d + 1) * piece].reshape(local, width))
     if own:
         ffn_v[...] = resid
-        store(ffn_v, outs[4], 4)
+        store(ffn_v, outs[5], 4)
     normed = (resid * rms(resid) * gain_ref[1:2, :]).astype(BF16)
     left_v[0] = normed
     position = lax.broadcasted_iota(jnp.int32, (rows, 1), 0) + row0
@@ -295,7 +302,7 @@
         gate = dot(left_v[0], gate_w)
         upper = dot(left_v[0], up_w)
         grad_hidden = dot(left_v[1], down_w, NT if shard == 0 else NN)
-        sigma = jax.nn.sigmoid(gate)
+        sigma = 0.5 + 0.5 * jnp.tanh(0.5 * gate)
         act = gate * sigma
         hidden = (act * upper).astype(BF16)
         grad_up = (grad_hidden * act).astype(BF16)
@@ -303,6 +310,7 @@
         act_v[0, :, cols] = grad_gate
         act_v[1, :, cols] = grad_up
         act_v[2, :, cols] = hidden
+        store(act_v.at[:, :, cols], outs[1].at[:, :, cols], 1 + 4 * shard)
         grad = dot(grad_gate, gate_w, NT) + dot(grad_up, up_w, NT)
         term = dot(hidden, down_w, NN if shard == 0 else NT)
         if shard == 0:
@@ -314,94 +322,96 @@
             low_v[0] = (gn2_v[...] + grad).astype(BF16)
             store(low_v.at[0], outs[2], 2)
             low_v[1] = (ffn_v[...] + term).astype(BF16)
-            store(low_v.at[1], outs[3], 3)
-    store(act_v, outs[1], 1)
+            cut = outs[3].shape[0]
+            store(low_v.at[1, pl.ds(0, cut)], outs[3], 3)
+            store(low_v.at[1, pl.ds(cut, rows - cut)], outs[4], 6)
     for copy in pending:
         copy.wait()
 
 
 def feed_forward(slot, index, lengths, picked, atts, tokens, cotangent, out_full, gate_up, down, partner, gains):
     parts = len(atts)
-    shares = len(out_full)
     rows, local = atts[0].shape
     width = tokens.shape[1]
     hidden = gate_up.shape[2]
+    early = rows * 5 // 8
+    out_rows, ow_row = out_full
+    shares = partner.shape[0]
+    part = width // shares
     anywhere = pl.BlockSpec(memory_space=pl.ANY)
     out_shape = [
         sds((2, rows, width), BF16), sds((3, rows, 2 * hidden), BF16),
-        sds((rows, width), BF16), sds((rows, width), BF16),
+        sds((rows, width), BF16), sds((early, width), BF16), sds((rows - early, width), BF16),
     ]
     if slot == 0:
         out_shape.append(sds((rows, width), F32))
     return call(
-        functools.partial(ffn_kernel, parts, shares, slot),
+        functools.partial(ffn_kernel, parts, ow_row, slot),
         (1,),
-        [smem(), smem(), whole(gains.shape)] + [anywhere] * (5 + parts + shares),
+        [smem(), smem(), whole(gains.shape)] + [anywhere] * (6 + parts),
         [anywhere] * len(out_shape),
         out_shape,
         scratch=[
             pltpu.VMEM((rows, width), BF16),
             pltpu.VMEM((rows, width), BF16),
             pltpu.VMEM((parts, rows, local), BF16),
-            pltpu.VMEM((shares,) + out_full[0].shape, BF16),
+            pltpu.VMEM((shares, parts * local // shares, width), BF16),
             pltpu.VMEM(gate_up.shape, BF16),
             pltpu.VMEM(down.shape, BF16),
-            pltpu.VMEM(partner.shape, BF16),
+            pltpu.VMEM((shares, 3 * part, hidden), BF16),
             pltpu.VMEM((2, rows, width), BF16),
             pltpu.VMEM((3, rows, 2 * hidden), BF16),
             pltpu.VMEM((rows, width), F32),
             pltpu.VMEM((rows, width), F32),
             pltpu.VMEM((2, rows, width), BF16),
-            pltpu.SemaphoreType.DMA((6 + parts + shares,)),
-            pltpu.SemaphoreType.DMA((5,)),
+            pltpu.SemaphoreType.DMA((7 + parts,)),
+            pltpu.SemaphoreType.DMA((7,)),
         ],
-        flops=2 * rows * width * (width + 12 * hidden),
-        nbytes=rows * width * 30 + 12 * width * hidden,
-        trans=rows * hidden * 2,
         prefetch=1,
-    )(index, lengths, picked, gains, tokens, cotangent, gate_up, down, partner, *atts, *out_full)
-
-
-def ffn_grad_kernel(sets, split, extra, idx_ref, *refs):
+    )(index, lengths, picked, gains, tokens, cotangent, gate_up, down, partner, out_rows, *atts)
+
+
+def ffn_grad_kernel(sets, split, extra, cuts, idx_ref, *refs):
     left = refs[:sets]
     act = refs[sets : 2 * sets]
     refs = refs[2 * sets :]
+    count = 2 if extra else 0
+    op, folds, outs = refs[:count], refs[count : count + 2 * len(cuts)], refs[count + 2 * len(cuts) :]
+    if cuts:
+        fold_kernel(cuts, idx_ref, *folds, *outs[1:])
+        outs = outs[:1]
     step = pl.program_id(0)
 
-    def write(total, outs):
+    def write(total):
         part = outs[0].shape[-2]
-        for out in outs:
-            count = out.shape[0]
-            for j in range(count):
-                if len(outs) == 1:
-                    out[j] = total[j * part : (j + 1) * part, :].astype(BF16)
-        if len(outs) == 2:
-            for keep in range(2):
-                for bit in range(2):
-
-                    @pl.when((idx_ref[1] & 1) == bit)
-                    def _():
-                        for j in range(outs[0].shape[0]):
-                            d = 2 * j + (bit if keep else 1 - bit)
-                            outs[keep][j] = total[d * part : (d + 1) * part, :].astype(BF16)
-
-    outs = refs[2:] if extra else refs
+        if not split:
+            for j in range(outs[0].shape[0]):
+                outs[0][j] = total[j * part : (j + 1) * part, :].astype(BF16)
+            return
+        for keep in range(2):
+            for bit in range(2):
+
+                @pl.when((idx_ref[1] & 1) == bit)
+                def _():
+                    for j in range(outs[0].shape[0]):
+                        d = 2 * j + (bit if keep else 1 - bit)
+                        outs[keep][j] = total[d * part : (d + 1) * part, :].astype(BF16)
 
     @pl.when(step < 3)
     def _():
         total = dot(left[0][0], act[0][0], TN)
         for e in range(1, sets):
             total = total + dot(left[e][0], act[e][0], TN)
-        write(total, outs)
+        write(total)
 
     if extra:
 
         @pl.when(step >= 3)
         def _():
-            write(dot(refs[0][...], refs[1][...], TN), outs)
-
-
-def ffn_grads(index, lefts, acts, shard, shares, split, grad_low=None, att_own=None):
+            write(dot(op[0][...], op[1][...], TN))
+
+
+def ffn_grads(index, lefts, acts, shard, shares, split, grad_low=None, att_own=None, lanes=()):
     sets = len(lefts)
     _, rows, width = lefts[0].shape
     hidden = acts[0].shape[2] // 2
@@ -418,23 +428,38 @@
         ]
         args += [grad_low, att_own]
     count = shares // 2 if split else shares
-    out_spec = pl.BlockSpec((count, part, hidden), lambda c, idx: (0, c, 0))
-    out_shape = sds((count, steps * part, hidden), BF16)
     outs = 2 if split else 1
-    return call(
-        functools.partial(ffn_grad_kernel, sets, split, extra),
+    out_specs = [pl.BlockSpec((count, part, hidden), lambda c, idx: (0, c, 0))] * outs
+    out_shape = [sds((count, steps * part, hidden), BF16)] * outs
+    cuts, info = [], []
+    for n, (keep, got, lead, order) in enumerate(lanes):
+        size, lane_rows, cols = keep.shape
+        lane_rows //= len(lanes)
+        block = lane_rows // 4 if lane_rows % 64 == 0 else lane_rows
+        last = lane_rows // block - 1
+        at = functools.partial(lambda n, last, c, idx: (0, n * (last + 1) + jnp.minimum(c, last), 0), n, last)
+        here = functools.partial(lambda last, c, idx: (0, jnp.minimum(c, last), 0), last)
+        specs += [pl.BlockSpec((size, block, cols), at)] * 2
+        args += [keep, got]
+        bit = order[0]
+        cuts.append((len(lead) - 1 - lead.index(bit), bit))
+        info.append(([b for b in lead if b != bit], order[1:], bit))
+        out_specs += [pl.BlockSpec((size // 2, block, cols), here)] * 2
+        out_shape += [sds((size // 2, lane_rows, cols), BF16)] * 2
+    res = call(
+        functools.partial(ffn_grad_kernel, sets, split, extra, cuts),
         (steps,),
         specs,
-        [out_spec] * outs,
-        [out_shape] * outs,
-        flops=2 * sets * rows * width * hidden * steps,
-        nbytes=sets * rows * (2 * width + 3 * hidden) * 2 + steps * width * hidden * 2,
+        out_specs,
+        out_shape,
         prefetch=1,
     )(index, *args)
-
-
-def resid_kernel(parts, members, shares, idx_ref, len_ref, weight_ref, cot_ref, resid_ref, gain_ref, *refs):
-    pieces, refs, ow_ref = refs[:shares], refs[shares:-1], refs[-1]
+    if not lanes:
+        return res
+    return res[0], [(res[1 + 2 * n], res[2 + 2 * n]) + info[n] for n in range(len(lanes))]
+
+
+def resid_kernel(parts, members, idx_ref, len_ref, weight_ref, cot_ref, resid_ref, ow_ref, gain_ref, *refs):
     gn2_refs = refs[:members]
     att_refs = refs[members : members + parts]
     gr_ref, low_ref, cat_ref, sum_ref = refs[members + parts : members + parts + 4]
@@ -459,12 +484,12 @@
     @pl.when(step == 0)
     def _():
         sum_ref[...] = jnp.zeros_like(sum_ref)
-        for x in range(shares):
-            ow_ref[idx_ref[1] ^ x] = pieces[x][...]
 
     sum_ref[...] += jnp.sum((gn2 * unit).reshape(rows // 8, 8, width), axis=0)
     for d in range(parts):
-        g_refs[d][...] = dot(low, ow_ref[:, d].reshape(local, width), NT).astype(BF16)
+        piece = ow_ref.shape[1] // parts
+        block = ow_ref[:, d * piece : (d + 1) * piece].reshape(local, width)
+        g_refs[d][...] = dot(low, block, NT).astype(BF16)
         cat_ref[:, d * local : (d + 1) * local] = att_refs[d][...]
 
 
@@ -472,27 +497,27 @@
     share, width = resid.shape
     parts, members = len(atts), len(gn2s)
     local = atts[0].shape[1]
+    out_rows, ow_row = out_full
+    ow_rows = parts * local // out_rows.shape[0]
     steps = share // block
     row = lambda n: pl.BlockSpec((block, n), lambda i, idx: (i, 0))
     return call(
-        functools.partial(resid_kernel, parts, members, len(out_full)),
+        functools.partial(resid_kernel, parts, members),
         (steps,),
         [
             smem(), smem(),
             pl.BlockSpec((block, width), lambda i, idx: (idx[0] * steps + i, 0)),
-            row(width), whole(gains.shape),
+            row(width),
+            pl.BlockSpec((out_rows.shape[0], ow_rows, width), lambda *_: (0, ow_row // ow_rows, 0), pipeline_mode=pl.Buffered(1)),
+            whole(gains.shape),
         ]
-        + [whole(p.shape) for p in out_full]
         + [row(width)] * members
         + [row(local)] * parts,
         [row(width), row(width), row(parts * local), whole((8, width))] + [row(local)] * parts,
         [sds((share, width), F32), sds((share, width), BF16), sds((share, parts * local), BF16), sds((8, width), F32)]
         + [sds((share, local), BF16)] * parts,
-        scratch=[pltpu.VMEM((len(out_full),) + out_full[0].shape, BF16)],
-        flops=2 * share * width * width,
-        nbytes=share * width * 20,
         prefetch=1,
-    )(index, lengths, picked, cotangent, resid, gains, *out_full, *gn2s, *atts)
+    )(index, lengths, picked, cotangent, resid, out_rows, gains, *gn2s, *atts)
 
 
 def attend_back_kernel(parts, idx_ref, q_ref, k_ref, v_ref, att_ref, cos_ref, sin_ref, *refs):
@@ -507,6 +532,9 @@
     def table(ref, d):
         return ref[pl.ds(pl.multiple_of((me ^ d) * rows, rows), rows), :]
 
+    def columns(ref, d):
+        return ref[:, pl.ds(pl.multiple_of((me ^ d) * rows, rows), rows)].T
+
     def back(v, d, scale):
         return ((v * table(cos_ref, d) - swap_halves(v) * table(sin_ref, d)) * scale).astype(BF16)
 
@@ -520,7 +548,7 @@
         grad = jnp.where(step == d, grad_refs[d][...], grad)
     prod = grad.astype(F32) * att_ref[...].astype(F32)
     zero = jnp.zeros((rows, 128), BF16)
-    dqs = []
+    dqs, probs_all, scores_all, grads_own, queries_own = [], [], [], [], []
     for s in range(2):
         first = HD * (1 - s)
         own = (lane >= HD * s) & (lane < HD * (s + 1))
@@ -531,11 +559,15 @@
         grad_aug = jnp.where(lane == first + 1, mid, grad_aug)
         grad_aug = jnp.where(lane == first, hi, grad_aug)
         q = q_ref[s]
-        probs = jnp.exp2(dot(k_ref[s], q, NT))
-        scores_grad = (probs * dot(v_ref[s], grad_aug, NT)).astype(BF16)
-        dv_acc[...] += dot(probs.astype(BF16), grad_own)
-        dk_acc[...] += dot(scores_grad, jnp.where(own, q, zero))
-        dqs.append(dot(k_ref[s], scores_grad, TN).T)
+        probs = jnp.exp2(dot(q, k_ref[s], NT))
+        scores_grad = (probs * dot(grad_aug, v_ref[s], NT)).astype(BF16)
+        probs_all.append(probs.astype(BF16))
+        scores_all.append(scores_grad)
+        grads_own.append(grad_own)
+        queries_own.append(jnp.where(own, q, zero))
+        dqs.append(dot(scores_grad, k_ref[s]))
+    dv_acc[...] += dot(jnp.concatenate(grads_own, axis=0).T, jnp.concatenate(probs_all, axis=0))
+    dk_acc[...] += dot(jnp.concatenate(queries_own, axis=0).T, jnp.concatenate(scores_all, axis=0))
     dq = jnp.where(lane < HD, dqs[0], dqs[1])
     for d in range(parts):
 
@@ -546,8 +578,8 @@
     @pl.when(step == parts - 1)
     def _():
         for d in range(parts):
-            outs[d][1] = back(table(dk_acc, d), d, LN2)
-            outs[d][2] = table(dv_acc, d).astype(BF16)
+            outs[d][1] = back(columns(dk_acc, d), d, LN2)
+            outs[d][2] = columns(dv_acc, d).astype(BF16)
 
 
 def attend_back(index, grads, q, k, v, att, cosine, sine, pair):
@@ -559,17 +591,17 @@
         functools.partial(attend_back_kernel, parts),
         (parts,),
         [
-            pl.BlockSpec((2, share, 128), lambda i, idx: (0, idx[0] ^ i, 0)),
+            pl.BlockSpec((2, share, 128), lambda i, idx: (pair, idx[0] ^ i, 0)),
             keys,
             keys,
-            pl.BlockSpec((share, 128), lambda i, idx: (idx[0] ^ i, 0)),
+            pl.BlockSpec((share, 128), lambda i, idx: (idx[0] ^ i, pair)),
             whole(cosine.shape),
             whole(sine.shape),
         ]
         + [pl.BlockSpec((share, 128), lambda i, idx: (0, pair))] * parts,
         [whole((3, share, 128))] * parts,
         [sds((3, share, 128), BF16)] * parts,
-        scratch=[pltpu.VMEM((rows, 128), F32)] * 2,
+        scratch=[pltpu.VMEM((128, rows), F32)] * 2,
         flops=2 * rows * rows * 128 * 10,
         nbytes=rows * 256 * 16,
         trans=2 * rows * rows,
@@ -634,7 +666,8 @@
     )(index, tokens, qkv_weight, gains, *flat)
 
 
-def token_grad_kernel(parts, pairs, idx_ref, x_ref, gr_ref, w_ref, gain_ref, own_ref, got_ref, *refs):
+def token_grad_kernel(order, pairs, idx_ref, x_ref, gr_ref, w_ref, gain_ref, own_ref, got_ref, *refs):
+    parts = len(order)
     act_refs = refs[: parts * pairs]
     out_ref, gu_ref, down_ref = refs[parts * pairs :]
     width = x_ref.shape[1]
@@ -643,7 +676,7 @@
     for d in range(parts):
         for c in range(3):
             act = jnp.concatenate([act_refs[j * parts + d][c] for j in range(pairs)], axis=1)
-            grad = grad + dot(act, w_ref[:, d, c].reshape(width, local), NT)
+            grad = grad + dot(act, w_ref[:, order.index(d), c].reshape(width, local), NT)
     x = x_ref[...].astype(F32)
     factor = rms(x)
     out_ref[...] = gr_ref[...] + norm_back(grad, gain_ref[0:1, :], x * factor, factor)
@@ -657,14 +690,14 @@
         down_ref[...] = total[2 * part :].T
 
 
-def token_grad(index, tokens, grad_resid, qkv_full, gains, acts, ffn_own, ffn_got, block=256):
+def token_grad(index, tokens, grad_resid, qkv_full, order, gains, acts, ffn_own, ffn_got, block=256):
     share, width = grad_resid.shape
     pairs, parts = len(acts), len(acts[0])
+    part, hidden = ffn_got.shape[0] // 3, ffn_got.shape[1]
     flat = [a for group in acts for a in group]
     steps = share // block
-    part, hidden = ffn_got.shape[0] // 3, ffn_got.shape[1]
     return call(
-        functools.partial(token_grad_kernel, parts, pairs),
+        functools.partial(token_grad_kernel, order, pairs),
         (steps,),
         [
             pl.BlockSpec((block, width), lambda i, idx: (idx[0] * steps + i, 0)),
@@ -675,16 +708,56 @@
             whole(ffn_got.shape),
         ]
         + [pl.BlockSpec((3, block, 128), lambda i, idx: (0, i, 0))] * len(flat),
-        [
-            pl.BlockSpec((block, width), lambda i, idx: (i, 0)),
-            whole((2, part, hidden)),
-            whole((hidden, part)),
-        ],
+        [pl.BlockSpec((block, width), lambda i, idx: (i, 0)), whole((2, part, hidden)), whole((hidden, part))],
         [sds((share, width), F32), sds((2, part, hidden), F32), sds((hidden, part), F32)],
-        flops=2 * share * width * width * 3,
-        nbytes=share * width * 10 + 6 * width * width,
         prefetch=1,
     )(index, tokens, grad_resid, qkv_full, gains, ffn_own, ffn_got, *flat)
+
+
+def fold_kernel(cuts, idx_ref, *refs):
+    ins, outs = list(refs[: 2 * len(cuts)]), list(refs[2 * len(cuts) :])
+    row = 0
+    for at in cuts:
+        keep, got = ins.pop(0), ins.pop(0)
+        if at is None:
+            rows = keep.shape[1]
+            outs[0][row : row + rows, :] = (keep[0].astype(F32) + got[0].astype(F32)).astype(BF16)
+            row += rows
+            continue
+        place, bit = at
+        mine = (idx_ref[1] >> bit) & 1
+        targets = ((outs.pop(0), mine), (outs.pop(0), 1 - mine))
+        for j in range(keep.shape[0] // 2):
+            rest = ((j >> place) << (place + 1)) | (j & ((1 << place) - 1))
+            for out, value in targets:
+                k = rest | (value << place)
+                out[j] = (keep[k].astype(F32) + got[k].astype(F32)).astype(BF16)
+
+
+def fold(index, lanes, cut_rows=False):
+    cuts, specs, args, out_shape, info, total = [], [], [], [], [], 0
+    for n, (keep, got, lead, order) in enumerate(lanes):
+        count, rows, cols = keep.shape
+        rows = rows // len(lanes) if cut_rows else rows
+        at = functools.partial(lambda n, i, idx: (0, n, 0), n if cut_rows else 0)
+        specs += [pl.BlockSpec((count, rows, cols), at)] * 2
+        args += [keep, got]
+        total += rows
+        if order:
+            bit = order[0]
+            cuts.append((len(lead) - 1 - lead.index(bit), bit))
+            info.append(([b for b in lead if b != bit], order[1:], bit))
+            out_shape += [sds((count // 2, rows, cols), BF16)] * 2
+        else:
+            cuts.append(None)
+    if not info:
+        out_shape = [sds((total, cols), BF16)]
+    res = call(
+        functools.partial(fold_kernel, cuts), (1,), specs, [whole(o.shape) for o in out_shape], out_shape, prefetch=1
+    )(index, *args)
+    if not info:
+        return res[0]
+    return [(res[2 * n], res[2 * n + 1]) + info[n] for n in range(len(lanes))]
 
 
 def after(value, *others):
@@ -699,8 +772,7 @@
     local = out_weight.shape[0]
     hidden = down_weight.shape[0]
     parts = lax.axis_size("tensor")
-    members = parts // 2
-    slots = list(range(members - 1, -1, -1))
+    slots = list(range(parts - 2, -1, -2))
     shares = lax.axis_size("dp")
     part = width // shares
     me = lax.axis_index("tensor")
@@ -727,182 +799,151 @@
     def outgoing(pieces):
         return [(pieces[d], d, "tensor") for d in range(1, parts)]
 
-    def exchange(pieces):
-        return [swap(*send) for send in outgoing(pieces)]
-
-    def add(a, b):
-        return (a.astype(F32) + b.astype(F32)).astype(BF16)
-
     bits = shares.bit_length() - 1
-
-    def lanes_of(total):
-        half = total.shape[1] // 2
-        lead = list(range(bits - 1, 0, -1))
-        shape = (2,) * (bits - 1) + (half, total.shape[2])
-        return [
-            (total[:, h * half : (h + 1) * half].reshape(shape), lead, order)
-            for h, order in enumerate((lead, lead[::-1]))
-        ]
-
-    def halve(lanes, step):
-        out = []
-        for a, lead, order in lanes:
-            bit = order[step]
-            at = lead.index(bit)
-            mine = (dp >> bit) & 1
-            pick = lambda b: lax.dynamic_index_in_dim(a, b, at, keepdims=False)
-            out.append((pick(mine), pick(1 - mine), [b for b in lead if b != bit], order, bit))
-        return out
+    lead = list(range(bits - 1, 0, -1))
+
+    def fold_first(keep, got):
+        return fold(index, [(keep, got, lead, lead), (keep, got, lead, lead[::-1])], cut_rows=True)
+
+    def fold_next(halves, got):
+        return fold(index, [(keep, g, left, order) for (keep, _, left, order, _), g in zip(halves, got)])
 
     def leaving(halves):
         return [(away, 1 << bit, "dp") for _, away, _, _, bit in halves]
 
-    def merge(halves, got):
-        return [(add(keep, g), lead, order) for (keep, _, lead, order, _), g in zip(halves, got)]
-
-    def joined(lanes):
-        return jnp.concatenate([a for a, _, _ in lanes], axis=0)
-
     matches = species_ids[:, None] == jnp.arange(species_weight.shape[0])[None, :]
     picked = jnp.sum(jnp.where(matches, species_weight[None, :], F32(0.0)), axis=1)
 
     mine = cut_weights(index[1:], gate_up_weight, down_weight, shares)
     ow_cut = cut(out_weight, dp * (local // shares), local // shares)
-    qkv_cut = cut(qkv_weight, dp * part, part, 1)
-
-    def first():
-        projected = project(lengths, tokens, qkv_weight, norm_gains, cosine, sine)
-        return projected, attend(index, *projected, parts, 0)
-
-    (partner_cut,), ((q, k, v), heads) = beside([(mine, members, "tensor")], first)
-    partner = lax.all_gather(partner_cut, "dp", axis=0)
-    heads = [heads]
-
-    def second():
-        more = heads[:]
-        for j in range(1, pairs):
-            more.append(attend(index, q, k, v, parts, j, more[-1][:parts]))
-        return more[1:]
-
-    ow, more = beside(outgoing([after(ow_cut, partner_cut)] * parts), second)
-    heads += more
-    att = heads[-1][:parts]
-    att_nat = [h[parts] for h in heads]
-    q_back = [h[parts + 1] for h in heads]
+    qkv_cut = cut(qkv_weight, dp * part, part, 1).reshape(3 * part, local)
+    top = parts // 2
+
+    (partner_cut, *ow), (q, k, v) = beside(
+        [(mine, 1, "tensor")] + outgoing([ow_cut] * parts),
+        lambda: project(lengths, tokens, qkv_weight, norm_gains, cosine, sine),
+    )
+    if hidden == width:
+        partner = lax.all_gather(pack([partner_cut, ow_cut, *ow]), "dp", axis=0)
+        out_full = (partner, 3 * part)
+    else:
+        partner = lax.all_gather(partner_cut, "dp", axis=0)
+        out_full = (lax.all_gather(pack([ow_cut, *ow]), "dp", axis=0), 0)
+    (qkv_got,), (*att, att_nat, q_back) = beside(
+        [(after(qkv_cut, partner_cut), top, "tensor")], lambda: attend(index, q, k, v, parts)
+    )
+    qkv_stack, order = pack([qkv_cut, qkv_got]), [0, top]
     rows_for = lambda e: outgoing([att[d ^ e] for d in range(parts)])
-    ow = jnp.stack([ow_cut] + ow)
-
-    def third():
-        even = [ow] + [swap(ow, x, "dp") for x in range(2, shares, 2)]
-        return [p for a in even for p in (a, swap(a, 1, "dp"))][1:]
-
-    def third_all():
-        rows = [swap(*x) for x in rows_for(slots[0])]
-        return rows, third()
-
-    rows_now, ow_got = region(third_all)
-    out_full = [ow] + ow_got
-
-    lefts, acts, gn2s, terms, gn2_got, qkv_all = {}, {}, {}, {}, {}, {0: qkv_cut}
+    rows_now = region(lambda: [swap(*x) for x in rows_for(slots[0])])
+
+    lefts, acts, gn2s, terms, gn2_got = {}, {}, {}, {}, {}
     tied = tokens
     for e in slots:
 
         def feed():
-            return feed_forward(
+            outs = feed_forward(
                 e, index, lengths, picked, [att[e]] + rows_now, tied, cotangent, out_full,
                 gate_up_weight, down_weight, partner, norm_gains
             )
-
-        later = rows_for(e - 1) if e else []
-        sums = [(gn2s[e + 1], e + 1, "tensor")] if e + 1 in gn2s else []
-        sent = [d for d in range(1, parts) if (d == 1) == (e == slots[0])] if e in (slots[0], 0) else []
-        got, outs = beside(later + sums + [(qkv_cut, d, "tensor") for d in sent], feed)
-        later, got = got[: len(later)], got[len(later) :]
-        if sums:
-            gn2_got[e + 1] = got.pop(0)
-        qkv_all.update(zip(sent, got))
+            if e:
+                return outs
+            away_b, keep_b = ffn_grads(
+                index, [*lefts.values(), outs[0]], [*acts.values(), outs[1]], 1, shares, True
+            )
+            return outs, keep_b, away_b
+
+        sends = rows_for(e - 2) if e else []
+        if e + 2 in gn2s:
+            sends.append((gn2s[e + 2], e + 2, "tensor"))
+        if len(order) < parts:
+            bit = parts // (2 * len(order))
+            sends.append((qkv_stack, bit, "tensor"))
+        got, outs = beside(sends, feed)
+        if len(order) < parts:
+            qkv_stack, order = pack([qkv_stack, got.pop()]), order + [d ^ bit for d in order]
+            if len(order) == parts:
+                qkv_stack = qkv_stack.reshape(parts, 3, part, local)
+                qkv_full = lax.all_gather(qkv_stack, "dp", axis=0)
+        if e + 2 in gn2s:
+            gn2_got[e + 2] = got.pop()
         if e:
-            rows_now = later
-        lefts[e], acts[e], gn2s[e], terms[e] = outs[:4]
+            rows_now = got
+        else:
+            outs, keep_b, away_b = outs
+        lefts[e], acts[e], gn2s[e], *terms[e] = outs[:5]
         tied = after(tokens, gn2s[e])
-    resid = outs[4]
-    qkv_full = lax.all_gather(jnp.stack([qkv_all[d] for d in range(parts)]), "dp", axis=0)
-    gn2_all = [gn2s[0]] + [gn2_got[e] for e in range(1, members)]
-    grad_resid, grad_low, att_own, gain_two, *grads = resid_back(
-        index, lengths, picked, cotangent, resid, gn2_all, out_full, norm_gains, [att[0]] + rows_now
+    resid = outs[5]
+    gn2_all = [gn2s[0]] + [gn2_got[e] for e in slots[:-1]]
+    (got_b,), (grad_resid, grad_low, att_own, gain_two, *grads) = beside(
+        [(away_b, 1, "dp")],
+        lambda: resid_back(
+            index, lengths, picked, cotangent, resid, gn2_all, out_full, norm_gains, [att[0]] + rows_now
+        ),
     )
     lefts, acts = [lefts[e] for e in slots], [acts[e] for e in slots]
-
-    near, (away_b, keep_b) = beside(
-        [(grads[d], d, "tensor") for d in range(1, parts - 1)],
-        lambda: ffn_grads(index, lefts, acts, 1, shares, True),
-    )
-    (far, got_b), (wg_a,) = beside(
-        [(grads[parts - 1], parts - 1, "tensor"), (away_b, 1, "dp")],
-        lambda: ffn_grads(index, lefts, acts, 0, shares, False, grad_low, att_own),
-    )
+    start = [(keep_b, got_b, lead, lead), (keep_b, got_b, lead, lead[::-1])]
+    ways = []
+
+    def grads_own():
+        wg_a, halves = ffn_grads(index, lefts, acts, 0, shares, False, grad_low, att_own, start)
+        ways[:] = [h[2:] for h in halves]
+        return wg_a, [h[:2] for h in halves]
+
+    got, (wg_a, halves) = beside(outgoing(grads), grads_own)
+    halves = [tuple(h) + way for h, way in zip(halves, ways)]
+    grads_all = [grads[0]] + got
     sum_a = lax.psum_scatter(after(wg_a, qkv_full), "dp", scatter_dimension=0, tiled=True)[0]
-    grads_all = [grads[0], *near, far]
-    halves = halve(lanes_of(add(keep_b, got_b)), 0)
+    step = 0
 
     def back(j):
-        return attend_back(index, grads_all, q_back[j], k, v, att_nat[j], cosine, sine, j)
-
-    terms_out = [(terms[e], e, "tensor") for e in range(1, members)]
-    got, group = beside(terms_out + leaving(halves), lambda: back(0))
-    others, got = got[: len(terms_out)], got[len(terms_out) :]
-    lanes = merge(halves, got)
-    step = 1
+        return attend_back(index, grads_all, q_back, k, v, att_nat, cosine, sine, j)
+
+    def terms_out(i):
+        return [(terms[e][i], e, "tensor") for e in slots[:-1]]
+
+    got, group = beside(terms_out(0) + leaving(halves), lambda: back(0))
+    first_terms, got = got[: len(slots) - 1], got[len(slots) - 1 :]
+    halves, step = fold_next(halves, got), step + 1
     qkv_acts, acts_got = [group], []
     for j in range(1, pairs):
-        halves = halve(lanes, step)
-
-        got, group = beside(outgoing(group) + leaving(halves), lambda: back(j))
-        group_got, got = got[: parts - 1], got[parts - 1 :]
-        acts_got.append([qkv_acts[-1][0]] + group_got)
+        now = leaving(halves) if step < bits - 1 else []
+        got, group = beside(outgoing(group) + now, lambda: back(j))
+        acts_got.append([qkv_acts[-1][0]] + got[: parts - 1])
         qkv_acts.append(group)
-        lanes = merge(halves, got)
-        step += 1
-
-    b_lanes = lanes
-    for s in range(step, bits - 1):
-        h = halve(b_lanes, s)
-        b_lanes = merge(h, [swap(*x) for x in leaving(h)])
-    sum_b = joined(b_lanes)
+        if now:
+            halves, step = fold_next(halves, got[parts - 1 :]), step + 1
+    while step < bits - 1:
+        halves, step = fold_next(halves, [swap(*x) for x in leaving(halves)]), step + 1
+    sum_b = halves
 
     def finish():
         away_q, keep_q, gain_one = project_grads(index, tokens, qkv_acts, qkv_weight, norm_gains, shares)
-        total = add(keep_q, swap(away_q, 1, "dp"))
-        one, two = lanes_of(total)
-        for s in range(bits - 1):
-            (h1,), (h2,) = halve([one], s), halve([two], s)
-            g1 = swap(*leaving([h1])[0])
-            g2 = swap(after(leaving([h2])[0][0], g1), 1 << h2[4], "dp")
-            one, two = merge([h1, h2], [g1, g2])
-        qkv_sum = joined([one, two]).astype(F32)
-        grad_qkv = jnp.stack([qkv_sum[:, c * local : (c + 1) * local] for c in range(3)])
-        gains_grad = after(jnp.stack([gain_one[:, 0] / norm_gains[0], jnp.sum(gain_two, axis=0)]), g2)
+        halves = fold(index, [(keep_q, swap(away_q, 1, "dp"), lead, lead)])
+        for s in range(bits - 2):
+            halves = fold_next(halves, [swap(*x) for x in leaving(halves)])
+        gains_grad = jnp.stack([gain_one[:, 0] / norm_gains[0], jnp.sum(gain_two, axis=0)])
+        gains_grad = after(gains_grad, *[h[0] for h in halves])
         for s in range(bits):
             gains_grad = gains_grad + swap(gains_grad, 1 << s, "dp")
-        out = resid + terms[0].astype(F32)
-        for term in others:
-            out = out + term.astype(F32)
-        return grad_qkv, gains_grad, out
-
-    got, (grad_qkv, gains_grad, out) = beside(
-        outgoing(group) + [(sum_b, members, "tensor")], finish, apart=True
-    )
-    *last, got_b = got
-    acts_got.append([group[0]] + last)
+        ways[:] = [h[2:] for h in halves]
+        return [h[:2] for h in halves], gains_grad
+
+    got, (halves, gains_grad) = beside(outgoing(group) + [(sum_b, 1, "tensor")], finish, apart=True)
+    halves = [tuple(h) + way for h, way in zip(halves, ways)]
+    acts_got.append([group[0]] + got[: parts - 1])
+    got_b = got[-1]
     op_sum = jnp.concatenate(
         [sum_a[(3 + c) * part : (4 + c) * part] for c in range(parts * local // hidden)], axis=1
     )
     gains_low = jnp.concatenate([a.reshape(-1, local) for a in split3(gains_grad)])
     pieces = [jnp.concatenate([op_sum[:, d * local : (d + 1) * local], gains_low]) for d in range(parts)]
     got, (grad_tok, grad_gu, grad_down) = beside(
-        outgoing(pieces),
-        lambda: token_grad(index, tokens, grad_resid, qkv_full, norm_gains, acts_got, sum_a, got_b),
+        leaving(halves) + terms_out(1) + outgoing(pieces),
+        lambda: token_grad(index, tokens, grad_resid, qkv_full, order, norm_gains, acts_got, sum_a, got_b),
     )
+    qkv_sum = fold_next(halves, got[:1]).astype(F32)
+    grad_qkv = jnp.stack([qkv_sum[:, c * local : (c + 1) * local] for c in range(3)])
+    second_terms, got = got[1 : len(slots)], got[len(slots) :]
     got = jnp.stack([pieces[0]] + got).astype(F32)
     grad_op = jnp.sum(got[:, :part], axis=0).T
     gains_all = got[:, part:].reshape(parts, 3, 2, width)
@@ -910,6 +951,11 @@
     gains_grad = jnp.zeros_like(gains_all[0])
     for z in range(parts):
         gains_grad = gains_grad + lax.dynamic_index_in_dim(gains_all, me ^ z, 0, keepdims=False)
+    ffn_rows = [
+        sum((t.astype(F32) for t in got), own.astype(F32))
+        for own, got in zip(terms[0], (first_terms, second_terms))
+    ]
+    out = resid + jnp.concatenate(ffn_rows)
     return (out, grad_tok, grad_qkv, grad_op, grad_gu, grad_down, gains_grad)
 
 

time: 408 us -> 382 us (0.936)
  starting transfers between devices: 70.8 us -> 60.7 us
  Pallas kernels: 201 us -> 211 us
  other arithmetic: 22.8 us -> 13.3 us
  loops' own time: 10.6 us -> 1.54 us
  waiting for transfers between devices: 75.9 us -> 69.5 us
    pallas_call x8 -> x15, Pallas kernels: 124 us -> 138 us  [the longest x2 42.6 us: feed_forward(): call(functools.partial(ffn_kernel, parts, ow_row, slot), (1,), [smem(), s...]
    ppermute x48 -> x39, starting transfers between devices: 70.5 us -> 60.6 us  [swap(): lax.ppermute(a, name, [(i, i ^ d) for i in range(lax.axis_size(name))])]
    convert_element_type x10 -> x1, other arithmetic: 10.9 us -> 0.95 us  [body(): qkv_sum = fold_next(halves, got[:1]).astype(F32)]
    another operation x12, loops' own time: 10.6 us -> 1.54 us  [region(): return lax.optimization_barrier(lax.cond(valid, f, zeros))]
    all_gather x2, waiting for transfers between devices: 8.04 us -> 0.01 us  [the longest x1 0.01 us: body(): partner = lax.all_gather(pack([partner_cut, ow_cut, *ow]), 'dp', axis=0)]
    pallas_call x2, Pallas kernels: 54.2 us -> 49.5 us  [attend_back(): call(functools.partial(attend_back_kernel, parts), (parts,), [pl.BlockSpe...]
    ppermute x48 -> x39, waiting for transfers between devices: 67.8 us -> 69.5 us  [swap(): lax.ppermute(a, name, [(i, i ^ d) for i in range(lax.axis_size(name))])]
  transfers between devices with their start and end apart: 51 -> 42, of which waited for: 18 -> 13; matrix products, arithmetic and copies ran while one was open for 6% -> 2% of each run, Pallas kernels for 49% -> 54%
where the time goes in v5:
time: 382 us; the launch traced here: 375 us
  Pallas kernels  211 us (55%)
  waiting for transfers between devices  69.5 us (18%)
  starting transfers between devices  60.7 us (16%)
  between operations  15.6 us (4%)
  other arithmetic  13.3 us (3%)
    ppermute x39, waiting for transfers between devices, swap(): lax.ppermute(a, name, [(i, i ^ d) for i in range(lax.axis_size(name))])  69.5 us
    ppermute x39, starting transfers between devices, swap(): lax.ppermute(a, name, [(i, i ^ d) for i in range(lax.axis_size(name))])  60.6 us
    pallas_call x2, Pallas kernels, attend_back(): call(functools.partial(attend_back_kernel, parts), (parts,), [pl.BlockSpe...  49.5 us
    pallas_call x2, Pallas kernels, feed_forward(): call(functools.partial(ffn_kernel, parts, ow_row, slot), (1,), [smem(), s...  42.6 us
    pallas_call x1, Pallas kernels, attend(): call(functools.partial(attend_kernel, min(sub, share), parts), (heads //...  29.1 us
    pallas_call x2, Pallas kernels, ffn_grads(): call(functools.partial(ffn_grad_kernel, sets, split, extra, cuts), (steps...  28.9 us
    pallas_call x5, Pallas kernels, fold(): call(functools.partial(fold_kernel, cuts), (1,), specs, [whole(o.shape) f...  14 us
    pallas_call x1, Pallas kernels, project_grads(): call(functools.partial(project_grad_kernel, parts, pairs), (parts,), [pl....  11.2 us
  transfers between devices with their start and end apart: 42, of which 13 were waited for; matrix products, arithmetic and copies ran while one was open for 2% of the time, Pallas kernels for 54%

profile of v5, /device:TPU:0, one launch (start us, length us, event | category | flops | bytes accessed | tf_op | source)
XLA Modules:
  0.0 374.8 jit_solution(8046677088517251274)
XLA Ops:
  10.5 27.4 %conditional.12 = (bf16[384,1024]{1,0:T(8,128)(2,1)}, bf16[32,1024]{1,0:T(8,128)(2,1)}, bf16[32,1024]{1,0:T(8,128)(2,1)}, bf16[32,1024]{1,0:T(8,128)(2,1)}, bf16...) conditional(s32[]{:T(128)} %convert_element_type.49, () %tuple.111, ...), branch_computations={%region_0.1_spmd, %region_1.2_spmd} | conditional | bytes 7274566 | solution.py:788
  10.6 3.1 collective-permute-start
  13.7 3.0 collective-permute-start.2
  18.0 9.2 %branch_1_fun.13 = (bf16[4,2048,128]{2,1,0:T(8,128)(2,1)}, bf16[4,2048,128]{2,1,0:T(8,128)(2,1)}, bf16[4,2048,128]{2,1,0:T(8,128)(2,1)}) custom-call(s32[1]{0:T(128)} %get-tuple-element.306.len_ref, bf16[2048,1024]{1,0:T(8,128)(2,1)} %get-tuple-element.307.x_ref, bf16[3,1024,256]{2,1,0:T(8,128)(2,1)S(1)} %get-tuple-element.308.w_ref, ...), custom_call_target="tpu_custom_call" | custom-call | tf_op jit(solution)/shard_map/cond/branch_1_fun/pallas_call | solution.py:134
  27.2 7.1 %collective-permute-done.1 = bf16[32,1024]{1,0:T(8,128)(2,1)} collective-permute-done((bf16[32,1024]{1,0:T(8,128)(2,1)S(1)}, bf16[32,1024]{1,0:T(8,128)(2,1)}, u32[]{:S(2)}, u32[]{:S(2)}) %collective-permute-start.1) | collective-permute-done | bytes 65568 | tf_op jit(solution)/shard_map/cond/branch_1_fun/ppermute | solution.py:794
  34.3 3.6 collective-permute-done.3
  40.3 29.2 %conditional.13 = (bf16[384,256]{1,0:T(8,128)(2,1)}, bf16[512,256]{1,0:T(8,128)(2,1)S(1)}, bf16[512,256]{1,0:T(8,128)(2,1)S(1)}, bf16[512,256]{1,0:T(8,128)(2,1)...) conditional(s32[]{:T(128)} %convert_element_type.49, () %tuple.110, ...), branch_computations={%region_2.3_spmd, %region_3.4_spmd} | conditional | bytes 4390982 | solution.py:788
  40.4 29.1 %branch_1_fun.14 = (bf16[512,256]{1,0:T(8,128)(2,1)S(1)}, bf16[512,256]{1,0:T(8,128)(2,1)S(1)}, bf16[512,256]{1,0:T(8,128)(2,1)S(1)}, bf16[512,256]{1,0:T(8,128)...) custom-call(s32[2]{0:T(128)S(1)} %get-tuple-element.316.idx_ref, ...), custom_call_target="tpu_custom_call" | custom-call | tf_op jit(solution)/shard_map/cond/branch_1_fun/pallas_call | solution.py:184
  69.5 23.4 %conditional.14 = (bf16[512,256]{1,0:T(8,128)(2,1)}, bf16[512,256]{1,0:T(8,128)(2,1)}, bf16[512,256]{1,0:T(8,128)(2,1)}) conditional(s32[]{:T(128)} %convert_element_type.49, () %tuple.115, (bf16[512,256]{1,0:T(8,128)(2,1)}, bf16[512,256]{1,0:T(8,128)(2,1)S(1)}, bf16[512,256]{1,0:T(8,128)(2,1)S(1)}) %tuple.116), branch_computations={%region_5.6_spmd, %region_6.7_spmd} | conditional | bytes 3145872 | solution.py:788
  74.1 6.5 %collective-permute-done.5 = bf16[512,256]{1,0:T(8,128)(2,1)} collective-permute-done((bf16[512,256]{1,0:T(8,128)(2,1)}, bf16[512,256]{1,0:T(8,128)(2,1)}, u32[]{:S(2)}, u32[]{:S(2)}) %collective-permute-start.5) | collective-permute-done | bytes 262176 | tf_op jit(solution)/shard_map/cond/branch_1_fun/ppermute | solution.py:794
  80.7 12.2 %collective-permute-done.6 = bf16[512,256]{1,0:T(8,128)(2,1)} collective-permute-done((bf16[512,256]{1,0:T(8,128)(2,1)S(1)}, bf16[512,256]{1,0:T(8,128)(2,1)}, u32[]{:S(2)}, u32[]{:S(2)}) %collective-permute-start.6) | collective-permute-done | bytes 262176 | tf_op jit(solution)/shard_map/cond/branch_1_fun/ppermute | solution.py:794
  95.1 28.2 %conditional.15 = (bf16[512,256]{1,0:T(8,128)(2,1)}, bf16[512,256]{1,0:T(8,128)(2,1)}, bf16[512,256]{1,0:T(8,128)(2,1)}, bf16[768,256]{1,0:T(8,128)(2,1)}, bf16[...) conditional(s32[]{:T(128)} %convert_element_type.49, () %tuple.109, ...), branch_computations={%region_7.8_spmd, %region_8.9_spmd} | conditional | bytes 11665498 | solution.py:788
  95.1 3.4 collective-permute-start.11
  102.0 21.1 %branch_1_fun.15 = (bf16[2,512,1024]{2,1,0:T(8,128)(2,1)}, bf16[3,512,2048]{2,1,0:T(8,128)(2,1)}, bf16[512,1024]{1,0:T(8,128)(2,1)}, bf16[320,1024]{1,0:T(8,128)(2,1)}, bf16[192,1024]{1,0:T(8,128)(2,1)}) custom-call(s32[2]{0:T(128)S(1)} %get-tuple-element.333.idx_ref, s32[1]{0:T(128)} %get-tuple-element.334.len_ref, f32[1]{0:T(128)} %get-tuple-element.335.weight_ref, ...), custom_call_target="tpu_custom_call" | custom-call | tf_op jit(solution)/shard_map/cond/branch_1_fun/pallas_call | solution.py:348
  125.3 46.0 %conditional.16 = (bf16[512,1024]{1,0:T(8,128)(2,1)}, bf16[2,512,1024]{2,1,0:T(8,128)(2,1)}, bf16[3,512,2048]{2,1,0:T(8,128)(2,1)}, bf16[512,1024]{1,0:T(8,128)(...) conditional(s32[]{:T(128)} %convert_element_type.49, () %tuple.108, ...), branch_computations={%region_9.10_spmd, %region_10.11_spmd} | conditional | bytes 19923036 | solution.py:788
  127.6 21.5 %branch_1_fun.16 = (bf16[2,512,1024]{2,1,0:T(8,128)(2,1)}, bf16[3,512,2048]{2,1,0:T(8,128)(2,1)}, bf16[512,1024]{1,0:T(8,128)(2,1)}, bf16[320,1024]{1,0:T(8,128)...) custom-call(s32[2]{0:T(128)S(1)} %get-tuple-element.351.idx_ref, s32[1]{0:T(128)} %get-tuple-element.352.len_ref, ...), custom_call_target="tpu_custom_call" | custom-call | tf_op jit(solution)/shard_map/cond/branch_1_fun/pallas_call | solution.py:348
  149.1 13.1 %branch_1_fun.17 = (bf16[4,384,1024]{2,1,0:T(8,128)(2,1)}, bf16[4,384,1024]{2,1,0:T(8,128)(2,1)}) custom-call(s32[2]{0:T(128)S(1)} %get-tuple-element.351.idx_ref, bf16[2,512,1024]{2,1,0:T(8,128)(2,1)} %get-tuple-element.370.refs_0_, bf16[2,512,1024]{2,1,0:T(8,128)(2,1)} %get-tuple-element.789.refs_1_, bf16[3,512,2048]{2,1,0:T(8,128)(2,1)} %get-tuple-element.371.refs_2_, ...), custom_call_target="tpu_custom_call" | custom-call | tf_op jit(solution)/shard_map/cond/branch_1_fun/pallas_call | solution.py:449
  162.3 8.7 %collective-permute-done.12 = bf16[512,1024]{1,0:T(8,128)(2,1)} collective-permute-done((bf16[512,1024]{1,0:T(8,128)(2,1)}, bf16[512,1024]{1,0:T(8,128)(2,1)}, u32[]{:S(2)}, u32[]{:S(2)}) %collective-permute-start.12) | collective-permute-done | bytes 1048608 | tf_op jit(solution)/shard_map/cond/branch_1_fun/ppermute | solution.py:794
  171.3 8.5 %conditional.17 = (bf16[4,384,1024]{2,1,0:T(8,128)(2,1)}, f32[512,1024]{1,0:T(8,128)S(1)}, bf16[512,1024]{1,0:T(8,128)(2,1)}, bf16[512,1024]{1,0:T(8,128)(2,1)},...) conditional(s32[]{:T(128)} %convert_element_type.49, () %tuple.122, ...), branch_computations={%region_11.12_spmd, %region_12.13_spmd} | conditional | bytes 12583024 | solution.py:788
  171.4 8.3 %branch_1_fun.18 = (f32[512,1024]{1,0:T(8,128)S(1)}, bf16[512,1024]{1,0:T(8,128)(2,1)}, bf16[512,1024]{1,0:T(8,128)(2,1)}, f32[8,1024]{1,0:T(8,128)S(1)}, bf16[5...) custom-call(s32[2]{0:T(128)S(1)} %get-tuple-element.375.idx_ref, ...), custom_call_target="tpu_custom_call" | custom-call | tf_op jit(solution)/shard_map/cond/branch_1_fun/pallas_call | solution.py:504
  179.8 22.7 %conditional.18 = (bf16[512,256]{1,0:T(8,128)(2,1)}, bf16[512,256]{1,0:T(8,128)(2,1)}, bf16[512,256]{1,0:T(8,128)(2,1)}, bf16[8,512,1024]{2,1,0:T(8,128)(2,1)}, ...) conditional(s32[]{:T(128)} %convert_element_type.49, () %tuple.121, ...), branch_computations={%region_13.14_spmd, %region_14.15_spmd} | conditional | bytes 12320848 | solution.py:788
  180.6 3.4 collective-permute-start.15
  184.3 15.8 %branch_1_fun.19 = (bf16[8,512,1024]{2,1,0:T(8,128)(2,1)}, bf16[2,192,1024]{2,1,0:T(8,128)(2,1)S(1)}, bf16[2,192,1024]{2,1,0:T(8,128)(2,1)}, bf16[2,192,1024]{2,1,0:T(8,128)(2,1)}, bf16[2,192,1024]{2,1,0:T(8,128)(2,1)}) custom-call(s32[2]{0:T(128)S(1)} %get-tuple-element.399.idx_ref, bf16[2,512,1024]{2,1,0:T(8,128)(2,1)} %get-tuple-element.400.refs_0_, ...), custom_call_target="tpu_custom_call" | custom-call | tf_op jit(solution)/shard_map/cond/branch_1_fun/pallas_call | solution.py:449
  200.1 2.4 collective-permute-done.15
  202.5 37.6 %conditional.19 = (bf16[320,1024]{1,0:T(8,128)(2,1)}, bf16[2,192,1024]{2,1,0:T(8,128)(2,1)}, bf16[2,192,1024]{2,1,0:T(8,128)(2,1)}, bf16[3,512,128]{2,1,0:T(8,12...) conditional(s32[]{:T(128)} %convert_element_type.49, () %tuple.120, ...), branch_computations={%region_15.16_spmd, %region_16.17_spmd} | conditional | flops 10737418240 | bytes 17301680 | solution.py:788
  204.9 6.7 %collective-permute-start.17 = (bf16[320,1024]{1,0:T(8,128)(2,1)}, bf16[320,1024]{1,0:T(8,128)(2,1)}, u32[]{:S(2)}, u32[]{:S(2)}) collective-permute-start(bf16[320,1024]{1,0:T(8,128)(2,1)} %get-tuple-element.413), channel_id=1, source_target_pairs={{0,2},{1,3},{2,0},{3,1},{4,6},{5,7},{6,4},{7,5},{8,10},{9,11},{10,... | collective-permute-start | bytes 1966088 | tf_op jit(solution)/shard_map/cond/branch_1_fun/ppermute | solution.py:794
  211.7 25.1 %branch_1_fun.20 = (bf16[3,512,128]{2,1,0:T(8,128)(2,1)}, bf16[3,512,128]{2,1,0:T(8,128)(2,1)}, bf16[3,512,128]{2,1,0:T(8,128)(2,1)}, bf16[3,512,128]{2,1,0:T(8,128)(2,1)}) custom-call(s32[2]{0:T(128)S(1)} %get-tuple-element.416.idx_ref, bf16[4,2048,128]{2,1,0:T(8,128)(2,1)} %get-tuple-element.417.q_ref, bf16[4,2048,128]{2,1,0:T(8,128)(2,1)} %get-tuple-element.418.k_ref, ...), custom_call_target="tpu_custom_call" | custom-call | flops 10737418240 | bytes 8388608 | tf_op jit(solution)/shard_map/cond/branch_1_fun/pallas_call | solution.py:590
  236.7 3.3 collective-permute-done.17
  240.1 3.4 shard_map.174
  243.4 31.1 %conditional.20 = (bf16[3,512,128]{2,1,0:T(8,128)(2,1)}, bf16[3,512,128]{2,1,0:T(8,128)(2,1)}, bf16[3,512,128]{2,1,0:T(8,128)(2,1)}, bf16[1,192,1024]{2,1,0:T(8,...) conditional(s32[]{:T(128)} %convert_element_type.49, () %tuple.128, ...), branch_computations={%region_17.18_spmd, %region_18.19_spmd} | conditional | flops 10737418240 | bytes 17301804 | solution.py:788
  245.6 2.5 collective-permute-start.22
  250.1 24.5 %branch_1_fun.21 = (bf16[3,512,128]{2,1,0:T(8,128)(2,1)S(1)}, bf16[3,512,128]{2,1,0:T(8,128)(2,1)}, bf16[3,512,128]{2,1,0:T(8,128)(2,1)}, bf16[3,512,128]{2,1,0:T(8,128)(2,1)}) custom-call(s32[2]{0:T(128)S(1)} %get-tuple-element.436.idx_ref, bf16[4,2048,128]{2,1,0:T(8,128)(2,1)} %get-tuple-element.437.q_ref, bf16[4,2048,128]{2,1,0:T(8,128)(2,1)} %get-tuple-element.438.k_ref, ...), custom_call_target="tpu_custom_call" | custom-call | flops 10737418240 | bytes 8388608 | tf_op jit(solution)/shard_map/cond/branch_1_fun/pallas_call | solution.py:590
  274.6 3.0 shard_map.175
  277.5 50.9 %conditional.21 = (bf16[3,512,128]{2,1,0:T(8,128)(2,1)}, bf16[3,512,128]{2,1,0:T(8,128)(2,1)}, bf16[3,512,128]{2,1,0:T(8,128)(2,1)}, bf16[384,1024]{1,0:T(8,128)...) conditional(s32[]{:T(128)} %convert_element_type.49, () %tuple.127, ...), branch_computations={%region_19.20_spmd, %region_20.24_spmd} | conditional | flops 3221241856 | bytes 23314984 | solution.py:788
  277.5 6.4 %collective-permute-start.38 = (bf16[384,1024]{1,0:T(8,128)(2,1)}, bf16[384,1024]{1,0:T(8,128)(2,1)}, u32[]{:S(2)}, u32[]{:S(2)}) collective-permute-start(bf16[384,1024]{1,0:T(8,128)(2,1)} %get-tuple-element.475), channel_id=1, source_target_pairs={{0,1},{1,0},{2,3},{3,2},{4,5},{5,4},{6,7},{7,6},{8,9},{9,8},{10,11... | collective-permute-start | bytes 2359304 | tf_op jit(solution)/shard_map/cond/branch_1_fun/ppermute | solution.py:794
  286.0 2.4 collective-permute-start.37
  288.3 39.8 %conditional = (bf16[1,128,768]{2,1,0:T(8,128)(2,1)}, bf16[1,128,768]{2,1,0:T(8,128)(2,1)}, f32[2,1024]{1,0:T(2,128)}) conditional(s32[]{:T(128)} %convert_element_type.2, () %tuple.76, (s32[2]{0:T(128)S(1)}, bf16[2048,1024]{1,0:T(8,128)(2,1)}, bf16[3,1024,256]{2,1,0:T(8,128)(2,1)}, f32[2,1024]{1,0:T(2,128)S(1)}, bf16[3,512,128]{2,1,0:T(8,128)(2,1)}, ...), branch_computations={%region_21.21_spmd, %region_22.0_spmd} | conditional | flops 3221241856 | bytes 15450340 | solution.py:788
  288.3 11.2 %branch_1_fun.22 = (bf16[4,128,768]{2,1,0:T(8,128)(2,1)}, bf16[4,128,768]{2,1,0:T(8,128)(2,1)}, f32[1024,128]{1,0:T(8,128)}) custom-call(s32[2]{0:T(128)S(1)} %get-tuple-element.451.idx_ref, bf16[2048,1024]{1,0:T(8,128)(2,1)} %get-tuple-element.452.x_ref, bf16[3,1024,256]{2,1,0:T(8,128)(2,1)} %get-tuple-element.453.w_ref, ...), custom_call_target="tpu_custom_call" | custom-call | flops 3221225472 | bytes 10485760 | tf_op jit(solution)/shard_map/cond/branch_1_fun/cond/branch_1_fun/pallas_call | solution.py:651
  299.6 2.6 collective-permute-done.30.refs_1_
  302.2 2.9 branch_1_fun.23
  307.8 8.8 %collective-permute-done.31.refs_1_ = bf16[2,128,768]{2,1,0:T(8,128)(2,1)} collective-permute-done((bf16[2,128,768]{2,1,0:T(8,128)(2,1)}, bf16[2,128,768]{2,1,0:T(8,128)(2,1)}, u32[]{:S(2)}, u32[]{:S(2)}) %collective-permute-start.31) | collective-permute-done | bytes 393248 | tf_op jit(solution)/shard_map/cond/branch_1_fun/cond/branch_1_fun/ppermute | solution.py:794
  316.6 2.4 branch_1_fun.24
  320.9 3.0 collective-permute-done.33
  329.3 2.4 convert_add_fusion
  332.7 23.3 %conditional.22 = (bf16[1,128,768]{2,1,0:T(8,128)(2,1)}, bf16[192,1024]{1,0:T(8,128)(2,1)}, bf16[152,256]{1,0:T(8,128)(2,1)}, bf16[152,256]{1,0:T(8,128)(2,1)}, ...) conditional(s32[]{:T(128)} %convert_element_type.49, () %tuple.126, ...), branch_computations={%region_25.26_spmd, %region_26.27_spmd} | conditional | bytes 4493398 | solution.py:788
  337.9 10.4 %branch_1_fun.25 = (f32[512,1024]{1,0:T(8,128)}, f32[2,128,1024]{2,1,0:T(8,128)}, f32[1024,128]{1,0:T(8,128)}) custom-call(s32[2]{0:T(128)S(1)} %get-tuple-element.495.idx_ref, bf16[2048,1024]{1,0:T(8,128)(2,1)} %get-tuple-element.496.x_ref, f32[512,1024]{1,0:T(8,128)S(1)} %get-tuple-element.497.gr_ref, ...), custom_call_target="tpu_custom_call" | custom-call | tf_op jit(solution)/shard_map/cond/branch_1_fun/pallas_call | solution.py:699
  348.3 7.7 %collective-permute-done.28 = bf16[152,256]{1,0:T(8,128)(2,1)} collective-permute-done((bf16[152,256]{1,0:T(8,128)(2,1)S(1)}, bf16[152,256]{1,0:T(8,128)(2,1)}, u32[]{:S(2)}, u32[]{:S(2)}) %collective-permute-start.28) | collective-permute-done | bytes 77856 | tf_op jit(solution)/shard_map/cond/branch_1_fun/ppermute | solution.py:794
  363.2 3.4 maximum_add_fusion
  (124 shorter events, 54.2 us)
Async XLA Ops:
  7.2 87.9 %all-gather.6.cloned.1.call-start = ((), (), s32[]{:S(2)}) async-start(), calls=%async_computation.3 | async-start | bytes 9437184 | tf_op jit(solution)/shard_map/all_gather | solution.py:827
  10.6 27.4 %collective-permute-start = (bf16[384,1024]{1,0:T(8,128)(2,1)}, bf16[384,1024]{1,0:T(8,128)(2,1)}, u32[]{:S(2)}, u32[]{:S(2)}) collective-permute-start(bf16[384,1024]{1,0:T(8,128)(2,1)} %get-tuple-element.304), channel_id=1, source_target_pairs={{0,1},{1,0},{2,3},{3,2},{4,5},{5,4},{6,7},{7,6},{8,9},{9,8},{10,11... | collective-permute-start | bytes 2359304 | tf_op jit(solution)/shard_map/cond/branch_1_fun/ppermute | solution.py:794
  13.7 20.7 %collective-permute-start.1 = (bf16[32,1024]{1,0:T(8,128)(2,1)S(1)}, bf16[32,1024]{1,0:T(8,128)(2,1)}, u32[]{:S(2)}, u32[]{:S(2)}) collective-permute-start(bf16[32,1024]{1,0:T(8,128)(2,1)S(1)} %get-tuple-element.305), channel_id=1, source_target_pairs={{0,1},{1,0},{2,3},{3,2},{4,5},{5,4},{6,7},{7,6},{8,9},{9,8},{10,11... | collective-permute-start | bytes 196616 | tf_op jit(solution)/shard_map/cond/branch_1_fun/ppermute | solution.py:794
  13.7 20.6 %collective-permute-start.2 = (bf16[32,1024]{1,0:T(8,128)(2,1)S(1)}, bf16[32,1024]{1,0:T(8,128)(2,1)}, u32[]{:S(2)}, u32[]{:S(2)}) collective-permute-start(bf16[32,1024]{1,0:T(8,128)(2,1)S(1)} %get-tuple-element.305), channel_id=1, source_target_pairs={{0,2},{1,3},{2,0},{3,1},{4,6},{5,7},{6,4},{7,5},{8,10},{9,11},{10,... | collective-permute-start | bytes 196616 | tf_op jit(solution)/shard_map/cond/branch_1_fun/ppermute | solution.py:794
  16.7 21.2 %collective-permute-start.3 = (bf16[32,1024]{1,0:T(8,128)(2,1)S(1)}, bf16[32,1024]{1,0:T(8,128)(2,1)}, u32[]{:S(2)}, u32[]{:S(2)}) collective-permute-start(bf16[32,1024]{1,0:T(8,128)(2,1)S(1)} %get-tuple-element.305), channel_id=1, source_target_pairs={{0,3},{1,2},{2,1},{3,0},{4,7},{5,6},{6,5},{7,4},{8,11},{9,10},{10,... | collective-permute-start | bytes 196616 | tf_op jit(solution)/shard_map/cond/branch_1_fun/ppermute | solution.py:794
  40.2 162.3 %all-gather.4.cloned.1.call-start = ((), (), s32[]{:S(2)}) async-start(), calls=%async_computation.1 | async-start | bytes 7077888 | tf_op jit(solution)/shard_map/all_gather | solution.py:866
  40.3 54.2 %copy-start.10 = (f32[850]{0:T(1024)S(1)}, f32[850]{0:T(1024)}, u32[]{:S(2)}) copy-start(f32[850]{0:T(1024)} %param.42) | copy-start | bytes 10204
  40.3 54.8 %copy-start.2 = (bf16[1024,1024]{1,0:T(8,128)(2,1)S(1)}, bf16[1024,1024]{1,0:T(8,128)(2,1)}, u32[]{:S(2)}) copy-start(bf16[1024,1024]{1,0:T(8,128)(2,1)} %dw_ref.1) | copy-start | bytes 6291460
  40.3 29.2 %collective-permute-start.4 = (bf16[384,256]{1,0:T(8,128)(2,1)S(1)}, bf16[384,256]{1,0:T(8,128)(2,1)}, u32[]{:S(2)}, u32[]{:S(2)}) collective-permute-start(bf16[384,256]{1,0:T(8,128)(2,1)S(1)} %get-tuple-element.315), channel_id=1, source_target_pairs={{0,2},{1,3},{2,0},{3,1},{4,6},{5,7},{6,4},{7,5},{8,10},{9,11},{10,... | collective-permute-start | bytes 589832 | tf_op jit(solution)/shard_map/cond/branch_1_fun/ppermute | solution.py:794
  69.5 11.1 %collective-permute-start.5 = (bf16[512,256]{1,0:T(8,128)(2,1)}, bf16[512,256]{1,0:T(8,128)(2,1)}, u32[]{:S(2)}, u32[]{:S(2)}) collective-permute-start(bf16[512,256]{1,0:T(8,128)(2,1)} %get-tuple-element.326), channel_id=1, source_target_pairs={{0,1},{1,0},{2,3},{3,2},{4,5},{5,4},{6,7},{7,6},{8,9},{9,8},{10,11... | collective-permute-start | bytes 786440 | tf_op jit(solution)/shard_map/cond/branch_1_fun/ppermute | solution.py:794
  71.7 21.2 %collective-permute-start.6 = (bf16[512,256]{1,0:T(8,128)(2,1)S(1)}, bf16[512,256]{1,0:T(8,128)(2,1)}, u32[]{:S(2)}, u32[]{:S(2)}) collective-permute-start(bf16[512,256]{1,0:T(8,128)(2,1)S(1)} %get-tuple-element.327), channel_id=1, source_target_pairs={{0,2},{1,3},{2,0},{3,1},{4,6},{5,7},{6,4},{7,5},{8,10},{9,11},{10,... | collective-permute-start | bytes 786440 | tf_op jit(solution)/shard_map/cond/branch_1_fun/ppermute | solution.py:794
  72.6 20.3 %collective-permute-start.7 = (bf16[512,256]{1,0:T(8,128)(2,1)S(1)}, bf16[512,256]{1,0:T(8,128)(2,1)}, u32[]{:S(2)}, u32[]{:S(2)}) collective-permute-start(bf16[512,256]{1,0:T(8,128)(2,1)S(1)} %get-tuple-element.328), channel_id=1, source_target_pairs={{0,3},{1,2},{2,1},{3,0},{4,7},{5,6},{6,5},{7,4},{8,11},{9,10},{10,... | collective-permute-start | bytes 786440 | tf_op jit(solution)/shard_map/cond/branch_1_fun/ppermute | solution.py:794
  95.1 28.0 %collective-permute-start.11 = (bf16[768,256]{1,0:T(8,128)(2,1)S(1)}, bf16[768,256]{1,0:T(8,128)(2,1)}, u32[]{:S(2)}, u32[]{:S(2)}) collective-permute-start(bf16[768,256]{1,0:T(8,128)(2,1)S(1)} %get-tuple-element.332), channel_id=1, source_target_pairs={{0,1},{1,0},{2,3},{3,2},{4,5},{5,4},{6,7},{7,6},{8,9},{9,8},{10,11... | collective-permute-start | bytes 1179656 | tf_op jit(solution)/shard_map/cond/branch_1_fun/ppermute | solution.py:794
  98.5 24.6 %collective-permute-start.9 = (bf16[512,256]{1,0:T(8,128)(2,1)S(1)}, bf16[512,256]{1,0:T(8,128)(2,1)}, u32[]{:S(2)}, u32[]{:S(2)}) collective-permute-start(bf16[512,256]{1,0:T(8,128)(2,1)S(1)} %get-tuple-element.330.refs_0_), channel_id=1, source_target_pairs={{0,2},{1,3},{2,0},{3,1},{4,6},{5,7},{6,4},{7,5},{8,10},{9,11},{10,... | collective-permute-start | bytes 786440 | tf_op jit(solution)/shard_map/cond/branch_1_fun/ppermute | solution.py:794
  99.5 23.5 %collective-permute-start.10 = (bf16[512,256]{1,0:T(8,128)(2,1)}, bf16[512,256]{1,0:T(8,128)(2,1)}, u32[]{:S(2)}, u32[]{:S(2)}) collective-permute-start(bf16[512,256]{1,0:T(8,128)(2,1)} %get-tuple-element.331), channel_id=1, source_target_pairs={{0,3},{1,2},{2,1},{3,0},{4,7},{5,6},{6,5},{7,4},{8,11},{9,10},{10,... | collective-permute-start | bytes 786440 | tf_op jit(solution)/shard_map/cond/branch_1_fun/ppermute | solution.py:794
  100.9 22.2 %collective-permute-start.8 = (bf16[512,256]{1,0:T(8,128)(2,1)S(1)}, bf16[512,256]{1,0:T(8,128)(2,1)}, u32[]{:S(2)}, u32[]{:S(2)}) collective-permute-start(bf16[512,256]{1,0:T(8,128)(2,1)S(1)} %get-tuple-element.329), channel_id=1, source_target_pairs={{0,1},{1,0},{2,3},{3,2},{4,5},{5,4},{6,7},{7,6},{8,9},{9,8},{10,11... | collective-permute-start | bytes 786440 | tf_op jit(solution)/shard_map/cond/branch_1_fun/ppermute | solution.py:794
  125.3 206.3 %reduce-scatter.2.cloned.1.call-start = ((), (), s32[]{:S(2)}) async-start(), calls=%async_computation.2 | async-start | bytes 9437184 | tf_op jit(solution)/shard_map/reduce_scatter | solution.py:895
  125.4 45.6 %collective-permute-start.12 = (bf16[512,1024]{1,0:T(8,128)(2,1)}, bf16[512,1024]{1,0:T(8,128)(2,1)}, u32[]{:S(2)}, u32[]{:S(2)}) collective-permute-start(bf16[512,1024]{1,0:T(8,128)(2,1)} %get-tuple-element.350), channel_id=1, source_target_pairs={{0,2},{1,3},{2,0},{3,1},{4,6},{5,7},{6,4},{7,5},{8,10},{9,11},{10,... | collective-permute-start | bytes 3145736 | tf_op jit(solution)/shard_map/cond/branch_1_fun/ppermute | solution.py:794
  171.4 8.4 %collective-permute-start.13 = (bf16[4,384,1024]{2,1,0:T(8,128)(2,1)}, bf16[4,384,1024]{2,1,0:T(8,128)(2,1)}, u32[]{:S(2)}, u32[]{:S(2)}) collective-permute-start(bf16[4,384,1024]{2,1,0:T(8,128)(2,1)} %get-tuple-element.374), channel_id=1, source_target_pairs={{0,4},{4,0},{8,12},{12,8},{16,20},{20,16},{24,28},{28,24},{1,5},{5... | collective-permute-start | bytes 9437192 | tf_op jit(solution)/shard_map/cond/branch_1_fun/ppermute | solution.py:794
  179.8 20.2 %collective-permute-start.14 = (bf16[512,256]{1,0:T(8,128)(2,1)S(1)}, bf16[512,256]{1,0:T(8,128)(2,1)}, u32[]{:S(2)}, u32[]{:S(2)}) collective-permute-start(bf16[512,256]{1,0:T(8,128)(2,1)S(1)} %get-tuple-element.396), channel_id=1, source_target_pairs={{0,1},{1,0},{2,3},{3,2},{4,5},{5,4},{6,7},{7,6},{8,9},{9,8},{10,11... | collective-permute-start | bytes 786440 | tf_op jit(solution)/shard_map/cond/branch_1_fun/ppermute | solution.py:794
  180.6 21.8 %collective-permute-start.15 = (bf16[512,256]{1,0:T(8,128)(2,1)S(1)}, bf16[512,256]{1,0:T(8,128)(2,1)}, u32[]{:S(2)}, u32[]{:S(2)}) collective-permute-start(bf16[512,256]{1,0:T(8,128)(2,1)S(1)} %get-tuple-element.397), channel_id=1, source_target_pairs={{0,2},{1,3},{2,0},{3,1},{4,6},{5,7},{6,4},{7,5},{8,10},{9,11},{10,... | collective-permute-start | bytes 786440 | tf_op jit(solution)/shard_map/cond/branch_1_fun/ppermute | solution.py:794
  184.0 18.5 %collective-permute-start.16 = (bf16[512,256]{1,0:T(8,128)(2,1)}, bf16[512,256]{1,0:T(8,128)(2,1)}, u32[]{:S(2)}, u32[]{:S(2)}) collective-permute-start(bf16[512,256]{1,0:T(8,128)(2,1)} %get-tuple-element.398), channel_id=1, source_target_pairs={{0,3},{1,2},{2,1},{3,0},{4,7},{5,6},{6,5},{7,4},{8,11},{9,10},{10,... | collective-permute-start | bytes 786440 | tf_op jit(solution)/shard_map/cond/branch_1_fun/ppermute | solution.py:794
  202.7 37.4 %collective-permute-start.18 = (bf16[2,192,1024]{2,1,0:T(8,128)(2,1)}, bf16[2,192,1024]{2,1,0:T(8,128)(2,1)}, u32[]{:S(2)}, u32[]{:S(2)}) collective-permute-start(bf16[2,192,1024]{2,1,0:T(8,128)(2,1)} %get-tuple-element.414), channel_id=1, source_target_pairs={{0,16},{4,20},{8,24},{12,28},{16,0},{20,4},{24,8},{28,12},{1,17},{... | collective-permute-start | bytes 2359304 | tf_op jit(solution)/shard_map/cond/branch_1_fun/ppermute | solution.py:794
  203.7 36.4 %collective-permute-start.19 = (bf16[2,192,1024]{2,1,0:T(8,128)(2,1)}, bf16[2,192,1024]{2,1,0:T(8,128)(2,1)}, u32[]{:S(2)}, u32[]{:S(2)}) collective-permute-start(bf16[2,192,1024]{2,1,0:T(8,128)(2,1)} %get-tuple-element.415), channel_id=1, source_target_pairs={{0,8},{4,12},{8,0},{12,4},{16,24},{20,28},{24,16},{28,20},{1,9},{5... | collective-permute-start | bytes 2359304 | tf_op jit(solution)/shard_map/cond/branch_1_fun/ppermute | solution.py:794
  204.9 35.1 %collective-permute-start.17 = (bf16[320,1024]{1,0:T(8,128)(2,1)}, bf16[320,1024]{1,0:T(8,128)(2,1)}, u32[]{:S(2)}, u32[]{:S(2)}) collective-permute-start(bf16[320,1024]{1,0:T(8,128)(2,1)} %get-tuple-element.413), channel_id=1, source_target_pairs={{0,2},{1,3},{2,0},{3,1},{4,6},{5,7},{6,4},{7,5},{8,10},{9,11},{10,... | collective-permute-start | bytes 1966088 | tf_op jit(solution)/shard_map/cond/branch_1_fun/ppermute | solution.py:794
  243.6 6.4 %copy-start.8 = (bf16[512,256]{1,0:T(8,128)(2,1)}, bf16[512,256]{1,0:T(8,128)(2,1)S(1)}, u32[]{:S(2)}) copy-start(bf16[512,256]{1,0:T(8,128)(2,1)S(1)} %get-tuple-element.443.refs_0_) | copy-start | bytes 786436 | tf_op jit(solution)/shard_map/cond
  243.7 30.9 %collective-permute-start.20 = (bf16[3,512,128]{2,1,0:T(8,128)(2,1)}, bf16[3,512,128]{2,1,0:T(8,128)(2,1)}, u32[]{:S(2)}, u32[]{:S(2)}) collective-permute-start(bf16[3,512,128]{2,1,0:T(8,128)(2,1)} %get-tuple-element.431), channel_id=1, source_target_pairs={{0,1},{1,0},{2,3},{3,2},{4,5},{5,4},{6,7},{7,6},{8,9},{9,8},{10,11... | collective-permute-start | bytes 1179656 | tf_op jit(solution)/shard_map/cond/branch_1_fun/ppermute | solution.py:794
  243.7 30.8 %collective-permute-start.21 = (bf16[3,512,128]{2,1,0:T(8,128)(2,1)}, bf16[3,512,128]{2,1,0:T(8,128)(2,1)}, u32[]{:S(2)}, u32[]{:S(2)}) collective-permute-start(bf16[3,512,128]{2,1,0:T(8,128)(2,1)} %get-tuple-element.432), channel_id=1, source_target_pairs={{0,2},{1,3},{2,0},{3,1},{4,6},{5,7},{6,4},{7,5},{8,10},{9,11},{10,... | collective-permute-start | bytes 1179656 | tf_op jit(solution)/shard_map/cond/branch_1_fun/ppermute | solution.py:794
  245.6 28.9 %collective-permute-start.22 = (bf16[3,512,128]{2,1,0:T(8,128)(2,1)}, bf16[3,512,128]{2,1,0:T(8,128)(2,1)}, u32[]{:S(2)}, u32[]{:S(2)}) collective-permute-start(bf16[3,512,128]{2,1,0:T(8,128)(2,1)} %get-tuple-element.433), channel_id=1, source_target_pairs={{0,3},{1,2},{2,1},{3,0},{4,7},{5,6},{6,5},{7,4},{8,11},{9,10},{10,... | collective-permute-start | bytes 1179656 | tf_op jit(solution)/shard_map/cond/branch_1_fun/ppermute | solution.py:794
  248.1 26.4 %collective-permute-start.23 = (bf16[1,192,1024]{2,1,0:T(8,128)(2,1)S(1)}, bf16[1,192,1024]{2,1,0:T(8,128)(2,1)}, u32[]{:S(2)}, u32[]{:S(2)}) collective-permute-start(bf16[1,192,1024]{2,1,0:T(8,128)(2,1)S(1)} %get-tuple-element.434), channel_id=1, source_target_pairs={{0,8},{4,12},{8,0},{12,4},{16,24},{20,28},{24,16},{28,20},{1,9},{5... | collective-permute-start | bytes 1179656 | tf_op jit(solution)/shard_map/cond/branch_1_fun/ppermute | solution.py:794
  249.1 25.5 %collective-permute-start.24 = (bf16[1,192,1024]{2,1,0:T(8,128)(2,1)}, bf16[1,192,1024]{2,1,0:T(8,128)(2,1)}, u32[]{:S(2)}, u32[]{:S(2)}) collective-permute-start(bf16[1,192,1024]{2,1,0:T(8,128)(2,1)} %get-tuple-element.435), channel_id=1, source_target_pairs={{0,16},{4,20},{8,24},{12,28},{16,0},{20,4},{24,8},{28,12},{1,17},{... | collective-permute-start | bytes 1179656 | tf_op jit(solution)/shard_map/cond/branch_1_fun/ppermute | solution.py:794
  277.5 51.7 %copy-start.4 = (bf16[320,1024]{1,0:T(8,128)(2,1)S(1)}, bf16[320,1024]{1,0:T(8,128)(2,1)}, u32[]{:S(2)}) copy-start(bf16[320,1024]{1,0:T(8,128)(2,1)} %get-tuple-element.634) | copy-start | bytes 1966084
  277.5 50.6 %collective-permute-start.38 = (bf16[384,1024]{1,0:T(8,128)(2,1)}, bf16[384,1024]{1,0:T(8,128)(2,1)}, u32[]{:S(2)}, u32[]{:S(2)}) collective-permute-start(bf16[384,1024]{1,0:T(8,128)(2,1)} %get-tuple-element.475), channel_id=1, source_target_pairs={{0,1},{1,0},{2,3},{3,2},{4,5},{5,4},{6,7},{7,6},{8,9},{9,8},{10,11... | collective-permute-start | bytes 2359304 | tf_op jit(solution)/shard_map/cond/branch_1_fun/ppermute | solution.py:794
  284.0 44.2 %collective-permute-start.35 = (bf16[3,512,128]{2,1,0:T(8,128)(2,1)}, bf16[3,512,128]{2,1,0:T(8,128)(2,1)}, u32[]{:S(2)}, u32[]{:S(2)}) collective-permute-start(bf16[3,512,128]{2,1,0:T(8,128)(2,1)} %get-tuple-element.472), channel_id=1, source_target_pairs={{0,1},{1,0},{2,3},{3,2},{4,5},{5,4},{6,7},{7,6},{8,9},{9,8},{10,11... | collective-permute-start | bytes 1179656 | tf_op jit(solution)/shard_map/cond/branch_1_fun/ppermute | solution.py:794
  284.0 44.2 %collective-permute-start.36 = (bf16[3,512,128]{2,1,0:T(8,128)(2,1)}, bf16[3,512,128]{2,1,0:T(8,128)(2,1)}, u32[]{:S(2)}, u32[]{:S(2)}) collective-permute-start(bf16[3,512,128]{2,1,0:T(8,128)(2,1)} %get-tuple-element.473), channel_id=1, source_target_pairs={{0,2},{1,3},{2,0},{3,1},{4,6},{5,7},{6,4},{7,5},{8,10},{9,11},{10,... | collective-permute-start | bytes 1179656 | tf_op jit(solution)/shard_map/cond/branch_1_fun/ppermute | solution.py:794
  286.0 42.2 %collective-permute-start.37 = (bf16[3,512,128]{2,1,0:T(8,128)(2,1)}, bf16[3,512,128]{2,1,0:T(8,128)(2,1)}, u32[]{:S(2)}, u32[]{:S(2)}) collective-permute-start(bf16[3,512,128]{2,1,0:T(8,128)(2,1)} %get-tuple-element.474), channel_id=1, source_target_pairs={{0,3},{1,2},{2,1},{3,0},{4,7},{5,6},{6,5},{7,4},{8,11},{9,10},{10,... | collective-permute-start | bytes 1179656 | tf_op jit(solution)/shard_map/cond/branch_1_fun/ppermute | solution.py:794
  299.6 2.6 collective-permute-start.30
  305.1 11.5 %collective-permute-start.31 = (bf16[2,128,768]{2,1,0:T(8,128)(2,1)}, bf16[2,128,768]{2,1,0:T(8,128)(2,1)}, u32[]{:S(2)}, u32[]{:S(2)}) collective-permute-start(bf16[2,128,768]{2,1,0:T(8,128)(2,1)} %get-tuple-element.466), channel_id=1, source_target_pairs={{0,16},{4,20},{8,24},{12,28},{16,0},{20,4},{24,8},{28,12},{1,17},{... | collective-permute-start | bytes 1179656 | tf_op jit(solution)/shard_map/cond/branch_1_fun/cond/branch_1_fun/ppermute | solution.py:794
  319.0 1.2 collective-permute-start.32
  320.2 3.7 collective-permute-start.33
  323.9 3.7 collective-permute-start.34
  332.7 23.3 %collective-permute-start.26 = (bf16[192,1024]{1,0:T(8,128)(2,1)}, bf16[192,1024]{1,0:T(8,128)(2,1)}, u32[]{:S(2)}, u32[]{:S(2)}) collective-permute-start(bf16[192,1024]{1,0:T(8,128)(2,1)} %get-tuple-element.491), channel_id=1, source_target_pairs={{0,2},{1,3},{2,0},{3,1},{4,6},{5,7},{6,4},{7,5},{8,10},{9,11},{10,... | collective-permute-start | bytes 1179656 | tf_op jit(solution)/shard_map/cond/branch_1_fun/ppermute | solution.py:794
  332.8 23.2 %collective-permute-start.25 = (bf16[1,128,768]{2,1,0:T(8,128)(2,1)}, bf16[1,128,768]{2,1,0:T(8,128)(2,1)}, u32[]{:S(2)}, u32[]{:S(2)}) collective-permute-start(bf16[1,128,768]{2,1,0:T(8,128)(2,1)} %get-tuple-element.490), channel_id=1, source_target_pairs={{0,8},{4,12},{8,0},{12,4},{16,24},{20,28},{24,16},{28,20},{1,9},{5... | collective-permute-start | bytes 589832 | tf_op jit(solution)/shard_map/cond/branch_1_fun/ppermute | solution.py:794
  333.5 14.8 %collective-permute-start.27 = (bf16[152,256]{1,0:T(8,128)(2,1)S(1)}, bf16[152,256]{1,0:T(8,128)(2,1)}, u32[]{:S(2)}, u32[]{:S(2)}) collective-permute-start(bf16[152,256]{1,0:T(8,128)(2,1)S(1)} %get-tuple-element.492), channel_id=1, source_target_pairs={{0,1},{1,0},{2,3},{3,2},{4,5},{5,4},{6,7},{7,6},{8,9},{9,8},{10,11... | collective-permute-start | bytes 233480 | tf_op jit(solution)/shard_map/cond/branch_1_fun/ppermute | solution.py:794
  335.3 20.7 %collective-permute-start.28 = (bf16[152,256]{1,0:T(8,128)(2,1)S(1)}, bf16[152,256]{1,0:T(8,128)(2,1)}, u32[]{:S(2)}, u32[]{:S(2)}) collective-permute-start(bf16[152,256]{1,0:T(8,128)(2,1)S(1)} %get-tuple-element.493), channel_id=1, source_target_pairs={{0,2},{1,3},{2,0},{3,1},{4,6},{5,7},{6,4},{7,5},{8,10},{9,11},{10,... | collective-permute-start | bytes 233480 | tf_op jit(solution)/shard_map/cond/branch_1_fun/ppermute | solution.py:794
  336.4 19.6 %collective-permute-start.29 = (bf16[152,256]{1,0:T(8,128)(2,1)S(1)}, bf16[152,256]{1,0:T(8,128)(2,1)}, u32[]{:S(2)}, u32[]{:S(2)}) collective-permute-start(bf16[152,256]{1,0:T(8,128)(2,1)S(1)} %get-tuple-element.494), channel_id=1, source_target_pairs={{0,3},{1,2},{2,1},{3,0},{4,7},{5,6},{6,5},{7,4},{8,11},{9,10},{10,... | collective-permute-start | bytes 233480 | tf_op jit(solution)/shard_map/cond/branch_1_fun/ppermute | solution.py:794
  357.9 5.3 %copy-start.3 = (f32[320,1024]{1,0:T(8,128)S(1)}, f32[320,1024]{1,0:T(8,128)}, u32[]{:S(2)}) copy-start(f32[320,1024]{1,0:T(8,128)} %convert_add_fusion) | copy-start | bytes 3932164
  362.0 6.0 %copy-start.1 = (bf16[256,1024]{1,0:T(8,128)(2,1)S(1)}, bf16[256,1024]{1,0:T(8,128)(2,1)}, u32[]{:S(2)}) copy-start(bf16[256,1024]{1,0:T(8,128)(2,1)} %param.38) | copy-start | bytes 1572868
  (5 other events, 13.2 us)
Sparse Core Ops, SparseCore 0:
  40.3 53.6 all-gather.5
  125.4 45.6 all-gather.3
  202.6 82.6 reduce-scatter.1

commit v6 on v5

--- a/solution.py
+++ b/solution.py
@@ -90,10 +90,11 @@
     return factor * (scaled - unit * jnp.mean(scaled * unit, axis=-1, keepdims=True))
 
 
-def qkv_kernel(len_ref, x_ref, w_ref, gain_ref, cos_ref, sin_ref, q_ref, k_ref, v_ref):
+def qkv_kernel(len_ref, x_ref, w_ref, gain_ref, cos_ref, sin_ref, q_ref, k_ref, v_ref, normed_ref):
     rows = x_ref.shape[0]
     x = x_ref[...].astype(F32)
     normed = (x * rms(x) * gain_ref[0:1, :]).astype(BF16)
+    normed_ref[...] = normed
     cosine = cos_ref[...]
     sine = sin_ref[...]
     lane = lax.broadcasted_iota(jnp.int32, (rows, 128), 1)
@@ -142,8 +143,8 @@
             pl.BlockSpec((block, 128), lambda i: (i, 0)),
             pl.BlockSpec((block, 128), lambda i: (i, 0)),
         ],
-        [spec] * 3,
-        [sds((heads, rows, 128), BF16)] * 3,
+        [spec] * 3 + [pl.BlockSpec((block, width), lambda i: (i, 0))],
+        [sds((heads, rows, 128), BF16)] * 3 + [sds((rows, width), BF16)],
     )(lengths, tokens, qkv_weight, gains, cosine, sine)
 
 
@@ -199,14 +200,17 @@
     )(index, q, k, v)
 
 
-def cut_kernel(idx_ref, gu_ref, dw_ref, out_ref):
+def cut_kernel(idx_ref, gu_ref, dw_ref, *refs):
     part = gu_ref.shape[1]
+    out_ref = refs[-1]
     out_ref[:part, :] = gu_ref[0]
     out_ref[part : 2 * part, :] = gu_ref[1]
-    out_ref[2 * part :, :] = dw_ref[...].T
-
-
-def cut_weights(dp, gate_up, down, shares):
+    out_ref[2 * part : 3 * part, :] = dw_ref[...].T
+    if len(refs) > 1:
+        out_ref[3 * part :, :] = refs[0][...]
+
+
+def cut_weights(dp, gate_up, down, shares, more):
     _, width, hidden = gate_up.shape
     part = width // shares
     if part % 128:
@@ -214,15 +218,15 @@
         spec = whole(down.shape)
     else:
         spec = pl.BlockSpec((hidden, part), lambda i, idx: (0, idx[0]))
+    shape = (3 * part + sum(a.shape[0] for a in more), hidden)
     return call(
         cut_kernel,
         (1,),
-        [pl.BlockSpec((2, part, hidden), lambda i, idx: (0, idx[0], 0)), spec],
-        whole((3 * part, hidden)),
-        sds((3 * part, hidden), BF16),
-        nbytes=12 * part * hidden,
+        [pl.BlockSpec((2, part, hidden), lambda i, idx: (0, idx[0], 0)), spec] + [whole(a.shape) for a in more],
+        whole(shape),
+        sds(shape, BF16),
         prefetch=1,
-    )(dp, gate_up, down)
+    )(dp, gate_up, down, *more)
 
 
 def pack_kernel(*refs):
@@ -237,11 +241,11 @@
     return call(pack_kernel, (1,), [whole(a.shape) for a in arrays], whole(shape), sds(shape, BF16))(*arrays)
 
 
-def ffn_kernel(parts, ow_row, slot, idx_ref, len_ref, weight_ref, gain_ref, x_h, cot_h, gu_h, dw_h, pb_h, ow_h, *refs):
+def ffn_kernel(parts, ow_row, ow_order, slot, idx_ref, len_ref, weight_ref, gain_ref, x_h, cot_h, gu_h, dw_h, pb_h, ow_h, *refs):
     own = slot == 0
     att_h = refs[:parts]
     refs = refs[parts:]
-    count = 6 if own else 5
+    count = 7 if own else 6
     outs, scratch = refs[:count], refs[count:]
     x_v, cot_v, att_v, ow_v, gu_v, dw_v, pb_v, left_v, act_v, ffn_v, gn2_v, low_v, sem_in, sem_out = scratch
     rows, width = x_v.shape
@@ -277,10 +281,11 @@
     resid = x_v[...].astype(F32)
     for d in range(parts):
         get_att[d].wait()
-        resid = resid + dot(att_v[d], ow_v[:, d * piece : (d + 1) * piece].reshape(local, width))
+        at = ow_order.index(d) * piece
+        resid = resid + dot(att_v[d], ow_v[:, at : at + piece].reshape(local, width))
     if own:
         ffn_v[...] = resid
-        store(ffn_v, outs[5], 4)
+        store(ffn_v, outs[6], 4)
     normed = (resid * rms(resid) * gain_ref[1:2, :]).astype(BF16)
     left_v[0] = normed
     position = lax.broadcasted_iota(jnp.int32, (rows, 1), 0) + row0
@@ -322,9 +327,11 @@
             low_v[0] = (gn2_v[...] + grad).astype(BF16)
             store(low_v.at[0], outs[2], 2)
             low_v[1] = (ffn_v[...] + term).astype(BF16)
-            cut = outs[3].shape[0]
-            store(low_v.at[1, pl.ds(0, cut)], outs[3], 3)
-            store(low_v.at[1, pl.ds(cut, rows - cut)], outs[4], 6)
+            row = 0
+            for n in range(3):
+                size = outs[3 + n].shape[0]
+                store(low_v.at[1, pl.ds(row, size)], outs[3 + n], (3, 6, 7)[n])
+                row += size
     for copy in pending:
         copy.wait()
 
@@ -334,19 +341,19 @@
     rows, local = atts[0].shape
     width = tokens.shape[1]
     hidden = gate_up.shape[2]
-    early = rows * 5 // 8
-    out_rows, ow_row = out_full
+    out_rows, ow_row, ow_order = out_full
     shares = partner.shape[0]
     part = width // shares
     anywhere = pl.BlockSpec(memory_space=pl.ANY)
     out_shape = [
         sds((2, rows, width), BF16), sds((3, rows, 2 * hidden), BF16),
-        sds((rows, width), BF16), sds((early, width), BF16), sds((rows - early, width), BF16),
+        sds((rows, width), BF16),
     ]
+    out_shape += [sds((rows * n // 16, width), BF16) for n in (2, 11, 3)]
     if slot == 0:
         out_shape.append(sds((rows, width), F32))
     return call(
-        functools.partial(ffn_kernel, parts, ow_row, slot),
+        functools.partial(ffn_kernel, parts, ow_row, ow_order, slot),
         (1,),
         [smem(), smem(), whole(gains.shape)] + [anywhere] * (6 + parts),
         [anywhere] * len(out_shape),
@@ -365,7 +372,7 @@
             pltpu.VMEM((rows, width), F32),
             pltpu.VMEM((2, rows, width), BF16),
             pltpu.SemaphoreType.DMA((7 + parts,)),
-            pltpu.SemaphoreType.DMA((7,)),
+            pltpu.SemaphoreType.DMA((8,)),
         ],
         prefetch=1,
     )(index, lengths, picked, gains, tokens, cotangent, gate_up, down, partner, out_rows, *atts)
@@ -459,7 +466,8 @@
     return res[0], [(res[1 + 2 * n], res[2 + 2 * n]) + info[n] for n in range(len(lanes))]
 
 
-def resid_kernel(parts, members, idx_ref, len_ref, weight_ref, cot_ref, resid_ref, ow_ref, gain_ref, *refs):
+def resid_kernel(ow_order, members, idx_ref, len_ref, weight_ref, cot_ref, resid_ref, ow_ref, gain_ref, *refs):
+    parts = len(ow_order)
     gn2_refs = refs[:members]
     att_refs = refs[members : members + parts]
     gr_ref, low_ref, cat_ref, sum_ref = refs[members + parts : members + parts + 4]
@@ -488,7 +496,8 @@
     sum_ref[...] += jnp.sum((gn2 * unit).reshape(rows // 8, 8, width), axis=0)
     for d in range(parts):
         piece = ow_ref.shape[1] // parts
-        block = ow_ref[:, d * piece : (d + 1) * piece].reshape(local, width)
+        at = ow_order.index(d) * piece
+        block = ow_ref[:, at : at + piece].reshape(local, width)
         g_refs[d][...] = dot(low, block, NT).astype(BF16)
         cat_ref[:, d * local : (d + 1) * local] = att_refs[d][...]
 
@@ -497,12 +506,12 @@
     share, width = resid.shape
     parts, members = len(atts), len(gn2s)
     local = atts[0].shape[1]
-    out_rows, ow_row = out_full
+    out_rows, ow_row, ow_order = out_full
     ow_rows = parts * local // out_rows.shape[0]
     steps = share // block
     row = lambda n: pl.BlockSpec((block, n), lambda i, idx: (i, 0))
     return call(
-        functools.partial(resid_kernel, parts, members),
+        functools.partial(resid_kernel, ow_order, members),
         (steps,),
         [
             smem(), smem(),
@@ -609,61 +618,55 @@
     )(index, q, k, v, att, cosine, sine, *grads)
 
 
-def project_grad_kernel(parts, pairs, idx_ref, x_ref, w_ref, gain_ref, *refs):
+def project_grad_kernel(parts, pairs, idx_ref, n_ref, w_ref, *refs):
     act_refs = refs[: parts * pairs]
-    away_ref, keep_ref, sum_ref, acc = refs[parts * pairs :]
-    step = pl.program_id(0)
-
-    @pl.when(step == 0)
+    away_ref, keep_ref, sum_ref = refs[parts * pairs :]
+    share = act_refs[0].shape[1]
+    me = idx_ref[0]
+    total = None
+    for d in range(parts):
+        rows = n_ref[pl.ds(pl.multiple_of((me ^ d) * share, share), share), :]
+        act = jnp.concatenate([act_refs[j * parts + d][0] for j in range(pairs)], axis=1)
+        term = dot(rows, act, TN)
+        total = term if total is None else total + term
+    count, part, _ = keep_ref.shape
+    for bit in range(2):
+
+        @pl.when((idx_ref[1] & 1) == bit)
+        def _():
+            for j in range(count):
+                keep, away = 2 * j + bit, 2 * j + 1 - bit
+                keep_ref[j] = total[keep * part : (keep + 1) * part, :].astype(BF16)
+                away_ref[j] = total[away * part : (away + 1) * part, :].astype(BF16)
+
+    gain_sum = jnp.sum(total * w_ref[0].astype(F32), axis=1, keepdims=True)
+
+    @pl.when(pl.program_id(0) == 0)
     def _():
-        acc[...] = jnp.zeros_like(acc)
-
-    x = x_ref[...].astype(F32)
-    normed = (x * rms(x) * gain_ref[0:1, :]).astype(BF16)
-    for d in range(parts):
-
-        @pl.when(step == d)
-        def _():
-            acts = [act_refs[j * parts + d][c] for c in range(3) for j in range(pairs)]
-            acc[...] += dot(normed, jnp.concatenate(acts, axis=1), TN)
-
-    @pl.when(step == pl.num_programs(0) - 1)
+        sum_ref[...] = jnp.broadcast_to(gain_sum, sum_ref.shape)
+
+    @pl.when(pl.program_id(0) > 0)
     def _():
-        count, part, _ = keep_ref.shape
-        local = w_ref.shape[2]
-        core = idx_ref[1] & 1
-        for j in range(count):
-            keep_ref[j] = acc[pl.ds(pl.multiple_of((2 * j + core) * part, part), part), :].astype(BF16)
-            away_ref[j] = acc[pl.ds(pl.multiple_of((2 * j + 1 - core) * part, part), part), :].astype(BF16)
-        gain_sum = acc[:, :local] * w_ref[0].astype(F32)
-        for c in (1, 2):
-            gain_sum += acc[:, c * local : (c + 1) * local] * w_ref[c].astype(F32)
-        sum_ref[...] = jnp.broadcast_to(jnp.sum(gain_sum, axis=1, keepdims=True), sum_ref.shape)
-
-
-def project_grads(index, tokens, acts, qkv_weight, gains, shares):
-    width = tokens.shape[1]
+        sum_ref[...] += jnp.broadcast_to(gain_sum, sum_ref.shape)
+
+
+def project_grads(index, normed, acts, qkv_weight, shares):
+    width = normed.shape[1]
     local = qkv_weight.shape[2]
     pairs, parts = len(acts), len(acts[0])
     share = acts[0][0].shape[1]
     flat = [a for group in acts for a in group]
     half = (shares // 2, width // shares, 3 * local)
+    out = pl.BlockSpec(half[:2] + (local,), lambda c, idx: (0, 0, c))
     return call(
         functools.partial(project_grad_kernel, parts, pairs),
-        (parts,),
-        [
-            pl.BlockSpec((share, width), lambda i, idx: (idx[0] ^ i, 0)),
-            whole(qkv_weight.shape),
-            whole(gains.shape),
-        ]
-        + [whole(a.shape) for a in flat],
-        [whole(half), whole(half), whole((width, 128))],
+        (3,),
+        [whole(normed.shape), pl.BlockSpec((1, width, local), lambda c, idx: (c, 0, 0))]
+        + [pl.BlockSpec((1, share, 128), lambda c, idx: (c, 0, 0))] * len(flat),
+        [out, out, whole((width, 128))],
         [sds(half, BF16), sds(half, BF16), sds((width, 128), F32)],
-        scratch=[pltpu.VMEM((width, 3 * local), F32)],
-        flops=2 * tokens.shape[0] * width * 3 * local,
-        nbytes=tokens.size * 2 + 8 * width * local * 3,
         prefetch=1,
-    )(index, tokens, qkv_weight, gains, *flat)
+    )(index, normed, qkv_weight, *flat)
 
 
 def token_grad_kernel(order, pairs, idx_ref, x_ref, gr_ref, w_ref, gain_ref, own_ref, got_ref, *refs):
@@ -760,6 +763,83 @@
     return [(res[2 * n], res[2 * n + 1]) + info[n] for n in range(len(lanes))]
 
 
+def pieces_kernel(first, part, op_ref, gains_ref, *outs):
+    local = outs[0].shape[1]
+    hidden = op_ref.shape[1]
+    rows = (outs[0].shape[0] - part) // 3
+    gains = gains_ref[...]
+    wide = gains.shape[1] // local
+    flat = jnp.concatenate(
+        [gains[r // wide : r // wide + 1, (r % wide) * local : (r % wide + 1) * local] for r in range(rows)]
+    )
+    parts3 = jnp.concatenate(split3(flat))
+    for d, out in enumerate(outs):
+        block = d * local // hidden
+        col = d * local % hidden
+        row = first + block * part
+        out[:part, :] = op_ref[row : row + part, col : col + local]
+        out[part:, :] = parts3
+
+
+def make_pieces(sum_a, gains, first, part, local, parts):
+    shape = (part + 3 * gains.size // local, local)
+    return call(
+        functools.partial(pieces_kernel, first, part),
+        (1,),
+        [whole(sum_a.shape), whole(gains.shape)],
+        [whole(shape)] * parts,
+        [sds(shape, BF16)] * parts,
+    )(sum_a, gains)
+
+
+def finish_kernel(count, parts, resid_ref, keep_ref, got_ref, *refs):
+    own, others, refs = refs[:3], refs[3 : 3 + 3 * count], refs[3 + 3 * count :]
+    pieces, (out_ref, qkv_ref, op_ref, gains_ref) = refs[:parts], refs[parts:]
+    row = 0
+    for n in range(3):
+        rows = own[n].shape[0]
+        total = resid_ref[row : row + rows, :] + own[n][...].astype(F32)
+        for e in range(count):
+            total = total + others[n * count + e][...].astype(F32)
+        out_ref[row : row + rows, :] = total
+        row += rows
+    local = qkv_ref.shape[2]
+    qkv = keep_ref[0].astype(F32) + got_ref[0].astype(F32)
+    for c in range(3):
+        qkv_ref[c] = qkv[:, c * local : (c + 1) * local]
+    part = op_ref.shape[1]
+    rows = (pieces[0].shape[0] - part) // 3
+
+    def gains_of(ref):
+        hi, mid, low = (ref[part + n * rows : part + (n + 1) * rows, :].astype(F32) for n in range(3))
+        return hi + mid + low
+
+    ops = [ref[:part, :].astype(F32) for ref in pieces]
+    gains = [gains_of(ref) for ref in pieces]
+    while len(ops) > 1:
+        ops = [ops[2 * n] + ops[2 * n + 1] for n in range(len(ops) // 2)]
+        gains = [gains[2 * n] + gains[2 * n + 1] for n in range(len(gains) // 2)]
+    op_ref[...] = ops[0].T
+    wide = gains_ref.shape[1] // local
+    for r in range(rows):
+        gains_ref[r // wide : r // wide + 1, (r % wide) * local : (r % wide + 1) * local] = gains[0][r : r + 1, :]
+
+
+def finish_outputs(resid, own, others, keep, got, pieces):
+    parts, count = len(pieces), len(others[0])
+    width = resid.shape[1]
+    part, local = keep.shape[1], keep.shape[2] // 3
+    args = [resid, keep, got, *own, *[a for group in others for a in group], *pieces]
+    shapes = [resid.shape, (3, part, local), (local, part), (2, width)]
+    return call(
+        functools.partial(finish_kernel, count, parts),
+        (1,),
+        [whole(a.shape) for a in args],
+        [whole(shape) for shape in shapes],
+        [sds(shape, F32) for shape in shapes],
+    )(*args)
+
+
 def after(value, *others):
     return lax.optimization_barrier((value, *others))[0]
 
@@ -814,21 +894,24 @@
     matches = species_ids[:, None] == jnp.arange(species_weight.shape[0])[None, :]
     picked = jnp.sum(jnp.where(matches, species_weight[None, :], F32(0.0)), axis=1)
 
-    mine = cut_weights(index[1:], gate_up_weight, down_weight, shares)
     ow_cut = cut(out_weight, dp * (local // shares), local // shares)
     qkv_cut = cut(qkv_weight, dp * part, part, 1).reshape(3 * part, local)
     top = parts // 2
-
-    (partner_cut, *ow), (q, k, v) = beside(
-        [(mine, 1, "tensor")] + outgoing([ow_cut] * parts),
+    together = hidden == width
+    mine = cut_weights(index[1:], gate_up_weight, down_weight, shares, [ow_cut] if together else [])
+    sends = [(ow_cut, d, "tensor") for d in range(2 if together else 1, parts)]
+
+    (partner_cut, *ow), (q, k, v, normed) = beside(
+        [(mine, 1, "tensor")] + sends,
         lambda: project(lengths, tokens, qkv_weight, norm_gains, cosine, sine),
     )
-    if hidden == width:
+    if together:
         partner = lax.all_gather(pack([partner_cut, ow_cut, *ow]), "dp", axis=0)
-        out_full = (partner, 3 * part)
+        out_full = (partner, 3 * part, [1, 0] + list(range(2, parts)))
     else:
         partner = lax.all_gather(partner_cut, "dp", axis=0)
-        out_full = (lax.all_gather(pack([ow_cut, *ow]), "dp", axis=0), 0)
+        out_full = (lax.all_gather(pack([ow_cut, *ow]), "dp", axis=0), 0, list(range(parts)))
+
     (qkv_got,), (*att, att_nat, q_back) = beside(
         [(after(qkv_cut, partner_cut), top, "tensor")], lambda: attend(index, q, k, v, parts)
     )
@@ -870,17 +953,23 @@
             rows_now = got
         else:
             outs, keep_b, away_b = outs
-        lefts[e], acts[e], gn2s[e], *terms[e] = outs[:5]
+        lefts[e], acts[e], gn2s[e], *terms[e] = outs[:6]
         tied = after(tokens, gn2s[e])
-    resid = outs[5]
+    resid = outs[6]
     gn2_all = [gn2s[0]] + [gn2_got[e] for e in slots[:-1]]
-    (got_b,), (grad_resid, grad_low, att_own, gain_two, *grads) = beside(
-        [(away_b, 1, "dp")],
+
+    def terms_out(i):
+        return [(terms[e][i], e, "tensor") for e in slots[:-1]]
+
+    terms_got = []
+    (got_b, *got), (grad_resid, grad_low, att_own, gain_two, *grads) = beside(
+        [(away_b, 1, "dp")] + terms_out(0),
         lambda: resid_back(
             index, lengths, picked, cotangent, resid, gn2_all, out_full, norm_gains, [att[0]] + rows_now
         ),
     )
     lefts, acts = [lefts[e] for e in slots], [acts[e] for e in slots]
+    terms_got.append(got)
     start = [(keep_b, got_b, lead, lead), (keep_b, got_b, lead, lead[::-1])]
     ways = []
 
@@ -898,11 +987,9 @@
     def back(j):
         return attend_back(index, grads_all, q_back, k, v, att_nat, cosine, sine, j)
 
-    def terms_out(i):
-        return [(terms[e][i], e, "tensor") for e in slots[:-1]]
-
-    got, group = beside(terms_out(0) + leaving(halves), lambda: back(0))
-    first_terms, got = got[: len(slots) - 1], got[len(slots) - 1 :]
+    got, group = beside(terms_out(1) + leaving(halves), lambda: back(0))
+    terms_got.append(got[: len(slots) - 1])
+    got = got[len(slots) - 1 :]
     halves, step = fold_next(halves, got), step + 1
     qkv_acts, acts_got = [group], []
     for j in range(1, pairs):
@@ -917,7 +1004,7 @@
     sum_b = halves
 
     def finish():
-        away_q, keep_q, gain_one = project_grads(index, tokens, qkv_acts, qkv_weight, norm_gains, shares)
+        away_q, keep_q, gain_one = project_grads(index, normed, qkv_acts, qkv_weight, shares)
         halves = fold(index, [(keep_q, swap(away_q, 1, "dp"), lead, lead)])
         for s in range(bits - 2):
             halves = fold_next(halves, [swap(*x) for x in leaving(halves)])
@@ -932,30 +1019,15 @@
     halves = [tuple(h) + way for h, way in zip(halves, ways)]
     acts_got.append([group[0]] + got[: parts - 1])
     got_b = got[-1]
-    op_sum = jnp.concatenate(
-        [sum_a[(3 + c) * part : (4 + c) * part] for c in range(parts * local // hidden)], axis=1
-    )
-    gains_low = jnp.concatenate([a.reshape(-1, local) for a in split3(gains_grad)])
-    pieces = [jnp.concatenate([op_sum[:, d * local : (d + 1) * local], gains_low]) for d in range(parts)]
+    pieces = make_pieces(sum_a, gains_grad, 3 * part, part, local, parts)
     got, (grad_tok, grad_gu, grad_down) = beside(
-        leaving(halves) + terms_out(1) + outgoing(pieces),
+        leaving(halves) + terms_out(2) + outgoing(pieces),
         lambda: token_grad(index, tokens, grad_resid, qkv_full, order, norm_gains, acts_got, sum_a, got_b),
     )
-    qkv_sum = fold_next(halves, got[:1]).astype(F32)
-    grad_qkv = jnp.stack([qkv_sum[:, c * local : (c + 1) * local] for c in range(3)])
-    second_terms, got = got[1 : len(slots)], got[len(slots) :]
-    got = jnp.stack([pieces[0]] + got).astype(F32)
-    grad_op = jnp.sum(got[:, :part], axis=0).T
-    gains_all = got[:, part:].reshape(parts, 3, 2, width)
-    gains_all = gains_all[:, 0] + gains_all[:, 1] + gains_all[:, 2]
-    gains_grad = jnp.zeros_like(gains_all[0])
-    for z in range(parts):
-        gains_grad = gains_grad + lax.dynamic_index_in_dim(gains_all, me ^ z, 0, keepdims=False)
-    ffn_rows = [
-        sum((t.astype(F32) for t in got), own.astype(F32))
-        for own, got in zip(terms[0], (first_terms, second_terms))
-    ]
-    out = resid + jnp.concatenate(ffn_rows)
+    terms_got.append(got[1 : len(slots)])
+    out, grad_qkv, grad_op, gains_grad = finish_outputs(
+        resid, terms[0], terms_got, halves[0][0], got[0], [pieces[0]] + got[len(slots) :]
+    )
     return (out, grad_tok, grad_qkv, grad_op, grad_gu, grad_down, gains_grad)
 
 

time: 382 us -> 367 us (0.961)
  other arithmetic: 13.3 us -> 1.33 us
  starting transfers between devices: 60.7 us -> 54.4 us
    add x5 -> x0, other arithmetic: 7.55 us -> none  [the longest x2 3.53 us: body(): sum((t.astype(F32) for t in got), own.astype(F32))]
    ppermute x39, starting transfers between devices: 60.6 us -> 54.3 us  [swap(): lax.ppermute(a, name, [(i, i ^ d) for i in range(lax.axis_size(name))])]
    pallas_call x4 -> x6, Pallas kernels: 62.2 us -> 66 us  [the longest x2 42.6 us: feed_forward(): call(functools.partial(ffn_kernel, parts, ow_row, ow_order, slot), (1,),...]
    pallas_call x5 -> x4, Pallas kernels: 14 us -> 12.1 us  [fold(): call(functools.partial(fold_kernel, cuts), (1,), specs, [whole(o.shape) f...]
  transfers between devices with their start and end apart: 42 -> 42, of which waited for: 13 -> 16; matrix products, arithmetic and copies ran while one was open for 2% -> 1% of each run, Pallas kernels for 54% -> 56%
where the time goes in v6:
time: 367 us; the launch traced here: 360 us
  Pallas kernels  212 us (58%)
  waiting for transfers between devices  72.3 us (20%)
  starting transfers between devices  54.4 us (15%)
  between operations  15.5 us (4%)
    ppermute x39, waiting for transfers between devices, swap(): lax.ppermute(a, name, [(i, i ^ d) for i in range(lax.axis_size(name))])  72.2 us
    ppermute x39, starting transfers between devices, swap(): lax.ppermute(a, name, [(i, i ^ d) for i in range(lax.axis_size(name))])  54.3 us
    pallas_call x2, Pallas kernels, attend_back(): call(functools.partial(attend_back_kernel, parts), (parts,), [pl.BlockSpe...  49.2 us
    pallas_call x2, Pallas kernels, feed_forward(): call(functools.partial(ffn_kernel, parts, ow_row, ow_order, slot), (1,),...  42.6 us
    pallas_call x1, Pallas kernels, attend(): call(functools.partial(attend_kernel, min(sub, share), parts), (heads //...  29.1 us
    pallas_call x2, Pallas kernels, ffn_grads(): call(functools.partial(ffn_grad_kernel, sets, split, extra, cuts), (steps...  28.2 us
    pallas_call x4, Pallas kernels, fold(): call(functools.partial(fold_kernel, cuts), (1,), specs, [whole(o.shape) f...  12.1 us
    pallas_call x1, Pallas kernels, token_grad(): call(functools.partial(token_grad_kernel, order, pairs), (steps,), [pl.Bl...  10.3 us
  transfers between devices with their start and end apart: 42, of which 16 were waited for; matrix products, arithmetic and copies ran while one was open for 1% of the time, Pallas kernels for 56%

profile of v6, /device:TPU:0, one launch (start us, length us, event | category | flops | bytes accessed | tf_op | source)
XLA Modules:
  0.0 359.6 jit_solution(16005012497205596629)
XLA Ops:
  8.3 2.3 shard_map.171
  10.6 27.4 %conditional.12 = (bf16[416,1024]{1,0:T(8,128)(2,1)}, bf16[32,1024]{1,0:T(8,128)(2,1)}, bf16[32,1024]{1,0:T(8,128)(2,1)}, bf16[4,2048,128]{2,1,0:T(8,128)(2,1)},...) conditional(s32[]{:T(128)} %convert_element_type.4, () %tuple.111, ...), branch_computations={%region_0.1_spmd, %region_1.2_spmd} | conditional | bytes 11468870 | solution.py:868
  10.6 3.1 collective-permute-start
  13.7 2.6 collective-permute-start.1
  16.3 10.0 %branch_1_fun.13 = (bf16[4,2048,128]{2,1,0:T(8,128)(2,1)}, bf16[4,2048,128]{2,1,0:T(8,128)(2,1)}, bf16[4,2048,128]{2,1,0:T(8,128)(2,1)}, bf16[2048,1024]{1,0:T(8,128)(2,1)}) custom-call(s32[1]{0:T(128)} %get-tuple-element.308.len_ref, bf16[2048,1024]{1,0:T(8,128)(2,1)} %get-tuple-element.309.x_ref, bf16[3,1024,256]{2,1,0:T(8,128)(2,1)S(1)} %get-tuple-element.310.w_ref, ...), custom_call_target="tpu_custom_call" | custom-call | tf_op jit(solution)/shard_map/cond/branch_1_fun/pallas_call | solution.py:135
  26.2 8.0 %collective-permute-done.1 = bf16[32,1024]{1,0:T(8,128)(2,1)} collective-permute-done((bf16[32,1024]{1,0:T(8,128)(2,1)S(1)}, bf16[32,1024]{1,0:T(8,128)(2,1)}, u32[]{:S(2)}, u32[]{:S(2)}) %collective-permute-start.1) | collective-permute-done | bytes 65568 | tf_op jit(solution)/shard_map/cond/branch_1_fun/ppermute | solution.py:874
  34.2 3.7 %collective-permute-done.2 = bf16[32,1024]{1,0:T(8,128)(2,1)} collective-permute-done((bf16[32,1024]{1,0:T(8,128)(2,1)S(1)}, bf16[32,1024]{1,0:T(8,128)(2,1)}, u32[]{:S(2)}, u32[]{:S(2)}) %collective-permute-start.2) | collective-permute-done | bytes 65568 | tf_op jit(solution)/shard_map/cond/branch_1_fun/ppermute | solution.py:874
  40.4 29.2 %conditional.13 = (bf16[384,256]{1,0:T(8,128)(2,1)}, bf16[512,256]{1,0:T(8,128)(2,1)S(1)}, bf16[512,256]{1,0:T(8,128)(2,1)S(1)}, bf16[512,256]{1,0:T(8,128)(2,1)...) conditional(s32[]{:T(128)} %convert_element_type.4, () %tuple.110, ...), branch_computations={%region_2.3_spmd, %region_3.4_spmd} | conditional | bytes 4390982 | solution.py:868
  40.5 29.1 %branch_1_fun.14 = (bf16[512,256]{1,0:T(8,128)(2,1)S(1)}, bf16[512,256]{1,0:T(8,128)(2,1)S(1)}, bf16[512,256]{1,0:T(8,128)(2,1)S(1)}, bf16[512,256]{1,0:T(8,128)...) custom-call(s32[2]{0:T(128)S(1)} %get-tuple-element.319.idx_ref, ...), custom_call_target="tpu_custom_call" | custom-call | tf_op jit(solution)/shard_map/cond/branch_1_fun/pallas_call | solution.py:185
  69.5 23.4 %conditional.14 = (bf16[512,256]{1,0:T(8,128)(2,1)}, bf16[512,256]{1,0:T(8,128)(2,1)}, bf16[512,256]{1,0:T(8,128)(2,1)}) conditional(s32[]{:T(128)} %convert_element_type.4, () %tuple.115, (bf16[512,256]{1,0:T(8,128)(2,1)}, bf16[512,256]{1,0:T(8,128)(2,1)S(1)}, bf16[512,256]{1,0:T(8,128)(2,1)S(1)}) %tuple.116), branch_computations={%region_5.6_spmd, %region_6.7_spmd} | conditional | bytes 3145872 | solution.py:868
  74.2 6.5 %collective-permute-done.4 = bf16[512,256]{1,0:T(8,128)(2,1)} collective-permute-done((bf16[512,256]{1,0:T(8,128)(2,1)}, bf16[512,256]{1,0:T(8,128)(2,1)}, u32[]{:S(2)}, u32[]{:S(2)}) %collective-permute-start.4) | collective-permute-done | bytes 262176 | tf_op jit(solution)/shard_map/cond/branch_1_fun/ppermute | solution.py:874
  80.7 12.3 %collective-permute-done.5 = bf16[512,256]{1,0:T(8,128)(2,1)} collective-permute-done((bf16[512,256]{1,0:T(8,128)(2,1)S(1)}, bf16[512,256]{1,0:T(8,128)(2,1)}, u32[]{:S(2)}, u32[]{:S(2)}) %collective-permute-start.5) | collective-permute-done | bytes 262176 | tf_op jit(solution)/shard_map/cond/branch_1_fun/ppermute | solution.py:874
  95.2 29.8 %conditional.15 = (bf16[512,256]{1,0:T(8,128)(2,1)}, bf16[512,256]{1,0:T(8,128)(2,1)}, bf16[512,256]{1,0:T(8,128)(2,1)}, bf16[768,256]{1,0:T(8,128)(2,1)}, bf16[...) conditional(s32[]{:T(128)} %convert_element_type.4, () %tuple.109, ...), branch_computations={%region_7.8_spmd, %region_8.9_spmd} | conditional | bytes 11665508 | solution.py:868
  95.2 3.4 collective-permute-start.10
  102.9 21.2 %branch_1_fun.15 = (bf16[2,512,1024]{2,1,0:T(8,128)(2,1)}, bf16[3,512,2048]{2,1,0:T(8,128)(2,1)}, bf16[512,1024]{1,0:T(8,128)(2,1)}, bf16[64,1024]{1,0:T(8,128)(...) custom-call(s32[2]{0:T(128)S(1)} %get-tuple-element.336.idx_ref, s32[1]{0:T(128)} %get-tuple-element.337.len_ref, ...), custom_call_target="tpu_custom_call" | custom-call | tf_op jit(solution)/shard_map/cond/branch_1_fun/pallas_call | solution.py:355
  127.0 45.0 %conditional.16 = (bf16[512,1024]{1,0:T(8,128)(2,1)}, bf16[2,512,1024]{2,1,0:T(8,128)(2,1)}, bf16[3,512,2048]{2,1,0:T(8,128)(2,1)}, bf16[512,1024]{1,0:T(8,128)(...) conditional(s32[]{:T(128)} %convert_element_type.4, () %tuple.108, ...), branch_computations={%region_9.10_spmd, %region_10.11_spmd} | conditional | bytes 19923046 | solution.py:868
  127.1 21.5 %branch_1_fun.16 = (bf16[2,512,1024]{2,1,0:T(8,128)(2,1)}, bf16[3,512,2048]{2,1,0:T(8,128)(2,1)}, bf16[512,1024]{1,0:T(8,128)(2,1)}, bf16[64,1024]{1,0:T(8,128)(...) custom-call(s32[2]{0:T(128)S(1)} %get-tuple-element.355.idx_ref, ...), custom_call_target="tpu_custom_call" | custom-call | tf_op jit(solution)/shard_map/cond/branch_1_fun/pallas_call | solution.py:355
  148.5 12.3 %branch_1_fun.17 = (bf16[4,384,1024]{2,1,0:T(8,128)(2,1)}, bf16[4,384,1024]{2,1,0:T(8,128)(2,1)}) custom-call(s32[2]{0:T(128)S(1)} %get-tuple-element.355.idx_ref, bf16[2,512,1024]{2,1,0:T(8,128)(2,1)} %get-tuple-element.375.refs_0_, bf16[2,512,1024]{2,1,0:T(8,128)(2,1)} %get-tuple-element.799.refs_1_, bf16[3,512,2048]{2,1,0:T(8,128)(2,1)} %get-tuple-element.376.refs_2_, ...), custom_call_target="tpu_custom_call" | custom-call | tf_op jit(solution)/shard_map/cond/branch_1_fun/pallas_call | solution.py:456
  160.8 10.9 %collective-permute-done.11 = bf16[512,1024]{1,0:T(8,128)(2,1)} collective-permute-done((bf16[512,1024]{1,0:T(8,128)(2,1)}, bf16[512,1024]{1,0:T(8,128)(2,1)}, u32[]{:S(2)}, u32[]{:S(2)}) %collective-permute-start.11) | collective-permute-done | bytes 1048608 | tf_op jit(solution)/shard_map/cond/branch_1_fun/ppermute | solution.py:874
  171.9 9.3 %conditional.17 = (bf16[4,384,1024]{2,1,0:T(8,128)(2,1)}, bf16[64,1024]{1,0:T(8,128)(2,1)}, f32[512,1024]{1,0:T(8,128)S(1)}, bf16[512,1024]{1,0:T(8,128)(2,1)}, ...) conditional(s32[]{:T(128)} %convert_element_type.4, () %tuple.124, ...), branch_computations={%region_11.12_spmd, %region_12.13_spmd} | conditional | bytes 13107360 | solution.py:868
  172.1 8.1 %branch_1_fun.18 = (f32[512,1024]{1,0:T(8,128)S(1)}, bf16[512,1024]{1,0:T(8,128)(2,1)}, bf16[512,1024]{1,0:T(8,128)(2,1)}, f32[8,1024]{1,0:T(8,128)}, bf16[512,2...) custom-call(s32[2]{0:T(128)S(1)} %get-tuple-element.381.idx_ref, ...), custom_call_target="tpu_custom_call" | custom-call | tf_op jit(solution)/shard_map/cond/branch_1_fun/pallas_call | solution.py:513
  181.3 23.0 %conditional.18 = (bf16[512,256]{1,0:T(8,128)(2,1)}, bf16[512,256]{1,0:T(8,128)(2,1)}, bf16[512,256]{1,0:T(8,128)(2,1)}, bf16[8,512,1024]{2,1,0:T(8,128)(2,1)}, ...) conditional(s32[]{:T(128)} %convert_element_type.4, () %tuple.123, ...), branch_computations={%region_13.14_spmd, %region_14.15_spmd} | conditional | bytes 12320848 | solution.py:868
  185.7 16.0 %branch_1_fun.19 = (bf16[8,512,1024]{2,1,0:T(8,128)(2,1)}, bf16[2,192,1024]{2,1,0:T(8,128)(2,1)}, bf16[2,192,1024]{2,1,0:T(8,128)(2,1)}, bf16[2,192,1024]{2,1,0:T(8,128)(2,1)}, bf16[2,192,1024]{2,1,0:T(8,128)(2,1)}) custom-call(s32[2]{0:T(128)S(1)} %get-tuple-element.405.idx_ref, bf16[2,512,1024]{2,1,0:T(8,128)(2,1)} %get-tuple-element.406.refs_0_, ...), custom_call_target="tpu_custom_call" | custom-call | tf_op jit(solution)/shard_map/cond/branch_1_fun/pallas_call | solution.py:456
  201.6 2.6 collective-permute-done.15
  204.3 39.6 %conditional.19 = (bf16[352,1024]{1,0:T(8,128)(2,1)}, bf16[2,192,1024]{2,1,0:T(8,128)(2,1)}, bf16[2,192,1024]{2,1,0:T(8,128)(2,1)}, bf16[3,512,128]{2,1,0:T(8,12...) conditional(s32[]{:T(128)} %convert_element_type.4, () %tuple.122, ...), branch_computations={%region_15.16_spmd, %region_16.17_spmd} | conditional | flops 10737418240 | bytes 17563824 | solution.py:868
  207.7 5.6 %collective-permute-start.17 = (bf16[352,1024]{1,0:T(8,128)(2,1)}, bf16[352,1024]{1,0:T(8,128)(2,1)}, u32[]{:S(2)}, u32[]{:S(2)}) collective-permute-start(bf16[352,1024]{1,0:T(8,128)(2,1)} %get-tuple-element.419), channel_id=1, source_target_pairs={{0,2},{1,3},{2,0},{3,1},{4,6},{5,7},{6,4},{7,5},{8,10},{9,11},{10,... | collective-permute-start | bytes 2162696 | tf_op jit(solution)/shard_map/cond/branch_1_fun/ppermute | solution.py:874
  213.3 24.8 %branch_1_fun.20 = (bf16[3,512,128]{2,1,0:T(8,128)(2,1)S(1)}, bf16[3,512,128]{2,1,0:T(8,128)(2,1)S(1)}, bf16[3,512,128]{2,1,0:T(8,128)(2,1)}, bf16[3,512,128]{2,1,0:T(8,128)(2,1)}) custom-call(s32[2]{0:T(128)S(1)} %get-tuple-element.422.idx_ref, bf16[4,2048,128]{2,1,0:T(8,128)(2,1)} %get-tuple-element.423.q_ref, ...), custom_call_target="tpu_custom_call" | custom-call | flops 10737418240 | bytes 8388608 | tf_op jit(solution)/shard_map/cond/branch_1_fun/pallas_call | solution.py:599
  238.1 5.7 %collective-permute-done.17 = bf16[352,1024]{1,0:T(8,128)(2,1)} collective-permute-done((bf16[352,1024]{1,0:T(8,128)(2,1)}, bf16[352,1024]{1,0:T(8,128)(2,1)}, u32[]{:S(2)}, u32[]{:S(2)}) %collective-permute-start.17) | collective-permute-done | bytes 720928 | tf_op jit(solution)/shard_map/cond/branch_1_fun/ppermute | solution.py:874
  243.9 3.7 %shard_map.174 = (bf16[1,192,1024]{2,1,0:T(8,128)(2,1)}, bf16[1,192,1024]{2,1,0:T(8,128)(2,1)S(1)}, bf16[1,192,1024]{2,1,0:T(8,128)(2,1)}, bf16[1,192,1024]{2,1,0:T(8,128)(2,1)}) custom-call(s32[2]{0:T(128)S(1)} %pad_add_fusion.idx_ref, bf16[2,192,1024]{2,1,0:T(8,128)(2,1)} %get-tuple-element.675.refs_0_, bf16[2,192,1024]{2,1,0:T(8,128)(2,1)} %get-tuple-element.676.refs_1_, ...), custom_call_target="tpu_custom_call" | custom-call | tf_op jit(solution)/shard_map/pallas_call | solution.py:758
  247.6 30.4 %conditional.20 = (bf16[3,512,128]{2,1,0:T(8,128)(2,1)}, bf16[3,512,128]{2,1,0:T(8,128)(2,1)}, bf16[3,512,128]{2,1,0:T(8,128)(2,1)}, bf16[1,192,1024]{2,1,0:T(8,...) conditional(s32[]{:T(128)} %convert_element_type.4, () %tuple.121, ...), branch_computations={%region_17.18_spmd, %region_18.19_spmd} | conditional | flops 10737418240 | bytes 17301804 | solution.py:868
  247.9 2.3 collective-permute-start.21
  253.3 24.4 %branch_1_fun.21 = (bf16[3,512,128]{2,1,0:T(8,128)(2,1)S(1)}, bf16[3,512,128]{2,1,0:T(8,128)(2,1)}, bf16[3,512,128]{2,1,0:T(8,128)(2,1)}, bf16[3,512,128]{2,1,0:T(8,128)(2,1)}) custom-call(s32[2]{0:T(128)S(1)} %get-tuple-element.442.idx_ref, bf16[4,2048,128]{2,1,0:T(8,128)(2,1)} %get-tuple-element.443.q_ref, bf16[4,2048,128]{2,1,0:T(8,128)(2,1)} %get-tuple-element.444.k_ref, ...), custom_call_target="tpu_custom_call" | custom-call | flops 10737418240 | bytes 8388608 | tf_op jit(solution)/shard_map/cond/branch_1_fun/pallas_call | solution.py:599
  278.1 3.0 shard_map.175
  281.0 49.2 %conditional.21 = (bf16[3,512,128]{2,1,0:T(8,128)(2,1)}, bf16[3,512,128]{2,1,0:T(8,128)(2,1)}, bf16[3,512,128]{2,1,0:T(8,128)(2,1)}, bf16[384,1024]{1,0:T(8,128)...) conditional(s32[]{:T(128)} %convert_element_type.4, () %tuple.120, ...), branch_computations={%region_19.20_spmd, %region_20.24_spmd} | conditional | flops 16385 | bytes 14402117 | solution.py:868
  281.0 6.2 %collective-permute-start.38 = (bf16[384,1024]{1,0:T(8,128)(2,1)}, bf16[384,1024]{1,0:T(8,128)(2,1)}, u32[]{:S(2)}, u32[]{:S(2)}) collective-permute-start(bf16[384,1024]{1,0:T(8,128)(2,1)} %get-tuple-element.481), channel_id=1, source_target_pairs={{0,1},{1,0},{2,3},{3,2},{4,5},{5,4},{6,7},{7,6},{8,9},{9,8},{10,11... | collective-permute-start | bytes 2359304 | tf_op jit(solution)/shard_map/cond/branch_1_fun/ppermute | solution.py:874
  287.3 2.4 collective-permute-start.36
  291.7 38.5 %conditional = (bf16[1,128,768]{2,1,0:T(8,128)(2,1)}, bf16[1,128,768]{2,1,0:T(8,128)(2,1)}, f32[2,1024]{1,0:T(2,128)}) conditional(s32[]{:T(128)} %convert_element_type.0, () %tuple.76, (s32[2]{0:T(128)S(1)}, bf16[2048,1024]{1,0:T(8,128)(2,1)}, bf16[3,1024,256]{2,1,0:T(8,128)(2,1)}, bf16[3,512,128]{2,1,0:T(8,128)(2,1)S(1)}, ...), branch_computations={%region_21.21_spmd, %region_22.0_spmd} | conditional | flops 16384 | bytes 6537472 | solution.py:868
  291.7 9.2 %branch_1_fun.22 = (bf16[4,128,768]{2,1,0:T(8,128)(2,1)}, bf16[4,128,768]{2,1,0:T(8,128)(2,1)}, f32[1024,128]{1,0:T(8,128)}) custom-call(s32[2]{0:T(128)S(1)} %get-tuple-element.457.idx_ref, bf16[2048,1024]{1,0:T(8,128)(2,1)} %get-tuple-element.458.n_ref, bf16[3,1024,256]{2,1,0:T(8,128)(2,1)} %get-tuple-element.459.w_ref, ...), custom_call_target="tpu_custom_call" | custom-call | tf_op jit(solution)/shard_map/cond/branch_1_fun/cond/branch_1_fun/pallas_call | solution.py:661
  301.0 2.6 collective-permute-done.30.refs_1_
  303.6 2.9 branch_1_fun.23
  308.2 9.7 %collective-permute-done.31.refs_1_ = bf16[2,128,768]{2,1,0:T(8,128)(2,1)S(1)} collective-permute-done((bf16[2,128,768]{2,1,0:T(8,128)(2,1)}, bf16[2,128,768]{2,1,0:T(8,128)(2,1)S(1)}, u32[]{:S(2)}, u32[]{:S(2)}) %collective-permute-start.31) | collective-permute-done | bytes 393248 | tf_op jit(solution)/shard_map/cond/branch_1_fun/cond/branch_1_fun/ppermute | solution.py:874
  318.6 2.5 branch_1_fun.24
  322.8 3.2 collective-permute-done.33
  326.3 3.3 collective-permute-done.34
  332.1 16.5 %conditional.22 = (bf16[1,128,768]{2,1,0:T(8,128)(2,1)}, bf16[96,1024]{1,0:T(8,128)(2,1)}, bf16[152,256]{1,0:T(8,128)(2,1)}, bf16[152,256]{1,0:T(8,128)(2,1)}, b...) conditional(s32[]{:T(128)} %convert_element_type.4, () %tuple.130, ...), branch_computations={%region_25.26_spmd, %region_26.27_spmd} | conditional | bytes 4296790 | solution.py:868
  332.9 2.6 collective-permute-start.27
  337.9 10.3 %branch_1_fun.25 = (f32[512,1024]{1,0:T(8,128)}, f32[2,128,1024]{2,1,0:T(8,128)}, f32[1024,128]{1,0:T(8,128)}) custom-call(s32[2]{0:T(128)S(1)} %get-tuple-element.501.idx_ref, bf16[2048,1024]{1,0:T(8,128)(2,1)} %get-tuple-element.502.x_ref, f32[512,1024]{1,0:T(8,128)S(1)} %get-tuple-element.503.gr_ref, ...), custom_call_target="tpu_custom_call" | custom-call | tf_op jit(solution)/shard_map/cond/branch_1_fun/pallas_call | solution.py:702
  348.7 4.2 %shard_map.178 = (f32[512,1024]{1,0:T(8,128)}, f32[3,128,256]{2,1,0:T(8,128)}, f32[256,128]{1,0:T(8,128)}, f32[2,1024]{1,0:T(2,128)}) custom-call(f32[512,1024]{1,0:T(8,128)} %get-tuple-element.649.resid_ref, bf16[1,128,768]{2,1,0:T(8,128)(2,1)} %get-tuple-element.692.keep_ref, bf16[1,128,768]{2,1,0:T(8,128)(2,1)} %get-tuple-element.710.got_ref, ...), custom_call_target="tpu_custom_call" | custom-call | tf_op jit(solution)/shard_map/pallas_call | solution.py:834
  (105 shorter events, 40.9 us)
Async XLA Ops:
  7.2 88.0 %all-gather.6.cloned.1.call-start = ((), (), s32[]{:S(2)}) async-start(), calls=%async_computation.3 | async-start | bytes 9437184 | tf_op jit(solution)/shard_map/all_gather | solution.py:909
  10.6 27.4 %collective-permute-start = (bf16[416,1024]{1,0:T(8,128)(2,1)}, bf16[416,1024]{1,0:T(8,128)(2,1)}, u32[]{:S(2)}, u32[]{:S(2)}) collective-permute-start(bf16[416,1024]{1,0:T(8,128)(2,1)} %get-tuple-element.306), channel_id=1, source_target_pairs={{0,1},{1,0},{2,3},{3,2},{4,5},{5,4},{6,7},{7,6},{8,9},{9,8},{10,11... | collective-permute-start | bytes 2555912 | tf_op jit(solution)/shard_map/cond/branch_1_fun/ppermute | solution.py:874
  13.7 20.5 %collective-permute-start.1 = (bf16[32,1024]{1,0:T(8,128)(2,1)S(1)}, bf16[32,1024]{1,0:T(8,128)(2,1)}, u32[]{:S(2)}, u32[]{:S(2)}) collective-permute-start(bf16[32,1024]{1,0:T(8,128)(2,1)S(1)} %get-tuple-element.307), channel_id=1, source_target_pairs={{0,2},{1,3},{2,0},{3,1},{4,6},{5,7},{6,4},{7,5},{8,10},{9,11},{10,... | collective-permute-start | bytes 196616 | tf_op jit(solution)/shard_map/cond/branch_1_fun/ppermute | solution.py:874
  16.3 21.7 %collective-permute-start.2 = (bf16[32,1024]{1,0:T(8,128)(2,1)S(1)}, bf16[32,1024]{1,0:T(8,128)(2,1)}, u32[]{:S(2)}, u32[]{:S(2)}) collective-permute-start(bf16[32,1024]{1,0:T(8,128)(2,1)S(1)} %get-tuple-element.307), channel_id=1, source_target_pairs={{0,3},{1,2},{2,1},{3,0},{4,7},{5,6},{6,5},{7,4},{8,11},{9,10},{10,... | collective-permute-start | bytes 196616 | tf_op jit(solution)/shard_map/cond/branch_1_fun/ppermute | solution.py:874
  40.2 164.0 %all-gather.4.cloned.1.call-start = ((), (), s32[]{:S(2)}) async-start(), calls=%async_computation.1 | async-start | bytes 7077888 | tf_op jit(solution)/shard_map/all_gather | solution.py:949
  40.4 54.2 %copy-start.10 = (f32[850]{0:T(1024)S(1)}, f32[850]{0:T(1024)}, u32[]{:S(2)}) copy-start(f32[850]{0:T(1024)} %param.42) | copy-start | bytes 10204
  40.4 54.8 %copy-start.2 = (bf16[1024,1024]{1,0:T(8,128)(2,1)S(1)}, bf16[1024,1024]{1,0:T(8,128)(2,1)}, u32[]{:S(2)}) copy-start(bf16[1024,1024]{1,0:T(8,128)(2,1)} %dw_ref.1) | copy-start | bytes 6291460
  40.4 29.2 %collective-permute-start.3 = (bf16[384,256]{1,0:T(8,128)(2,1)S(1)}, bf16[384,256]{1,0:T(8,128)(2,1)}, u32[]{:S(2)}, u32[]{:S(2)}) collective-permute-start(bf16[384,256]{1,0:T(8,128)(2,1)S(1)} %get-tuple-element.318), channel_id=1, source_target_pairs={{0,2},{1,3},{2,0},{3,1},{4,6},{5,7},{6,4},{7,5},{8,10},{9,11},{10,... | collective-permute-start | bytes 589832 | tf_op jit(solution)/shard_map/cond/branch_1_fun/ppermute | solution.py:874
  69.5 11.1 %collective-permute-start.4 = (bf16[512,256]{1,0:T(8,128)(2,1)}, bf16[512,256]{1,0:T(8,128)(2,1)}, u32[]{:S(2)}, u32[]{:S(2)}) collective-permute-start(bf16[512,256]{1,0:T(8,128)(2,1)} %get-tuple-element.329), channel_id=1, source_target_pairs={{0,1},{1,0},{2,3},{3,2},{4,5},{5,4},{6,7},{7,6},{8,9},{9,8},{10,11... | collective-permute-start | bytes 786440 | tf_op jit(solution)/shard_map/cond/branch_1_fun/ppermute | solution.py:874
  71.7 21.2 %collective-permute-start.5 = (bf16[512,256]{1,0:T(8,128)(2,1)S(1)}, bf16[512,256]{1,0:T(8,128)(2,1)}, u32[]{:S(2)}, u32[]{:S(2)}) collective-permute-start(bf16[512,256]{1,0:T(8,128)(2,1)S(1)} %get-tuple-element.330), channel_id=1, source_target_pairs={{0,2},{1,3},{2,0},{3,1},{4,6},{5,7},{6,4},{7,5},{8,10},{9,11},{10,... | collective-permute-start | bytes 786440 | tf_op jit(solution)/shard_map/cond/branch_1_fun/ppermute | solution.py:874
  72.6 20.3 %collective-permute-start.6 = (bf16[512,256]{1,0:T(8,128)(2,1)S(1)}, bf16[512,256]{1,0:T(8,128)(2,1)}, u32[]{:S(2)}, u32[]{:S(2)}) collective-permute-start(bf16[512,256]{1,0:T(8,128)(2,1)S(1)} %get-tuple-element.331), channel_id=1, source_target_pairs={{0,3},{1,2},{2,1},{3,0},{4,7},{5,6},{6,5},{7,4},{8,11},{9,10},{10,... | collective-permute-start | bytes 786440 | tf_op jit(solution)/shard_map/cond/branch_1_fun/ppermute | solution.py:874
  95.2 29.6 %collective-permute-start.10 = (bf16[768,256]{1,0:T(8,128)(2,1)S(1)}, bf16[768,256]{1,0:T(8,128)(2,1)}, u32[]{:S(2)}, u32[]{:S(2)}) collective-permute-start(bf16[768,256]{1,0:T(8,128)(2,1)S(1)} %get-tuple-element.335), channel_id=1, source_target_pairs={{0,1},{1,0},{2,3},{3,2},{4,5},{5,4},{6,7},{7,6},{8,9},{9,8},{10,11... | collective-permute-start | bytes 1179656 | tf_op jit(solution)/shard_map/cond/branch_1_fun/ppermute | solution.py:874
  98.5 25.6 %collective-permute-start.8 = (bf16[512,256]{1,0:T(8,128)(2,1)S(1)}, bf16[512,256]{1,0:T(8,128)(2,1)}, u32[]{:S(2)}, u32[]{:S(2)}) collective-permute-start(bf16[512,256]{1,0:T(8,128)(2,1)S(1)} %get-tuple-element.333.refs_0_), channel_id=1, source_target_pairs={{0,2},{1,3},{2,0},{3,1},{4,6},{5,7},{6,4},{7,5},{8,10},{9,11},{10,... | collective-permute-start | bytes 786440 | tf_op jit(solution)/shard_map/cond/branch_1_fun/ppermute | solution.py:874
  99.6 24.5 %collective-permute-start.7 = (bf16[512,256]{1,0:T(8,128)(2,1)S(1)}, bf16[512,256]{1,0:T(8,128)(2,1)}, u32[]{:S(2)}, u32[]{:S(2)}) collective-permute-start(bf16[512,256]{1,0:T(8,128)(2,1)S(1)} %get-tuple-element.332), channel_id=1, source_target_pairs={{0,1},{1,0},{2,3},{3,2},{4,5},{5,4},{6,7},{7,6},{8,9},{9,8},{10,11... | collective-permute-start | bytes 786440 | tf_op jit(solution)/shard_map/cond/branch_1_fun/ppermute | solution.py:874
  101.6 23.2 %collective-permute-start.9 = (bf16[512,256]{1,0:T(8,128)(2,1)}, bf16[512,256]{1,0:T(8,128)(2,1)}, u32[]{:S(2)}, u32[]{:S(2)}) collective-permute-start(bf16[512,256]{1,0:T(8,128)(2,1)} %get-tuple-element.334), channel_id=1, source_target_pairs={{0,3},{1,2},{2,1},{3,0},{4,7},{5,6},{6,5},{7,4},{8,11},{9,10},{10,... | collective-permute-start | bytes 786440 | tf_op jit(solution)/shard_map/cond/branch_1_fun/ppermute | solution.py:874
  126.9 203.3 %reduce-scatter.2.cloned.1.call-start = ((), (), s32[]{:S(2)}) async-start(), calls=%async_computation.2 | async-start | bytes 9437184 | tf_op jit(solution)/shard_map/reduce_scatter | solution.py:984
  127.0 44.7 %collective-permute-start.11 = (bf16[512,1024]{1,0:T(8,128)(2,1)}, bf16[512,1024]{1,0:T(8,128)(2,1)}, u32[]{:S(2)}, u32[]{:S(2)}) collective-permute-start(bf16[512,1024]{1,0:T(8,128)(2,1)} %get-tuple-element.354), channel_id=1, source_target_pairs={{0,2},{1,3},{2,0},{3,1},{4,6},{5,7},{6,4},{7,5},{8,10},{9,11},{10,... | collective-permute-start | bytes 3145736 | tf_op jit(solution)/shard_map/cond/branch_1_fun/ppermute | solution.py:874
  171.9 9.3 %collective-permute-start.12 = (bf16[4,384,1024]{2,1,0:T(8,128)(2,1)}, bf16[4,384,1024]{2,1,0:T(8,128)(2,1)}, u32[]{:S(2)}, u32[]{:S(2)}) collective-permute-start(bf16[4,384,1024]{2,1,0:T(8,128)(2,1)} %get-tuple-element.379), channel_id=1, source_target_pairs={{0,4},{4,0},{8,12},{12,8},{16,20},{20,16},{24,28},{28,24},{1,5},{5... | collective-permute-start | bytes 9437192 | tf_op jit(solution)/shard_map/cond/branch_1_fun/ppermute | solution.py:874
  172.0 9.2 %collective-permute-start.13 = (bf16[64,1024]{1,0:T(8,128)(2,1)}, bf16[64,1024]{1,0:T(8,128)(2,1)}, u32[]{:S(2)}, u32[]{:S(2)}) collective-permute-start(bf16[64,1024]{1,0:T(8,128)(2,1)} %get-tuple-element.380), channel_id=1, source_target_pairs={{0,2},{1,3},{2,0},{3,1},{4,6},{5,7},{6,4},{7,5},{8,10},{9,11},{10,... | collective-permute-start | bytes 393224 | tf_op jit(solution)/shard_map/cond/branch_1_fun/ppermute | solution.py:874
  181.3 20.4 %collective-permute-start.14 = (bf16[512,256]{1,0:T(8,128)(2,1)S(1)}, bf16[512,256]{1,0:T(8,128)(2,1)}, u32[]{:S(2)}, u32[]{:S(2)}) collective-permute-start(bf16[512,256]{1,0:T(8,128)(2,1)S(1)} %get-tuple-element.402), channel_id=1, source_target_pairs={{0,1},{1,0},{2,3},{3,2},{4,5},{5,4},{6,7},{7,6},{8,9},{9,8},{10,11... | collective-permute-start | bytes 786440 | tf_op jit(solution)/shard_map/cond/branch_1_fun/ppermute | solution.py:874
  182.8 21.4 %collective-permute-start.15 = (bf16[512,256]{1,0:T(8,128)(2,1)S(1)}, bf16[512,256]{1,0:T(8,128)(2,1)}, u32[]{:S(2)}, u32[]{:S(2)}) collective-permute-start(bf16[512,256]{1,0:T(8,128)(2,1)S(1)} %get-tuple-element.403), channel_id=1, source_target_pairs={{0,2},{1,3},{2,0},{3,1},{4,6},{5,7},{6,4},{7,5},{8,10},{9,11},{10,... | collective-permute-start | bytes 786440 | tf_op jit(solution)/shard_map/cond/branch_1_fun/ppermute | solution.py:874
  183.7 20.5 %collective-permute-start.16 = (bf16[512,256]{1,0:T(8,128)(2,1)S(1)}, bf16[512,256]{1,0:T(8,128)(2,1)}, u32[]{:S(2)}, u32[]{:S(2)}) collective-permute-start(bf16[512,256]{1,0:T(8,128)(2,1)S(1)} %get-tuple-element.404), channel_id=1, source_target_pairs={{0,3},{1,2},{2,1},{3,0},{4,7},{5,6},{6,5},{7,4},{8,11},{9,10},{10,... | collective-permute-start | bytes 786440 | tf_op jit(solution)/shard_map/cond/branch_1_fun/ppermute | solution.py:874
  204.7 39.2 %collective-permute-start.18 = (bf16[2,192,1024]{2,1,0:T(8,128)(2,1)}, bf16[2,192,1024]{2,1,0:T(8,128)(2,1)}, u32[]{:S(2)}, u32[]{:S(2)}) collective-permute-start(bf16[2,192,1024]{2,1,0:T(8,128)(2,1)} %get-tuple-element.420), channel_id=1, source_target_pairs={{0,16},{4,20},{8,24},{12,28},{16,0},{20,4},{24,8},{28,12},{1,17},{... | collective-permute-start | bytes 2359304 | tf_op jit(solution)/shard_map/cond/branch_1_fun/ppermute | solution.py:874
  206.2 37.7 %collective-permute-start.19 = (bf16[2,192,1024]{2,1,0:T(8,128)(2,1)}, bf16[2,192,1024]{2,1,0:T(8,128)(2,1)}, u32[]{:S(2)}, u32[]{:S(2)}) collective-permute-start(bf16[2,192,1024]{2,1,0:T(8,128)(2,1)} %get-tuple-element.421), channel_id=1, source_target_pairs={{0,8},{4,12},{8,0},{12,4},{16,24},{20,28},{24,16},{28,20},{1,9},{5... | collective-permute-start | bytes 2359304 | tf_op jit(solution)/shard_map/cond/branch_1_fun/ppermute | solution.py:874
  207.7 36.2 %collective-permute-start.17 = (bf16[352,1024]{1,0:T(8,128)(2,1)}, bf16[352,1024]{1,0:T(8,128)(2,1)}, u32[]{:S(2)}, u32[]{:S(2)}) collective-permute-start(bf16[352,1024]{1,0:T(8,128)(2,1)} %get-tuple-element.419), channel_id=1, source_target_pairs={{0,2},{1,3},{2,0},{3,1},{4,6},{5,7},{6,4},{7,5},{8,10},{9,11},{10,... | collective-permute-start | bytes 2162696 | tf_op jit(solution)/shard_map/cond/branch_1_fun/ppermute | solution.py:874
  247.8 5.5 %copy-start.7 = (bf16[512,256]{1,0:T(8,128)(2,1)}, bf16[512,256]{1,0:T(8,128)(2,1)S(1)}, u32[]{:S(2)}) copy-start(bf16[512,256]{1,0:T(8,128)(2,1)S(1)} %get-tuple-element.449.refs_0_) | copy-start | bytes 786436 | tf_op jit(solution)/shard_map/cond
  247.8 29.9 %collective-permute-start.20 = (bf16[3,512,128]{2,1,0:T(8,128)(2,1)S(1)}, bf16[3,512,128]{2,1,0:T(8,128)(2,1)}, u32[]{:S(2)}, u32[]{:S(2)}) collective-permute-start(bf16[3,512,128]{2,1,0:T(8,128)(2,1)S(1)} %get-tuple-element.437), channel_id=1, source_target_pairs={{0,1},{1,0},{2,3},{3,2},{4,5},{5,4},{6,7},{7,6},{8,9},{9,8},{10,11... | collective-permute-start | bytes 1179656 | tf_op jit(solution)/shard_map/cond/branch_1_fun/ppermute | solution.py:874
  247.9 30.2 %collective-permute-start.21 = (bf16[3,512,128]{2,1,0:T(8,128)(2,1)}, bf16[3,512,128]{2,1,0:T(8,128)(2,1)}, u32[]{:S(2)}, u32[]{:S(2)}) collective-permute-start(bf16[3,512,128]{2,1,0:T(8,128)(2,1)} %get-tuple-element.438), channel_id=1, source_target_pairs={{0,2},{1,3},{2,0},{3,1},{4,6},{5,7},{6,4},{7,5},{8,10},{9,11},{10,... | collective-permute-start | bytes 1179656 | tf_op jit(solution)/shard_map/cond/branch_1_fun/ppermute | solution.py:874
  250.1 27.9 %collective-permute-start.22 = (bf16[3,512,128]{2,1,0:T(8,128)(2,1)}, bf16[3,512,128]{2,1,0:T(8,128)(2,1)}, u32[]{:S(2)}, u32[]{:S(2)}) collective-permute-start(bf16[3,512,128]{2,1,0:T(8,128)(2,1)} %get-tuple-element.439), channel_id=1, source_target_pairs={{0,3},{1,2},{2,1},{3,0},{4,7},{5,6},{6,5},{7,4},{8,11},{9,10},{10,... | collective-permute-start | bytes 1179656 | tf_op jit(solution)/shard_map/cond/branch_1_fun/ppermute | solution.py:874
  252.2 25.8 %collective-permute-start.23 = (bf16[1,192,1024]{2,1,0:T(8,128)(2,1)S(1)}, bf16[1,192,1024]{2,1,0:T(8,128)(2,1)}, u32[]{:S(2)}, u32[]{:S(2)}) collective-permute-start(bf16[1,192,1024]{2,1,0:T(8,128)(2,1)S(1)} %get-tuple-element.440), channel_id=1, source_target_pairs={{0,8},{4,12},{8,0},{12,4},{16,24},{20,28},{24,16},{28,20},{1,9},{5... | collective-permute-start | bytes 1179656 | tf_op jit(solution)/shard_map/cond/branch_1_fun/ppermute | solution.py:874
  252.8 25.2 %collective-permute-start.24 = (bf16[1,192,1024]{2,1,0:T(8,128)(2,1)}, bf16[1,192,1024]{2,1,0:T(8,128)(2,1)}, u32[]{:S(2)}, u32[]{:S(2)}) collective-permute-start(bf16[1,192,1024]{2,1,0:T(8,128)(2,1)} %get-tuple-element.441), channel_id=1, source_target_pairs={{0,16},{4,20},{8,24},{12,28},{16,0},{20,4},{24,8},{28,12},{1,17},{... | collective-permute-start | bytes 1179656 | tf_op jit(solution)/shard_map/cond/branch_1_fun/ppermute | solution.py:874
  278.1 3.0 copy-start.9
  281.0 49.2 %collective-permute-start.38 = (bf16[384,1024]{1,0:T(8,128)(2,1)}, bf16[384,1024]{1,0:T(8,128)(2,1)}, u32[]{:S(2)}, u32[]{:S(2)}) collective-permute-start(bf16[384,1024]{1,0:T(8,128)(2,1)} %get-tuple-element.481), channel_id=1, source_target_pairs={{0,1},{1,0},{2,3},{3,2},{4,5},{5,4},{6,7},{7,6},{8,9},{9,8},{10,11... | collective-permute-start | bytes 2359304 | tf_op jit(solution)/shard_map/cond/branch_1_fun/ppermute | solution.py:874
  287.3 42.9 %collective-permute-start.35 = (bf16[3,512,128]{2,1,0:T(8,128)(2,1)}, bf16[3,512,128]{2,1,0:T(8,128)(2,1)}, u32[]{:S(2)}, u32[]{:S(2)}) collective-permute-start(bf16[3,512,128]{2,1,0:T(8,128)(2,1)} %get-tuple-element.478), channel_id=1, source_target_pairs={{0,1},{1,0},{2,3},{3,2},{4,5},{5,4},{6,7},{7,6},{8,9},{9,8},{10,11... | collective-permute-start | bytes 1179656 | tf_op jit(solution)/shard_map/cond/branch_1_fun/ppermute | solution.py:874
  287.3 42.9 %collective-permute-start.36 = (bf16[3,512,128]{2,1,0:T(8,128)(2,1)}, bf16[3,512,128]{2,1,0:T(8,128)(2,1)}, u32[]{:S(2)}, u32[]{:S(2)}) collective-permute-start(bf16[3,512,128]{2,1,0:T(8,128)(2,1)} %get-tuple-element.479), channel_id=1, source_target_pairs={{0,2},{1,3},{2,0},{3,1},{4,6},{5,7},{6,4},{7,5},{8,10},{9,11},{10,... | collective-permute-start | bytes 1179656 | tf_op jit(solution)/shard_map/cond/branch_1_fun/ppermute | solution.py:874
  289.7 40.5 %collective-permute-start.37 = (bf16[3,512,128]{2,1,0:T(8,128)(2,1)}, bf16[3,512,128]{2,1,0:T(8,128)(2,1)}, u32[]{:S(2)}, u32[]{:S(2)}) collective-permute-start(bf16[3,512,128]{2,1,0:T(8,128)(2,1)} %get-tuple-element.480), channel_id=1, source_target_pairs={{0,3},{1,2},{2,1},{3,0},{4,7},{5,6},{6,5},{7,4},{8,11},{9,10},{10,... | collective-permute-start | bytes 1179656 | tf_op jit(solution)/shard_map/cond/branch_1_fun/ppermute | solution.py:874
  300.9 2.7 collective-permute-start.30
  306.5 11.4 %collective-permute-start.31 = (bf16[2,128,768]{2,1,0:T(8,128)(2,1)}, bf16[2,128,768]{2,1,0:T(8,128)(2,1)S(1)}, u32[]{:S(2)}, u32[]{:S(2)}) collective-permute-start(bf16[2,128,768]{2,1,0:T(8,128)(2,1)} %get-tuple-element.471), channel_id=1, source_target_pairs={{0,16},{4,20},{8,24},{12,28},{16,0},{20,4},{24,8},{28,12},{1,17},{... | collective-permute-start | bytes 1179656 | tf_op jit(solution)/shard_map/cond/branch_1_fun/cond/branch_1_fun/ppermute | solution.py:874
  321.1 1.2 collective-permute-start.32
  322.3 3.7 %collective-permute-start.33 = (f32[2,1024]{1,0:T(2,128)S(1)}, f32[2,1024]{1,0:T(2,128)S(1)}, u32[]{:S(2)}, u32[]{:S(2)}) collective-permute-start(f32[2,1024]{1,0:T(2,128)S(1)} %add.12), channel_id=1, source_target_pairs={{0,8},{4,12},{8,0},{12,4},{16,24},{20,28},{24,16},{28,20},{1,9},{5... | collective-permute-start | bytes 24584 | tf_op jit(solution)/shard_map/cond/branch_1_fun/cond/branch_1_fun/ppermute | solution.py:874
  325.9 3.7 %collective-permute-start.34 = (f32[2,1024]{1,0:T(2,128)S(1)}, f32[2,1024]{1,0:T(2,128)S(1)}, u32[]{:S(2)}, u32[]{:S(2)}) collective-permute-start(f32[2,1024]{1,0:T(2,128)S(1)} %add.13), channel_id=1, source_target_pairs={{0,16},{4,20},{8,24},{12,28},{16,0},{20,4},{24,8},{28,12},{1,17},{... | collective-permute-start | bytes 24584 | tf_op jit(solution)/shard_map/cond/branch_1_fun/cond/branch_1_fun/ppermute | solution.py:874
  332.1 16.5 %copy-start.5 = (bf16[96,1024]{1,0:T(8,128)(2,1)S(1)}, bf16[96,1024]{1,0:T(8,128)(2,1)}, u32[]{:S(2)}) copy-start(bf16[96,1024]{1,0:T(8,128)(2,1)} %get-tuple-element.713.refs_2_) | copy-start | bytes 589828
  332.3 16.3 %collective-permute-start.25 = (bf16[1,128,768]{2,1,0:T(8,128)(2,1)}, bf16[1,128,768]{2,1,0:T(8,128)(2,1)}, u32[]{:S(2)}, u32[]{:S(2)}) collective-permute-start(bf16[1,128,768]{2,1,0:T(8,128)(2,1)} %get-tuple-element.496), channel_id=1, source_target_pairs={{0,8},{4,12},{8,0},{12,4},{16,24},{20,28},{24,16},{28,20},{1,9},{5... | collective-permute-start | bytes 589832 | tf_op jit(solution)/shard_map/cond/branch_1_fun/ppermute | solution.py:874
  332.9 15.8 %collective-permute-start.26 = (bf16[96,1024]{1,0:T(8,128)(2,1)}, bf16[96,1024]{1,0:T(8,128)(2,1)}, u32[]{:S(2)}, u32[]{:S(2)}) collective-permute-start(bf16[96,1024]{1,0:T(8,128)(2,1)} %get-tuple-element.497), channel_id=1, source_target_pairs={{0,2},{1,3},{2,0},{3,1},{4,6},{5,7},{6,4},{7,5},{8,10},{9,11},{10,... | collective-permute-start | bytes 589832 | tf_op jit(solution)/shard_map/cond/branch_1_fun/ppermute | solution.py:874
  332.9 15.3 %collective-permute-start.27 = (bf16[152,256]{1,0:T(8,128)(2,1)S(1)}, bf16[152,256]{1,0:T(8,128)(2,1)}, u32[]{:S(2)}, u32[]{:S(2)}) collective-permute-start(bf16[152,256]{1,0:T(8,128)(2,1)S(1)} %get-tuple-element.498), channel_id=1, source_target_pairs={{0,1},{1,0},{2,3},{3,2},{4,5},{5,4},{6,7},{7,6},{8,9},{9,8},{10,11... | collective-permute-start | bytes 233480 | tf_op jit(solution)/shard_map/cond/branch_1_fun/ppermute | solution.py:874
  335.5 13.1 %collective-permute-start.28 = (bf16[152,256]{1,0:T(8,128)(2,1)S(1)}, bf16[152,256]{1,0:T(8,128)(2,1)}, u32[]{:S(2)}, u32[]{:S(2)}) collective-permute-start(bf16[152,256]{1,0:T(8,128)(2,1)S(1)} %get-tuple-element.499), channel_id=1, source_target_pairs={{0,2},{1,3},{2,0},{3,1},{4,6},{5,7},{6,4},{7,5},{8,10},{9,11},{10,... | collective-permute-start | bytes 233480 | tf_op jit(solution)/shard_map/cond/branch_1_fun/ppermute | solution.py:874
  335.8 12.8 %collective-permute-start.29 = (bf16[152,256]{1,0:T(8,128)(2,1)S(1)}, bf16[152,256]{1,0:T(8,128)(2,1)}, u32[]{:S(2)}, u32[]{:S(2)}) collective-permute-start(bf16[152,256]{1,0:T(8,128)(2,1)S(1)} %get-tuple-element.500), channel_id=1, source_target_pairs={{0,3},{1,2},{2,1},{3,0},{4,7},{5,6},{6,5},{7,4},{8,11},{9,10},{10,... | collective-permute-start | bytes 233480 | tf_op jit(solution)/shard_map/cond/branch_1_fun/ppermute | solution.py:874
  348.6 4.2 %copy-start.1 = (bf16[256,1024]{1,0:T(8,128)(2,1)S(1)}, bf16[256,1024]{1,0:T(8,128)(2,1)}, u32[]{:S(2)}) copy-start(bf16[256,1024]{1,0:T(8,128)(2,1)} %param.38) | copy-start | bytes 1572868
  (5 other events, 8.8 us)
Sparse Core Ops, SparseCore 0:
  40.3 53.6 all-gather.5
  127.0 45.0 all-gather.3
  204.4 80.9 reduce-scatter.1

commit v7 on v6

--- a/solution.py
+++ b/solution.py
@@ -47,6 +47,58 @@
 
 def whole(shape):
     return pl.BlockSpec(shape, lambda *_: (0,) * len(shape), pipeline_mode=pl.Buffered(1))
+
+
+def staged(body, index, smalls, ins, outs, stores, scratch=()):
+    n_small, n_in, n_out = len(smalls), len(ins), len(outs)
+
+    def kernel(idx_ref, *refs):
+        refs = list(refs)
+        take = lambda n: [refs.pop(0) for _ in range(n)]
+        small, far_in, far_out = take(n_small), take(n_in), take(n_out)
+        near_in, near_out, extra = take(n_in), take(n_out), take(len(scratch))
+        sem_in, sem_out = refs
+        copies = []
+        for n, (_, _, pick) in enumerate(ins):
+            part = pick(idx_ref, far_in[n]) if pick else far_in[n]
+            copies.append(pltpu.make_async_copy(part, near_in[n], sem_in.at[n]))
+            copies[n].start()
+        there, sent = set(), []
+
+        def get(n):
+            if n not in there:
+                copies[n].wait()
+                there.add(n)
+            return near_in[n]
+
+        def put(n, part=None):
+            src, dst = near_out[n], far_out[n]
+            if part is not None:
+                src, dst = src.at[part], dst.at[part]
+            copy = pltpu.make_async_copy(src, dst, sem_out.at[len(sent)])
+            copy.start()
+            sent.append(copy)
+
+        body(idx_ref, small, get, near_out, put, extra)
+        for n in range(n_in):
+            get(n)
+        for copy in sent:
+            copy.wait()
+
+    anywhere = pl.BlockSpec(memory_space=pl.ANY)
+    specs = [smem() if a.ndim == 1 else whole(a.shape) for a in smalls]
+    return call(
+        kernel,
+        (1,),
+        specs + [anywhere] * n_in,
+        [anywhere] * n_out,
+        [sds(shape, dtype) for shape, dtype in outs],
+        scratch=[pltpu.VMEM(shape, a.dtype) for a, shape, _ in ins]
+        + [pltpu.VMEM(shape, dtype) for shape, dtype in outs]
+        + list(scratch)
+        + [pltpu.SemaphoreType.DMA((n_in,)), pltpu.SemaphoreType.DMA((stores,))],
+        prefetch=1,
+    )(index, *smalls, *[a for a, _, _ in ins])
 
 
 def smem():
@@ -278,11 +330,11 @@
     get_x.wait()
     get_ow.wait()
     piece = ow_v.shape[1] // parts
-    resid = x_v[...].astype(F32)
-    for d in range(parts):
-        get_att[d].wait()
-        at = ow_order.index(d) * piece
-        resid = resid + dot(att_v[d], ow_v[:, at : at + piece].reshape(local, width))
+    for copy in get_att:
+        copy.wait()
+    att = jnp.concatenate([att_v[d] for d in ow_order], axis=1)
+    out_w = [ow_v[:, n * piece : (n + 1) * piece].reshape(local, width) for n in range(parts)]
+    resid = x_v[...].astype(F32) + dot(att, jnp.concatenate(out_w, axis=0))
     if own:
         ffn_v[...] = resid
         store(ffn_v, outs[6], 4)
@@ -316,7 +368,9 @@
         act_v[1, :, cols] = grad_up
         act_v[2, :, cols] = hidden
         store(act_v.at[:, :, cols], outs[1].at[:, :, cols], 1 + 4 * shard)
-        grad = dot(grad_gate, gate_w, NT) + dot(grad_up, up_w, NT)
+        grad = dot(
+            jnp.concatenate([grad_gate, grad_up], axis=1), jnp.concatenate([gate_w, up_w], axis=1), NT
+        )
         term = dot(hidden, down_w, NN if shard == 0 else NT)
         if shard == 0:
             gn2_v[...] = grad
@@ -349,7 +403,7 @@
         sds((2, rows, width), BF16), sds((3, rows, 2 * hidden), BF16),
         sds((rows, width), BF16),
     ]
-    out_shape += [sds((rows * n // 16, width), BF16) for n in (2, 11, 3)]
+    out_shape += [sds((rows * n // 16, width), BF16) for n in (2, 10, 4)]
     if slot == 0:
         out_shape.append(sds((rows, width), F32))
     return call(
@@ -378,102 +432,68 @@
     )(index, lengths, picked, gains, tokens, cotangent, gate_up, down, partner, out_rows, *atts)
 
 
-def ffn_grad_kernel(sets, split, extra, cuts, idx_ref, *refs):
+def write_shares(out, total):
+    part = out.shape[-2]
+    for j in range(out.shape[0]):
+        out[j] = total[j * part : (j + 1) * part, :].astype(BF16)
+
+
+def ffn_grad_kernel(sets, *refs):
     left = refs[:sets]
     act = refs[sets : 2 * sets]
-    refs = refs[2 * sets :]
-    count = 2 if extra else 0
-    op, folds, outs = refs[:count], refs[count : count + 2 * len(cuts)], refs[count + 2 * len(cuts) :]
-    if cuts:
-        fold_kernel(cuts, idx_ref, *folds, *outs[1:])
-        outs = outs[:1]
-    step = pl.program_id(0)
-
-    def write(total):
-        part = outs[0].shape[-2]
-        if not split:
-            for j in range(outs[0].shape[0]):
-                outs[0][j] = total[j * part : (j + 1) * part, :].astype(BF16)
-            return
-        for keep in range(2):
-            for bit in range(2):
-
-                @pl.when((idx_ref[1] & 1) == bit)
-                def _():
-                    for j in range(outs[0].shape[0]):
-                        d = 2 * j + (bit if keep else 1 - bit)
-                        outs[keep][j] = total[d * part : (d + 1) * part, :].astype(BF16)
-
-    @pl.when(step < 3)
-    def _():
-        total = dot(left[0][0], act[0][0], TN)
-        for e in range(1, sets):
-            total = total + dot(left[e][0], act[e][0], TN)
-        write(total)
-
-    if extra:
-
-        @pl.when(step >= 3)
-        def _():
-            write(dot(op[0][...], op[1][...], TN))
-
-
-def ffn_grads(index, lefts, acts, shard, shares, split, grad_low=None, att_own=None, lanes=()):
+    total = dot(left[0][0], act[0][0], TN)
+    for e in range(1, sets):
+        total = total + dot(left[e][0], act[e][0], TN)
+    write_shares(refs[-1], total)
+
+
+def ffn_grads(lefts, acts, shares):
     sets = len(lefts)
     _, rows, width = lefts[0].shape
     hidden = acts[0].shape[2] // 2
     part = width // shares
-    extra = 0 if grad_low is None else att_own.shape[1] // hidden
-    steps = 3 + extra
-    specs = [pl.BlockSpec((1, rows, width), lambda c, idx: (jnp.minimum(c // 2, 1), 0, 0))] * sets
-    specs += [pl.BlockSpec((1, rows, hidden), lambda c, idx: (jnp.minimum(c, 2), 0, shard))] * sets
-    args = list(lefts) + list(acts)
-    if extra:
-        specs += [
-            pl.BlockSpec(grad_low.shape, lambda c, idx: (0, 0)),
-            pl.BlockSpec((att_own.shape[0], hidden), lambda c, idx: (0, jnp.maximum(c - 3, 0))),
-        ]
-        args += [grad_low, att_own]
-    count = shares // 2 if split else shares
-    outs = 2 if split else 1
-    out_specs = [pl.BlockSpec((count, part, hidden), lambda c, idx: (0, c, 0))] * outs
-    out_shape = [sds((count, steps * part, hidden), BF16)] * outs
-    cuts, info = [], []
-    for n, (keep, got, lead, order) in enumerate(lanes):
-        size, lane_rows, cols = keep.shape
-        lane_rows //= len(lanes)
-        block = lane_rows // 4 if lane_rows % 64 == 0 else lane_rows
-        last = lane_rows // block - 1
-        at = functools.partial(lambda n, last, c, idx: (0, n * (last + 1) + jnp.minimum(c, last), 0), n, last)
-        here = functools.partial(lambda last, c, idx: (0, jnp.minimum(c, last), 0), last)
-        specs += [pl.BlockSpec((size, block, cols), at)] * 2
-        args += [keep, got]
-        bit = order[0]
-        cuts.append((len(lead) - 1 - lead.index(bit), bit))
-        info.append(([b for b in lead if b != bit], order[1:], bit))
-        out_specs += [pl.BlockSpec((size // 2, block, cols), here)] * 2
-        out_shape += [sds((size // 2, lane_rows, cols), BF16)] * 2
-    res = call(
-        functools.partial(ffn_grad_kernel, sets, split, extra, cuts),
+    specs = [pl.BlockSpec((1, rows, width), lambda c: (c % 3 // 2, 0, 0))] * sets
+    specs += [pl.BlockSpec((1, rows, hidden), lambda c: (c % 3, 0, c // 3))] * sets
+    return call(
+        functools.partial(ffn_grad_kernel, sets),
+        (6,),
+        specs,
+        pl.BlockSpec((shares, part, hidden), lambda c: (0, c, 0)),
+        sds((shares, 6 * part, hidden), BF16),
+    )(*lefts, *acts)
+
+
+def out_grad_kernel(low_ref, *refs):
+    *att_refs, out = refs
+    each = out.shape[2] // att_refs[0].shape[1]
+    for c in range(len(att_refs) // each):
+
+        @pl.when(pl.program_id(0) == c)
+        def _():
+            rows = jnp.concatenate([ref[...] for ref in att_refs[c * each : (c + 1) * each]], axis=1)
+            write_shares(out, dot(low_ref[...], rows, TN))
+
+
+def out_grads(grad_low, att_own, shares, hidden):
+    width = grad_low.shape[1]
+    part = width // shares
+    steps = len(att_own) * att_own[0].shape[1] // hidden
+    return call(
+        out_grad_kernel,
         (steps,),
-        specs,
-        out_specs,
-        out_shape,
-        prefetch=1,
-    )(index, *args)
-    if not lanes:
-        return res
-    return res[0], [(res[1 + 2 * n], res[2 + 2 * n]) + info[n] for n in range(len(lanes))]
+        [whole(a.shape) for a in (grad_low, *att_own)],
+        pl.BlockSpec((shares, part, hidden), lambda c: (0, c, 0)),
+        sds((shares, steps * part, hidden), BF16),
+    )(grad_low, *att_own)
 
 
 def resid_kernel(ow_order, members, idx_ref, len_ref, weight_ref, cot_ref, resid_ref, ow_ref, gain_ref, *refs):
     parts = len(ow_order)
     gn2_refs = refs[:members]
-    att_refs = refs[members : members + parts]
-    gr_ref, low_ref, cat_ref, sum_ref = refs[members + parts : members + parts + 4]
-    g_refs = refs[members + parts + 4 :]
+    gr_ref, low_ref, sum_ref = refs[members : members + 3]
+    g_refs = refs[members + 3 :]
     rows, width = cot_ref.shape
-    local = att_refs[0].shape[1]
+    local = g_refs[0].shape[1]
     step = pl.program_id(0)
     first = (idx_ref[0] * pl.num_programs(0) + step) * rows
     slot = lax.broadcasted_iota(jnp.int32, (rows, 1), 0) + first
@@ -499,13 +519,11 @@
         at = ow_order.index(d) * piece
         block = ow_ref[:, at : at + piece].reshape(local, width)
         g_refs[d][...] = dot(low, block, NT).astype(BF16)
-        cat_ref[:, d * local : (d + 1) * local] = att_refs[d][...]
-
-
-def resid_back(index, lengths, picked, cotangent, resid, gn2s, out_full, gains, atts, block=256):
+
+
+def resid_back(index, lengths, picked, cotangent, resid, gn2s, out_full, gains, local, block=256):
     share, width = resid.shape
-    parts, members = len(atts), len(gn2s)
-    local = atts[0].shape[1]
+    parts, members = width // local, len(gn2s)
     out_rows, ow_row, ow_order = out_full
     ow_rows = parts * local // out_rows.shape[0]
     steps = share // block
@@ -520,13 +538,12 @@
             pl.BlockSpec((out_rows.shape[0], ow_rows, width), lambda *_: (0, ow_row // ow_rows, 0), pipeline_mode=pl.Buffered(1)),
             whole(gains.shape),
         ]
-        + [row(width)] * members
-        + [row(local)] * parts,
-        [row(width), row(width), row(parts * local), whole((8, width))] + [row(local)] * parts,
-        [sds((share, width), F32), sds((share, width), BF16), sds((share, parts * local), BF16), sds((8, width), F32)]
+        + [row(width)] * members,
+        [row(width), row(width), whole((8, width))] + [row(local)] * parts,
+        [sds((share, width), F32), sds((share, width), BF16), sds((8, width), F32)]
         + [sds((share, local), BF16)] * parts,
         prefetch=1,
-    )(index, lengths, picked, cotangent, resid, out_rows, gains, *gn2s, *atts)
+    )(index, lengths, picked, cotangent, resid, out_rows, gains, *gn2s)
 
 
 def attend_back_kernel(parts, idx_ref, q_ref, k_ref, v_ref, att_ref, cos_ref, sin_ref, *refs):
@@ -618,116 +635,114 @@
     )(index, q, k, v, att, cosine, sine, *grads)
 
 
-def project_grad_kernel(parts, pairs, idx_ref, n_ref, w_ref, *refs):
-    act_refs = refs[: parts * pairs]
-    away_ref, keep_ref, sum_ref = refs[parts * pairs :]
-    share = act_refs[0].shape[1]
-    me = idx_ref[0]
-    total = None
+def project_grads(index, normed, acts, qkv_weight, shares, pair, prev=None):
+    width = normed.shape[1]
+    local = 128 * (pair + 1)
+    parts = len(acts)
+    share = acts[0].shape[1]
+    part = width // shares
+    half = (shares // 2, part, 3 * local)
+    ins = []
     for d in range(parts):
-        rows = n_ref[pl.ds(pl.multiple_of((me ^ d) * share, share), share), :]
-        act = jnp.concatenate([act_refs[j * parts + d][0] for j in range(pairs)], axis=1)
-        term = dot(rows, act, TN)
-        total = term if total is None else total + term
-    count, part, _ = keep_ref.shape
-    for bit in range(2):
-
-        @pl.when((idx_ref[1] & 1) == bit)
-        def _():
-            for j in range(count):
-                keep, away = 2 * j + bit, 2 * j + 1 - bit
-                keep_ref[j] = total[keep * part : (keep + 1) * part, :].astype(BF16)
-                away_ref[j] = total[away * part : (away + 1) * part, :].astype(BF16)
-
-    gain_sum = jnp.sum(total * w_ref[0].astype(F32), axis=1, keepdims=True)
-
-    @pl.when(pl.program_id(0) == 0)
-    def _():
-        sum_ref[...] = jnp.broadcast_to(gain_sum, sum_ref.shape)
-
-    @pl.when(pl.program_id(0) > 0)
-    def _():
-        sum_ref[...] += jnp.broadcast_to(gain_sum, sum_ref.shape)
-
-
-def project_grads(index, normed, acts, qkv_weight, shares):
-    width = normed.shape[1]
-    local = qkv_weight.shape[2]
-    pairs, parts = len(acts), len(acts[0])
-    share = acts[0][0].shape[1]
-    flat = [a for group in acts for a in group]
-    half = (shares // 2, width // shares, 3 * local)
-    out = pl.BlockSpec(half[:2] + (local,), lambda c, idx: (0, 0, c))
-    return call(
-        functools.partial(project_grad_kernel, parts, pairs),
-        (3,),
-        [whole(normed.shape), pl.BlockSpec((1, width, local), lambda c, idx: (c, 0, 0))]
-        + [pl.BlockSpec((1, share, 128), lambda c, idx: (c, 0, 0))] * len(flat),
-        [out, out, whole((width, 128))],
-        [sds(half, BF16), sds(half, BF16), sds((width, 128), F32)],
-        prefetch=1,
-    )(index, normed, qkv_weight, *flat)
-
-
-def token_grad_kernel(order, pairs, idx_ref, x_ref, gr_ref, w_ref, gain_ref, own_ref, got_ref, *refs):
-    parts = len(order)
-    act_refs = refs[: parts * pairs]
-    out_ref, gu_ref, down_ref = refs[parts * pairs :]
-    width = x_ref.shape[1]
-    local = 128 * pairs
-    grad = jnp.zeros(x_ref.shape, F32)
-    for d in range(parts):
-        for c in range(3):
-            act = jnp.concatenate([act_refs[j * parts + d][c] for j in range(pairs)], axis=1)
-            grad = grad + dot(act, w_ref[:, order.index(d), c].reshape(width, local), NT)
-    x = x_ref[...].astype(F32)
-    factor = rms(x)
-    out_ref[...] = gr_ref[...] + norm_back(grad, gain_ref[0:1, :], x * factor, factor)
-
-    @pl.when(pl.program_id(0) == 0)
-    def _():
-        part = gu_ref.shape[1]
-        total = own_ref[: 3 * part, :].astype(F32) + got_ref[...].astype(F32)
-        gu_ref[0] = total[:part]
-        gu_ref[1] = total[part : 2 * part]
-        down_ref[...] = total[2 * part :].T
-
-
-def token_grad(index, tokens, grad_resid, qkv_full, order, gains, acts, ffn_own, ffn_got, block=256):
+        pick = functools.partial(
+            lambda d, idx, ref: ref.at[pl.ds(pl.multiple_of((idx[0] ^ d) * share, share), share)], d
+        )
+        ins += [(normed, (share, width), pick), (acts[d], acts[d].shape, None)]
+    weight_cols = pl.ds(128 * pair, 128)
+    ins.append((qkv_weight, (3, width, 128), lambda idx, ref: ref.at[:, :, weight_cols]))
+    if prev:
+        ins += [(a, a.shape, None) for a in prev]
+
+    def body(idx_ref, _, get, outs, put, scratch):
+        away_ref, keep_ref, sum_ref = outs
+        (acc,) = scratch
+        for d in range(parts):
+            act_ref = get(2 * d + 1)
+            act = jnp.concatenate([act_ref[c] for c in range(3)], axis=1)
+            term = dot(get(2 * d)[...], act, TN)
+            acc[...] = acc[...] + term if d else term
+        core = idx_ref[1] & 1
+        before = local - 128
+        for n, (ref, bit) in enumerate(((away_ref, 1 - core), (keep_ref, core))):
+            for c in range(3):
+                if prev:
+                    ref[:, :, c * local : c * local + before] = get(2 * parts + 1 + n)[
+                        :, :, c * before : (c + 1) * before
+                    ]
+                for j in range(shares // 2):
+                    rows = pl.ds(pl.multiple_of((2 * j + bit) * part, part), part)
+                    ref[j, :, c * local + before : (c + 1) * local] = acc[rows, c * 128 : (c + 1) * 128].astype(BF16)
+            put(n)
+        weight = get(2 * parts)
+        gain_sum = acc[:, :128] * weight[0].astype(F32)
+        for c in (1, 2):
+            gain_sum += acc[:, c * 128 : (c + 1) * 128] * weight[c].astype(F32)
+        total = jnp.broadcast_to(jnp.sum(gain_sum, axis=1, keepdims=True), sum_ref.shape)
+        sum_ref[...] = total + get(2 * parts + 3)[...] if prev else total
+        put(2)
+
+    outs = [(half, BF16), (half, BF16), ((width, 128), F32)]
+    return staged(body, index, [], ins, outs, 3, [pltpu.VMEM((width, 3 * 128), F32)])
+
+
+def token_grad(index, tokens, grad_resid, qkv_weight, qkv_full, gains, acts, ffn_own, ffn_got):
     share, width = grad_resid.shape
     pairs, parts = len(acts), len(acts[0])
     part, hidden = ffn_got.shape[0] // 3, ffn_got.shape[1]
-    flat = [a for group in acts for a in group]
-    steps = share // block
-    return call(
-        functools.partial(token_grad_kernel, order, pairs),
-        (steps,),
-        [
-            pl.BlockSpec((block, width), lambda i, idx: (idx[0] * steps + i, 0)),
-            pl.BlockSpec((block, width), lambda i, idx: (i, 0)),
-            whole(qkv_full.shape),
-            whole(gains.shape),
-            whole(ffn_own.shape),
-            whole(ffn_got.shape),
-        ]
-        + [pl.BlockSpec((3, block, 128), lambda i, idx: (0, i, 0))] * len(flat),
-        [pl.BlockSpec((block, width), lambda i, idx: (i, 0)), whole((2, part, hidden)), whole((hidden, part))],
-        [sds((share, width), F32), sds((2, part, hidden), F32), sds((hidden, part), F32)],
-        prefetch=1,
-    )(index, tokens, grad_resid, qkv_full, gains, ffn_own, ffn_got, *flat)
+    local = qkv_weight.shape[2]
+    ins = []
+    for d in range(parts):
+        ins += [(acts[j][d], acts[j][d].shape, None) for j in range(pairs)]
+        if d:
+            rows = pl.ds((d - 1) * 3 * part, 3 * part)
+            pick = functools.partial(lambda rows, idx, ref: ref.at[:, rows], rows)
+            ins.append((qkv_full, (qkv_full.shape[0], 3 * part, local), pick))
+        else:
+            ins.append((qkv_weight, qkv_weight.shape, None))
+        if d == 0:
+            ins.append((ffn_own, ffn_got.shape, lambda idx, ref: ref.at[pl.ds(0, 3 * part)]))
+            ins.append((ffn_got, ffn_got.shape, None))
+    ins.append((tokens, (share, width), lambda idx, ref: ref.at[pl.ds(pl.multiple_of(idx[0] * share, share), share)]))
+    ins.append((grad_resid, grad_resid.shape, None))
+
+    def body(idx_ref, smalls, get, outs, put, scratch):
+        out_ref, gu_ref, down_ref = outs
+        (acc,) = scratch
+        at = 0
+        for n in range(parts):
+            group = [get(at + j) for j in range(pairs)]
+            weight = get(at + pairs)
+            at += pairs + 1
+            act = jnp.concatenate([ref[c] for c in range(3) for ref in group], axis=1)
+            cut = lambda c: weight[:, c * part : (c + 1) * part].reshape(width, local) if n else weight[c]
+            weight_all = jnp.concatenate([cut(c) for c in range(3)], axis=1)
+            term = dot(act, weight_all, NT)
+            acc[...] = acc[...] + term if n else term
+            if n == 0:
+                total = get(at)[...].astype(F32) + get(at + 1)[...].astype(F32)
+                at += 2
+                gu_ref[0] = total[:part]
+                gu_ref[1] = total[part : 2 * part]
+                down_ref[...] = total[2 * part :].T
+                put(1)
+                put(2)
+        x_ref, gr_ref = get(at), get(at + 1)
+        half = share // 2
+        for c in range(2):
+            rows = slice(c * half, (c + 1) * half)
+            x = x_ref[rows, :].astype(F32)
+            factor = rms(x)
+            out_ref[rows, :] = gr_ref[rows, :] + norm_back(acc[rows, :], smalls[0][0:1, :], x * factor, factor)
+            put(0, pl.ds(c * half, half))
+
+    outs = [((share, width), F32), ((2, part, hidden), F32), ((hidden, part), F32)]
+    return staged(body, index, [gains], ins, outs, 4, [pltpu.VMEM((share, width), F32)])
 
 
 def fold_kernel(cuts, idx_ref, *refs):
     ins, outs = list(refs[: 2 * len(cuts)]), list(refs[2 * len(cuts) :])
-    row = 0
-    for at in cuts:
+    for place, bit in cuts:
         keep, got = ins.pop(0), ins.pop(0)
-        if at is None:
-            rows = keep.shape[1]
-            outs[0][row : row + rows, :] = (keep[0].astype(F32) + got[0].astype(F32)).astype(BF16)
-            row += rows
-            continue
-        place, bit = at
         mine = (idx_ref[1] >> bit) & 1
         targets = ((outs.pop(0), mine), (outs.pop(0), 1 - mine))
         for j in range(keep.shape[0] // 2):
@@ -737,33 +752,40 @@
                 out[j] = (keep[k].astype(F32) + got[k].astype(F32)).astype(BF16)
 
 
-def fold(index, lanes, cut_rows=False):
-    cuts, specs, args, out_shape, info, total = [], [], [], [], [], 0
-    for n, (keep, got, lead, order) in enumerate(lanes):
+def fold(index, lanes):
+    ins, outs, info, total = [], [], [], 0
+    for keep, got, lead, order in lanes:
         count, rows, cols = keep.shape
-        rows = rows // len(lanes) if cut_rows else rows
-        at = functools.partial(lambda n, i, idx: (0, n, 0), n if cut_rows else 0)
-        specs += [pl.BlockSpec((count, rows, cols), at)] * 2
-        args += [keep, got]
+        ins += [(a, a.shape, None) for a in (keep, got)]
+        if order:
+            info.append((len(lead) - 1 - lead.index(order[0]), [b for b in lead if b != order[0]], order[1:], order[0]))
+            outs += [((count // 2, rows, cols), BF16)] * 2
         total += rows
-        if order:
-            bit = order[0]
-            cuts.append((len(lead) - 1 - lead.index(bit), bit))
-            info.append(([b for b in lead if b != bit], order[1:], bit))
-            out_shape += [sds((count // 2, rows, cols), BF16)] * 2
-        else:
-            cuts.append(None)
     if not info:
-        out_shape = [sds((total, cols), BF16)]
-    res = call(
-        functools.partial(fold_kernel, cuts), (1,), specs, [whole(o.shape) for o in out_shape], out_shape, prefetch=1
-    )(index, *args)
+        outs = [((total, cols), BF16)]
+
+    def body(idx_ref, _, get, out_refs, put, __):
+        row = 0
+        for n in range(len(lanes)):
+            keep, got = get(2 * n), get(2 * n + 1)
+            if info:
+                place, _, _, bit = info[n]
+                fold_kernel([(place, bit)], idx_ref, keep, got, *out_refs[2 * n : 2 * n + 2])
+                put(2 * n)
+                put(2 * n + 1)
+            else:
+                rows = keep.shape[1]
+                out_refs[0][row : row + rows, :] = (keep[0].astype(F32) + got[0].astype(F32)).astype(BF16)
+                put(0, pl.ds(row, rows))
+                row += rows
+
+    res = staged(body, index, [], ins, outs, max(len(outs), len(lanes)))
     if not info:
         return res[0]
-    return [(res[2 * n], res[2 * n + 1]) + info[n] for n in range(len(lanes))]
-
-
-def pieces_kernel(first, part, op_ref, gains_ref, *outs):
+    return [(res[2 * n], res[2 * n + 1]) + info[n][1:] for n in range(len(lanes))]
+
+
+def pieces_kernel(part, op_ref, gains_ref, *outs):
     local = outs[0].shape[1]
     hidden = op_ref.shape[1]
     rows = (outs[0].shape[0] - part) // 3
@@ -776,68 +798,71 @@
     for d, out in enumerate(outs):
         block = d * local // hidden
         col = d * local % hidden
-        row = first + block * part
+        row = block * part
         out[:part, :] = op_ref[row : row + part, col : col + local]
         out[part:, :] = parts3
 
 
-def make_pieces(sum_a, gains, first, part, local, parts):
+def make_pieces(sum_op, gains, part, local, parts):
     shape = (part + 3 * gains.size // local, local)
     return call(
-        functools.partial(pieces_kernel, first, part),
+        functools.partial(pieces_kernel, part),
         (1,),
-        [whole(sum_a.shape), whole(gains.shape)],
+        [whole(sum_op.shape), whole(gains.shape)],
         [whole(shape)] * parts,
         [sds(shape, BF16)] * parts,
-    )(sum_a, gains)
-
-
-def finish_kernel(count, parts, resid_ref, keep_ref, got_ref, *refs):
-    own, others, refs = refs[:3], refs[3 : 3 + 3 * count], refs[3 + 3 * count :]
-    pieces, (out_ref, qkv_ref, op_ref, gains_ref) = refs[:parts], refs[parts:]
-    row = 0
-    for n in range(3):
-        rows = own[n].shape[0]
-        total = resid_ref[row : row + rows, :] + own[n][...].astype(F32)
-        for e in range(count):
-            total = total + others[n * count + e][...].astype(F32)
-        out_ref[row : row + rows, :] = total
-        row += rows
-    local = qkv_ref.shape[2]
-    qkv = keep_ref[0].astype(F32) + got_ref[0].astype(F32)
-    for c in range(3):
-        qkv_ref[c] = qkv[:, c * local : (c + 1) * local]
-    part = op_ref.shape[1]
-    rows = (pieces[0].shape[0] - part) // 3
-
-    def gains_of(ref):
-        hi, mid, low = (ref[part + n * rows : part + (n + 1) * rows, :].astype(F32) for n in range(3))
-        return hi + mid + low
-
-    ops = [ref[:part, :].astype(F32) for ref in pieces]
-    gains = [gains_of(ref) for ref in pieces]
-    while len(ops) > 1:
-        ops = [ops[2 * n] + ops[2 * n + 1] for n in range(len(ops) // 2)]
-        gains = [gains[2 * n] + gains[2 * n + 1] for n in range(len(gains) // 2)]
-    op_ref[...] = ops[0].T
-    wide = gains_ref.shape[1] // local
-    for r in range(rows):
-        gains_ref[r // wide : r // wide + 1, (r % wide) * local : (r % wide + 1) * local] = gains[0][r : r + 1, :]
-
-
-def finish_outputs(resid, own, others, keep, got, pieces):
+    )(sum_op, gains)
+
+
+def finish_outputs(index, resid, own, others, keep, got, pieces):
     parts, count = len(pieces), len(others[0])
     width = resid.shape[1]
     part, local = keep.shape[1], keep.shape[2] // 3
-    args = [resid, keep, got, *own, *[a for group in others for a in group], *pieces]
+    ins, row = [], 0
+    for n, a in enumerate(own):
+        rows = pl.ds(row, a.shape[0])
+        ins.append((resid, a.shape, functools.partial(lambda rows, idx, ref: ref.at[rows], rows)))
+        ins += [(b, a.shape, None) for b in (a, *others[n])]
+        row += a.shape[0]
+    ins += [(a, a.shape, None) for a in (keep, got, *pieces)]
+
+    def body(idx_ref, _, get, outs, put, __):
+        out_ref, qkv_ref, op_ref, gains_ref = outs
+        at = row = 0
+        for a in own:
+            total = get(at)[...]
+            for n in range(count + 1):
+                total = total + get(at + 1 + n)[...].astype(F32)
+            out_ref[row : row + a.shape[0], :] = total
+            put(0, pl.ds(row, a.shape[0]))
+            row += a.shape[0]
+            at += count + 2
+        qkv = get(at)[0].astype(F32) + get(at + 1)[0].astype(F32)
+        for c in range(3):
+            qkv_ref[c] = qkv[:, c * local : (c + 1) * local]
+        put(1)
+        piece_refs = [get(at + 2 + d) for d in range(parts)]
+        rows = (piece_refs[0].shape[0] - part) // 3
+
+        def gains_of(ref):
+            hi, mid, low = (ref[part + n * rows : part + (n + 1) * rows, :].astype(F32) for n in range(3))
+            return hi + mid + low
+
+        ops = [ref[:part, :].astype(F32) for ref in piece_refs]
+        gains = [gains_of(ref) for ref in piece_refs]
+        while len(ops) > 1:
+            ops = [ops[2 * n] + ops[2 * n + 1] for n in range(len(ops) // 2)]
+            gains = [gains[2 * n] + gains[2 * n + 1] for n in range(len(gains) // 2)]
+        op_ref[...] = ops[0].T
+        put(2)
+        wide = width // local
+        for r in range(rows):
+            cols = slice((r % wide) * local, (r % wide + 1) * local)
+            gains_ref[r // wide : r // wide + 1, cols] = gains[0][r : r + 1, :]
+        put(3)
+
     shapes = [resid.shape, (3, part, local), (local, part), (2, width)]
-    return call(
-        functools.partial(finish_kernel, count, parts),
-        (1,),
-        [whole(a.shape) for a in args],
-        [whole(shape) for shape in shapes],
-        [sds(shape, F32) for shape in shapes],
-    )(*args)
+    return staged(body, index, [], ins, [(shape, F32) for shape in shapes], len(own) + 3)
 
 
 def after(value, *others):
@@ -882,9 +907,6 @@
     bits = shares.bit_length() - 1
     lead = list(range(bits - 1, 0, -1))
 
-    def fold_first(keep, got):
-        return fold(index, [(keep, got, lead, lead), (keep, got, lead, lead[::-1])], cut_rows=True)
-
     def fold_next(halves, got):
         return fold(index, [(keep, g, left, order) for (keep, _, left, order, _), g in zip(halves, got)])
 
@@ -896,7 +918,6 @@
 
     ow_cut = cut(out_weight, dp * (local // shares), local // shares)
     qkv_cut = cut(qkv_weight, dp * part, part, 1).reshape(3 * part, local)
-    top = parts // 2
     together = hidden == width
     mine = cut_weights(index[1:], gate_up_weight, down_weight, shares, [ow_cut] if together else [])
     sends = [(ow_cut, d, "tensor") for d in range(2 if together else 1, parts)]
@@ -912,12 +933,11 @@
         partner = lax.all_gather(partner_cut, "dp", axis=0)
         out_full = (lax.all_gather(pack([ow_cut, *ow]), "dp", axis=0), 0, list(range(parts)))
 
-    (qkv_got,), (*att, att_nat, q_back) = beside(
-        [(after(qkv_cut, partner_cut), top, "tensor")], lambda: attend(index, q, k, v, parts)
-    )
-    qkv_stack, order = pack([qkv_cut, qkv_got]), [0, top]
+    sends = [(after(qkv_cut, partner_cut, picked), d, "tensor") for d in range(1, parts)]
+    qkv_got, (*att, att_nat, q_back) = beside(sends, lambda: attend(index, q, k, v, parts))
     rows_for = lambda e: outgoing([att[d ^ e] for d in range(parts)])
-    rows_now = region(lambda: [swap(*x) for x in rows_for(slots[0])])
+    rows_now, qkv_stack = beside(rows_for(slots[0]), lambda: pack(qkv_got))
+    qkv_full = lax.all_gather(qkv_stack, "dp", axis=0)
 
     lefts, acts, gn2s, terms, gn2_got = {}, {}, {}, {}, {}
     tied = tokens
@@ -930,29 +950,18 @@
             )
             if e:
                 return outs
-            away_b, keep_b = ffn_grads(
-                index, [*lefts.values(), outs[0]], [*acts.values(), outs[1]], 1, shares, True
-            )
-            return outs, keep_b, away_b
+            return outs, ffn_grads([*lefts.values(), outs[0]], [*acts.values(), outs[1]], shares)
 
         sends = rows_for(e - 2) if e else []
         if e + 2 in gn2s:
             sends.append((gn2s[e + 2], e + 2, "tensor"))
-        if len(order) < parts:
-            bit = parts // (2 * len(order))
-            sends.append((qkv_stack, bit, "tensor"))
         got, outs = beside(sends, feed)
-        if len(order) < parts:
-            qkv_stack, order = pack([qkv_stack, got.pop()]), order + [d ^ bit for d in order]
-            if len(order) == parts:
-                qkv_stack = qkv_stack.reshape(parts, 3, part, local)
-                qkv_full = lax.all_gather(qkv_stack, "dp", axis=0)
         if e + 2 in gn2s:
             gn2_got[e + 2] = got.pop()
         if e:
             rows_now = got
         else:
-            outs, keep_b, away_b = outs
+            outs, wg_ffn = outs
         lefts[e], acts[e], gn2s[e], *terms[e] = outs[:6]
         tied = after(tokens, gn2s[e])
     resid = outs[6]
@@ -962,49 +971,39 @@
         return [(terms[e][i], e, "tensor") for e in slots[:-1]]
 
     terms_got = []
-    (got_b, *got), (grad_resid, grad_low, att_own, gain_two, *grads) = beside(
-        [(away_b, 1, "dp")] + terms_out(0),
+    got, (grad_resid, grad_low, gain_two, *grads) = beside(
+        terms_out(0),
         lambda: resid_back(
-            index, lengths, picked, cotangent, resid, gn2_all, out_full, norm_gains, [att[0]] + rows_now
+            index, lengths, picked, cotangent, resid, gn2_all, out_full, norm_gains, local
         ),
     )
-    lefts, acts = [lefts[e] for e in slots], [acts[e] for e in slots]
     terms_got.append(got)
-    start = [(keep_b, got_b, lead, lead), (keep_b, got_b, lead, lead[::-1])]
-    ways = []
-
-    def grads_own():
-        wg_a, halves = ffn_grads(index, lefts, acts, 0, shares, False, grad_low, att_own, start)
-        ways[:] = [h[2:] for h in halves]
-        return wg_a, [h[:2] for h in halves]
-
-    got, (wg_a, halves) = beside(outgoing(grads), grads_own)
-    halves = [tuple(h) + way for h, way in zip(halves, ways)]
+    sum_ffn = lax.psum_scatter(wg_ffn, "dp", scatter_dimension=0, tiled=True)[0]
+    got, wg_op = beside(outgoing(grads), lambda: out_grads(grad_low, [att[0]] + rows_now, shares, hidden))
     grads_all = [grads[0]] + got
-    sum_a = lax.psum_scatter(after(wg_a, qkv_full), "dp", scatter_dimension=0, tiled=True)[0]
-    step = 0
 
     def back(j):
         return attend_back(index, grads_all, q_back, k, v, att_nat, cosine, sine, j)
 
-    got, group = beside(terms_out(1) + leaving(halves), lambda: back(0))
-    terms_got.append(got[: len(slots) - 1])
-    got = got[len(slots) - 1 :]
-    halves, step = fold_next(halves, got), step + 1
-    qkv_acts, acts_got = [group], []
+    terms_got.append([swap(after(a, wg_op), *way) for a, *way in terms_out(1)])
+    group = region(lambda: back(0))
+    group = after(group, *terms_got[1])
+    sum_op = lax.psum_scatter(after(wg_op, qkv_full), "dp", scatter_dimension=0, tiled=True)[0]
+    qkv_acts, acts_got, qkv_sums = [group], [], None
     for j in range(1, pairs):
-        now = leaving(halves) if step < bits - 1 else []
-        got, group = beside(outgoing(group) + now, lambda: back(j))
-        acts_got.append([qkv_acts[-1][0]] + got[: parts - 1])
+
+        def back_next():
+            return back(j), project_grads(index, normed, qkv_acts[-1], qkv_weight, shares, j - 1, qkv_sums)
+
+        got, (group, qkv_sums) = beside(outgoing(group), back_next)
+        acts_got.append([qkv_acts[-1][0]] + got)
         qkv_acts.append(group)
-        if now:
-            halves, step = fold_next(halves, got[parts - 1 :]), step + 1
-    while step < bits - 1:
-        halves, step = fold_next(halves, [swap(*x) for x in leaving(halves)]), step + 1
-    sum_b = halves
+    ways = []
 
     def finish():
-        away_q, keep_q, gain_one = project_grads(index, normed, qkv_acts, qkv_weight, shares)
+        away_q, keep_q, gain_one = project_grads(
+            index, normed, qkv_acts[-1], qkv_weight, shares, pairs - 1, qkv_sums
+        )
         halves = fold(index, [(keep_q, swap(away_q, 1, "dp"), lead, lead)])
         for s in range(bits - 2):
             halves = fold_next(halves, [swap(*x) for x in leaving(halves)])
@@ -1015,18 +1014,18 @@
         ways[:] = [h[2:] for h in halves]
         return [h[:2] for h in halves], gains_grad
 
-    got, (halves, gains_grad) = beside(outgoing(group) + [(sum_b, 1, "tensor")], finish, apart=True)
+    got, (halves, gains_grad) = beside(outgoing(group) + [(sum_ffn[3 * part :], 1, "tensor")], finish, apart=True)
     halves = [tuple(h) + way for h, way in zip(halves, ways)]
     acts_got.append([group[0]] + got[: parts - 1])
     got_b = got[-1]
-    pieces = make_pieces(sum_a, gains_grad, 3 * part, part, local, parts)
+    pieces = make_pieces(sum_op, gains_grad, part, local, parts)
     got, (grad_tok, grad_gu, grad_down) = beside(
         leaving(halves) + terms_out(2) + outgoing(pieces),
-        lambda: token_grad(index, tokens, grad_resid, qkv_full, order, norm_gains, acts_got, sum_a, got_b),
+        lambda: token_grad(index, tokens, grad_resid, qkv_weight, qkv_full, norm_gains, acts_got, sum_ffn, got_b),
     )
     terms_got.append(got[1 : len(slots)])
     out, grad_qkv, grad_op, gains_grad = finish_outputs(
-        resid, terms[0], terms_got, halves[0][0], got[0], [pieces[0]] + got[len(slots) :]
+        index, resid, terms[0], terms_got, halves[0][0], got[0], [pieces[0]] + got[len(slots) :]
     )
     return (out, grad_tok, grad_qkv, grad_op, grad_gu, grad_down, gains_grad)
 

time: 367 us -> 355 us (0.967)
  Pallas kernels: 212 us -> 199 us
  waiting for transfers between devices: 72.3 us -> 68.5 us
  local copies, waits for them, and re-layouts: 2.36 us -> 6.12 us
    pallas_call x10 -> x9, Pallas kernels: 65.9 us -> 54.9 us  [the longest x6 29.6 us: staged(): call(kernel, (1,), specs + [anywhere] * n_in, [anywhere] * n_out, [sds(sh...]
    ppermute x39 -> x35, waiting for transfers between devices: 72.2 us -> 68.4 us  [swap(): lax.ppermute(a, name, [(i, i ^ d) for i in range(lax.axis_size(name))])]
    ppermute x39 -> x35, starting transfers between devices: 54.3 us -> 55.6 us  [swap(): lax.ppermute(a, name, [(i, i ^ d) for i in range(lax.axis_size(name))])]
  transfers between devices with their start and end apart: 42 -> 39, of which waited for: 16 -> 15; matrix products, arithmetic and copies ran while one was open for 1% -> 1% of each run, Pallas kernels for 56% -> 54%
where the time goes in v7:
time: 355 us; the launch traced here: 348 us
  Pallas kernels  199 us (56%)
  waiting for transfers between devices  68.5 us (19%)
  starting transfers between devices  55.7 us (16%)
  between operations  15.8 us (4%)
  local copies, waits for them, and re-layouts  6.12 us (2%)
    ppermute x35, waiting for transfers between devices, swap(): lax.ppermute(a, name, [(i, i ^ d) for i in range(lax.axis_size(name))])  68.4 us
    ppermute x35, starting transfers between devices, swap(): lax.ppermute(a, name, [(i, i ^ d) for i in range(lax.axis_size(name))])  55.6 us
    pallas_call x2, Pallas kernels, attend_back(): call(functools.partial(attend_back_kernel, parts), (parts,), [pl.BlockSpe...  48.8 us
    pallas_call x2, Pallas kernels, feed_forward(): call(functools.partial(ffn_kernel, parts, ow_row, ow_order, slot), (1,),...  42.9 us
    pallas_call x6, Pallas kernels, staged(): call(kernel, (1,), specs + [anywhere] * n_in, [anywhere] * n_out, [sds(sh...  29.6 us
    pallas_call x1, Pallas kernels, attend(): call(functools.partial(attend_kernel, min(sub, share), parts), (heads //...  29.3 us
    pallas_call x1, Pallas kernels, ffn_grads(): call(functools.partial(ffn_grad_kernel, sets), (6,), specs, pl.BlockSpec(...  19.2 us
    pallas_call x1, Pallas kernels, project(): call(qkv_kernel, (rows // block,), [smem(), pl.BlockSpec((block, width),...  9.95 us
  transfers between devices with their start and end apart: 39, of which 15 were waited for; matrix products, arithmetic and copies ran while one was open for 1% of the time, Pallas kernels for 54%

profile of v7, /device:TPU:0, one launch (start us, length us, event | category | flops | bytes accessed | tf_op | source)
XLA Modules:
  0.0 348.1 jit_solution(4585904231279897772)
XLA Ops:
  8.3 2.3 shard_map.171
  10.6 27.4 %conditional.12 = (bf16[416,1024]{1,0:T(8,128)(2,1)}, bf16[32,1024]{1,0:T(8,128)(2,1)}, bf16[32,1024]{1,0:T(8,128)(2,1)}, bf16[4,2048,128]{2,1,0:T(8,128)(2,1)},...) conditional(s32[]{:T(128)} %convert_element_type.4, () %tuple.114, ...), branch_computations={%region_0.1_spmd, %region_1.2_spmd} | conditional | bytes 11468870 | solution.py:893
  10.6 3.1 collective-permute-start
  13.7 2.6 collective-permute-start.1
  16.3 9.9 %branch_1_fun.15 = (bf16[4,2048,128]{2,1,0:T(8,128)(2,1)}, bf16[4,2048,128]{2,1,0:T(8,128)(2,1)}, bf16[4,2048,128]{2,1,0:T(8,128)(2,1)}, bf16[2048,1024]{1,0:T(8,128)(2,1)}) custom-call(s32[1]{0:T(128)} %get-tuple-element.297.len_ref, bf16[2048,1024]{1,0:T(8,128)(2,1)} %get-tuple-element.298.x_ref, bf16[3,1024,256]{2,1,0:T(8,128)(2,1)S(1)} %get-tuple-element.299.w_ref, ...), custom_call_target="tpu_custom_call" | custom-call | tf_op jit(solution)/shard_map/cond/branch_1_fun/pallas_call | solution.py:187
  26.2 8.0 %collective-permute-done.1 = bf16[32,1024]{1,0:T(8,128)(2,1)} collective-permute-done((bf16[32,1024]{1,0:T(8,128)(2,1)S(1)}, bf16[32,1024]{1,0:T(8,128)(2,1)}, u32[]{:S(2)}, u32[]{:S(2)}) %collective-permute-start.1) | collective-permute-done | bytes 65568 | tf_op jit(solution)/shard_map/cond/branch_1_fun/ppermute | solution.py:899
  34.2 3.7 %collective-permute-done.2 = bf16[32,1024]{1,0:T(8,128)(2,1)} collective-permute-done((bf16[32,1024]{1,0:T(8,128)(2,1)S(1)}, bf16[32,1024]{1,0:T(8,128)(2,1)}, u32[]{:S(2)}, u32[]{:S(2)}) %collective-permute-start.2) | collective-permute-done | bytes 65568 | tf_op jit(solution)/shard_map/cond/branch_1_fun/ppermute | solution.py:899
  41.6 33.8 %conditional.13 = (bf16[384,256]{1,0:T(8,128)(2,1)}, bf16[384,256]{1,0:T(8,128)(2,1)}, bf16[384,256]{1,0:T(8,128)(2,1)}, bf16[512,256]{1,0:T(8,128)(2,1)S(1)}, b...) conditional(s32[]{:T(128)} %convert_element_type.4, () %tuple.113, ...), branch_computations={%region_3.4_spmd, %region_4.5_spmd} | conditional | bytes 4784218 | solution.py:893
  46.0 29.3 %branch_1_fun.16 = (bf16[512,256]{1,0:T(8,128)(2,1)S(1)}, bf16[512,256]{1,0:T(8,128)(2,1)S(1)}, bf16[512,256]{1,0:T(8,128)(2,1)S(1)}, bf16[512,256]{1,0:T(8,128)...) custom-call(s32[2]{0:T(128)S(1)} %get-tuple-element.308.idx_ref, ...), custom_call_target="tpu_custom_call" | custom-call | tf_op jit(solution)/shard_map/cond/branch_1_fun/pallas_call | solution.py:237
  75.4 20.6 %conditional.14 = (bf16[512,256]{1,0:T(8,128)(2,1)}, bf16[512,256]{1,0:T(8,128)(2,1)}, bf16[512,256]{1,0:T(8,128)(2,1)}, bf16[1152,256]{1,0:T(8,128)(2,1)S(1)}) conditional(s32[]{:T(128)} %convert_element_type.4, () %tuple.118, (bf16[512,256]{1,0:T(8,128)(2,1)}, bf16[512,256]{1,0:T(8,128)(2,1)S(1)}, bf16[512,256]{1,0:T(8,128)(2,1)S(1)}, ...), branch_computations={%region_5.6_spmd, %region_6.7_spmd} | conditional | bytes 3145880 | solution.py:893
  77.5 2.4 collective-permute-start.8
  81.0 6.2 %collective-permute-done.6 = bf16[512,256]{1,0:T(8,128)(2,1)} collective-permute-done((bf16[512,256]{1,0:T(8,128)(2,1)}, bf16[512,256]{1,0:T(8,128)(2,1)}, u32[]{:S(2)}, u32[]{:S(2)}) %collective-permute-start.6) | collective-permute-done | bytes 262176 | tf_op jit(solution)/shard_map/cond/branch_1_fun/ppermute | solution.py:899
  87.3 8.7 %collective-permute-done.7 = bf16[512,256]{1,0:T(8,128)(2,1)} collective-permute-done((bf16[512,256]{1,0:T(8,128)(2,1)S(1)}, bf16[512,256]{1,0:T(8,128)(2,1)}, u32[]{:S(2)}, u32[]{:S(2)}) %collective-permute-start.7) | collective-permute-done | bytes 262176 | tf_op jit(solution)/shard_map/cond/branch_1_fun/ppermute | solution.py:899
  96.9 28.1 %conditional.15 = (bf16[512,256]{1,0:T(8,128)(2,1)}, bf16[512,256]{1,0:T(8,128)(2,1)}, bf16[512,256]{1,0:T(8,128)(2,1)}, bf16[2,512,1024]{2,1,0:T(8,128)(2,1)}, ...) conditional(s32[]{:T(128)} %convert_element_type.4, () %tuple.112, ...), branch_computations={%region_7.8_spmd, %region_8.9_spmd} | conditional | bytes 11272282 | solution.py:893
  97.2 3.8 %collective-permute-start.10 = (bf16[512,256]{1,0:T(8,128)(2,1)S(1)}, bf16[512,256]{1,0:T(8,128)(2,1)}, u32[]{:S(2)}, u32[]{:S(2)}) collective-permute-start(bf16[512,256]{1,0:T(8,128)(2,1)S(1)} %get-tuple-element.325.refs_0_), channel_id=1, source_target_pairs={{0,2},{1,3},{2,0},{3,1},{4,6},{5,7},{6,4},{7,5},{8,10},{9,11},{10,... | collective-permute-start | bytes 786440 | tf_op jit(solution)/shard_map/cond/branch_1_fun/ppermute | solution.py:899
  101.0 2.8 collective-permute-start.11
  103.8 21.2 %branch_1_fun.18 = (bf16[2,512,1024]{2,1,0:T(8,128)(2,1)}, bf16[3,512,2048]{2,1,0:T(8,128)(2,1)}, bf16[512,1024]{1,0:T(8,128)(2,1)}, bf16[64,1024]{1,0:T(8,128)(...) custom-call(s32[2]{0:T(128)S(1)} %get-tuple-element.327.idx_ref, s32[1]{0:T(128)} %get-tuple-element.328.len_ref, ...), custom_call_target="tpu_custom_call" | custom-call | tf_op jit(solution)/shard_map/cond/branch_1_fun/pallas_call | solution.py:409
  125.0 46.2 %conditional.16 = (bf16[512,1024]{1,0:T(8,128)(2,1)}, bf16[2,512,1024]{2,1,0:T(8,128)(2,1)}, bf16[3,512,2048]{2,1,0:T(8,128)(2,1)}, bf16[512,1024]{1,0:T(8,128)(...) conditional(s32[]{:T(128)} %convert_element_type.4, () %tuple.111, ...), branch_computations={%region_9.10_spmd, %region_10.11_spmd} | conditional | bytes 26214492 | solution.py:893
  127.4 21.7 %branch_1_fun.19 = (bf16[2,512,1024]{2,1,0:T(8,128)(2,1)}, bf16[3,512,2048]{2,1,0:T(8,128)(2,1)}, bf16[512,1024]{1,0:T(8,128)(2,1)}, bf16[64,1024]{1,0:T(8,128)(...) custom-call(s32[2]{0:T(128)S(1)} %get-tuple-element.346.idx_ref, ...), custom_call_target="tpu_custom_call" | custom-call | tf_op jit(solution)/shard_map/cond/branch_1_fun/pallas_call | solution.py:409
  149.1 19.2 %branch_1_fun.20 = bf16[8,768,1024]{2,1,0:T(8,128)(2,1)} custom-call(bf16[2,512,1024]{2,1,0:T(8,128)(2,1)} %get-tuple-element.366.refs_0_, bf16[2,512,1024]{2,1,0:T(8,128)(2,1)} %get-tuple-element.770.refs_1_, bf16[3,512,2048]{2,1,0:T(8,128)(2,1)} %get-tuple-element.367.refs_2_, bf16[3,512,2048]{2,1,0:T(8,128)(2,1)} %get-tuple-element.771.refs_3_), custom_call_target="tpu_custom_call" | custom-call | tf_op jit(solution)/shard_map/cond/branch_1_fun/pallas_call | solution.py:457
  168.3 2.7 collective-permute-done.12
  172.1 7.6 %conditional.17 = (bf16[64,1024]{1,0:T(8,128)(2,1)}, f32[512,1024]{1,0:T(8,128)}, bf16[512,1024]{1,0:T(8,128)(2,1)}, f32[8,1024]{1,0:T(8,128)}, bf16[512,256]{1,...) conditional(s32[]{:T(128)} %convert_element_type.4, () %tuple.124, ...), branch_computations={%region_11.12_spmd, %region_12.13_spmd} | conditional | bytes 4358228 | solution.py:893
  172.1 7.6 %branch_1_fun.21 = (f32[512,1024]{1,0:T(8,128)}, bf16[512,1024]{1,0:T(8,128)(2,1)}, f32[8,1024]{1,0:T(8,128)}, bf16[512,256]{1,0:T(8,128)(2,1)S(1)}, bf16[512,25...) custom-call(s32[2]{0:T(128)S(1)} %get-tuple-element.369.idx_ref, ...), custom_call_target="tpu_custom_call" | custom-call | tf_op jit(solution)/shard_map/cond/branch_1_fun/pallas_call | solution.py:531
  179.7 23.4 %conditional.18 = (bf16[512,256]{1,0:T(8,128)(2,1)}, bf16[512,256]{1,0:T(8,128)(2,1)}, bf16[512,256]{1,0:T(8,128)(2,1)}, bf16[8,128,1024]{2,1,0:T(8,128)(2,1)}) conditional(s32[]{:T(128)} %convert_element_type.4, () %tuple.126, (bf16[512,256]{1,0:T(8,128)(2,1)S(1)}, bf16[512,256]{1,0:T(8,128)(2,1)S(1)}, bf16[512,256]{1,0:T(8,128)(2,1)S(1)}, ...), branch_computations={%region_13.14_spmd, %region_14.15_spmd} | conditional | bytes 3145880 | solution.py:893
  184.4 4.5 %branch_1_fun.22 = bf16[8,128,1024]{2,1,0:T(8,128)(2,1)} custom-call(bf16[512,1024]{1,0:T(8,128)(2,1)} %get-tuple-element.388.low_ref, bf16[512,256]{1,0:T(8,128)(2,1)S(1)} %get-tuple-element.389.refs_0_, bf16[512,256]{1,0:T(8,128)(2,1)} %get-tuple-element.390.refs_1_, bf16[512,256]{1,0:T(8,128)(2,1)} %get-tuple-element.391.refs_2_, ...), custom_call_target="tpu_custom_call" | custom-call | tf_op jit(solution)/shard_map/cond/branch_1_fun/pallas_call | solution.py:481
  190.7 12.4 %collective-permute-done.15 = bf16[512,256]{1,0:T(8,128)(2,1)} collective-permute-done((bf16[512,256]{1,0:T(8,128)(2,1)S(1)}, bf16[512,256]{1,0:T(8,128)(2,1)}, u32[]{:S(2)}, u32[]{:S(2)}) %collective-permute-start.15) | collective-permute-done | bytes 262176 | tf_op jit(solution)/shard_map/cond/branch_1_fun/ppermute | solution.py:899
  203.1 4.9 %collective-permute-start.34 = (bf16[320,1024]{1,0:T(8,128)(2,1)}, bf16[320,1024]{1,0:T(8,128)(2,1)}, u32[]{:S(2)}, u32[]{:S(2)}) collective-permute-start(bf16[320,1024]{1,0:T(8,128)(2,1)} %get-tuple-element.640), channel_id=1, source_target_pairs={{0,2},{1,3},{2,0},{3,1},{4,6},{5,7},{6,4},{7,5},{8,10},{9,11},{10,... | collective-permute-start | bytes 1966088 | tf_op jit(solution)/shard_map/ppermute | solution.py:899
  208.1 24.3 %conditional.19 = ((bf16[3,512,128]{2,1,0:T(8,128)(2,1)S(1)}, bf16[3,512,128]{2,1,0:T(8,128)(2,1)}, bf16[3,512,128]{2,1,0:T(8,128)(2,1)}, bf16[3,512,128]{2,1,0:T(8,128)(2,1)})) conditional(s32[]{:T(128)} %convert_element_type.4, () %tuple.132, (s32[2]{0:T(128)S(1)}, bf16[4,2048,128]{2,1,0:T(8,128)(2,1)}, bf16[4,2048,128]{2,1,0:T(8,128)(2,1)}, ...), branch_computations={%region_15.16_spmd, %region_16.17_spmd} | conditional | flops 10737418240 | bytes 8388616 | solution.py:893
  208.1 24.3 %branch_1_fun.23 = (bf16[3,512,128]{2,1,0:T(8,128)(2,1)S(1)}, bf16[3,512,128]{2,1,0:T(8,128)(2,1)}, bf16[3,512,128]{2,1,0:T(8,128)(2,1)}, bf16[3,512,128]{2,1,0:T(8,128)(2,1)}) custom-call(s32[2]{0:T(128)S(1)} %get-tuple-element.393.idx_ref, bf16[4,2048,128]{2,1,0:T(8,128)(2,1)} %get-tuple-element.394.q_ref, bf16[4,2048,128]{2,1,0:T(8,128)(2,1)} %get-tuple-element.395.k_ref, ...), custom_call_target="tpu_custom_call" | custom-call | flops 10737418240 | bytes 8388608 | tf_op jit(solution)/shard_map/cond/branch_1_fun/pallas_call | solution.py:616
  234.4 34.8 %conditional.20 = (bf16[3,512,128]{2,1,0:T(8,128)(2,1)}, bf16[3,512,128]{2,1,0:T(8,128)(2,1)}, bf16[3,512,128]{2,1,0:T(8,128)(2,1)}, bf16[3,512,128]{2,1,0:T(8,1...) conditional(s32[]{:T(128)} %convert_element_type.4, () %tuple.131, ...), branch_computations={%region_17.18_spmd, %region_18.19_spmd} | conditional | flops 10737418240 | bytes 14156004 | solution.py:893
  234.7 2.5 collective-permute-start.18
  239.1 24.5 %branch_1_fun.24 = (bf16[3,512,128]{2,1,0:T(8,128)(2,1)S(1)}, bf16[3,512,128]{2,1,0:T(8,128)(2,1)}, bf16[3,512,128]{2,1,0:T(8,128)(2,1)}, bf16[3,512,128]{2,1,0:T(8,128)(2,1)}) custom-call(s32[2]{0:T(128)S(1)} %get-tuple-element.407.idx_ref, bf16[4,2048,128]{2,1,0:T(8,128)(2,1)} %get-tuple-element.408.q_ref, bf16[4,2048,128]{2,1,0:T(8,128)(2,1)} %get-tuple-element.409.k_ref, ...), custom_call_target="tpu_custom_call" | custom-call | flops 10737418240 | bytes 8388608 | tf_op jit(solution)/shard_map/cond/branch_1_fun/pallas_call | solution.py:616
  263.5 5.6 %branch_1_fun.25 = (bf16[4,128,384]{2,1,0:T(8,128)(2,1)}, bf16[4,128,384]{2,1,0:T(8,128)(2,1)}, f32[1024,128]{1,0:T(8,128)S(1)}) custom-call(s32[2]{0:T(128)S(1)} %get-tuple-element.407.idx_ref, bf16[2048,1024]{1,0:T(8,128)(2,1)} %get-tuple-element.422.refs_0_.refs_2_.refs_4_.refs_6_, bf16[3,512,128]{2,1,0:T(8,128)(2,1)S(1)} %get-tuple-element.423.refs_1_, ...), custom_call_target="tpu_custom_call" | custom-call | tf_op jit(solution)/shard_map/cond/branch_1_fun/pallas_call | solution.py:90
  271.3 44.8 %conditional.21 = (bf16[3,512,128]{2,1,0:T(8,128)(2,1)}, bf16[3,512,128]{2,1,0:T(8,128)(2,1)}, bf16[3,512,128]{2,1,0:T(8,128)(2,1)}, bf16[384,1024]{1,0:T(8,128)...) conditional(s32[]{:T(128)} %convert_element_type.4, () %tuple.130, ...), branch_computations={%region_20.21_spmd, %region_21.25_spmd} | conditional | flops 16385 | bytes 14533209 | solution.py:893
  271.3 2.7 collective-permute-start.33
  275.9 2.4 collective-permute-start.32
  278.3 37.4 %conditional = (bf16[1,128,768]{2,1,0:T(8,128)(2,1)}, bf16[1,128,768]{2,1,0:T(8,128)(2,1)}, f32[2,1024]{1,0:T(2,128)}) conditional(s32[]{:T(128)} %convert_element_type.0, () %tuple.76, (s32[2]{0:T(128)S(1)}, bf16[2048,1024]{1,0:T(8,128)(2,1)}, bf16[3,512,128]{2,1,0:T(8,128)(2,1)S(1)}, bf16[3,512,128]{2,1,0:T(8,128)(2,1)}, ...), branch_computations={%region_22.22_spmd, %region_23.0_spmd} | conditional | flops 16384 | bytes 6668572 | solution.py:893
  278.3 6.0 %branch_1_fun.26 = (bf16[4,128,768]{2,1,0:T(8,128)(2,1)}, bf16[4,128,768]{2,1,0:T(8,128)(2,1)}, f32[1024,128]{1,0:T(8,128)}) custom-call(s32[2]{0:T(128)S(1)} %get-tuple-element.428.idx_ref, bf16[2048,1024]{1,0:T(8,128)(2,1)} %get-tuple-element.429.refs_0_.refs_2_.refs_4_.refs_6_, bf16[3,512,128]{2,1,0:T(8,128)(2,1)S(1)} %get-tuple-element.430.refs_1_, ...), custom_call_target="tpu_custom_call" | custom-call | tf_op jit(solution)/shard_map/cond/branch_1_fun/cond/branch_1_fun/pallas_call | solution.py:90
  284.5 2.6 collective-permute-done.25.refs_1_
  287.1 2.9 branch_1_fun.27
  292.5 10.8 %collective-permute-done.26.refs_1_ = bf16[2,128,768]{2,1,0:T(8,128)(2,1)S(1)} collective-permute-done((bf16[2,128,768]{2,1,0:T(8,128)(2,1)}, bf16[2,128,768]{2,1,0:T(8,128)(2,1)S(1)}, u32[]{:S(2)}, u32[]{:S(2)}) %collective-permute-start.26) | collective-permute-done | bytes 393248 | tf_op jit(solution)/shard_map/cond/branch_1_fun/cond/branch_1_fun/ppermute | solution.py:899
  304.0 2.5 branch_1_fun.28
  311.9 3.2 collective-permute-done.29
  317.7 19.5 %conditional.22 = (bf16[1,128,768]{2,1,0:T(8,128)(2,1)}, bf16[128,1024]{1,0:T(8,128)(2,1)}, bf16[152,256]{1,0:T(8,128)(2,1)}, bf16[152,256]{1,0:T(8,128)(2,1)}, ...) conditional(s32[]{:T(128)} %convert_element_type.4, () %tuple.129, ...), branch_computations={%region_26.27_spmd, %region_27.28_spmd} | conditional | bytes 4362326 | solution.py:893
  323.5 2.4 collective-permute-start.24
  325.9 8.7 %branch_1_fun.29 = (f32[512,1024]{1,0:T(8,128)}, f32[2,128,1024]{2,1,0:T(8,128)}, f32[1024,128]{1,0:T(8,128)}) custom-call(s32[2]{0:T(128)S(1)} %get-tuple-element.470.idx_ref, f32[2,1024]{1,0:T(2,128)S(1)} %get-tuple-element.471.refs_0_, bf16[3,512,128]{2,1,0:T(8,128)(2,1)S(1)} %get-tuple-element.472.refs_1_, ...), custom_call_target="tpu_custom_call" | custom-call | tf_op jit(solution)/shard_map/cond/branch_1_fun/pallas_call | solution.py:90
  334.6 2.6 collective-permute-done.23
  337.3 3.8 %shard_map.174 = (f32[512,1024]{1,0:T(8,128)}, f32[3,128,256]{2,1,0:T(8,128)}, f32[256,128]{1,0:T(8,128)}, f32[2,1024]{1,0:T(2,128)}) custom-call(s32[2]{0:T(128)S(1)} %pad_add_fusion.idx_ref, f32[512,1024]{1,0:T(8,128)S(1)} %get-tuple-element.627.refs_0_.refs_3_.refs_6_, bf16[64,1024]{1,0:T(8,128)(2,1)S(1)} %copy-done.8, ...), custom_call_target="tpu_custom_call" | custom-call | tf_op jit(solution)/shard_map/pallas_call | solution.py:90
  (107 shorter events, 46.1 us)
Async XLA Ops:
  7.2 89.7 %all-gather.5.cloned.1.call-start = ((), (), s32[]{:S(2)}) async-start(), calls=%async_computation.4 | async-start | bytes 9437184 | tf_op jit(solution)/shard_map/all_gather | solution.py:930
  8.2 2.3 copy-start.2
  8.2 2.3 copy-start.6
  10.6 27.4 %collective-permute-start = (bf16[416,1024]{1,0:T(8,128)(2,1)}, bf16[416,1024]{1,0:T(8,128)(2,1)}, u32[]{:S(2)}, u32[]{:S(2)}) collective-permute-start(bf16[416,1024]{1,0:T(8,128)(2,1)} %get-tuple-element.295), channel_id=1, source_target_pairs={{0,1},{1,0},{2,3},{3,2},{4,5},{5,4},{6,7},{7,6},{8,9},{9,8},{10,11... | collective-permute-start | bytes 2555912 | tf_op jit(solution)/shard_map/cond/branch_1_fun/ppermute | solution.py:899
  13.7 20.5 %collective-permute-start.1 = (bf16[32,1024]{1,0:T(8,128)(2,1)S(1)}, bf16[32,1024]{1,0:T(8,128)(2,1)}, u32[]{:S(2)}, u32[]{:S(2)}) collective-permute-start(bf16[32,1024]{1,0:T(8,128)(2,1)S(1)} %get-tuple-element.296), channel_id=1, source_target_pairs={{0,2},{1,3},{2,0},{3,1},{4,6},{5,7},{6,4},{7,5},{8,10},{9,11},{10,... | collective-permute-start | bytes 196616 | tf_op jit(solution)/shard_map/cond/branch_1_fun/ppermute | solution.py:899
  16.3 21.7 %collective-permute-start.2 = (bf16[32,1024]{1,0:T(8,128)(2,1)S(1)}, bf16[32,1024]{1,0:T(8,128)(2,1)}, u32[]{:S(2)}, u32[]{:S(2)}) collective-permute-start(bf16[32,1024]{1,0:T(8,128)(2,1)S(1)} %get-tuple-element.296), channel_id=1, source_target_pairs={{0,3},{1,2},{2,1},{3,0},{4,7},{5,6},{6,5},{7,4},{8,11},{9,10},{10,... | collective-permute-start | bytes 196616 | tf_op jit(solution)/shard_map/cond/branch_1_fun/ppermute | solution.py:899
  37.9 3.0 copy-start.14
  40.2 162.9 %all-gather.7.cloned.1.call-start = ((), (), s32[]{:S(2)}) async-start(), calls=%async_computation.5 | async-start | bytes 5308416 | tf_op jit(solution)/shard_map/all_gather | solution.py:940
  41.6 33.8 %collective-permute-start.3 = (bf16[384,256]{1,0:T(8,128)(2,1)S(1)}, bf16[384,256]{1,0:T(8,128)(2,1)}, u32[]{:S(2)}, u32[]{:S(2)}) collective-permute-start(bf16[384,256]{1,0:T(8,128)(2,1)S(1)} %get-tuple-element.307), channel_id=1, source_target_pairs={{0,1},{1,0},{2,3},{3,2},{4,5},{5,4},{6,7},{7,6},{8,9},{9,8},{10,11... | collective-permute-start | bytes 589832 | tf_op jit(solution)/shard_map/cond/branch_1_fun/ppermute | solution.py:899
  41.7 33.7 %collective-permute-start.4 = (bf16[384,256]{1,0:T(8,128)(2,1)S(1)}, bf16[384,256]{1,0:T(8,128)(2,1)}, u32[]{:S(2)}, u32[]{:S(2)}) collective-permute-start(bf16[384,256]{1,0:T(8,128)(2,1)S(1)} %get-tuple-element.307), channel_id=1, source_target_pairs={{0,2},{1,3},{2,0},{3,1},{4,6},{5,7},{6,4},{7,5},{8,10},{9,11},{10,... | collective-permute-start | bytes 589832 | tf_op jit(solution)/shard_map/cond/branch_1_fun/ppermute | solution.py:899
  43.8 31.6 %collective-permute-start.5 = (bf16[384,256]{1,0:T(8,128)(2,1)S(1)}, bf16[384,256]{1,0:T(8,128)(2,1)}, u32[]{:S(2)}, u32[]{:S(2)}) collective-permute-start(bf16[384,256]{1,0:T(8,128)(2,1)S(1)} %get-tuple-element.307), channel_id=1, source_target_pairs={{0,3},{1,2},{2,1},{3,0},{4,7},{5,6},{6,5},{7,4},{8,11},{9,10},{10,... | collective-permute-start | bytes 589832 | tf_op jit(solution)/shard_map/cond/branch_1_fun/ppermute | solution.py:899
  75.4 21.5 %copy-start.3 = (bf16[1024,1024]{1,0:T(8,128)(2,1)S(1)}, bf16[1024,1024]{1,0:T(8,128)(2,1)}, u32[]{:S(2)}) copy-start(bf16[1024,1024]{1,0:T(8,128)(2,1)} %dw_ref.1) | copy-start | bytes 6291460
  75.4 11.9 %collective-permute-start.6 = (bf16[512,256]{1,0:T(8,128)(2,1)}, bf16[512,256]{1,0:T(8,128)(2,1)}, u32[]{:S(2)}, u32[]{:S(2)}) collective-permute-start(bf16[512,256]{1,0:T(8,128)(2,1)} %get-tuple-element.318), channel_id=1, source_target_pairs={{0,1},{1,0},{2,3},{3,2},{4,5},{5,4},{6,7},{7,6},{8,9},{9,8},{10,11... | collective-permute-start | bytes 786440 | tf_op jit(solution)/shard_map/cond/branch_1_fun/ppermute | solution.py:899
  75.5 20.5 %collective-permute-start.7 = (bf16[512,256]{1,0:T(8,128)(2,1)S(1)}, bf16[512,256]{1,0:T(8,128)(2,1)}, u32[]{:S(2)}, u32[]{:S(2)}) collective-permute-start(bf16[512,256]{1,0:T(8,128)(2,1)S(1)} %get-tuple-element.319), channel_id=1, source_target_pairs={{0,2},{1,3},{2,0},{3,1},{4,6},{5,7},{6,4},{7,5},{8,10},{9,11},{10,... | collective-permute-start | bytes 786440 | tf_op jit(solution)/shard_map/cond/branch_1_fun/ppermute | solution.py:899
  77.5 18.5 %collective-permute-start.8 = (bf16[512,256]{1,0:T(8,128)(2,1)S(1)}, bf16[512,256]{1,0:T(8,128)(2,1)}, u32[]{:S(2)}, u32[]{:S(2)}) collective-permute-start(bf16[512,256]{1,0:T(8,128)(2,1)S(1)} %get-tuple-element.320), channel_id=1, source_target_pairs={{0,3},{1,2},{2,1},{3,0},{4,7},{5,6},{6,5},{7,4},{8,11},{9,10},{10,... | collective-permute-start | bytes 786440 | tf_op jit(solution)/shard_map/cond/branch_1_fun/ppermute | solution.py:899
  96.9 172.3 %reduce-scatter.3.cloned.1.call-start = ((), (), s32[]{:S(2)}) async-start(), calls=%async_computation.2 | async-start | bytes 14155776 | tf_op jit(solution)/shard_map/reduce_scatter | solution.py:981
  97.2 27.8 %collective-permute-start.10 = (bf16[512,256]{1,0:T(8,128)(2,1)S(1)}, bf16[512,256]{1,0:T(8,128)(2,1)}, u32[]{:S(2)}, u32[]{:S(2)}) collective-permute-start(bf16[512,256]{1,0:T(8,128)(2,1)S(1)} %get-tuple-element.325.refs_0_), channel_id=1, source_target_pairs={{0,2},{1,3},{2,0},{3,1},{4,6},{5,7},{6,4},{7,5},{8,10},{9,11},{10,... | collective-permute-start | bytes 786440 | tf_op jit(solution)/shard_map/cond/branch_1_fun/ppermute | solution.py:899
  101.0 24.0 %collective-permute-start.11 = (bf16[512,256]{1,0:T(8,128)(2,1)}, bf16[512,256]{1,0:T(8,128)(2,1)}, u32[]{:S(2)}, u32[]{:S(2)}) collective-permute-start(bf16[512,256]{1,0:T(8,128)(2,1)} %get-tuple-element.326), channel_id=1, source_target_pairs={{0,3},{1,2},{2,1},{3,0},{4,7},{5,6},{6,5},{7,4},{8,11},{9,10},{10,... | collective-permute-start | bytes 786440 | tf_op jit(solution)/shard_map/cond/branch_1_fun/ppermute | solution.py:899
  103.8 21.2 %collective-permute-start.9 = (bf16[512,256]{1,0:T(8,128)(2,1)S(1)}, bf16[512,256]{1,0:T(8,128)(2,1)}, u32[]{:S(2)}, u32[]{:S(2)}) collective-permute-start(bf16[512,256]{1,0:T(8,128)(2,1)S(1)} %get-tuple-element.324), channel_id=1, source_target_pairs={{0,1},{1,0},{2,3},{3,2},{4,5},{5,4},{6,7},{7,6},{8,9},{9,8},{10,11... | collective-permute-start | bytes 786440 | tf_op jit(solution)/shard_map/cond/branch_1_fun/ppermute | solution.py:899
  125.5 45.5 %collective-permute-start.12 = (bf16[512,1024]{1,0:T(8,128)(2,1)}, bf16[512,1024]{1,0:T(8,128)(2,1)}, u32[]{:S(2)}, u32[]{:S(2)}) collective-permute-start(bf16[512,1024]{1,0:T(8,128)(2,1)} %get-tuple-element.345), channel_id=1, source_target_pairs={{0,2},{1,3},{2,0},{3,1},{4,6},{5,7},{6,4},{7,5},{8,10},{9,11},{10,... | collective-permute-start | bytes 3145736 | tf_op jit(solution)/shard_map/cond/branch_1_fun/ppermute | solution.py:899
  171.2 144.9 %reduce-scatter.5.cloned.1.call-start = ((), (), s32[]{:S(2)}) async-start(), calls=%async_computation.3 | async-start | bytes 2359296 | tf_op jit(solution)/shard_map/reduce_scatter | solution.py:991
  172.1 7.6 %collective-permute-start.13 = (bf16[64,1024]{1,0:T(8,128)(2,1)S(1)}, bf16[64,1024]{1,0:T(8,128)(2,1)}, u32[]{:S(2)}, u32[]{:S(2)}) collective-permute-start(bf16[64,1024]{1,0:T(8,128)(2,1)S(1)} %get-tuple-element.368), channel_id=1, source_target_pairs={{0,2},{1,3},{2,0},{3,1},{4,6},{5,7},{6,4},{7,5},{8,10},{9,11},{10,... | collective-permute-start | bytes 393224 | tf_op jit(solution)/shard_map/cond/branch_1_fun/ppermute | solution.py:899
  179.7 11.0 %collective-permute-start.14 = (bf16[512,256]{1,0:T(8,128)(2,1)S(1)}, bf16[512,256]{1,0:T(8,128)(2,1)}, u32[]{:S(2)}, u32[]{:S(2)}) collective-permute-start(bf16[512,256]{1,0:T(8,128)(2,1)S(1)} %get-tuple-element.385), channel_id=1, source_target_pairs={{0,1},{1,0},{2,3},{3,2},{4,5},{5,4},{6,7},{7,6},{8,9},{9,8},{10,11... | collective-permute-start | bytes 786440 | tf_op jit(solution)/shard_map/cond/branch_1_fun/ppermute | solution.py:899
  182.0 21.1 %collective-permute-start.15 = (bf16[512,256]{1,0:T(8,128)(2,1)S(1)}, bf16[512,256]{1,0:T(8,128)(2,1)}, u32[]{:S(2)}, u32[]{:S(2)}) collective-permute-start(bf16[512,256]{1,0:T(8,128)(2,1)S(1)} %get-tuple-element.386), channel_id=1, source_target_pairs={{0,2},{1,3},{2,0},{3,1},{4,6},{5,7},{6,4},{7,5},{8,10},{9,11},{10,... | collective-permute-start | bytes 786440 | tf_op jit(solution)/shard_map/cond/branch_1_fun/ppermute | solution.py:899
  182.9 20.2 %collective-permute-start.16 = (bf16[512,256]{1,0:T(8,128)(2,1)S(1)}, bf16[512,256]{1,0:T(8,128)(2,1)}, u32[]{:S(2)}, u32[]{:S(2)}) collective-permute-start(bf16[512,256]{1,0:T(8,128)(2,1)S(1)} %get-tuple-element.387), channel_id=1, source_target_pairs={{0,3},{1,2},{2,1},{3,0},{4,7},{5,6},{6,5},{7,4},{8,11},{9,10},{10,... | collective-permute-start | bytes 786440 | tf_op jit(solution)/shard_map/cond/branch_1_fun/ppermute | solution.py:899
  203.1 31.3 %collective-permute-start.34 = (bf16[320,1024]{1,0:T(8,128)(2,1)}, bf16[320,1024]{1,0:T(8,128)(2,1)}, u32[]{:S(2)}, u32[]{:S(2)}) collective-permute-start(bf16[320,1024]{1,0:T(8,128)(2,1)} %get-tuple-element.640), channel_id=1, source_target_pairs={{0,2},{1,3},{2,0},{3,1},{4,6},{5,7},{6,4},{7,5},{8,10},{9,11},{10,... | collective-permute-start | bytes 1966088 | tf_op jit(solution)/shard_map/ppermute | solution.py:899
  234.6 4.5 %copy-start.10 = (bf16[512,256]{1,0:T(8,128)(2,1)}, bf16[512,256]{1,0:T(8,128)(2,1)S(1)}, u32[]{:S(2)}) copy-start(bf16[512,256]{1,0:T(8,128)(2,1)S(1)} %get-tuple-element.414.refs_0_) | copy-start | bytes 786436 | tf_op jit(solution)/shard_map/cond
  234.6 34.5 %collective-permute-start.17 = (bf16[3,512,128]{2,1,0:T(8,128)(2,1)}, bf16[3,512,128]{2,1,0:T(8,128)(2,1)}, u32[]{:S(2)}, u32[]{:S(2)}) collective-permute-start(bf16[3,512,128]{2,1,0:T(8,128)(2,1)} %get-tuple-element.404.refs_3_), channel_id=1, source_target_pairs={{0,1},{1,0},{2,3},{3,2},{4,5},{5,4},{6,7},{7,6},{8,9},{9,8},{10,11... | collective-permute-start | bytes 1179656 | tf_op jit(solution)/shard_map/cond/branch_1_fun/ppermute | solution.py:899
  234.7 34.5 %collective-permute-start.18 = (bf16[3,512,128]{2,1,0:T(8,128)(2,1)}, bf16[3,512,128]{2,1,0:T(8,128)(2,1)}, u32[]{:S(2)}, u32[]{:S(2)}) collective-permute-start(bf16[3,512,128]{2,1,0:T(8,128)(2,1)} %get-tuple-element.405.refs_5_), channel_id=1, source_target_pairs={{0,2},{1,3},{2,0},{3,1},{4,6},{5,7},{6,4},{7,5},{8,10},{9,11},{10,... | collective-permute-start | bytes 1179656 | tf_op jit(solution)/shard_map/cond/branch_1_fun/ppermute | solution.py:899
  237.2 32.0 %collective-permute-start.19 = (bf16[3,512,128]{2,1,0:T(8,128)(2,1)}, bf16[3,512,128]{2,1,0:T(8,128)(2,1)}, u32[]{:S(2)}, u32[]{:S(2)}) collective-permute-start(bf16[3,512,128]{2,1,0:T(8,128)(2,1)} %get-tuple-element.406.refs_7_), channel_id=1, source_target_pairs={{0,3},{1,2},{2,1},{3,0},{4,7},{5,6},{6,5},{7,4},{8,11},{9,10},{10,... | collective-permute-start | bytes 1179656 | tf_op jit(solution)/shard_map/cond/branch_1_fun/ppermute | solution.py:899
  271.3 44.6 %collective-permute-start.33 = (bf16[384,1024]{1,0:T(8,128)(2,1)}, bf16[384,1024]{1,0:T(8,128)(2,1)}, u32[]{:S(2)}, u32[]{:S(2)}) collective-permute-start(bf16[384,1024]{1,0:T(8,128)(2,1)} %get-tuple-element.451), channel_id=1, source_target_pairs={{0,1},{1,0},{2,3},{3,2},{4,5},{5,4},{6,7},{7,6},{8,9},{9,8},{10,11... | collective-permute-start | bytes 2359304 | tf_op jit(solution)/shard_map/cond/branch_1_fun/ppermute | solution.py:899
  273.9 41.8 %collective-permute-start.30 = (bf16[3,512,128]{2,1,0:T(8,128)(2,1)}, bf16[3,512,128]{2,1,0:T(8,128)(2,1)}, u32[]{:S(2)}, u32[]{:S(2)}) collective-permute-start(bf16[3,512,128]{2,1,0:T(8,128)(2,1)} %get-tuple-element.448), channel_id=1, source_target_pairs={{0,1},{1,0},{2,3},{3,2},{4,5},{5,4},{6,7},{7,6},{8,9},{9,8},{10,11... | collective-permute-start | bytes 1179656 | tf_op jit(solution)/shard_map/cond/branch_1_fun/ppermute | solution.py:899
  274.0 41.8 %collective-permute-start.31 = (bf16[3,512,128]{2,1,0:T(8,128)(2,1)}, bf16[3,512,128]{2,1,0:T(8,128)(2,1)}, u32[]{:S(2)}, u32[]{:S(2)}) collective-permute-start(bf16[3,512,128]{2,1,0:T(8,128)(2,1)} %get-tuple-element.449), channel_id=1, source_target_pairs={{0,2},{1,3},{2,0},{3,1},{4,6},{5,7},{6,4},{7,5},{8,10},{9,11},{10,... | collective-permute-start | bytes 1179656 | tf_op jit(solution)/shard_map/cond/branch_1_fun/ppermute | solution.py:899
  275.9 40.0 %collective-permute-start.32 = (bf16[3,512,128]{2,1,0:T(8,128)(2,1)}, bf16[3,512,128]{2,1,0:T(8,128)(2,1)}, u32[]{:S(2)}, u32[]{:S(2)}) collective-permute-start(bf16[3,512,128]{2,1,0:T(8,128)(2,1)} %get-tuple-element.450), channel_id=1, source_target_pairs={{0,3},{1,2},{2,1},{3,0},{4,7},{5,6},{6,5},{7,4},{8,11},{9,10},{10,... | collective-permute-start | bytes 1179656 | tf_op jit(solution)/shard_map/cond/branch_1_fun/ppermute | solution.py:899
  284.4 8.1 %copy-start.13 = (f32[8,1024]{1,0:T(8,128)S(1)}, f32[8,1024]{1,0:T(8,128)}, u32[]{:S(2)}) copy-start(f32[8,1024]{1,0:T(8,128)} %get-tuple-element.446) | copy-start | bytes 98308 | tf_op jit(solution)/shard_map/cond/branch_1_fun/cond
  284.4 2.7 collective-permute-start.25
  290.0 13.3 %collective-permute-start.26 = (bf16[2,128,768]{2,1,0:T(8,128)(2,1)}, bf16[2,128,768]{2,1,0:T(8,128)(2,1)S(1)}, u32[]{:S(2)}, u32[]{:S(2)}) collective-permute-start(bf16[2,128,768]{2,1,0:T(8,128)(2,1)} %get-tuple-element.441), channel_id=1, source_target_pairs={{0,16},{4,20},{8,24},{12,28},{16,0},{20,4},{24,8},{28,12},{1,17},{... | collective-permute-start | bytes 1179656 | tf_op jit(solution)/shard_map/cond/branch_1_fun/cond/branch_1_fun/ppermute | solution.py:899
  306.6 1.2 collective-permute-start.27
  307.8 3.7 %collective-permute-start.28 = (f32[2,1024]{1,0:T(2,128)S(1)}, f32[2,1024]{1,0:T(2,128)S(1)}, u32[]{:S(2)}, u32[]{:S(2)}) collective-permute-start(f32[2,1024]{1,0:T(2,128)S(1)} %add.14), channel_id=1, source_target_pairs={{0,8},{4,12},{8,0},{12,4},{16,24},{20,28},{24,16},{28,20},{1,9},{5... | collective-permute-start | bytes 24584 | tf_op jit(solution)/shard_map/cond/branch_1_fun/cond/branch_1_fun/ppermute | solution.py:899
  311.5 3.7 %collective-permute-start.29 = (f32[2,1024]{1,0:T(2,128)S(1)}, f32[2,1024]{1,0:T(2,128)S(1)}, u32[]{:S(2)}, u32[]{:S(2)}) collective-permute-start(f32[2,1024]{1,0:T(2,128)S(1)} %add.15), channel_id=1, source_target_pairs={{0,16},{4,20},{8,24},{12,28},{16,0},{20,4},{24,8},{28,12},{1,17},{... | collective-permute-start | bytes 24584 | tf_op jit(solution)/shard_map/cond/branch_1_fun/cond/branch_1_fun/ppermute | solution.py:899
  317.7 19.5 %copy-start.7 = (bf16[128,1024]{1,0:T(8,128)(2,1)S(1)}, bf16[128,1024]{1,0:T(8,128)(2,1)}, u32[]{:S(2)}) copy-start(bf16[128,1024]{1,0:T(8,128)(2,1)} %get-tuple-element.641.refs_7_) | copy-start | bytes 786436
  317.7 19.5 %copy-start.8 = (bf16[64,1024]{1,0:T(8,128)(2,1)S(1)}, bf16[64,1024]{1,0:T(8,128)(2,1)}, u32[]{:S(2)}) copy-start(bf16[64,1024]{1,0:T(8,128)(2,1)} %get-tuple-element.628.refs_1_) | copy-start | bytes 393220
  317.7 19.5 %collective-permute-start.21 = (bf16[128,1024]{1,0:T(8,128)(2,1)}, bf16[128,1024]{1,0:T(8,128)(2,1)}, u32[]{:S(2)}, u32[]{:S(2)}) collective-permute-start(bf16[128,1024]{1,0:T(8,128)(2,1)} %get-tuple-element.466), channel_id=1, source_target_pairs={{0,2},{1,3},{2,0},{3,1},{4,6},{5,7},{6,4},{7,5},{8,10},{9,11},{10,... | collective-permute-start | bytes 786440 | tf_op jit(solution)/shard_map/cond/branch_1_fun/ppermute | solution.py:899
  320.0 17.2 %collective-permute-start.20 = (bf16[1,128,768]{2,1,0:T(8,128)(2,1)}, bf16[1,128,768]{2,1,0:T(8,128)(2,1)}, u32[]{:S(2)}, u32[]{:S(2)}) collective-permute-start(bf16[1,128,768]{2,1,0:T(8,128)(2,1)} %get-tuple-element.465), channel_id=1, source_target_pairs={{0,8},{4,12},{8,0},{12,4},{16,24},{20,28},{24,16},{28,20},{1,9},{5... | collective-permute-start | bytes 589832 | tf_op jit(solution)/shard_map/cond/branch_1_fun/ppermute | solution.py:899
  321.5 13.1 %collective-permute-start.22 = (bf16[152,256]{1,0:T(8,128)(2,1)S(1)}, bf16[152,256]{1,0:T(8,128)(2,1)}, u32[]{:S(2)}, u32[]{:S(2)}) collective-permute-start(bf16[152,256]{1,0:T(8,128)(2,1)S(1)} %get-tuple-element.467), channel_id=1, source_target_pairs={{0,1},{1,0},{2,3},{3,2},{4,5},{5,4},{6,7},{7,6},{8,9},{9,8},{10,11... | collective-permute-start | bytes 233480 | tf_op jit(solution)/shard_map/cond/branch_1_fun/ppermute | solution.py:899
  323.0 14.3 %collective-permute-start.23 = (bf16[152,256]{1,0:T(8,128)(2,1)S(1)}, bf16[152,256]{1,0:T(8,128)(2,1)}, u32[]{:S(2)}, u32[]{:S(2)}) collective-permute-start(bf16[152,256]{1,0:T(8,128)(2,1)S(1)} %get-tuple-element.468), channel_id=1, source_target_pairs={{0,2},{1,3},{2,0},{3,1},{4,6},{5,7},{6,4},{7,5},{8,10},{9,11},{10,... | collective-permute-start | bytes 233480 | tf_op jit(solution)/shard_map/cond/branch_1_fun/ppermute | solution.py:899
  323.5 13.7 %collective-permute-start.24 = (bf16[152,256]{1,0:T(8,128)(2,1)S(1)}, bf16[152,256]{1,0:T(8,128)(2,1)}, u32[]{:S(2)}, u32[]{:S(2)}) collective-permute-start(bf16[152,256]{1,0:T(8,128)(2,1)S(1)} %get-tuple-element.469), channel_id=1, source_target_pairs={{0,3},{1,2},{2,1},{3,0},{4,7},{5,6},{6,5},{7,4},{8,11},{9,10},{10,... | collective-permute-start | bytes 233480 | tf_op jit(solution)/shard_map/cond/branch_1_fun/ppermute | solution.py:899
  337.3 3.9 %copy-start.1 = (bf16[256,1024]{1,0:T(8,128)(2,1)S(1)}, bf16[256,1024]{1,0:T(8,128)(2,1)}, u32[]{:S(2)}) copy-start(bf16[256,1024]{1,0:T(8,128)(2,1)} %param.38) | copy-start | bytes 1572868
  (6 other events, 7.8 us)
Sparse Core Ops, SparseCore 0:
  40.3 53.5 all-gather.4
  97.0 40.7 all-gather.6
  171.4 91.4 reduce-scatter.2
  266.0 45.7 reduce-scatter.4
